TPU v7x, 32 devices: a whole 2x2x4 slice. The times are simulated.
32 devices in a mesh: dp: 4 (over x, core), ctx: 8 (over z, y).
Axes of the slice: x: 2, y: 2, z: 4, core: 2. Of those that a mesh axis runs over, the one named last changes fastest.
Arguments:
- tokens: bfloat16 [8, 1024, 1152], P('dp', 'ctx'), may hold values from -6 to 6
- lengths: int32 [8], P('dp'), may hold values from 256 to 1024, as said below
- w_qkv: float32 [1536, 1152], P('ctx', 'dp'), may hold values from -0.1875 to 0.1875
- w_out: float32 [1024, 1152], P('ctx', 'dp'), may hold values from -0.1875 to 0.1875
- w_gate_up: float32 [13824, 1152], P('ctx', 'dp'), may hold values from -0.1875 to 0.1875
- w_down: float32 [6912, 1152], P('ctx', 'dp'), may hold values from -0.078125 to 0.078125
- gains: float32 [5120], P(('dp', 'ctx')), may hold values from -0.5 to 0.5
- cotangent: bfloat16 [8, 1024, 1152], P('dp', 'ctx'), may hold values from -6 to 6
Outputs:
- result: bfloat16 [8, 1024, 1152], P('dp', 'ctx')
- grad_input: float32 [8, 1024, 1152], P('dp', 'ctx')
- grad_qkv: float32 [1536, 1152], P('ctx', 'dp')
- grad_out: float32 [1024, 1152], P('ctx', 'dp')
- grad_gate_up: float32 [13824, 1152], P('ctx', 'dp')
- grad_down: float32 [6912, 1152], P('ctx', 'dp')
- grad_gains: float32 [5120], P(('dp', 'ctx'))
Inputs may be any that keep to these rules, and one draw needn't show every extreme that they name: `lengths`: in every group of 2 sequences held by one index of dp, one sequence has length 1024.
All inputs are finite; a program needn't handle non-finite values.
Results may differ from a plain program's by a relative error of at most 0.02.
Values may be sent and summed in bfloat16 or wider, within the bound.
A program may use at most 256 MiB of HBM per device.

v0:
```python
from functools import partial
import math

import jax
import jax.numpy as jnp
from jax import lax
from jax.sharding import PartitionSpec as P

D = 1152
HEADS = 4
HD = 256
WINDOW = 512


EPS = 1e-06
BIG = 1e30


def shifted(value, axis, steps):
    count = lax.axis_size(axis)
    leading, last = (max(0, -steps), min(count, count - steps))
    return lax.ppermute(value, axis, [(source, source + steps) for source in range(leading, last)])


def norm_scaled(v, gain):
    return v * lax.rsqrt(jnp.mean(v * v, axis=-1, keepdims=True) + EPS) * (1.0 + gain)


def rotate(v, angle):
    half = v.shape[-1] // 2
    cosine = jnp.cos(angle)
    sine = jnp.sin(angle)
    first = v[..., :half]
    second = v[..., half:]
    return jnp.concatenate(
        [first * cosine - second * sine, second * cosine + first * sine], axis=-1
    )


def angles_of(positions):
    inverse = 1.0 / 10000.0 ** (jnp.arange(HD // 2, dtype=jnp.float32) * (2.0 / HD))
    return positions.astype(jnp.float32)[:, None] * inverse[None, :]


def head_inputs(projected, gain_query, gain_key, angle):
    query = projected[..., : HEADS * HD].reshape(projected.shape[:-1] + (HEADS, HD))
    key_rows = projected[..., HEADS * HD : (HEADS + 1) * HD]
    value_rows = projected[..., (HEADS + 1) * HD :]
    query = rotate(norm_scaled(query, gain_query), angle[:, None, :])
    key_rows = rotate(norm_scaled(key_rows, gain_key), angle)
    return (query, key_rows, value_rows)


def gate_times_up(gate_up):
    paired = gate_up.reshape(gate_up.shape[:-1] + (gate_up.shape[-1] // 2, 2))
    return jax.nn.gelu(paired[..., 0], approximate=True) * paired[..., 1]


def contract(left, right, dims_left, dims_right):
    return lax.dot_general(
        left, right, ((dims_left, dims_right), ((), ())), preferred_element_type=jnp.float32
    )


def per_device(tokens, lengths, w_qkv, w_out, w_gate_up, w_down, gains, cotangent):
    seq_count = tokens.shape[0]
    local_len = tokens.shape[1]
    reach = (WINDOW - 1) // local_len + 1
    scale = 1.0 / math.sqrt(HD)
    attn_masters = (
        w_qkv.astype(jnp.bfloat16),
        w_out.astype(jnp.bfloat16),
        gains.astype(jnp.bfloat16),
    )
    row_qkv, row_out, row_gain = (
        lax.all_gather(attn_masters[0], "ctx", axis=0, tiled=True),
        lax.all_gather(attn_masters[1], "ctx", axis=0, tiled=True),
        lax.all_gather(attn_masters[2], "ctx", axis=0, tiled=True),
    )
    full_qkv, full_out, gain_low = (
        lax.all_gather(row_qkv, "dp", axis=1, tiled=True),
        lax.all_gather(row_out, "dp", axis=1, tiled=True),
        lax.all_gather(row_gain, "dp", axis=0, tiled=True),
    )
    ffn_masters = (w_gate_up.astype(jnp.bfloat16), w_down.astype(jnp.bfloat16))
    tall_gate_up, tall_down = (
        lax.all_gather(ffn_masters[0], "ctx", axis=0, tiled=True),
        lax.all_gather(ffn_masters[1], "ctx", axis=0, tiled=True),
    )
    share_gate_up, share_down = (
        lax.all_gather(tall_gate_up, "dp", axis=1, tiled=True),
        lax.all_gather(tall_down, "dp", axis=1, tiled=True),
    )
    gain_all = gain_low.astype(jnp.float32)
    gain_in = gain_all[:D]
    gain_attn = gain_all[D : 2 * D]
    gain_pre = gain_all[2 * D : 3 * D]
    gain_post = gain_all[3 * D : 4 * D]
    gain_query = gain_all[4 * D : 4 * D + HD]
    gain_key = gain_all[4 * D + HD :]
    offset = lax.axis_index("ctx") * local_len
    positions = offset + jnp.arange(local_len, dtype=jnp.int32)
    angle = angles_of(positions)
    valid = positions[None, :] < lengths[:, None]
    inputs = tokens.astype(jnp.float32)
    normed_in, pull_in = jax.vjp(norm_scaled, inputs, gain_in)
    normed_low = normed_in.astype(jnp.bfloat16)
    projected = contract(normed_low, full_qkv, (2,), (1,))
    (query, key_rot, value_rows), pull_heads = jax.vjp(
        partial(head_inputs, angle=angle), projected, gain_query, gain_key
    )
    query_low = query.astype(jnp.bfloat16)
    own_pair = jnp.concatenate(
        [key_rot.astype(jnp.bfloat16), value_rows.astype(jnp.bfloat16)], axis=-1
    )
    earlier = []
    for distance in range(reach, 0, -1):
        earlier.append(shifted(own_pair, "ctx", distance))
    key_pairs = jnp.concatenate(earlier + [own_pair], axis=1)
    keys_low = key_pairs[..., :HD]
    values_low = key_pairs[..., HD:]
    key_pos = offset - reach * local_len + jnp.arange((reach + 1) * local_len, dtype=jnp.int32)
    key_grid = key_pos[None, None, :]
    query_grid = positions[None, :, None]
    allowed = (
        (key_grid >= 0)
        & (key_grid <= query_grid)
        & (query_grid - key_grid < WINDOW)
        & ((key_grid < lengths[:, None, None]) | (key_grid == query_grid))
    )

    def scores_of():
        raw = jnp.einsum("schd,skd->shck", query_low, keys_low, preferred_element_type=jnp.float32)
        return jnp.where(allowed[:, None], raw * scale, -BIG)

    scores = scores_of()
    top = jnp.max(scores, axis=-1, keepdims=True)
    expo = jnp.exp(scores - top)
    total = jnp.sum(expo, axis=-1, keepdims=True)
    probs = expo / total
    log_total = top + jnp.log(total)
    probs_low = probs.astype(jnp.bfloat16)
    attended = jnp.einsum(
        "shck,skd->schd", probs_low, values_low, preferred_element_type=jnp.float32
    )
    attended_low = attended.reshape(seq_count, local_len, HEADS * HD).astype(jnp.bfloat16)
    out_proj = contract(attended_low, full_out, (2,), (0,))
    normed_out, pull_out = jax.vjp(norm_scaled, out_proj, gain_attn)
    mixed = inputs + normed_out
    normed_mid, pull_mid = jax.vjp(norm_scaled, mixed, gain_pre)
    mid_low = normed_mid.astype(jnp.bfloat16)
    gate_up = contract(mid_low, share_gate_up, (2,), (1,))
    hidden, pull_act = jax.vjp(gate_times_up, gate_up)
    hidden_low = hidden.astype(jnp.bfloat16)
    down = contract(hidden_low, share_down, (2,), (0,))
    normed_down, pull_down = jax.vjp(norm_scaled, down, gain_post)
    result = jnp.where(valid[..., None], mixed + normed_down, 0.0).astype(jnp.bfloat16)
    upstream = jnp.where(valid[..., None], cotangent.astype(jnp.float32), 0.0)
    grad_down_in, grad_gain_post = pull_down(upstream)
    down_low = grad_down_in.astype(jnp.bfloat16)
    grad_hidden = contract(down_low, share_down, (2,), (1,))
    grad_w_down = contract(hidden_low, down_low, (0, 1), (0, 1))
    (grad_gate_up,) = pull_act(grad_hidden)
    gate_up_low = grad_gate_up.astype(jnp.bfloat16)
    grad_w_gate_up = contract(gate_up_low, mid_low, (0, 1), (0, 1))
    grad_mid = contract(gate_up_low, share_gate_up, (2,), (0,))
    grad_mixed_in, grad_gain_pre = pull_mid(grad_mid)
    grad_mixed = upstream + grad_mixed_in
    grad_proj, grad_gain_attn = pull_out(grad_mixed)
    proj_low = grad_proj.astype(jnp.bfloat16)
    grad_attended = contract(proj_low, full_out, (2,), (1,))
    grad_w_out = contract(attended_low, proj_low, (0, 1), (0, 1))
    attn_low = grad_attended.astype(jnp.bfloat16).reshape(seq_count, local_len, HEADS, HD)
    again_probs = jnp.exp(scores_of() - log_total)
    again_low = again_probs.astype(jnp.bfloat16)
    grad_values = jnp.einsum(
        "shck,schd->skd", again_low, attn_low, preferred_element_type=jnp.float32
    )
    grad_probs = jnp.einsum(
        "schd,skd->shck", attn_low, values_low, preferred_element_type=jnp.float32
    )
    row_dot = jnp.sum(again_probs * grad_probs, axis=-1, keepdims=True)
    grad_scores = (scale * again_probs * (grad_probs - row_dot)).astype(jnp.bfloat16)
    grad_query = jnp.einsum(
        "shck,skd->schd", grad_scores, keys_low, preferred_element_type=jnp.float32
    )
    grad_keys = jnp.einsum(
        "shck,schd->skd", grad_scores, query_low, preferred_element_type=jnp.float32
    )
    grad_pairs = jnp.concatenate([grad_keys, grad_values], axis=-1)
    own_grad = grad_pairs[:, reach * local_len :]
    for distance in range(1, reach + 1):
        piece = grad_pairs[:, (reach - distance) * local_len : (reach - distance + 1) * local_len]
        own_grad = own_grad + shifted(piece.astype(jnp.bfloat16), "ctx", -distance).astype(
            piece.dtype
        )
    grad_projected, grad_gain_query, grad_gain_key = pull_heads(
        (grad_query, own_grad[..., :HD], own_grad[..., HD:])
    )
    qkv_low = grad_projected.astype(jnp.bfloat16)
    grad_w_qkv = contract(qkv_low, normed_low, (0, 1), (0, 1))
    grad_normed = contract(qkv_low, full_qkv, (2,), (0,))
    grad_in_norm, grad_gain_in = pull_in(grad_normed)
    grad_input = grad_mixed + grad_in_norm
    grad_gain_all = jnp.concatenate(
        [
            grad_gain_in,
            grad_gain_attn,
            grad_gain_pre,
            grad_gain_post,
            grad_gain_query,
            grad_gain_key,
        ]
    )
    col_qkv, col_out, col_gains = (
        lax.psum_scatter(
            grad_w_qkv.astype(jnp.bfloat16), "dp", scatter_dimension=1, tiled=True
        ).astype(jnp.float32),
        lax.psum_scatter(
            grad_w_out.astype(jnp.bfloat16), "dp", scatter_dimension=1, tiled=True
        ).astype(jnp.float32),
        lax.psum_scatter(
            grad_gain_all.astype(jnp.bfloat16), "dp", scatter_dimension=0, tiled=True
        ).astype(jnp.float32),
    )
    part_qkv, part_out, part_gains = (
        lax.psum_scatter(
            col_qkv.astype(jnp.bfloat16), "ctx", scatter_dimension=0, tiled=True
        ).astype(jnp.float32),
        lax.psum_scatter(
            col_out.astype(jnp.bfloat16), "ctx", scatter_dimension=0, tiled=True
        ).astype(jnp.float32),
        lax.psum_scatter(
            col_gains.astype(jnp.bfloat16), "ctx", scatter_dimension=0, tiled=True
        ).astype(jnp.float32),
    )
    col_gate_up, col_down = (
        lax.psum_scatter(
            grad_w_gate_up.astype(jnp.bfloat16), "dp", scatter_dimension=1, tiled=True
        ).astype(jnp.float32),
        lax.psum_scatter(
            grad_w_down.astype(jnp.bfloat16), "dp", scatter_dimension=1, tiled=True
        ).astype(jnp.float32),
    )
    part_gate_up, part_down = (
        lax.psum_scatter(
            col_gate_up.astype(jnp.bfloat16), "ctx", scatter_dimension=0, tiled=True
        ).astype(jnp.float32),
        lax.psum_scatter(
            col_down.astype(jnp.bfloat16), "ctx", scatter_dimension=0, tiled=True
        ).astype(jnp.float32),
    )
    return (result, grad_input, part_qkv, part_out, part_gate_up, part_down, part_gains)


def solution(mesh):
    placed = (
        P("dp", "ctx", None),
        P("dp"),
        P("ctx", "dp"),
        P("ctx", "dp"),
        P("ctx", "dp"),
        P("ctx", "dp"),
        P(("dp", "ctx")),
        P("dp", "ctx", None),
    )
    return jax.shard_map(
        per_device,
        mesh=mesh,
        in_specs=placed,
        out_specs=(
            P("dp", "ctx", None),
            P("dp", "ctx", None),
            P("ctx", "dp"),
            P("ctx", "dp"),
            P("ctx", "dp"),
            P("ctx", "dp"),
            P(("dp", "ctx")),
        ),
        check_vma=False,
    )
```

profile of v0, /device:TPU:9, one launch (start us, length us, event | category | flops | bytes accessed | tf_op | source)
XLA Modules:
  0.0 1547.0 jit_solution(7426427047952039315)
XLA Ops:
  11.0 33.5 %all_gather.32 = bf16[1536,288]{1,0:T(8,128)(2,1)S(1)} all-gather(bf16[192,288]{1,0:T(8,128)(2,1)S(1)} %convert_element_type.140), channel_id=1, replica_groups=mesh['dp'=4,'ctx'=8] {'ctx'}, dimensions={0}, use_global_device_ids=true | all-gather | bytes 995328 | tf_op jit(solution)/shard_map/all_gather | solution.py:76
  45.9 28.9 %all_gather.34 = bf16[1024,288]{0,1:T(8,128)(2,1)} all-gather(bf16[128,288]{0,1:T(8,128)(2,1)S(1)} %convert_element_type.146), channel_id=1, replica_groups=mesh['dp'=4,'ctx'=8] {'ctx'}, dimensions={0}, use_global_device_ids=true | all-gather | bytes 663552 | tf_op jit(solution)/shard_map/all_gather | solution.py:77
  74.8 75.4 %all-gather.18.cloned.1.call-done = bf16[8,1728,288]{1,2,0:T(8,128)(2,1)} async-done(((bf16[1,1728,288]{1,2,0:T(8,128)(2,1)}), bf16[8,1728,288]{1,2,0:T(8,128)(2,1)}) %all-gather.18.cloned.1.call-update) | async-done | bytes 7962640 | tf_op jit(solution)/shard_map/all_gather | solution.py:87
  150.2 11.1 copy.151
  161.3 13.7 reshape.479
  175.1 48.9 %all-gather.20.cloned.1.call-done = bf16[8,864,288]{1,2,0:T(8,128)(2,1)} async-done(((bf16[1,864,288]{1,2,0:T(8,128)(2,1)}), bf16[8,864,288]{1,2,0:T(8,128)(2,1)}) %all-gather.20.cloned.1.call-update) | async-done | bytes 3981328 | tf_op jit(solution)/shard_map/all_gather | solution.py:88
  239.7 14.2 all-reduce.9
  254.0 9.0 all-gather
  309.2 166.8 %all-gather.14.cloned.1.call-done = bf16[13824,1152]{0,1:T(8,128)(2,1)} async-done(((bf16[13824,288]{0,1:T(8,128)(2,1)}), bf16[13824,1152]{0,1:T(8,128)(2,1)}) %all-gather.14.cloned.1.call-update) | async-done | bytes 31850512 | tf_op jit(solution)/shard_map/all_gather | solution.py:91
  476.1 24.5 %fusion.2 = f32[2,128,13824]{1,2,0:T(8,128)} fusion(bf16[13824,1152]{0,1:T(8,128)(2,1)} %all-gather.14.cloned.1.call-done, f32[2,128,1152]{2,1,0:T(8,128)} %get-tuple-element.56, f32[1152]{0:T(1024)S(1)} %get-tuple-element.76, f32[2,128]{1,0:T(2,128)S(1)} %fusion.67), kind=kOutput, calls=%fused_computation.4 | convolution fusion | flops 8154611712 | bytes 47191552 | tf_op jit(solution)/shard_map/dot_general | solution.py:60
  500.6 17.0 %fusion.73 = (f32[2,128,6912,1]{1,3,2,0:T(1,128)}, f32[2,128,6912,1]{1,3,2,0:T(1,128)}) fusion(f32[2,128,6912,2]{1,3,2,0:T(2,128)} %bitcast.166), kind=kLoop, calls=%fused_computation.177 | loop fusion | bytes 28311552 | tf_op jit(solution)/shard_map/jvp()/slice | solution.py:56
  517.6 15.5 %copy.213 = f32[2,128,6912,1]{2,1,0,3:T(8,128)} copy(f32[2,128,6912,1]{1,3,2,0:T(1,128)} %get-tuple-element.59) | data formatting | bytes 14155776
  533.1 15.5 %copy.214 = f32[2,128,6912,1]{2,1,0,3:T(8,128)} copy(f32[2,128,6912,1]{1,3,2,0:T(1,128)} %get-tuple-element.60) | data formatting | bytes 14155776
  556.1 22.5 %all-gather.16.cloned.1.call-done = bf16[6912,1152]{0,1:T(8,128)(2,1)} async-done(((bf16[6912,288]{0,1:T(8,128)(2,1)}), bf16[6912,1152]{0,1:T(8,128)(2,1)}) %all-gather.16.cloned.1.call-update) | async-done | bytes 15925264 | tf_op jit(solution)/shard_map/all_gather | solution.py:92
  578.6 12.4 multiply_reduce_fusion.6
  595.7 19.4 %multiply_bitcast_fusion = (f32[2,128,6912,1]{2,1,0,3:T(8,128)}, f32[2,128,6912,1]{2,1,0,3:T(8,128)}) fusion(f32[2,128,6912,1]{2,1,0,3:T(8,128)} %copy.213, f32[2,128,6912,1]{2,1,0,3:T(8,128)} %copy.214, bf16[2,128,1152]{2,1,0:T(8,128)(2,1)S(1)} %get-tuple-element.65, bf16[6912,1152]{0,1:T(8,128)(2,1)} %all-gather.16.cloned.1.call-done), kind=kOutput, calls=%fused_computation.29 | convolution fusion | flops 4115791872 | bytes 44826624 | tf_op jit(solution)/shard_map/dot_general | solution.py:60
  615.1 8.6 add_convert_fusion
  623.7 18.0 %copy.156 = bf16[2,128,6912,2]{1,3,2,0:T(2,128)(2,1)} copy(bf16[2,128,6912,2]{2,1,0,3:T(8,128)(2,1)} %add_convert_fusion) | data formatting | bytes 14155776 | tf_op jit(solution)/shard_map/convert_element_type | solution.py:164
  641.7 19.6 %multiply_reduce_fusion.1 = (bf16[1152]{0:T(1024)(128)(2,1)}, f32[2,128]{1,0:T(2,128)S(1)}, f32[2,128,1152]{2,1,0:T(8,128)}) fusion(f32[2,128,1152]{2,1,0:T(8,128)} %get-tuple-element.56, f32[2,128]{1,0:T(2,128)S(1)} %fusion.67, f32[1152]{0:T(1024)S(1)} %get-tuple-element.76, bf16[2,128,13824]{1,2,0:T(8,128)(2,1)} %bitcast.167, ...), kind=kOutput, calls=%fused_computation.83 | convolution fusion | flops 8155495424 | bytes 41296640 | tf_op jit(solution)/shard_map/dot_general | solution.py:60
  697.8 10.3 collective-permute-done.7
  716.2 9.0 bitcast_convert_fusion.1
  726.4 16.6 %bitcast_convert_fusion = bf16[13824,1152]{0,1:T(8,128)(2,1)} fusion(bf16[2,128,13824]{1,2,0:T(8,128)(2,1)} %bitcast.168, f32[2,128,1152]{2,1,0:T(8,128)S(1)} %copy-done.1, f32[1152]{0:T(1024)S(1)} %get-tuple-element.76, f32[2,128]{1,0:T(2,128)S(1)} %fusion.67), kind=kOutput, calls=%fused_computation | convolution fusion | flops 8170536960 | bytes 40113664 | tf_op jit(solution)/shard_map/dot_general | solution.py:60
  745.6 17.5 %reduce-scatter.17.cloned.1.call-done = bf16[1536,288]{0,1:T(8,128)(2,1)} async-done(((bf16[1536,1152]{0,1:T(8,128)(2,1)}), bf16[1536,288]{0,1:T(8,128)(2,1)}) %reduce-scatter.17.cloned.1.call-update) | async-done | bytes 884752 | tf_op jit(solution)/shard_map/reduce_scatter | solution.py:216
  765.5 121.3 %reduce-scatter.23.cloned.1.call-done = bf16[6912,288]{0,1:T(8,128)(2,1)} async-done(((bf16[6912,1152]{0,1:T(8,128)(2,1)}), bf16[6912,288]{0,1:T(8,128)(2,1)}) %reduce-scatter.23.cloned.1.call-update) | async-done | bytes 3981328 | tf_op jit(solution)/shard_map/reduce_scatter | solution.py:241
  893.5 220.9 %reduce-scatter.21.cloned.1.call-done = bf16[13824,288]{0,1:T(8,128)(2,1)} async-done(((bf16[13824,1152]{0,1:T(8,128)(2,1)}), bf16[13824,288]{0,1:T(8,128)(2,1)}) %reduce-scatter.21.cloned.1.call-update) | async-done | bytes 7962640 | tf_op jit(solution)/shard_map/reduce_scatter | solution.py:238
  1114.5 11.9 copy.209
  1134.3 10.0 all-reduce.10
  1144.4 15.1 all-reduce.11
  1161.5 17.3 %reduce-scatter.27.cloned.1.call-done = bf16[128,288]{1,0:T(8,128)(2,1)} async-done(((bf16[1024,288]{1,0:T(8,128)(2,1)}), bf16[128,288]{1,0:T(8,128)(2,1)}) %reduce-scatter.27.cloned.1.call-update) | async-done | bytes 73744
  1180.5 65.6 %reduce-scatter.25.cloned.1.call-done = bf16[192,288]{1,0:T(8,128)(2,1)} async-done(((bf16[1536,288]{1,0:T(8,128)(2,1)}), bf16[192,288]{1,0:T(8,128)(2,1)}) %reduce-scatter.25.cloned.1.call-update) | async-done | bytes 110608
  1248.0 107.3 %reduce-scatter.31.cloned.1.call-done = bf16[864,288]{1,0:T(8,128)(2,1)} async-done(((bf16[6912,288]{1,0:T(8,128)(2,1)}), bf16[864,288]{1,0:T(8,128)(2,1)}) %reduce-scatter.31.cloned.1.call-update) | async-done | bytes 497680
  1357.7 179.2 %reduce-scatter.29.cloned.1.call-done = bf16[1728,288]{1,0:T(8,128)(2,1)} async-done(((bf16[13824,288]{1,0:T(8,128)(2,1)}), bf16[1728,288]{1,0:T(8,128)(2,1)}) %reduce-scatter.29.cloned.1.call-update) | async-done | bytes 995344
  (287 shorter events, 153.2 us)
Async XLA Ops:
  7.2 143.0 %all-gather.18.cloned.1.call-start = ((), (), s32[]{:S(2)}) async-start(), calls=%async_computation.16 | async-start | bytes 9289728 | tf_op jit(solution)/shard_map/all_gather | solution.py:87
  10.0 214.0 %all-gather.20.cloned.1.call-start = ((), (), s32[]{:S(2)}) async-start(), calls=%async_computation.17 | async-start | bytes 4644864 | tf_op jit(solution)/shard_map/all_gather | solution.py:88
  10.9 255.7 %all-gather.10.cloned.1.call-start = ((), (), s32[]{:S(2)}) async-start(), calls=%async_computation.8 | async-start | bytes 4423680 | tf_op jit(solution)/shard_map/all_gather | solution.py:81
  45.8 257.4 %all-gather.12.cloned.1.call-start = ((), (), s32[]{:S(2)}) async-start(), calls=%async_computation.9 | async-start | bytes 2949120 | tf_op jit(solution)/shard_map/all_gather | solution.py:82
  74.8 401.3 %all-gather.14.cloned.1.call-start = ((), (), s32[]{:S(2)}) async-start(), calls=%async_computation.10 | async-start | bytes 39813120 | tf_op jit(solution)/shard_map/all_gather | solution.py:91
  175.0 403.6 %all-gather.16.cloned.1.call-start = ((), (), s32[]{:S(2)}) async-start(), calls=%async_computation.11 | async-start | bytes 19906560 | tf_op jit(solution)/shard_map/all_gather | solution.py:92
  237.5 25.5 %copy-start.9 = (bf16[2,128,1152]{2,1,0:T(8,128)(2,1)S(1)}, bf16[2,128,1152]{2,1,0:T(8,128)(2,1)}, u32[]{:S(2)}) copy-start(bf16[2,128,1152]{2,1,0:T(8,128)(2,1)} %param.8) | copy-start | bytes 1769476
  237.5 25.7 %copy-start.63 = (s32[2]{0:T(128)S(1)}, s32[2]{0:T(128)}, u32[]{:S(2)}) copy-start(s32[2]{0:T(128)} %param.9) | copy-start | bytes 28
  237.5 505.8 %reduce-scatter.19.cloned.1.call-start = ((), (), s32[]{:S(2)}) async-start(), calls=%async_computation.13 | async-start | bytes 2949120 | tf_op jit(solution)/shard_map/reduce_scatter | solution.py:219
  265.2 41.7 %copy-start.34 = (f32[1152]{0:T(1024)}, f32[1152]{0:T(1024)S(1)}, u32[]{:S(2)}) copy-start(f32[1152]{0:T(1024)S(1)} %get-tuple-element.77) | copy-start | bytes 13828
  271.7 13.7 collective-permute-start
  274.7 16.4 %collective-permute-start.1 = (bf16[2,128,512]{2,1,0:T(8,128)(2,1)}, bf16[2,128,512]{2,1,0:T(8,128)(2,1)}, u32[]{:S(2)}, u32[]{:S(2)}) collective-permute-start(bf16[2,128,512]{2,1,0:T(8,128)(2,1)} %pad_maximum_fusion.4), channel_id=1, source_target_pairs={{0,3},{1,4},{2,5},{3,6},{4,7},{8,11},{9,12},{10,13},{11,14},{12,15... | collective-permute-start | bytes 786440 | tf_op jit(solution)/shard_map/ppermute | solution.py:22
  277.0 19.7 %collective-permute-start.2 = (bf16[2,128,512]{2,1,0:T(8,128)(2,1)}, bf16[2,128,512]{2,1,0:T(8,128)(2,1)}, u32[]{:S(2)}, u32[]{:S(2)}) collective-permute-start(bf16[2,128,512]{2,1,0:T(8,128)(2,1)} %pad_maximum_fusion.4), channel_id=1, source_target_pairs={{0,2},{1,3},{2,4},{3,5},{4,6},{5,7},{8,10},{9,11},{10,12},{11,13},... | collective-permute-start | bytes 786440 | tf_op jit(solution)/shard_map/ppermute | solution.py:22
  279.8 19.7 %collective-permute-start.3 = (bf16[2,128,512]{2,1,0:T(8,128)(2,1)}, bf16[2,128,512]{2,1,0:T(8,128)(2,1)}, u32[]{:S(2)}, u32[]{:S(2)}) collective-permute-start(bf16[2,128,512]{2,1,0:T(8,128)(2,1)} %pad_maximum_fusion.4), channel_id=1, source_target_pairs={{0,1},{1,2},{2,3},{3,4},{4,5},{5,6},{6,7},{8,9},{9,10},{10,11},{11... | collective-permute-start | bytes 786440 | tf_op jit(solution)/shard_map/ppermute | solution.py:22
  556.1 34.9 %copy-start.36 = (f32[1152]{0:T(1024)S(1)}, f32[1152]{0:T(1024)}, u32[]{:S(2)}) copy-start(f32[1152]{0:T(1024)} %get-tuple-element.75) | copy-start | bytes 13828
  556.1 34.9 %copy-start.55 = (pred[2,128]{1,0:T(4,128)(4,1)S(1)}, pred[2,128]{1,0:T(4,128)(4,1)}, u32[]{:S(2)}) copy-start(pred[2,128]{1,0:T(4,128)(4,1)} %broadcast_compare_fusion.3) | copy-start | bytes 772
  595.7 19.4 %copy-start.14 = (bf16[2,128,1152]{2,1,0:T(8,128)(2,1)}, bf16[2,128,1152]{2,1,0:T(8,128)(2,1)S(1)}, u32[]{:S(2)}) copy-start(bf16[2,128,1152]{2,1,0:T(8,128)(2,1)S(1)} %get-tuple-element.65) | copy-start | bytes 1769476
  641.7 19.6 %copy-start.35 = (f32[1152]{0:T(1024)S(1)}, f32[1152]{0:T(1024)}, u32[]{:S(2)}) copy-start(f32[1152]{0:T(1024)} %copy-done.34) | copy-start | bytes 13828
  669.0 94.1 %reduce-scatter.17.cloned.1.call-start = ((), (), s32[]{:S(2)}) async-start(), calls=%async_computation.12 | async-start | bytes 4423680 | tf_op jit(solution)/shard_map/reduce_scatter | solution.py:216
  679.7 10.9 collective-permute-start.4
  682.8 13.1 collective-permute-start.5
  684.8 13.0 collective-permute-start.6
  686.1 22.0 %collective-permute-start.7 = (bf16[2,128,512]{2,1,0:T(8,128)(2,1)S(1)}, bf16[2,128,512]{2,1,0:T(8,128)(2,1)S(1)}, u32[]{:S(2)}, u32[]{:S(2)}) collective-permute-start(bf16[2,128,512]{2,1,0:T(8,128)(2,1)S(1)} %get-tuple-element.62), channel_id=1, source_target_pairs={{4,0},{5,1},{6,2},{7,3},{12,8},{13,9},{14,10},{15,11},{20,16},{21,... | collective-permute-start | bytes 786440 | tf_op jit(solution)/shard_map/ppermute | solution.py:22
  690.6 20.6 %copy-start.19 = (f32[2,4,16,8,256]{4,3,1,2,0:T(8,128)}, f32[2,4,16,8,256]{4,3,1,2,0:T(8,128)S(1)}, u32[]{:S(2)}) copy-start(f32[2,4,16,8,256]{4,3,1,2,0:T(8,128)S(1)} %copy.217) | copy-start | bytes 3145732
  714.2 172.6 %reduce-scatter.23.cloned.1.call-start = ((), (), s32[]{:S(2)}) async-start(), calls=%async_computation.15 | async-start | bytes 19906560 | tf_op jit(solution)/shard_map/reduce_scatter | solution.py:241
  725.2 389.3 %reduce-scatter.21.cloned.1.call-start = ((), (), s32[]{:S(2)}) async-start(), calls=%async_computation.14 | async-start | bytes 39813120 | tf_op jit(solution)/shard_map/reduce_scatter | solution.py:238
  743.0 435.8 %reduce-scatter.27.cloned.1.call-start = ((), (), s32[]{:S(2)}) async-start(), calls=%async_computation.19 | async-start | bytes 884736
  745.6 500.5 %reduce-scatter.25.cloned.1.call-start = ((), (), s32[]{:S(2)}) async-start(), calls=%async_computation.18 | async-start | bytes 1327104
  765.4 589.8 %reduce-scatter.31.cloned.1.call-start = ((), (), s32[]{:S(2)}) async-start(), calls=%async_computation.21 | async-start | bytes 5971968
  893.5 643.4 %reduce-scatter.29.cloned.1.call-start = ((), (), s32[]{:S(2)}) async-start(), calls=%async_computation.20 | async-start | bytes 11943936
  1129.0 31.1 %copy-start.52 = (f32[2,128]{1,0:T(2,128)S(1)}, f32[2,128]{1,0:T(2,128)}, u32[]{:S(2)}) copy-start(f32[2,128]{1,0:T(2,128)} %copy-done.51) | copy-start | bytes 3076
  1129.0 31.1 %copy-start.8 = (f32[2,128,1152]{2,1,0:T(8,128)S(1)}, f32[2,128,1152]{2,1,0:T(8,128)}, u32[]{:S(2)}) copy-start(f32[2,128,1152]{2,1,0:T(8,128)} %copy-done.7) | copy-start | bytes 3538948
  (56 other events, 229.4 us)
Sparse Core Ops, SparseCore 0:
  10.8 139.3 all-gather.17
  153.0 70.9 all-gather.19
  226.1 31.0 all-gather.9
  258.7 24.0 all-gather.11
  284.2 191.8 all-gather.13
  477.5 101.0 all-gather.15
  669.2 32.6 reduce-scatter.18
  714.3 48.7 reduce-scatter.16
  765.7 121.0 reduce-scatter.22
  889.5 224.9 reduce-scatter.20
  1118.3 60.4 reduce-scatter.26
  1183.0 63.0 reduce-scatter.24
  1250.1 105.0 reduce-scatter.30
  1358.7 178.1 reduce-scatter.28
where the time goes:
time: 1560 us; the launch traced here: 1550 us
  waiting for transfers between devices  1070 us (69%)
  local copies, waits for them, and re-layouts  155 us (10%)
  matrix products  127 us (8%)
  blocking collectives  111 us (7%)
  other arithmetic  45.6 us (3%)
  starting transfers between devices  20 us (1%)
  between operations  17.4 us (1%)
    unnamed x18, waiting for transfers between devices  370 us
    reduce_scatter x1, waiting for transfers between devices, per_device(): lax.psum_scatter(grad_w_gate_up.astype(jnp.bfloat16), 'dp', scatter_dimen...  221 us
    all_gather x1, waiting for transfers between devices, per_device(): lax.all_gather(tall_gate_up, 'dp', axis=1, tiled=True)  167 us
    reduce_scatter x1, waiting for transfers between devices, per_device(): lax.psum_scatter(grad_w_down.astype(jnp.bfloat16), 'dp', scatter_dimensio...  121 us
    dot_general x12, matrix products, contract(): lax.dot_general(left, right, ((dims_left, dims_right), ((), ())), preferr...  121 us
    unnamed x160, local copies, waits for them, and re-layouts  98.9 us
    all_gather x1, waiting for transfers between devices, per_device(): lax.all_gather(ffn_masters[0], 'ctx', axis=0, tiled=True)  75.4 us
    all_gather x1, waiting for transfers between devices, per_device(): lax.all_gather(ffn_masters[1], 'ctx', axis=0, tiled=True)  48.9 us
  transfers between devices with their start and end apart: 22, of which 18 were waited for; matrix products, arithmetic and copies ran while one was open for 14% of the time, Pallas kernels for 0%

commit v1 on v0

--- a/solution.py
+++ b/solution.py
@@ -4,16 +4,172 @@
 import jax
 import jax.numpy as jnp
 from jax import lax
+from jax.experimental import pallas as pl
+from jax.experimental.pallas import tpu as pltpu
 from jax.sharding import PartitionSpec as P
 
 D = 1152
 HEADS = 4
 HD = 256
 WINDOW = 512
-
+GROUP = 8
 
 EPS = 1e-06
 BIG = 1e30
+MESH = pl.DeviceIdType.MESH
+VMEM_LIMIT = 56 * 2**20
+
+
+class Layout:
+    def __init__(self, mesh):
+        self.dp = mesh.shape["dp"]
+        self.ctx = mesh.shape["ctx"]
+        self.lo = max(1, GROUP // self.dp)
+        self.hi = self.ctx // self.lo
+        self.wide = self.dp // 2
+        self.chips = self.wide * self.lo
+        self.group = self.dp * self.lo
+        self.hi_groups = [
+            [h * self.lo + low for h in range(self.hi)] for low in range(self.lo)
+        ]
+
+    def place(self):
+        dp = lax.axis_index("dp")
+        ctx = lax.axis_index("ctx")
+        chip = lax.rem(ctx, self.lo) * self.wide + dp // 2
+        return chip, lax.rem(dp, 2), ctx // self.lo
+
+    def device(self, chip, core, high):
+        return (lax.rem(chip, self.wide) * 2 + core, high * self.lo + chip // self.wide)
+
+
+def remote(src, dst, send, recv, device):
+    return pltpu.make_async_remote_copy(
+        src_ref=src, dst_ref=dst, send_sem=send, recv_sem=recv, device_id=device, device_id_type=MESH
+    )
+
+
+def greet(devices):
+    barrier = pltpu.get_barrier_semaphore()
+    for device in devices:
+        pl.semaphore_signal(barrier, inc=1, device_id=device, device_id_type=MESH)
+    pl.semaphore_wait(barrier, len(devices))
+
+
+def gather_tokens_kernel(lay, own, out, local_sem, send, recv, core_send, core_recv):
+    chip, core, high = lay.place()
+    n = lay.chips
+    peers = [lay.device(lax.rem(chip + k, n), core, high) for k in range(1, n)]
+    partner = lay.device(chip, 1 - core, high)
+    greet(peers + [partner])
+    mine = chip * 2 + core
+    pushes = [
+        remote(own, out.at[mine], send.at[k], recv.at[k], peers[k]) for k in range(n - 1)
+    ]
+    for push in pushes:
+        push.start()
+    shares = [remote(own, out.at[mine], core_send.at[0], core_recv.at[0], partner)]
+    shares[0].start()
+    keep = pltpu.make_async_copy(own, out.at[mine], local_sem)
+    keep.start()
+    for k in range(1, n):
+        source = lax.rem(chip + n - k, n) * 2 + core
+        pushes[k - 1].wait_recv()
+        share = remote(out.at[source], out.at[source], core_send.at[k], core_recv.at[k], partner)
+        share.start()
+        shares.append(share)
+    keep.wait()
+    for push in pushes:
+        push.wait_send()
+    for share in shares:
+        share.wait()
+
+
+def gather_tokens(lay, value, collective_id):
+    n = lay.chips
+    return pl.pallas_call(
+        partial(gather_tokens_kernel, lay),
+        out_shape=jax.ShapeDtypeStruct((lay.group,) + value.shape, value.dtype),
+        in_specs=[pl.BlockSpec(memory_space=pl.ANY)],
+        out_specs=pl.BlockSpec(memory_space=pl.ANY),
+        scratch_shapes=[
+            pltpu.SemaphoreType.DMA,
+            pltpu.SemaphoreType.DMA((n - 1,)),
+            pltpu.SemaphoreType.DMA((n - 1,)),
+            pltpu.SemaphoreType.DMA((n,)),
+            pltpu.SemaphoreType.DMA((n,)),
+        ],
+        compiler_params=pltpu.CompilerParams(
+            collective_id=collective_id, has_side_effects=True, vmem_limit_bytes=VMEM_LIMIT
+        ),
+    )(value)
+
+
+def scatter_tokens_kernel(lay, parts, out, from_core, sums, landed, send, recv, core_send, core_recv):
+    chip, core, high = lay.place()
+    n = lay.chips
+    peers = [lay.device(lax.rem(chip + k, n), core, high) for k in range(1, n)]
+    partner = lay.device(chip, 1 - core, high)
+    greet(peers + [partner])
+    shares = []
+    for k in list(range(1, n)) + [0]:
+        target = lax.rem(chip + k, n)
+        share = remote(
+            parts.at[target * 2 + 1 - core],
+            from_core.at[k],
+            core_send.at[k],
+            core_recv.at[k],
+            partner,
+        )
+        share.start()
+        shares.append((k, share))
+    pushes = []
+    for k, share in shares:
+        share.wait_recv()
+        target = lax.rem(chip + k, n)
+        total = parts[target * 2 + core].astype(jnp.float32) + from_core[k].astype(jnp.float32)
+        if k:
+            sums[k - 1] = total.astype(sums.dtype)
+            push = remote(
+                sums.at[k - 1], landed.at[k - 1], send.at[k - 1], recv.at[k - 1], peers[k - 1]
+            )
+            push.start()
+            pushes.append(push)
+        else:
+            out[...] = total
+    for push in pushes:
+        push.wait_recv()
+    total = out[...]
+    for k in range(n - 1):
+        total = total + landed[k].astype(jnp.float32)
+    out[...] = total
+    for push in pushes:
+        push.wait_send()
+    for _, share in shares:
+        share.wait_send()
+
+
+def scatter_tokens(lay, parts, collective_id):
+    n = lay.chips
+    rows, cols = parts.shape[1:]
+    return pl.pallas_call(
+        partial(scatter_tokens_kernel, lay),
+        out_shape=jax.ShapeDtypeStruct((rows, cols), jnp.float32),
+        in_specs=[pl.BlockSpec(memory_space=pltpu.VMEM)],
+        out_specs=pl.BlockSpec(memory_space=pltpu.VMEM),
+        scratch_shapes=[
+            pltpu.VMEM((n, rows, cols), jnp.bfloat16),
+            pltpu.VMEM((n - 1, rows, cols), jnp.bfloat16),
+            pltpu.VMEM((n - 1, rows, cols), jnp.bfloat16),
+            pltpu.SemaphoreType.DMA((n - 1,)),
+            pltpu.SemaphoreType.DMA((n - 1,)),
+            pltpu.SemaphoreType.DMA((n,)),
+            pltpu.SemaphoreType.DMA((n,)),
+        ],
+        compiler_params=pltpu.CompilerParams(
+            collective_id=collective_id, has_side_effects=True, vmem_limit_bytes=VMEM_LIMIT
+        ),
+    )(parts)
 
 
 def shifted(value, axis, steps):
@@ -51,9 +207,24 @@
     return (query, key_rows, value_rows)
 
 
-def gate_times_up(gate_up):
-    paired = gate_up.reshape(gate_up.shape[:-1] + (gate_up.shape[-1] // 2, 2))
-    return jax.nn.gelu(paired[..., 0], approximate=True) * paired[..., 1]
+def gate_times_up(gate, up):
+    return jax.nn.gelu(gate, approximate=True) * up
+
+
+def to_group(lay, quarters):
+    rows, cols = quarters.shape
+    per = rows // lay.dp
+    padded = -(-per // 16) * 16
+    value = quarters.astype(jnp.bfloat16).reshape(lay.dp, per, cols)
+    return jnp.pad(value, ((0, 0), (0, padded - per), (0, 0)))
+
+
+def across(lay, stacked):
+    return lax.all_to_all(stacked, "dp", split_axis=0, concat_axis=2, tiled=True)[0]
+
+
+def back_across(lay, rows):
+    return lax.all_to_all(rows[None], "dp", split_axis=2, concat_axis=0, tiled=True)
 
 
 def contract(left, right, dims_left, dims_right):
@@ -62,7 +233,7 @@
     )
 
 
-def per_device(tokens, lengths, w_qkv, w_out, w_gate_up, w_down, gains, cotangent):
+def per_device(lay, tokens, lengths, w_qkv, w_out, w_gate_up, w_down, gains, cotangent):
     seq_count = tokens.shape[0]
     local_len = tokens.shape[1]
     reach = (WINDOW - 1) // local_len + 1
@@ -82,14 +253,22 @@
         lax.all_gather(row_out, "dp", axis=1, tiled=True),
         lax.all_gather(row_gain, "dp", axis=0, tiled=True),
     )
-    ffn_masters = (w_gate_up.astype(jnp.bfloat16), w_down.astype(jnp.bfloat16))
-    tall_gate_up, tall_down = (
-        lax.all_gather(ffn_masters[0], "ctx", axis=0, tiled=True),
-        lax.all_gather(ffn_masters[1], "ctx", axis=0, tiled=True),
-    )
-    share_gate_up, share_down = (
-        lax.all_gather(tall_gate_up, "dp", axis=1, tiled=True),
-        lax.all_gather(tall_down, "dp", axis=1, tiled=True),
+    pairs = w_gate_up.reshape(w_gate_up.shape[0] // 2, 2, w_gate_up.shape[1])
+    per = pairs.shape[0] // lay.dp
+    stacked = jnp.concatenate(
+        [to_group(lay, pairs[:, 0]), to_group(lay, pairs[:, 1]), to_group(lay, w_down)], axis=1
+    )
+    padded = stacked.shape[1] // 3
+    moved = across(lay, stacked)
+    w_gate, w_up, w_low = (
+        lax.all_gather(
+            moved[i * padded : (i + 1) * padded],
+            "ctx",
+            axis=0,
+            tiled=True,
+            axis_index_groups=lay.hi_groups,
+        )
+        for i in range(3)
     )
     gain_all = gain_low.astype(jnp.float32)
     gain_in = gain_all[:D]
@@ -149,21 +328,29 @@
     mixed = inputs + normed_out
     normed_mid, pull_mid = jax.vjp(norm_scaled, mixed, gain_pre)
     mid_low = normed_mid.astype(jnp.bfloat16)
-    gate_up = contract(mid_low, share_gate_up, (2,), (1,))
-    hidden, pull_act = jax.vjp(gate_times_up, gate_up)
+    token_count = seq_count * local_len
+    mid_all = gather_tokens(lay, mid_low.reshape(token_count, D), 1)
+    gate = contract(mid_all, w_gate, (2,), (1,))
+    up = contract(mid_all, w_up, (2,), (1,))
+    hidden, pull_act = jax.vjp(gate_times_up, gate, up)
     hidden_low = hidden.astype(jnp.bfloat16)
-    down = contract(hidden_low, share_down, (2,), (0,))
+    down_parts = contract(hidden_low, w_low, (2,), (0,)).astype(jnp.bfloat16)
+    down = scatter_tokens(lay, down_parts, 2).reshape(seq_count, local_len, D)
     normed_down, pull_down = jax.vjp(norm_scaled, down, gain_post)
     result = jnp.where(valid[..., None], mixed + normed_down, 0.0).astype(jnp.bfloat16)
     upstream = jnp.where(valid[..., None], cotangent.astype(jnp.float32), 0.0)
     grad_down_in, grad_gain_post = pull_down(upstream)
     down_low = grad_down_in.astype(jnp.bfloat16)
-    grad_hidden = contract(down_low, share_down, (2,), (1,))
-    grad_w_down = contract(hidden_low, down_low, (0, 1), (0, 1))
-    (grad_gate_up,) = pull_act(grad_hidden)
-    gate_up_low = grad_gate_up.astype(jnp.bfloat16)
-    grad_w_gate_up = contract(gate_up_low, mid_low, (0, 1), (0, 1))
-    grad_mid = contract(gate_up_low, share_gate_up, (2,), (0,))
+    down_all = gather_tokens(lay, down_low.reshape(token_count, D), 3)
+    grad_hidden = contract(down_all, w_low, (2,), (1,))
+    grad_low = contract(hidden_low, down_all, (0, 1), (0, 1)).astype(jnp.bfloat16)
+    grad_gate, grad_up = pull_act(grad_hidden)
+    gate_low = grad_gate.astype(jnp.bfloat16)
+    up_low = grad_up.astype(jnp.bfloat16)
+    mid_parts = contract(gate_low, w_gate, (2,), (0,)) + contract(up_low, w_up, (2,), (0,))
+    grad_mid = scatter_tokens(lay, mid_parts.astype(jnp.bfloat16), 4).reshape(mixed.shape)
+    grad_w_gate = contract(gate_low, mid_all, (0, 1), (0, 1)).astype(jnp.bfloat16)
+    grad_w_up = contract(up_low, mid_all, (0, 1), (0, 1)).astype(jnp.bfloat16)
     grad_mixed_in, grad_gain_pre = pull_mid(grad_mid)
     grad_mixed = upstream + grad_mixed_in
     grad_proj, grad_gain_attn = pull_out(grad_mixed)
@@ -234,22 +421,17 @@
             col_gains.astype(jnp.bfloat16), "ctx", scatter_dimension=0, tiled=True
         ).astype(jnp.float32),
     )
-    col_gate_up, col_down = (
-        lax.psum_scatter(
-            grad_w_gate_up.astype(jnp.bfloat16), "dp", scatter_dimension=1, tiled=True
-        ).astype(jnp.float32),
-        lax.psum_scatter(
-            grad_w_down.astype(jnp.bfloat16), "dp", scatter_dimension=1, tiled=True
-        ).astype(jnp.float32),
-    )
-    part_gate_up, part_down = (
-        lax.psum_scatter(
-            col_gate_up.astype(jnp.bfloat16), "ctx", scatter_dimension=0, tiled=True
-        ).astype(jnp.float32),
-        lax.psum_scatter(
-            col_down.astype(jnp.bfloat16), "ctx", scatter_dimension=0, tiled=True
-        ).astype(jnp.float32),
-    )
+    owned = [
+        lax.psum_scatter(
+            piece, "ctx", scatter_dimension=0, tiled=True, axis_index_groups=lay.hi_groups
+        )
+        for piece in (grad_low, grad_w_gate, grad_w_up)
+    ]
+    returned = back_across(lay, jnp.concatenate(owned, axis=0)).astype(jnp.float32)
+    part_down = returned[:, :per].reshape(w_down.shape)
+    part_gate_up = jnp.stack(
+        [returned[:, padded : padded + per], returned[:, 2 * padded : 2 * padded + per]], axis=2
+    ).reshape(w_gate_up.shape)
     return (result, grad_input, part_qkv, part_out, part_gate_up, part_down, part_gains)
 
 
@@ -265,7 +447,7 @@
         P("dp", "ctx", None),
     )
     return jax.shard_map(
-        per_device,
+        partial(per_device, Layout(mesh)),
         mesh=mesh,
         in_specs=placed,
         out_specs=(

time: 1560 us -> 835 us (0.54)
  waiting for transfers between devices: 1070 us -> 221 us
  Pallas kernels: 0 us -> 165 us
  local copies, waits for them, and re-layouts: 155 us -> 79.6 us
  blocking collectives: 111 us -> 153 us
    all_gather x4 -> x3, waiting for transfers between devices: 314 us -> 0.02 us  [per_device(): lax.all_gather(moved[i * padded:(i + 1) * padded], 'ctx', axis=0, tiled=T...]
    unnamed x18 -> x14, waiting for transfers between devices: 370 us -> 73.9 us
    reduce_scatter x2 -> x3, waiting for transfers between devices: 342 us -> 75.7 us  [per_device(): lax.psum_scatter(piece, 'ctx', scatter_dimension=0, tiled=True, axis_inde...]
    pallas_call x0 -> x4, Pallas kernels: none -> 165 us  [the longest x2 96.2 us: gather_tokens(): pl.pallas_call(partial(gather_tokens_kernel, lay), out_shape=jax.ShapeDty...]
    unnamed x160 -> x162, local copies, waits for them, and re-layouts: 98.9 us -> 34.4 us
    ppermute x8, waiting for transfers between devices: 28.8 us -> 71.2 us  [shifted(): lax.ppermute(value, axis, [(source, source + steps) for source in range(l...]
    all_to_all x0 -> x1, blocking collectives: none -> 35.4 us  [across(): lax.all_to_all(stacked, 'dp', split_axis=0, concat_axis=2, tiled=True)[0]]
    reduce_scatter x1, waiting for transfers between devices: 17.5 us -> 0.02 us  [per_device(): lax.psum_scatter(grad_w_qkv.astype(jnp.bfloat16), 'dp', scatter_dimension...]
  transfers between devices with their start and end apart: 22 -> 21, of which waited for: 18 -> 11; matrix products, arithmetic and copies ran while one was open for 14% -> 22% of each run, Pallas kernels for 0% -> 8%
where the time goes in v1:
time: 835 us; the launch traced here: 821 us
  waiting for transfers between devices  221 us (26%)
  Pallas kernels  165 us (20%)
  blocking collectives  153 us (18%)
  matrix products  117 us (14%)
  local copies, waits for them, and re-layouts  79.6 us (10%)
  other arithmetic  42.9 us (5%)
  starting transfers between devices  24.6 us (3%)
  between operations  17.7 us (2%)
    dot_general x15, matrix products, contract(): lax.dot_general(left, right, ((dims_left, dims_right), ((), ())), preferr...  112 us
    pallas_call x2, Pallas kernels, gather_tokens(): pl.pallas_call(partial(gather_tokens_kernel, lay), out_shape=jax.ShapeDty...  96.2 us
    reduce_scatter x3, waiting for transfers between devices, per_device(): lax.psum_scatter(piece, 'ctx', scatter_dimension=0, tiled=True, axis_inde...  75.7 us
    unnamed x14, waiting for transfers between devices  73.9 us
    ppermute x8, waiting for transfers between devices, shifted(): lax.ppermute(value, axis, [(source, source + steps) for source in range(l...  71.2 us
    pallas_call x2, Pallas kernels, scatter_tokens(): pl.pallas_call(partial(scatter_tokens_kernel, lay), out_shape=jax.ShapeDt...  69.1 us
    unnamed x3, blocking collectives  56.3 us
    all_to_all x1, blocking collectives, across(): lax.all_to_all(stacked, 'dp', split_axis=0, concat_axis=2, tiled=True)[0]  35.4 us
  transfers between devices with their start and end apart: 21, of which 11 were waited for; matrix products, arithmetic and copies ran while one was open for 22% of the time, Pallas kernels for 8%

profile of v1, /device:TPU:9, one launch (start us, length us, event | category | flops | bytes accessed | tf_op | source)
XLA Modules:
  0.0 821.1 jit_solution(8073825502162688838)
XLA Ops:
  8.2 26.2 %all_gather.29 = bf16[1536,288]{1,0:T(8,128)(2,1)S(1)} all-gather(bf16[192,288]{1,0:T(8,128)(2,1)S(1)} %convert_element_type.162), channel_id=1, replica_groups=mesh['dp'=4,'ctx'=8] {'ctx'}, dimensions={0}, use_global_device_ids=true | all-gather | bytes 995328 | tf_op jit(solution)/shard_map/all_gather | solution.py:247
  35.8 26.3 %all_gather.31 = bf16[1024,288]{0,1:T(8,128)(2,1)} all-gather(bf16[128,288]{0,1:T(8,128)(2,1)S(1)} %convert_element_type.168), channel_id=1, replica_groups=mesh['dp'=4,'ctx'=8] {'ctx'}, dimensions={0}, use_global_device_ids=true | all-gather | bytes 663552 | tf_op jit(solution)/shard_map/all_gather | solution.py:248
  82.3 35.4 %all_to_all.24 = bf16[4,672,288]{1,2,0:T(8,128)(2,1)S(1)} all-to-all(bf16[4,672,288]{1,2,0:T(8,128)(2,1)S(1)} %copy.207), channel_id=1, replica_groups=mesh['dp'=4,'ctx'=8] {'dp'}, dimensions={0} | all-to-all | bytes 3096576 | tf_op jit(solution)/shard_map/all_to_all | solution.py:223
  122.0 15.9 %all-reduce.10 = bf16[1280]{0:T(1024)(128)(2,1)S(1)} all-reduce(bf16[1280]{0:T(1024)(128)(2,1)S(1)} %dynamic-update-slice), channel_id=1, replica_groups=mesh['dp'=4,'ctx'=8] {'ctx'}, use_global_device_ids=true, to_apply=%add.10 | all-reduce | flops 1280 | bytes 5120
  138.0 8.8 %all-gather = bf16[4,1,1280]{2,1,0:T(2,128)(2,1)S(1)} all-gather(bf16[1,1,1280]{2,1,0:T(2,128)(2,1)S(1)} %reshape.527), channel_id=1, replica_groups=mesh['dp'=4,'ctx'=8] {'dp'}, dimensions={0}, use_global_device_ids=true | all-gather | bytes 12800 | tf_op jit(solution)/shard_map/all_gather | solution.py:254
  174.1 4.6 collective-permute-done.1
  195.0 64.1 %shard_map.135 = bf16[8,256,1152]{2,1,0:T(8,128)(2,1)} custom-call(bf16[256,1152]{1,0:T(8,128)(2,1)} %bitcast.193), custom_call_target="tpu_custom_call" | custom-call | tf_op jit(solution)/shard_map/pallas_call | solution.py:90
  259.1 9.8 %fusion.33 = f32[8,256,896]{2,1,0:T(8,128)} fusion(bf16[8,256,1152]{2,1,0:T(8,128)(2,1)} %shard_map.135, bf16[896,1152]{1,0:T(8,128)(2,1)} %all-gather.11.cloned.1.call-done), kind=kOutput, calls=%fused_computation.65 | convolution fusion | flops 4227858432 | bytes 14123008 | tf_op jit(solution)/shard_map/dot_general | solution.py:231
  268.9 12.3 %multiply_convert_fusion.1 = (bf16[8,256,896]{2,1,0:T(8,128)(2,1)}, f32[8,256,896]{2,1,0:T(8,128)}) fusion(f32[8,256,896]{2,1,0:T(8,128)} %fusion.33, bf16[8,256,1152]{2,1,0:T(8,128)(2,1)} %shard_map.135, bf16[896,1152]{1,0:T(8,128)(2,1)} %all-gather.13.cloned.1.call-done), kind=kOutput, calls=%fused_computation.13 | convolution fusion | flops 4246208512 | bytes 25133056 | tf_op jit(solution)/shard_map/dot_general | solution.py:231
  281.2 9.3 %convolution_convert_fusion.parts = bf16[8,256,1152]{2,1,0:T(8,128)(2,1)} fusion(bf16[8,256,896]{2,1,0:T(8,128)(2,1)} %get-tuple-element.103, bf16[896,1152]{1,0:T(8,128)(2,1)} %all-gather.15.cloned.1.call-done), kind=kOutput, calls=%fused_computation.15 | convolution fusion | flops 4230217728 | bytes 10452992 | tf_op jit(solution)/shard_map/dot_general | solution.py:231
  290.5 34.6 %shard_map.136 = f32[256,1152]{1,0:T(8,128)} custom-call(bf16[8,256,1152]{2,1,0:T(8,128)(2,1)} %convolution_convert_fusion.parts), custom_call_target="tpu_custom_call" | custom-call | tf_op jit(solution)/shard_map/pallas_call | solution.py:155
  329.5 32.2 %shard_map.137 = bf16[8,256,1152]{2,1,0:T(8,128)(2,1)} custom-call(bf16[256,1152]{1,0:T(8,128)(2,1)} %bitcast.194), custom_call_target="tpu_custom_call" | custom-call | tf_op jit(solution)/shard_map/pallas_call | solution.py:90
  361.6 14.6 %multiply_convert_fusion = (bf16[8,256,896]{2,1,0:T(8,128)(2,1)S(1)}, bf16[8,256,896]{2,1,0:T(8,128)(2,1)S(1)}) fusion(f32[8,256,896]{2,1,0:T(8,128)} %fusion.33, f32[8,256,896]{2,1,0:T(8,128)} %get-tuple-element.104, bf16[8,256,1152]{2,1,0:T(8,128)(2,1)} %shard_map.137, bf16[896,1152]{1,0:T(8,128)(2,1)} %all-gather.15.cloned.1.call-done), kind=kOutput, calls=%fused_computation.12 | convolution fusion | flops 4271898624 | bytes 28803072 | tf_op jit(solution)/shard_map/dot_general | solution.py:231
  376.3 7.9 fusion.31
  384.2 9.7 %add_convert_fusion.parts = bf16[8,256,1152]{2,1,0:T(8,128)(2,1)} fusion(f32[8,256,1152]{2,1,0:T(8,128)} %fusion.31, bf16[8,256,896]{2,1,0:T(8,128)(2,1)S(1)} %get-tuple-element.63, bf16[896,1152]{1,0:T(8,128)(2,1)S(1)} %copy-done.64), kind=kOutput, calls=%fused_computation.2 | convolution fusion | flops 4232577024 | bytes 19890176 | tf_op jit(solution)/shard_map/dot_general | solution.py:231
  393.9 34.5 %shard_map.138 = f32[256,1152]{1,0:T(8,128)} custom-call(bf16[8,256,1152]{2,1,0:T(8,128)(2,1)} %add_convert_fusion.parts), custom_call_target="tpu_custom_call" | custom-call | tf_op jit(solution)/shard_map/pallas_call | solution.py:155
  436.7 9.7 %bitcast_convert_fusion.1 = bf16[896,1152]{1,0:T(8,128)(2,1)} fusion(bf16[8,256,896]{2,1,0:T(8,128)(2,1)} %copy-done.68, bf16[8,256,1152]{2,1,0:T(8,128)(2,1)} %shard_map.135), kind=kOutput, calls=%fused_computation.19 | convolution fusion | flops 4228890624 | bytes 10452992 | tf_op jit(solution)/shard_map/dot_general | solution.py:231
  446.5 10.1 %bitcast_convert_fusion.2 = bf16[896,1152]{1,0:T(8,128)(2,1)} fusion(bf16[8,256,896]{2,1,0:T(8,128)(2,1)} %copy-done.67, bf16[8,256,1152]{2,1,0:T(8,128)(2,1)} %shard_map.135), kind=kOutput, calls=%fused_computation.20 | convolution fusion | flops 4228890624 | bytes 10452992 | tf_op jit(solution)/shard_map/dot_general | solution.py:231
  462.7 9.9 %bitcast_convert_fusion.3 = bf16[896,1152]{1,0:T(8,128)(2,1)} fusion(bf16[8,256,896]{2,1,0:T(8,128)(2,1)} %get-tuple-element.103, bf16[8,256,1152]{2,1,0:T(8,128)(2,1)} %shard_map.137), kind=kOutput, calls=%fused_computation.21 | convolution fusion | flops 4228890624 | bytes 10452992 | tf_op jit(solution)/shard_map/dot_general | solution.py:231
  487.3 5.8 collective-permute-done.7
  493.1 29.5 %collective-permute-done.6 = bf16[2,128,512]{2,1,0:T(8,128)(2,1)S(1)} collective-permute-done((bf16[2,128,512]{2,1,0:T(8,128)(2,1)S(1)}, bf16[2,128,512]{2,1,0:T(8,128)(2,1)S(1)}, u32[]{:S(2)}, u32[]{:S(2)}) %collective-permute-start.6) | collective-permute-done | bytes 262176 | tf_op jit(solution)/shard_map/ppermute | solution.py:178
  522.6 21.2 %collective-permute-done.5 = bf16[2,128,512]{2,1,0:T(8,128)(2,1)S(1)} collective-permute-done((bf16[2,128,512]{2,1,0:T(8,128)(2,1)S(1)}, bf16[2,128,512]{2,1,0:T(8,128)(2,1)S(1)}, u32[]{:S(2)}, u32[]{:S(2)}) %collective-permute-start.5) | collective-permute-done | bytes 262176 | tf_op jit(solution)/shard_map/ppermute | solution.py:178
  555.3 30.8 %reduce-scatter.18.cloned.1.call-done = bf16[224,1152]{1,0:T(8,128)(2,1)} async-done(((bf16[896,1152]{1,0:T(8,128)(2,1)}), bf16[224,1152]{1,0:T(8,128)(2,1)}) %reduce-scatter.18.cloned.1.call-update) | async-done | bytes 516112 | tf_op jit(solution)/shard_map/reduce_scatter | solution.py:425
  586.1 44.9 %reduce-scatter.16.cloned.1.call-done = bf16[224,1152]{1,0:T(8,128)(2,1)} async-done(((bf16[896,1152]{1,0:T(8,128)(2,1)}), bf16[224,1152]{1,0:T(8,128)(2,1)}) %reduce-scatter.16.cloned.1.call-update) | async-done | bytes 516112 | tf_op jit(solution)/shard_map/reduce_scatter | solution.py:425
  633.6 8.8 %copy.230 = bf16[1,672,1152]{1,0,2:T(2,128)(2,1)S(1)} copy(bf16[1,672,1152]{2,1,0:T(8,128)(2,1)} %maximum_bitcast_fusion) | data formatting | bytes 3096576 | tf_op jit(solution)/shard_map/broadcast_in_dim | solution.py:227
  643.0 11.9 %reduce.1 = bf16[1152,672]{1,0:T(8,128)(2,1)} reduce(bf16[1152,1,672]{2,1,0:T(2,128)(2,1)S(1)} %bitcast.184, bf16[]{:T(256)} %broadcast.548), dimensions={1}, to_apply=%bitcast.142.reduce_sub_computation | reduce | bytes 3096578
  654.8 4.9 reshape.554
  659.8 6.2 all-to-all-start.1
  671.0 25.4 %all-reduce.11 = bf16[5120]{0:T(1024)(128)(2,1)S(1)} all-reduce(bf16[5120]{0:T(1024)(128)(2,1)S(1)} %dynamic-update-slice.6), channel_id=9, replica_groups=mesh['dp'=4,'ctx'=8] {'dp'}, use_global_device_ids=true, to_apply=%region_28.29.clone | all-reduce | flops 5120 | bytes 20480
  696.4 15.0 %all-reduce.12 = bf16[1280]{0:T(1024)(128)(2,1)S(1)} all-reduce(bf16[1280]{0:T(1024)(128)(2,1)S(1)} %dynamic-slice.2), channel_id=10, replica_groups=mesh['dp'=4,'ctx'=8] {'ctx'}, use_global_device_ids=true, to_apply=%region_29.30.clone | all-reduce | flops 1280 | bytes 5120
  736.8 9.1 %reduce-scatter.24.cloned.1.call-done = bf16[128,288]{1,0:T(8,128)(2,1)} async-done(((bf16[1024,288]{1,0:T(8,128)(2,1)}), bf16[128,288]{1,0:T(8,128)(2,1)}) %reduce-scatter.24.cloned.1.call-update) | async-done | bytes 73744
  747.5 64.6 %reduce-scatter.22.cloned.1.call-done = bf16[192,288]{1,0:T(8,128)(2,1)} async-done(((bf16[1536,288]{1,0:T(8,128)(2,1)}), bf16[192,288]{1,0:T(8,128)(2,1)}) %reduce-scatter.22.cloned.1.call-update) | async-done | bytes 110608
  (314 shorter events, 149.3 us)
Async XLA Ops:
  7.2 144.4 %all-gather.7.cloned.1.call-start = ((), (), s32[]{:S(2)}) async-start(), calls=%async_computation.9 | async-start | bytes 4423680 | tf_op jit(solution)/shard_map/all_gather | solution.py:252
  35.8 154.0 %all-gather.9.cloned.1.call-start = ((), (), s32[]{:S(2)}) async-start(), calls=%async_computation.10 | async-start | bytes 2949120 | tf_op jit(solution)/shard_map/all_gather | solution.py:253
  62.1 197.0 %all-gather.11.cloned.1.call-start = ((), (), s32[]{:S(2)}) async-start(), calls=%async_computation.11 | async-start | bytes 2580480 | tf_op jit(solution)/shard_map/all_gather | solution.py:264
  118.2 28.7 %copy-start.10 = (bf16[2,128,1152]{2,1,0:T(8,128)(2,1)S(1)}, bf16[2,128,1152]{2,1,0:T(8,128)(2,1)}, u32[]{:S(2)}) copy-start(bf16[2,128,1152]{2,1,0:T(8,128)(2,1)} %param.8) | copy-start | bytes 1769476
  118.2 28.8 %copy-start.62 = (s32[2]{0:T(128)S(1)}, s32[2]{0:T(128)}, u32[]{:S(2)}) copy-start(s32[2]{0:T(128)} %param.9) | copy-start | bytes 28
  119.3 149.6 %all-gather.13.cloned.1.call-start = ((), (), s32[]{:S(2)}) async-start(), calls=%async_computation.12 | async-start | bytes 2580480 | tf_op jit(solution)/shard_map/all_gather | solution.py:264
  120.4 160.8 %all-gather.15.cloned.1.call-start = ((), (), s32[]{:S(2)}) async-start(), calls=%async_computation.13 | async-start | bytes 2580480 | tf_op jit(solution)/shard_map/all_gather | solution.py:264
  151.5 399.4 %reduce-scatter.14.cloned.1.call-start = ((), (), s32[]{:S(2)}) async-start(), calls=%async_computation.15 | async-start | bytes 2949120 | tf_op jit(solution)/shard_map/reduce_scatter | solution.py:406
  156.1 17.0 %collective-permute-start = (bf16[2,128,512]{2,1,0:T(8,128)(2,1)S(1)}, bf16[2,128,512]{2,1,0:T(8,128)(2,1)}, u32[]{:S(2)}, u32[]{:S(2)}) collective-permute-start(bf16[2,128,512]{2,1,0:T(8,128)(2,1)S(1)} %pad_maximum_fusion.5), channel_id=1, source_target_pairs={{0,4},{1,5},{2,6},{3,7},{8,12},{9,13},{10,14},{11,15},{16,20},{17,... | collective-permute-start | bytes 786440 | tf_op jit(solution)/shard_map/ppermute | solution.py:178
  159.2 19.6 %collective-permute-start.1 = (bf16[2,128,512]{2,1,0:T(8,128)(2,1)S(1)}, bf16[2,128,512]{2,1,0:T(8,128)(2,1)}, u32[]{:S(2)}, u32[]{:S(2)}) collective-permute-start(bf16[2,128,512]{2,1,0:T(8,128)(2,1)S(1)} %pad_maximum_fusion.5), channel_id=1, source_target_pairs={{0,3},{1,4},{2,5},{3,6},{4,7},{8,11},{9,12},{10,13},{11,14},{12,15... | collective-permute-start | bytes 786440 | tf_op jit(solution)/shard_map/ppermute | solution.py:178
  161.2 23.2 %collective-permute-start.2 = (bf16[2,128,512]{2,1,0:T(8,128)(2,1)S(1)}, bf16[2,128,512]{2,1,0:T(8,128)(2,1)}, u32[]{:S(2)}, u32[]{:S(2)}) collective-permute-start(bf16[2,128,512]{2,1,0:T(8,128)(2,1)S(1)} %pad_maximum_fusion.5), channel_id=1, source_target_pairs={{0,2},{1,3},{2,4},{3,5},{4,6},{5,7},{8,10},{9,11},{10,12},{11,13},... | collective-permute-start | bytes 786440 | tf_op jit(solution)/shard_map/ppermute | solution.py:178
  163.1 23.0 %collective-permute-start.3 = (bf16[2,128,512]{2,1,0:T(8,128)(2,1)S(1)}, bf16[2,128,512]{2,1,0:T(8,128)(2,1)}, u32[]{:S(2)}, u32[]{:S(2)}) collective-permute-start(bf16[2,128,512]{2,1,0:T(8,128)(2,1)S(1)} %pad_maximum_fusion.5), channel_id=1, source_target_pairs={{0,1},{1,2},{2,3},{3,4},{4,5},{5,6},{6,7},{8,9},{9,10},{10,11},{11... | collective-permute-start | bytes 786440 | tf_op jit(solution)/shard_map/ppermute | solution.py:178
  290.5 36.1 %copy-start.12 = (bf16[2,128,1152]{2,1,0:T(8,128)(2,1)S(1)}, bf16[2,128,1152]{2,1,0:T(8,128)(2,1)}, u32[]{:S(2)}) copy-start(bf16[2,128,1152]{2,1,0:T(8,128)(2,1)} %param.15) | copy-start | bytes 1769476
  290.5 36.1 %copy-start.36 = (f32[1152]{0:T(1024)S(1)}, f32[1152]{0:T(1024)}, u32[]{:S(2)}) copy-start(f32[1152]{0:T(1024)} %get-tuple-element.88) | copy-start | bytes 13828
  290.5 36.2 %copy-start.56 = (pred[2,128]{1,0:T(4,128)(4,1)S(1)}, pred[2,128]{1,0:T(4,128)(4,1)}, u32[]{:S(2)}) copy-start(pred[2,128]{1,0:T(4,128)(4,1)} %broadcast_compare_fusion.3) | copy-start | bytes 772
  436.5 118.8 %reduce-scatter.20.cloned.1.call-start = ((), (), s32[]{:S(2)}) async-start(), calls=%async_computation.18 | async-start | bytes 2580480 | tf_op jit(solution)/shard_map/reduce_scatter | solution.py:425
  446.5 139.6 %reduce-scatter.18.cloned.1.call-start = ((), (), s32[]{:S(2)}) async-start(), calls=%async_computation.17 | async-start | bytes 2580480 | tf_op jit(solution)/shard_map/reduce_scatter | solution.py:425
  456.7 174.3 %reduce-scatter.16.cloned.1.call-start = ((), (), s32[]{:S(2)}) async-start(), calls=%async_computation.16 | async-start | bytes 2580480 | tf_op jit(solution)/shard_map/reduce_scatter | solution.py:425
  472.7 238.8 %reduce-scatter.12.cloned.1.call-start = ((), (), s32[]{:S(2)}) async-start(), calls=%async_computation.14 | async-start | bytes 4423680 | tf_op jit(solution)/shard_map/reduce_scatter | solution.py:403
  477.5 15.7 %collective-permute-start.7 = (bf16[2,128,512]{2,1,0:T(8,128)(2,1)S(1)}, bf16[2,128,512]{2,1,0:T(8,128)(2,1)S(1)}, u32[]{:S(2)}, u32[]{:S(2)}) collective-permute-start(bf16[2,128,512]{2,1,0:T(8,128)(2,1)S(1)} %get-tuple-element.74), channel_id=1, source_target_pairs={{4,0},{5,1},{6,2},{7,3},{12,8},{13,9},{14,10},{15,11},{20,16},{21,... | collective-permute-start | bytes 786440 | tf_op jit(solution)/shard_map/ppermute | solution.py:178
  478.9 43.8 %collective-permute-start.6 = (bf16[2,128,512]{2,1,0:T(8,128)(2,1)S(1)}, bf16[2,128,512]{2,1,0:T(8,128)(2,1)S(1)}, u32[]{:S(2)}, u32[]{:S(2)}) collective-permute-start(bf16[2,128,512]{2,1,0:T(8,128)(2,1)S(1)} %get-tuple-element.75), channel_id=1, source_target_pairs={{3,0},{4,1},{5,2},{6,3},{7,4},{11,8},{12,9},{13,10},{14,11},{15,12... | collective-permute-start | bytes 786440 | tf_op jit(solution)/shard_map/ppermute | solution.py:178
  480.2 63.7 %collective-permute-start.5 = (bf16[2,128,512]{2,1,0:T(8,128)(2,1)S(1)}, bf16[2,128,512]{2,1,0:T(8,128)(2,1)S(1)}, u32[]{:S(2)}, u32[]{:S(2)}) collective-permute-start(bf16[2,128,512]{2,1,0:T(8,128)(2,1)S(1)} %get-tuple-element.76), channel_id=1, source_target_pairs={{2,0},{3,1},{4,2},{5,3},{6,4},{7,5},{10,8},{11,9},{12,10},{13,11},... | collective-permute-start | bytes 786440 | tf_op jit(solution)/shard_map/ppermute | solution.py:178
  482.1 61.8 %collective-permute-start.4 = (bf16[2,128,512]{2,1,0:T(8,128)(2,1)S(1)}, bf16[2,128,512]{2,1,0:T(8,128)(2,1)S(1)}, u32[]{:S(2)}, u32[]{:S(2)}) collective-permute-start(bf16[2,128,512]{2,1,0:T(8,128)(2,1)S(1)} %get-tuple-element.73), channel_id=1, source_target_pairs={{1,0},{2,1},{3,2},{4,3},{5,4},{6,5},{7,6},{9,8},{10,9},{11,10},{12... | collective-permute-start | bytes 786440 | tf_op jit(solution)/shard_map/ppermute | solution.py:178
  487.2 59.8 %copy-start.21 = (f32[2,4,16,8,256]{4,3,1,2,0:T(8,128)}, f32[2,4,16,8,256]{4,3,1,2,0:T(8,128)S(1)}, u32[]{:S(2)}) copy-start(f32[2,4,16,8,256]{4,3,1,2,0:T(8,128)S(1)} %copy.267) | copy-start | bytes 3145732
  487.2 56.9 %copy-start.44 = (f32[2,128]{1,0:T(2,128)S(1)}, f32[2,128]{1,0:T(2,128)}, u32[]{:S(2)}) copy-start(f32[2,128]{1,0:T(2,128)} %copy-done.43) | copy-start | bytes 3076
  487.3 56.9 %copy-start.46 = (f32[256]{0:T(256)S(1)}, f32[256]{0:T(256)}, u32[]{:S(2)}) copy-start(f32[256]{0:T(256)} %copy-done.45) | copy-start | bytes 3076
  487.3 58.6 %copy-start.55 = (f32[2,128]{1,0:T(2,128)S(1)}, f32[2,128]{1,0:T(2,128)}, u32[]{:S(2)}) copy-start(f32[2,128]{1,0:T(2,128)} %copy-done.54) | copy-start | bytes 3076
  550.7 195.1 %reduce-scatter.24.cloned.1.call-start = ((), (), s32[]{:S(2)}) async-start(), calls=%async_computation.20 | async-start | bytes 884736
  659.8 56.1 %all-to-all-start.1 = ((bf16[4,2,96768]{2,1,0:T(2,128)(2,1)}), bf16[4,2,96768]{2,1,0:T(2,128)(2,1)}, u32[]{:S(2)}, u32[]{:S(2)}) async-start(bf16[4,2,96768]{2,1,0:T(2,128)(2,1)} %reshape.554), calls=%async_computation.6 | async-start | bytes 3096576 | tf_op jit(solution)/shard_map/all_to_all | solution.py:227
  666.0 146.1 %reduce-scatter.22.cloned.1.call-start = ((), (), s32[]{:S(2)}) async-start(), calls=%async_computation.19 | async-start | bytes 1327104
  669.4 45.1 %copy-start.53 = (f32[2,128]{1,0:T(2,128)S(1)}, f32[2,128]{1,0:T(2,128)}, u32[]{:S(2)}) copy-start(f32[2,128]{1,0:T(2,128)} %copy-done.52) | copy-start | bytes 3076
  669.4 45.1 %copy-start.6 = (f32[2,128,1152]{2,1,0:T(8,128)S(1)}, f32[2,128,1152]{2,1,0:T(8,128)}, u32[]{:S(2)}) copy-start(f32[2,128,1152]{2,1,0:T(8,128)} %copy-done.5) | copy-start | bytes 3538948
  (58 other events, 301.4 us)
Sparse Core Ops, SparseCore 0:
  35.9 39.2 all-gather.6
  76.7 26.0 all-gather.8
  119.4 49.8 all-gather.10
  170.7 52.3 all-gather.12
  224.6 51.9 all-gather.14
  436.6 34.6 reduce-scatter.13
  474.3 69.6 reduce-scatter.19
  546.4 39.6 reduce-scatter.17
  588.5 42.4 reduce-scatter.15
  633.4 46.6 reduce-scatter.11
  683.8 62.0 reduce-scatter.23
  749.1 63.0 reduce-scatter.21

commit v2 on v1

--- a/solution.py
+++ b/solution.py
@@ -172,6 +172,522 @@
     )(parts)
 
 
+def lane_tiles(cols):
+    return [(first, min(128, cols - first)) for first in range(0, cols, 128)]
+
+
+def exchange_in_kernel(
+    lay, pack, pairs, lows, attn_out, gate_out, up_out, low_out,
+    attn_land, stack, land, lanes, attn_send, attn_recv, send, recv,
+):
+    n = lay.dp
+    dp = lax.axis_index("dp")
+    ctx = lax.axis_index("ctx")
+    per = lows.shape[1]
+    padded = gate_out.shape[0]
+    cols = lows.shape[2]
+    targets = [lax.rem(dp + k, n) for k in range(n)]
+    greet([(target, ctx) for target in targets[1:]])
+    attn_pushes = []
+    for k in range(1, n):
+        push = remote(
+            pack.at[targets[k]], attn_land.at[dp], attn_send.at[k], attn_recv.at[k], (targets[k], ctx)
+        )
+        push.start()
+        attn_pushes.append(push)
+    attn_land[dp] = pack[dp]
+    pushes = []
+    blank = jnp.zeros((padded - per, cols), jnp.bfloat16)
+    for k in list(range(2, n)) + [1, 0]:
+        target = targets[k]
+        for j, (first, width) in enumerate(lane_tiles(cols)):
+            lanes[j, :, :width] = pairs[target, :, first : first + width]
+        for i in range(3):
+            for j, (first, width) in enumerate(lane_tiles(cols)):
+                if i == 2:
+                    piece = lows[target, :, first : first + width]
+                else:
+                    piece = lanes[j, pl.ds(i, per, stride=2), :][:, :width]
+                if k:
+                    stack[k - 1, i, :per, first : first + width] = piece.astype(jnp.bfloat16)
+                else:
+                    land[dp, i, :per, first : first + width] = piece.astype(jnp.bfloat16)
+            if k:
+                stack[k - 1, i, per:] = blank
+            else:
+                land[dp, i, per:] = blank
+        if k:
+            push = remote(stack.at[k - 1], land.at[dp], send.at[k], recv.at[k], (target, ctx))
+            push.start()
+            pushes.append(push)
+    for push in attn_pushes:
+        push.wait_recv()
+    for q in range(n):
+        attn_out[:, q * cols : (q + 1) * cols] = attn_land[q]
+    for push in pushes:
+        push.wait_recv()
+    for q in range(n):
+        for i, out in enumerate((gate_out, up_out, low_out)):
+            out[:, q * cols : (q + 1) * cols] = land[q, i]
+    for push in attn_pushes + pushes:
+        push.wait_send()
+
+
+def exchange_in(lay, pack, pairs, lows, collective_id):
+    n, per, cols = lows.shape
+    rows = pack.shape[1]
+    padded = -(-per // 16) * 16
+    wide = jax.ShapeDtypeStruct((padded, n * cols), jnp.bfloat16)
+    vmem = pl.BlockSpec(memory_space=pltpu.VMEM)
+    return pl.pallas_call(
+        partial(exchange_in_kernel, lay),
+        out_shape=(jax.ShapeDtypeStruct((rows, n * cols), jnp.bfloat16), wide, wide, wide),
+        in_specs=[vmem] * 3,
+        out_specs=(vmem,) * 4,
+        scratch_shapes=[
+            pltpu.VMEM((n, rows, cols), jnp.bfloat16),
+            pltpu.VMEM((n - 1, 3, padded, cols), jnp.bfloat16),
+            pltpu.VMEM((n, 3, padded, cols), jnp.bfloat16),
+            pltpu.VMEM((len(lane_tiles(cols)), 2 * per, 128), jnp.float32),
+        ]
+        + [pltpu.SemaphoreType.DMA((n,))] * 4,
+        compiler_params=pltpu.CompilerParams(
+            collective_id=collective_id, has_side_effects=True, vmem_limit_bytes=VMEM_LIMIT
+        ),
+    )(pack, pairs, lows)
+
+
+def gather_attn_kernel(lay, own, out, local_sem, chain_send, chain_recv, low_send, low_recv,
+                       wide_send, wide_recv, core_send, core_recv):
+    dp = lax.axis_index("dp")
+    ctx = lax.axis_index("ctx")
+    hi, lo, wide = lay.hi, lay.lo, lay.wide
+    high, low = ctx // lo, lax.rem(ctx, lo)
+    across, core = dp // 2, lax.rem(dp, 2)
+    partner = (across * 2 + 1 - core, ctx)
+    low_peers = [(dp, high * lo + lax.rem(low + k, lo)) for k in range(1, lo)]
+    wide_peers = [(lax.rem(across + k, wide) * 2 + core, ctx) for k in range(1, wide)]
+    right, left = (dp, ctx + lo), (dp, ctx - lo)
+    has_right, has_left = high < hi - 1, high > 0
+    barrier = pltpu.get_barrier_semaphore()
+    for device in low_peers + wide_peers + [partner]:
+        pl.semaphore_signal(barrier, inc=1, device_id=device, device_id_type=MESH)
+    for there, device in ((has_right, right), (has_left, left)):
+        @pl.when(there)
+        def _():
+            pl.semaphore_signal(barrier, inc=1, device_id=device, device_id_type=MESH)
+    sides = jnp.where(has_right, 1, 0) + jnp.where(has_left, 1, 0)
+    pl.semaphore_wait(barrier, len(low_peers) + len(wide_peers) + 1 + sides)
+
+    def to_core(source, c, d, slot):
+        return remote(source, out.at[c, d], core_send.at[slot], core_recv.at[slot], partner)
+
+    def to_wide(source, c, d, slot):
+        return [
+            remote(source, out.at[c, d], wide_send.at[slot, k], wide_recv.at[slot, k], wide_peers[k])
+            for k in range(wide - 1)
+        ]
+
+    def to_low(source, c, d, slot):
+        return [
+            remote(source, out.at[c, d], low_send.at[slot, k], low_recv.at[slot, k], low_peers[k])
+            for k in range(lo - 1)
+        ]
+
+    def chain(source, c, side, step):
+        return remote(
+            source, out.at[c, dp], chain_send.at[side, step], chain_recv.at[side, step],
+            right if side == 0 else left,
+        )
+
+    def blocks():
+        yield 0, 0, jnp.bool_(True), high
+        for step in range(1, hi):
+            yield 0, step, high - step >= 0, high - step
+            yield 1, step, high + step < hi, high + step
+
+    everything = list(blocks())
+    number = {(side, step): i for i, (side, step, _, _) in enumerate(everything)}
+    per_low = lo
+    per_wide = lo * wide
+
+    def core_slot(i, a, b):
+        return (i * per_low + a) * wide + b
+
+    def stage_low_arrivals(i, where):
+        for k in range(lo - 1):
+            c = where * lo + lax.rem(low + lo - 1 - k, lo)
+            low_copy = remote(own, out.at[c, dp], low_send.at[i, k], low_recv.at[i, k], low_peers[k])
+            low_copy.wait_recv()
+            for push in to_wide(out.at[c, dp], c, dp, i * per_low + k + 1):
+                push.start()
+            to_core(out.at[c, dp], c, dp, core_slot(i, k + 1, 0)).start()
+
+    def stage_wide_arrivals(i, where):
+        for a in range(lo):
+            c = where * lo + (low if a == 0 else lax.rem(low + lo - a, lo))
+            for k in range(wide - 1):
+                d = lax.rem(across + wide - 1 - k, wide) * 2 + core
+                copy = remote(
+                    own, out.at[c, d], wide_send.at[i * per_low + a, k],
+                    wide_recv.at[i * per_low + a, k], wide_peers[k],
+                )
+                copy.wait_recv()
+                to_core(out.at[c, d], c, d, core_slot(i, a, k + 1)).start()
+
+    def stage_own(i, side, step, where):
+        c = where * lo + low
+        source = own if step == 0 else out.at[c, dp]
+        if step:
+            chain(own, c, side, step - 1).wait_recv()
+        for go_side, there in ((0, has_right), (1, has_left)):
+            if step and go_side != side:
+                continue
+            if step < hi - 1:
+                @pl.when(there)
+                def _():
+                    chain(source, c, go_side, step).start()
+        for push in to_low(source, c, dp, i):
+            push.start()
+        for push in to_wide(source, c, dp, i * per_low):
+            push.start()
+        to_core(source, c, dp, core_slot(i, 0, 0)).start()
+
+    def finish(i, side, step, where):
+        c = where * lo + low
+        for go_side, there in ((0, has_right), (1, has_left)):
+            if step and go_side != side:
+                continue
+            if step < hi - 1:
+                @pl.when(there)
+                def _():
+                    chain(own, c, go_side, step).wait_send()
+        for push in to_low(own, c, dp, i):
+            push.wait_send()
+        for a in range(lo):
+            for push in to_wide(own, c, dp, i * per_low + a):
+                push.wait_send()
+            for b in range(wide):
+                to_core(own, c, dp, core_slot(i, a, b)).wait()
+
+    keep = pltpu.make_async_copy(own, out.at[ctx, dp], local_sem)
+    keep.start()
+    previous = []
+    for step in range(hi + 2):
+        for stage, age in ((stage_own, 0), (stage_low_arrivals, 1), (stage_wide_arrivals, 2)):
+            for i, (side, s, there, where) in enumerate(everything):
+                if s != step - age:
+                    continue
+                if stage is stage_own:
+                    call = partial(stage_own, i, side, s, where)
+                else:
+                    call = partial(stage, i, where)
+                if s == 0:
+                    call()
+                else:
+                    pl.when(there)(call)
+    keep.wait()
+    for i, (side, s, there, where) in enumerate(everything):
+        call = partial(finish, i, side, s, where)
+        if s == 0:
+            call()
+        else:
+            pl.when(there)(call)
+
+
+def gather_attn(lay, own, collective_id):
+    count = 2 * lay.hi - 1
+    lows, wides = max(1, lay.lo - 1), max(1, lay.wide - 1)
+    return pl.pallas_call(
+        partial(gather_attn_kernel, lay),
+        out_shape=jax.ShapeDtypeStruct((lay.ctx, lay.dp) + own.shape, own.dtype),
+        in_specs=[pl.BlockSpec(memory_space=pl.ANY)],
+        out_specs=pl.BlockSpec(memory_space=pl.ANY),
+        scratch_shapes=[pltpu.SemaphoreType.DMA]
+        + [pltpu.SemaphoreType.DMA((2, lay.hi))] * 2
+        + [pltpu.SemaphoreType.DMA((count, lows))] * 2
+        + [pltpu.SemaphoreType.DMA((count * lay.lo, wides))] * 2
+        + [pltpu.SemaphoreType.DMA((count * lay.lo * lay.wide,))] * 2,
+        compiler_params=pltpu.CompilerParams(
+            collective_id=collective_id, has_side_effects=True, vmem_limit_bytes=VMEM_LIMIT
+        ),
+    )(own)
+
+
+def flip(index, bit):
+    return index + bit * (1 - 2 * lax.rem(index // bit, 2))
+
+
+def scatter_attn_kernel(lay, with_gains, *refs):
+    refs = list(refs)
+    parts = refs.pop(0)
+    gains = refs.pop(0) if with_gains else None
+    out = refs.pop(0)
+    gains_out = refs.pop(0) if with_gains else None
+    core_land, wide_sum, wide_land, keep, low_sum, low_land, hi_sum, hi_land, last, last_land = refs[:10]
+    (core_send, core_recv, wide_send, wide_recv, low_send, low_recv, hi_send, hi_recv,
+     last_send, last_recv) = refs[10:20]
+    if with_gains:
+        gains_sum, gains_land, gains_send, gains_recv = refs[20:]
+    dp = lax.axis_index("dp")
+    ctx = lax.axis_index("ctx")
+    hi, lo, wide, n = lay.hi, lay.lo, lay.wide, lay.dp
+    high, low = ctx // lo, lax.rem(ctx, lo)
+    across, core = dp // 2, lax.rem(dp, 2)
+    cols = out.shape[1]
+    rows = parts.shape[2]
+    partner = (across * 2 + 1 - core, ctx)
+    low_peers = [(dp, high * lo + lax.rem(low + k, lo)) for k in range(1, lo)]
+    wide_peers = [(lax.rem(across + k, wide) * 2 + core, ctx) for k in range(1, wide)]
+    hi_peers = [(dp, lax.rem(high + k, hi) * lo + low) for k in range(1, hi)]
+    last_peers = [(lax.rem(dp + k, n), ctx) for k in range(1, n)]
+    steps = [1 << i for i in range((n - 1).bit_length())]
+    gain_peers = [(flip(dp, bit), ctx) for bit in steps]
+    gain_peers += [(dp, flip(ctx, 1 << i)) for i in range((lay.ctx - 1).bit_length())]
+    greet(
+        low_peers + hi_peers + last_peers + (gain_peers if with_gains else [])
+    )
+
+    order = [(k, a) for k in list(range(1, hi)) + [0] for a in list(range(1, lo)) + [0]]
+
+    def block(k, a):
+        return lax.rem(high + k, hi) * lo + lax.rem(low + a, lo)
+
+    def slot(k, a):
+        return k * lo + a
+
+    sends = []
+    core_copies = {}
+    for k, a in order:
+        for b in list(range(1, wide)) + [0]:
+            there = lax.rem(across + b, wide)
+            copy = remote(
+                parts.at[block(k, a), there * 2 + 1 - core],
+                core_land.at[slot(k, a), b],
+                core_send.at[slot(k, a), b],
+                core_recv.at[slot(k, a), b],
+                partner,
+            )
+            copy.start()
+            core_copies[k, a, b] = copy
+            sends.append(copy)
+    gain_copies = []
+
+    def gains_step(i):
+        if not with_gains or i > len(gain_peers):
+            return
+        if i == 0:
+            gains_sum[0] = gains[...]
+        else:
+            gain_copies[i - 1].wait_recv()
+            gains_sum[i] = gains_sum[i - 1] + gains_land[i - 1]
+        if i < len(gain_peers):
+            copy = remote(
+                gains_sum.at[i], gains_land.at[i], gains_send.at[i], gains_recv.at[i], gain_peers[i]
+            )
+            copy.start()
+            gain_copies.append(copy)
+            sends.append(copy)
+        else:
+            gains_out[...] = gains_sum[i]
+
+    wide_copies, low_copies, hi_copies = {}, {}, {}
+
+    def sum_cores(k, a):
+        s = slot(k, a)
+        for b in list(range(1, wide)) + [0]:
+            there = lax.rem(across + b, wide)
+            core_copies[k, a, b].wait_recv()
+            total = parts[block(k, a), there * 2 + core].astype(jnp.float32) + core_land[
+                s, b
+            ].astype(jnp.float32)
+            if b:
+                wide_sum[s, b - 1] = total.astype(jnp.bfloat16)
+                copy = remote(
+                    wide_sum.at[s, b - 1], wide_land.at[s, b - 1], wide_send.at[s, b - 1],
+                    wide_recv.at[s, b - 1], wide_peers[b - 1],
+                )
+                copy.start()
+                wide_copies[k, a, b] = copy
+                sends.append(copy)
+            else:
+                keep[s] = total
+
+    def sum_wide(k, a):
+        s = slot(k, a)
+        total = keep[s]
+        for b in range(1, wide):
+            wide_copies[k, a, b].wait_recv()
+            total = total + wide_land[s, b - 1].astype(jnp.float32)
+        if a:
+            low_sum[k, a - 1] = total.astype(jnp.bfloat16)
+            copy = remote(
+                low_sum.at[k, a - 1], low_land.at[k, a - 1], low_send.at[k, a - 1],
+                low_recv.at[k, a - 1], low_peers[a - 1],
+            )
+            copy.start()
+            low_copies[k, a] = copy
+            sends.append(copy)
+        else:
+            keep[s] = total
+
+    def sum_low(k):
+        total = keep[slot(k, 0)]
+        for a in range(1, lo):
+            low_copies[k, a].wait_recv()
+            total = total + low_land[k, a - 1].astype(jnp.float32)
+        if k:
+            hi_sum[k - 1] = total.astype(jnp.bfloat16)
+            copy = remote(
+                hi_sum.at[k - 1], hi_land.at[k - 1], hi_send.at[k - 1], hi_recv.at[k - 1], hi_peers[k - 1]
+            )
+            copy.start()
+            hi_copies[k] = copy
+            sends.append(copy)
+        else:
+            keep[slot(0, 0)] = total
+
+    gains_step(0)
+    ks = list(range(1, hi)) + [0]
+    offsets = list(range(1, lo)) + [0]
+    for i in range(hi + 2):
+        if i < hi:
+            for a in offsets:
+                sum_cores(ks[i], a)
+        gains_step(i + 1)
+        if 1 <= i <= hi:
+            for a in offsets:
+                sum_wide(ks[i - 1], a)
+        if 2 <= i:
+            sum_low(ks[i - 2])
+    for i in range(hi + 3, len(gain_peers) + 1):
+        gains_step(i)
+    total = keep[slot(0, 0)]
+    for k in range(1, hi):
+        hi_copies[k].wait_recv()
+        total = total + hi_land[k - 1].astype(jnp.float32)
+    keep[slot(0, 0)] = total
+    for q in range(n):
+        last[q] = keep[slot(0, 0), :, q * cols : (q + 1) * cols].astype(jnp.bfloat16)
+    last_copies = []
+    for k in range(1, n):
+        copy = remote(
+            last.at[lax.rem(dp + k, n)], last_land.at[dp], last_send.at[k], last_recv.at[k], last_peers[k - 1]
+        )
+        copy.start()
+        last_copies.append(copy)
+        sends.append(copy)
+    last_land[dp] = last[dp]
+    for copy in last_copies:
+        copy.wait_recv()
+    for q in range(n):
+        out[q * rows : (q + 1) * rows] = last_land[q].astype(jnp.float32)
+    for copy in sends:
+        copy.wait_send()
+
+
+def scatter_attn(lay, parts, gains, collective_id):
+    rows = parts.shape[2]
+    cols = D // lay.dp
+    with_gains = gains is not None
+    lows, wides, his = max(1, lay.lo - 1), max(1, lay.wide - 1), max(1, lay.hi - 1)
+    vmem = pl.BlockSpec(memory_space=pltpu.VMEM)
+    dma = pltpu.SemaphoreType.DMA
+    out_shape = [jax.ShapeDtypeStruct((lay.dp * rows, cols), jnp.float32)]
+    scratch = [
+        pltpu.VMEM((lay.ctx, lay.wide, rows, D), jnp.bfloat16),
+        pltpu.VMEM((lay.ctx, wides, rows, D), jnp.bfloat16),
+        pltpu.VMEM((lay.ctx, wides, rows, D), jnp.bfloat16),
+        pltpu.VMEM((lay.ctx, rows, D), jnp.float32),
+        pltpu.VMEM((lay.hi, lows, rows, D), jnp.bfloat16),
+        pltpu.VMEM((lay.hi, lows, rows, D), jnp.bfloat16),
+        pltpu.VMEM((his, rows, D), jnp.bfloat16),
+        pltpu.VMEM((his, rows, D), jnp.bfloat16),
+        pltpu.VMEM((lay.dp, rows, cols), jnp.bfloat16),
+        pltpu.VMEM((lay.dp, rows, cols), jnp.bfloat16),
+    ]
+    for shape in ((lay.ctx, lay.wide), (lay.ctx, wides), (lay.hi, lows), (his,), (lay.dp,)):
+        scratch += [dma(shape), dma(shape)]
+    if with_gains:
+        count = (lay.dp - 1).bit_length() + (lay.ctx - 1).bit_length()
+        out_shape.append(jax.ShapeDtypeStruct(gains.shape, jnp.float32))
+        scratch += [
+            pltpu.VMEM((count + 1,) + gains.shape, jnp.float32),
+            pltpu.VMEM((count,) + gains.shape, jnp.float32),
+            dma((count,)),
+            dma((count,)),
+        ]
+    return pl.pallas_call(
+        partial(scatter_attn_kernel, lay, with_gains),
+        out_shape=tuple(out_shape),
+        in_specs=[vmem] * (2 if with_gains else 1),
+        out_specs=(vmem,) * len(out_shape),
+        scratch_shapes=scratch,
+        compiler_params=pltpu.CompilerParams(
+            collective_id=collective_id, has_side_effects=True, vmem_limit_bytes=VMEM_LIMIT
+        ),
+    )(*([parts, gains] if with_gains else [parts]))
+
+
+def exchange_out_kernel(lay, gate, up, down, pairs_out, lows_out, stack, land, lanes, send, recv):
+    n = lay.dp
+    dp = lax.axis_index("dp")
+    ctx = lax.axis_index("ctx")
+    cols = lows_out.shape[2]
+    per = lows_out.shape[1]
+    greet([(lax.rem(dp + k, n), ctx) for k in range(1, n)])
+    for q in range(n):
+        for i, piece in enumerate((gate, up, down)):
+            stack[q, i] = piece[:, q * cols : (q + 1) * cols]
+    pushes = []
+    for k in range(1, n):
+        target = lax.rem(dp + k, n)
+        push = remote(stack.at[target], land.at[dp], send.at[k], recv.at[k], (target, ctx))
+        push.start()
+        pushes.append(push)
+    land[dp] = stack[dp]
+    for push in pushes:
+        push.wait_recv()
+    for q in range(n):
+        for j, (first, width) in enumerate(lane_tiles(cols)):
+            for i in range(2):
+                piece = land[q, i, :per, first : first + width].astype(jnp.float32)
+                if width < 128:
+                    piece = jnp.concatenate(
+                        [piece, jnp.zeros((per, 128 - width), jnp.float32)], axis=1
+                    )
+                lanes[j, pl.ds(i, per, stride=2), :] = piece
+            pairs_out[q, :, first : first + width] = lanes[j, :, :width]
+        lows_out[q] = land[q, 2, :per].astype(jnp.float32)
+    for push in pushes:
+        push.wait_send()
+
+
+def exchange_out(lay, gate, up, down, per, collective_id):
+    padded = gate.shape[0]
+    n, cols = lay.dp, gate.shape[1] // lay.dp
+    vmem = pl.BlockSpec(memory_space=pltpu.VMEM)
+    return pl.pallas_call(
+        partial(exchange_out_kernel, lay),
+        out_shape=(
+            jax.ShapeDtypeStruct((n, 2 * per, cols), jnp.float32),
+            jax.ShapeDtypeStruct((n, per, cols), jnp.float32),
+        ),
+        in_specs=[vmem] * 3,
+        out_specs=(vmem,) * 2,
+        scratch_shapes=[
+            pltpu.VMEM((n, 3, padded, cols), jnp.bfloat16),
+            pltpu.VMEM((n, 3, padded, cols), jnp.bfloat16),
+            pltpu.VMEM((len(lane_tiles(cols)), 2 * per, 128), jnp.float32),
+            pltpu.SemaphoreType.DMA((n,)),
+            pltpu.SemaphoreType.DMA((n,)),
+        ],
+        compiler_params=pltpu.CompilerParams(
+            collective_id=collective_id, has_side_effects=True, vmem_limit_bytes=VMEM_LIMIT
+        ),
+    )(gate, up, down)
+
+
 def shifted(value, axis, steps):
     count = lax.axis_size(axis)
     leading, last = (max(0, -steps), min(count, count - steps))
@@ -211,22 +727,6 @@
     return jax.nn.gelu(gate, approximate=True) * up
 
 
-def to_group(lay, quarters):
-    rows, cols = quarters.shape
-    per = rows // lay.dp
-    padded = -(-per // 16) * 16
-    value = quarters.astype(jnp.bfloat16).reshape(lay.dp, per, cols)
-    return jnp.pad(value, ((0, 0), (0, padded - per), (0, 0)))
-
-
-def across(lay, stacked):
-    return lax.all_to_all(stacked, "dp", split_axis=0, concat_axis=2, tiled=True)[0]
-
-
-def back_across(lay, rows):
-    return lax.all_to_all(rows[None], "dp", split_axis=2, concat_axis=0, tiled=True)
-
-
 def contract(left, right, dims_left, dims_right):
     return lax.dot_general(
         left, right, ((dims_left, dims_right), ((), ())), preferred_element_type=jnp.float32
@@ -238,39 +738,38 @@
     local_len = tokens.shape[1]
     reach = (WINDOW - 1) // local_len + 1
     scale = 1.0 / math.sqrt(HD)
-    attn_masters = (
-        w_qkv.astype(jnp.bfloat16),
-        w_out.astype(jnp.bfloat16),
-        gains.astype(jnp.bfloat16),
-    )
-    row_qkv, row_out, row_gain = (
-        lax.all_gather(attn_masters[0], "ctx", axis=0, tiled=True),
-        lax.all_gather(attn_masters[1], "ctx", axis=0, tiled=True),
-        lax.all_gather(attn_masters[2], "ctx", axis=0, tiled=True),
-    )
-    full_qkv, full_out, gain_low = (
-        lax.all_gather(row_qkv, "dp", axis=1, tiled=True),
-        lax.all_gather(row_out, "dp", axis=1, tiled=True),
-        lax.all_gather(row_gain, "dp", axis=0, tiled=True),
-    )
-    pairs = w_gate_up.reshape(w_gate_up.shape[0] // 2, 2, w_gate_up.shape[1])
-    per = pairs.shape[0] // lay.dp
-    stacked = jnp.concatenate(
-        [to_group(lay, pairs[:, 0]), to_group(lay, pairs[:, 1]), to_group(lay, w_down)], axis=1
-    )
-    padded = stacked.shape[1] // 3
-    moved = across(lay, stacked)
+    units = w_down.shape[0]
+    per = units // lay.dp
+    qkv_rows, out_rows = w_qkv.shape[0], w_out.shape[0]
+    cols = w_qkv.shape[1]
+    used = qkv_rows + out_rows + 1
+    block = 16 * lay.dp
+    pack_rows = -(-used // block) * block
+    gain_row = jnp.pad(gains, (0, cols - gains.shape[0]))[None]
+    pack = jnp.concatenate(
+        [w_qkv, w_out, gain_row, jnp.zeros((pack_rows - used, cols), jnp.float32)], axis=0
+    ).astype(jnp.bfloat16)
+    own_attn, gate_rows, up_rows, low_rows = exchange_in(
+        lay,
+        pack.reshape(lay.dp, pack_rows // lay.dp, cols),
+        w_gate_up.reshape(lay.dp, 2 * per, cols),
+        w_down.reshape(lay.dp, per, cols),
+        5,
+    )
     w_gate, w_up, w_low = (
-        lax.all_gather(
-            moved[i * padded : (i + 1) * padded],
-            "ctx",
-            axis=0,
-            tiled=True,
-            axis_index_groups=lay.hi_groups,
-        )
-        for i in range(3)
-    )
-    gain_all = gain_low.astype(jnp.float32)
+        lax.all_gather(rows, "ctx", axis=0, tiled=True, axis_index_groups=lay.hi_groups)
+        for rows in (gate_rows, up_rows, low_rows)
+    )
+    attn_all = gather_attn(lay, own_attn, 6).reshape(lay.ctx, pack_rows, D)
+    full_qkv = attn_all[:, :qkv_rows].reshape(lay.ctx * qkv_rows, D)
+    full_out = attn_all[:, qkv_rows : qkv_rows + out_rows].reshape(lay.ctx * out_rows, D)
+    gain_all = (
+        attn_all[:, used - 1]
+        .reshape(lay.ctx, lay.dp, cols)[:, :, : gains.shape[0]]
+        .transpose(1, 0, 2)
+        .reshape(-1)
+        .astype(jnp.float32)
+    )
     gain_in = gain_all[:D]
     gain_attn = gain_all[D : 2 * D]
     gain_pre = gain_all[2 * D : 3 * D]
@@ -399,39 +898,29 @@
             grad_gain_key,
         ]
     )
-    col_qkv, col_out, col_gains = (
-        lax.psum_scatter(
-            grad_w_qkv.astype(jnp.bfloat16), "dp", scatter_dimension=1, tiled=True
-        ).astype(jnp.float32),
-        lax.psum_scatter(
-            grad_w_out.astype(jnp.bfloat16), "dp", scatter_dimension=1, tiled=True
-        ).astype(jnp.float32),
-        lax.psum_scatter(
-            grad_gain_all.astype(jnp.bfloat16), "dp", scatter_dimension=0, tiled=True
-        ).astype(jnp.float32),
-    )
-    part_qkv, part_out, part_gains = (
-        lax.psum_scatter(
-            col_qkv.astype(jnp.bfloat16), "ctx", scatter_dimension=0, tiled=True
-        ).astype(jnp.float32),
-        lax.psum_scatter(
-            col_out.astype(jnp.bfloat16), "ctx", scatter_dimension=0, tiled=True
-        ).astype(jnp.float32),
-        lax.psum_scatter(
-            col_gains.astype(jnp.bfloat16), "ctx", scatter_dimension=0, tiled=True
-        ).astype(jnp.float32),
-    )
+    def own_blocks(grad, rows):
+        whole = grad.astype(jnp.bfloat16).reshape(lay.ctx, rows, D)
+        padded = -(-rows // block) * block
+        whole = jnp.pad(whole, ((0, 0), (0, padded - rows), (0, 0)))
+        return whole.reshape(lay.ctx, lay.dp, padded // lay.dp, D)
+
+    (part_out,) = scatter_attn(lay, own_blocks(grad_w_out, out_rows), None, 7)
+    part_qkv, gains_sum = scatter_attn(
+        lay, own_blocks(grad_w_qkv, qkv_rows), grad_gain_all.reshape(-1, 128), 8
+    )
+    part_out = part_out[:out_rows]
+    part_qkv = part_qkv[:qkv_rows]
+    place = (lax.axis_index("dp") * lay.ctx + lax.axis_index("ctx")) * gains.shape[0]
+    part_gains = lax.dynamic_slice_in_dim(gains_sum.reshape(-1), place, gains.shape[0])
     owned = [
         lax.psum_scatter(
             piece, "ctx", scatter_dimension=0, tiled=True, axis_index_groups=lay.hi_groups
         )
         for piece in (grad_low, grad_w_gate, grad_w_up)
     ]
-    returned = back_across(lay, jnp.concatenate(owned, axis=0)).astype(jnp.float32)
-    part_down = returned[:, :per].reshape(w_down.shape)
-    part_gate_up = jnp.stack(
-        [returned[:, padded : padded + per], returned[:, 2 * padded : 2 * padded + per]], axis=2
-    ).reshape(w_gate_up.shape)
+    part_gate_up, part_down = exchange_out(lay, owned[1], owned[2], owned[0], per, 9)
+    part_gate_up = part_gate_up.reshape(w_gate_up.shape)
+    part_down = part_down.reshape(w_down.shape)
     return (result, grad_input, part_qkv, part_out, part_gate_up, part_down, part_gains)
 
 

time: 835 us -> 638 us (0.76)
  Pallas kernels: 165 us -> 382 us
  waiting for transfers between devices: 221 us -> 30.7 us
  blocking collectives: 153 us -> 0 us
  local copies, waits for them, and re-layouts: 79.6 us -> 37.9 us
  other arithmetic: 42.9 us -> 26.7 us
    pallas_call x0 -> x5, Pallas kernels: none -> 233 us  [the longest x2 116 us: scatter_attn(): pl.pallas_call(partial(scatter_attn_kernel, lay, with_gains), out_shape=t...]
    reduce_scatter x3, waiting for transfers between devices: 75.7 us -> 0.01 us  [per_device(): lax.psum_scatter(piece, 'ctx', scatter_dimension=0, tiled=True, axis_inde...]
    unnamed x14 -> x6, waiting for transfers between devices: 73.9 us -> 0.78 us
    all_gather x3 -> x0, blocking collectives: 61.3 us -> none  [the longest x1 26.3 us: per_device(): lax.all_gather(attn_masters[1], 'ctx', axis=0, tiled=True)]
    unnamed x3 -> x0, blocking collectives: 56.3 us -> none
    ppermute x8, waiting for transfers between devices: 71.2 us -> 29.9 us  [shifted(): lax.ppermute(value, axis, [(source, source + steps) for source in range(l...]
    all_to_all x1 -> x0, blocking collectives: 35.4 us -> none  [across(): lax.all_to_all(stacked, 'dp', split_axis=0, concat_axis=2, tiled=True)[0]]
    pallas_call x2, Pallas kernels: 96.2 us -> 79.3 us  [gather_tokens(): pl.pallas_call(partial(gather_tokens_kernel, lay), out_shape=jax.ShapeDty...]
  transfers between devices with their start and end apart: 21 -> 14, of which waited for: 11 -> 6; matrix products, arithmetic and copies ran while one was open for 22% -> 21% of each run, Pallas kernels for 8% -> 40%
where the time goes in v2:
time: 638 us; the launch traced here: 630 us
  Pallas kernels  382 us (60%)
  matrix products  110 us (17%)
  local copies, waits for them, and re-layouts  37.9 us (6%)
  waiting for transfers between devices  30.7 us (5%)
  starting transfers between devices  27.1 us (4%)
  other arithmetic  26.7 us (4%)
  between operations  15.6 us (2%)
    pallas_call x2, Pallas kernels, scatter_attn(): pl.pallas_call(partial(scatter_attn_kernel, lay, with_gains), out_shape=t...  116 us
    dot_general x15, matrix products, contract(): lax.dot_general(left, right, ((dims_left, dims_right), ((), ())), preferr...  103 us
    pallas_call x2, Pallas kernels, gather_tokens(): pl.pallas_call(partial(gather_tokens_kernel, lay), out_shape=jax.ShapeDty...  79.3 us
    pallas_call x2, Pallas kernels, scatter_tokens(): pl.pallas_call(partial(scatter_tokens_kernel, lay), out_shape=jax.ShapeDt...  69.4 us
    pallas_call x1, Pallas kernels, gather_attn(): pl.pallas_call(partial(gather_attn_kernel, lay), out_shape=jax.ShapeDtype...  54.6 us
    pallas_call x1, Pallas kernels, exchange_in(): pl.pallas_call(partial(exchange_in_kernel, lay), out_shape=(jax.ShapeDtyp...  32.5 us
    pallas_call x1, Pallas kernels, exchange_out(): pl.pallas_call(partial(exchange_out_kernel, lay), out_shape=(jax.ShapeDty...  30.4 us
    ppermute x8, waiting for transfers between devices, shifted(): lax.ppermute(value, axis, [(source, source + steps) for source in range(l...  29.9 us
  transfers between devices with their start and end apart: 14, of which 6 were waited for; matrix products, arithmetic and copies ran while one was open for 21% of the time, Pallas kernels for 40%

profile of v2, /device:TPU:9, one launch (start us, length us, event | category | flops | bytes accessed | tf_op | source)
XLA Modules:
  0.0 630.2 jit_solution(16914818330022733622)
XLA Ops:
  7.2 3.2 copy.136
  13.1 32.5 %shard_map.135 = (bf16[96,1152]{1,0:T(8,128)(2,1)}, bf16[224,1152]{1,0:T(8,128)(2,1)}, bf16[224,1152]{1,0:T(8,128)(2,1)}, bf16[224,1152]{1,0:T(8,128)(2,1)}) custom-call(bf16[4,96,288]{2,1,0:T(8,128)(2,1)} %bitcast.179, f32[4,432,288]{2,1,0:T(8,128)} %bitcast.161, f32[4,216,288]{2,1,0:T(8,128)} %bitcast.165), custom_call_target="tpu_custom_call" | custom-call | tf_op jit(solution)/shard_map/pallas_call | solution.py:242
  46.5 54.6 %shard_map.136 = bf16[8,4,96,1152]{3,2,1,0:T(8,128)(2,1)} custom-call(bf16[96,1152]{1,0:T(8,128)(2,1)} %get-tuple-element.15.own), custom_call_target="tpu_custom_call" | custom-call | tf_op jit(solution)/shard_map/pallas_call | solution.py:401
  102.1 4.2 slice.111
  107.3 3.5 fusion.49
  114.3 13.4 %collective-permute-start = (bf16[2,128,512]{2,1,0:T(8,128)(2,1)}, bf16[2,128,512]{2,1,0:T(8,128)(2,1)}, u32[]{:S(2)}, u32[]{:S(2)}) collective-permute-start(bf16[2,128,512]{2,1,0:T(8,128)(2,1)} %pad_maximum_fusion.4), channel_id=1, source_target_pairs={{0,4},{1,5},{2,6},{3,7},{8,12},{9,13},{10,14},{11,15},{16,20},{17,... | collective-permute-start | bytes 786440 | tf_op jit(solution)/shard_map/ppermute | solution.py:694
  131.6 2.4 collective-permute-start.3
  138.5 3.2 slice.123
  141.7 9.7 %collective-permute-done = bf16[2,128,512]{2,1,0:T(8,128)(2,1)} collective-permute-done((bf16[2,128,512]{2,1,0:T(8,128)(2,1)}, bf16[2,128,512]{2,1,0:T(8,128)(2,1)}, u32[]{:S(2)}, u32[]{:S(2)}) %collective-permute-start) | collective-permute-done | bytes 262176 | tf_op jit(solution)/shard_map/ppermute | solution.py:694
  152.4 7.2 %collective-permute-done.1 = bf16[2,128,512]{2,1,0:T(8,128)(2,1)} collective-permute-done((bf16[2,128,512]{2,1,0:T(8,128)(2,1)}, bf16[2,128,512]{2,1,0:T(8,128)(2,1)}, u32[]{:S(2)}, u32[]{:S(2)}) %collective-permute-start.1) | collective-permute-done | bytes 262176 | tf_op jit(solution)/shard_map/ppermute | solution.py:694
  160.6 4.6 collective-permute-done.2
  175.4 47.2 %shard_map.137 = bf16[8,256,1152]{2,1,0:T(8,128)(2,1)} custom-call(bf16[256,1152]{1,0:T(8,128)(2,1)} %bitcast.174), custom_call_target="tpu_custom_call" | custom-call | tf_op jit(solution)/shard_map/pallas_call | solution.py:90
  222.6 9.8 %fusion.21 = f32[8,256,896]{2,1,0:T(8,128)} fusion(bf16[8,256,1152]{2,1,0:T(8,128)(2,1)} %shard_map.137, bf16[896,1152]{1,0:T(8,128)(2,1)} %all-gather.4.cloned.1.call-done), kind=kOutput, calls=%fused_computation.47 | convolution fusion | flops 4227858432 | bytes 14123008 | tf_op jit(solution)/shard_map/dot_general | solution.py:731
  232.5 12.3 %multiply_convert_fusion.1 = (bf16[8,256,896]{2,1,0:T(8,128)(2,1)}, f32[8,256,896]{2,1,0:T(8,128)}) fusion(f32[8,256,896]{2,1,0:T(8,128)} %fusion.21, bf16[8,256,1152]{2,1,0:T(8,128)(2,1)} %shard_map.137, bf16[896,1152]{1,0:T(8,128)(2,1)} %all-gather.6.cloned.1.call-done), kind=kOutput, calls=%fused_computation.13 | convolution fusion | flops 4246208512 | bytes 25133056 | tf_op jit(solution)/shard_map/dot_general | solution.py:731
  244.7 9.4 %convolution_convert_fusion.parts = bf16[8,256,1152]{2,1,0:T(8,128)(2,1)} fusion(bf16[8,256,896]{2,1,0:T(8,128)(2,1)} %get-tuple-element.102, bf16[896,1152]{1,0:T(8,128)(2,1)} %all-gather.8.cloned.1.call-done), kind=kOutput, calls=%fused_computation.15 | convolution fusion | flops 4230217728 | bytes 10452992 | tf_op jit(solution)/shard_map/dot_general | solution.py:731
  254.2 34.7 %shard_map.138 = f32[256,1152]{1,0:T(8,128)} custom-call(bf16[8,256,1152]{2,1,0:T(8,128)(2,1)} %convolution_convert_fusion.parts), custom_call_target="tpu_custom_call" | custom-call | tf_op jit(solution)/shard_map/pallas_call | solution.py:155
  294.2 32.2 %shard_map.139 = bf16[8,256,1152]{2,1,0:T(8,128)(2,1)} custom-call(bf16[256,1152]{1,0:T(8,128)(2,1)} %bitcast.175), custom_call_target="tpu_custom_call" | custom-call | tf_op jit(solution)/shard_map/pallas_call | solution.py:90
  326.4 8.6 %bitcast_convert_fusion.1 = bf16[896,1152]{1,0:T(8,128)(2,1)} fusion(bf16[8,256,896]{2,1,0:T(8,128)(2,1)S(1)} %copy-done.66, bf16[8,256,1152]{2,1,0:T(8,128)(2,1)} %shard_map.139), kind=kOutput, calls=%fused_computation.17 | convolution fusion | flops 4228890624 | bytes 10452992 | tf_op jit(solution)/shard_map/dot_general | solution.py:731
  335.1 15.0 %multiply_convert_fusion = (bf16[8,256,896]{2,1,0:T(8,128)(2,1)S(1)}, bf16[8,256,896]{2,1,0:T(8,128)(2,1)S(1)}) fusion(f32[8,256,896]{2,1,0:T(8,128)} %fusion.21, f32[8,256,896]{2,1,0:T(8,128)} %get-tuple-element.103, bf16[8,256,1152]{2,1,0:T(8,128)(2,1)} %shard_map.139, bf16[896,1152]{1,0:T(8,128)(2,1)} %all-gather.8.cloned.1.call-done), kind=kOutput, calls=%fused_computation.12 | convolution fusion | flops 4271898624 | bytes 28803072 | tf_op jit(solution)/shard_map/dot_general | solution.py:731
  350.1 7.9 %fusion.19 = f32[8,256,1152]{2,1,0:T(8,128)} fusion(bf16[8,256,896]{2,1,0:T(8,128)(2,1)S(1)} %get-tuple-element.73, bf16[896,1152]{1,0:T(8,128)(2,1)S(1)} %copy-done.59), kind=kOutput, calls=%fused_computation.45 | convolution fusion | flops 4227858432 | bytes 15171584 | tf_op jit(solution)/shard_map/dot_general | solution.py:731
  358.0 9.9 %add_convert_fusion.parts = bf16[8,256,1152]{2,1,0:T(8,128)(2,1)} fusion(f32[8,256,1152]{2,1,0:T(8,128)} %fusion.19, bf16[8,256,896]{2,1,0:T(8,128)(2,1)S(1)} %get-tuple-element.72, bf16[896,1152]{1,0:T(8,128)(2,1)S(1)} %copy-done.60), kind=kOutput, calls=%fused_computation.2 | convolution fusion | flops 4232577024 | bytes 19890176 | tf_op jit(solution)/shard_map/dot_general | solution.py:731
  367.9 34.6 %shard_map.140 = f32[256,1152]{1,0:T(8,128)} custom-call(bf16[8,256,1152]{2,1,0:T(8,128)(2,1)} %add_convert_fusion.parts), custom_call_target="tpu_custom_call" | custom-call | tf_op jit(solution)/shard_map/pallas_call | solution.py:155
  407.5 8.6 %bitcast_convert_fusion.2 = bf16[896,1152]{1,0:T(8,128)(2,1)} fusion(bf16[8,256,896]{2,1,0:T(8,128)(2,1)S(1)} %copy-done.65, bf16[8,256,1152]{2,1,0:T(8,128)(2,1)} %shard_map.137), kind=kOutput, calls=%fused_computation.18 | convolution fusion | flops 4228890624 | bytes 10452992 | tf_op jit(solution)/shard_map/dot_general | solution.py:731
  419.0 2.3 bitcast_convert_fusion
  421.3 39.8 %shard_map.142 = f32[128,288]{1,0:T(8,128)} custom-call(bf16[8,4,32,1152]{3,2,1,0:T(8,128)(2,1)} %bitcast.164), custom_call_target="tpu_custom_call" | custom-call | tf_op jit(solution)/shard_map/pallas_call | solution.py:620
  462.9 3.5 convolution_convert_fusion.1
  483.6 6.4 %bitcast_convert_fusion.3 = bf16[896,1152]{1,0:T(8,128)(2,1)} fusion(bf16[8,256,896]{2,1,0:T(8,128)(2,1)S(1)} %copy-done.63, bf16[8,256,1152]{2,1,0:T(8,128)(2,1)S(1)} %bitcast.169), kind=kOutput, calls=%fused_computation.19 | convolution fusion | flops 4228890624 | bytes 10452992 | tf_op jit(solution)/shard_map/dot_general | solution.py:731
  492.6 6.6 %collective-permute-done.6 = bf16[2,128,512]{2,1,0:T(8,128)(2,1)} collective-permute-done((bf16[2,128,512]{2,1,0:T(8,128)(2,1)}, bf16[2,128,512]{2,1,0:T(8,128)(2,1)}, u32[]{:S(2)}, u32[]{:S(2)}) %collective-permute-start.6) | collective-permute-done | bytes 262176 | tf_op jit(solution)/shard_map/ppermute | solution.py:694
  505.6 3.0 fusion
  508.6 76.0 %shard_map.141 = (f32[192,288]{1,0:T(8,128)}, f32[40,128]{1,0:T(8,128)}) custom-call(bf16[8,4,48,1152]{3,2,1,0:T(8,128)(2,1)} %bitcast.172, f32[40,128]{1,0:T(8,128)} %bitcast.185), custom_call_target="tpu_custom_call" | custom-call | tf_op jit(solution)/shard_map/pallas_call | solution.py:620
  587.4 30.4 %shard_map.143 = (f32[4,432,288]{2,1,0:T(8,128)}, f32[4,216,288]{2,1,0:T(8,128)}) custom-call(bf16[224,1152]{1,0:T(8,128)(2,1)} %reduce-scatter.4.cloned.1.call-done.gate, bf16[224,1152]{1,0:T(8,128)(2,1)} %reduce-scatter.6.cloned.1.call-done.up, bf16[224,1152]{1,0:T(8,128)(2,1)} %reduce-scatter.8.cloned.1.call-done.down), custom_call_target="tpu_custom_call" | custom-call | tf_op jit(solution)/shard_map/pallas_call | solution.py:670
  617.8 3.2 copy.163
  (268 shorter events, 74.3 us)
Async XLA Ops:
  7.2 215.5 %all-gather.4.cloned.1.call-start = ((), (), s32[]{:S(2)}) async-start(), calls=%async_computation.3 | async-start | bytes 2580480 | tf_op jit(solution)/shard_map/all_gather | solution.py:760
  45.7 186.8 %all-gather.6.cloned.1.call-start = ((), (), s32[]{:S(2)}) async-start(), calls=%async_computation.4 | async-start | bytes 2580480 | tf_op jit(solution)/shard_map/all_gather | solution.py:760
  46.4 198.3 %all-gather.8.cloned.1.call-start = ((), (), s32[]{:S(2)}) async-start(), calls=%async_computation.5 | async-start | bytes 2580480 | tf_op jit(solution)/shard_map/all_gather | solution.py:760
  110.8 23.6 %copy-start.21 = (f32[2,128,1536]{2,1,0:T(8,128)}, f32[2,128,1536]{2,1,0:T(8,128)S(1)}, u32[]{:S(2)}) copy-start(f32[2,128,1536]{2,1,0:T(8,128)S(1)} %fusion.49) | copy-start | bytes 4718596
  114.3 37.1 %collective-permute-start = (bf16[2,128,512]{2,1,0:T(8,128)(2,1)}, bf16[2,128,512]{2,1,0:T(8,128)(2,1)}, u32[]{:S(2)}, u32[]{:S(2)}) collective-permute-start(bf16[2,128,512]{2,1,0:T(8,128)(2,1)} %pad_maximum_fusion.4), channel_id=1, source_target_pairs={{0,4},{1,5},{2,6},{3,7},{8,12},{9,13},{10,14},{11,15},{16,20},{17,... | collective-permute-start | bytes 786440 | tf_op jit(solution)/shard_map/ppermute | solution.py:694
  127.7 31.9 %collective-permute-start.1 = (bf16[2,128,512]{2,1,0:T(8,128)(2,1)}, bf16[2,128,512]{2,1,0:T(8,128)(2,1)}, u32[]{:S(2)}, u32[]{:S(2)}) collective-permute-start(bf16[2,128,512]{2,1,0:T(8,128)(2,1)} %pad_maximum_fusion.4), channel_id=1, source_target_pairs={{0,3},{1,4},{2,5},{3,6},{4,7},{8,11},{9,12},{10,13},{11,14},{12,15... | collective-permute-start | bytes 786440 | tf_op jit(solution)/shard_map/ppermute | solution.py:694
  129.7 35.5 %collective-permute-start.2 = (bf16[2,128,512]{2,1,0:T(8,128)(2,1)}, bf16[2,128,512]{2,1,0:T(8,128)(2,1)}, u32[]{:S(2)}, u32[]{:S(2)}) collective-permute-start(bf16[2,128,512]{2,1,0:T(8,128)(2,1)} %pad_maximum_fusion.4), channel_id=1, source_target_pairs={{0,2},{1,3},{2,4},{3,5},{4,6},{5,7},{8,10},{9,11},{10,12},{11,13},... | collective-permute-start | bytes 786440 | tf_op jit(solution)/shard_map/ppermute | solution.py:694
  131.6 35.2 %collective-permute-start.3 = (bf16[2,128,512]{2,1,0:T(8,128)(2,1)}, bf16[2,128,512]{2,1,0:T(8,128)(2,1)}, u32[]{:S(2)}, u32[]{:S(2)}) collective-permute-start(bf16[2,128,512]{2,1,0:T(8,128)(2,1)} %pad_maximum_fusion.4), channel_id=1, source_target_pairs={{0,1},{1,2},{2,3},{3,4},{4,5},{5,6},{6,7},{8,9},{9,10},{10,11},{11... | collective-permute-start | bytes 786440 | tf_op jit(solution)/shard_map/ppermute | solution.py:694
  134.1 453.3 %reduce-scatter.8.cloned.1.call-start = ((), (), s32[]{:S(2)}) async-start(), calls=%async_computation.8 | async-start | bytes 2580480 | tf_op jit(solution)/shard_map/reduce_scatter | solution.py:916
  141.7 26.1 %copy-start.32 = (bf16[2,128,128]{2,1,0:T(8,128)(2,1)S(1)}, bf16[2,128,128]{2,1,0:T(8,128)(2,1)}, u32[]{:S(2)}) copy-start(bf16[2,128,128]{2,1,0:T(8,128)(2,1)} %copy-done.31) | copy-start | bytes 196612
  254.2 36.4 %copy-start.17 = (bf16[2,128,1152]{2,1,0:T(8,128)(2,1)S(1)}, bf16[2,128,1152]{2,1,0:T(8,128)(2,1)}, u32[]{:S(2)}) copy-start(bf16[2,128,1152]{2,1,0:T(8,128)(2,1)} %param.15) | copy-start | bytes 1769476
  254.2 36.4 %copy-start.36 = (f32[1152]{0:T(1024)S(1)}, f32[1152]{0:T(1024)}, u32[]{:S(2)}) copy-start(f32[1152]{0:T(1024)} %get-tuple-element.89) | copy-start | bytes 13828
  254.2 36.4 %copy-start.55 = (pred[2,128]{1,0:T(4,128)(4,1)S(1)}, pred[2,128]{1,0:T(4,128)(4,1)}, u32[]{:S(2)}) copy-start(pred[2,128]{1,0:T(4,128)(4,1)} %broadcast_compare_fusion.3) | copy-start | bytes 772
  294.2 32.2 %copy-start.66 = (bf16[8,256,896]{2,1,0:T(8,128)(2,1)S(1)}, bf16[8,256,896]{2,1,0:T(8,128)(2,1)}, u32[]{:S(2)}) copy-start(bf16[8,256,896]{2,1,0:T(8,128)(2,1)} %get-tuple-element.102) | copy-start | bytes 11010052
  335.1 252.3 %reduce-scatter.6.cloned.1.call-start = ((), (), s32[]{:S(2)}) async-start(), calls=%async_computation.7 | async-start | bytes 2580480 | tf_op jit(solution)/shard_map/reduce_scatter | solution.py:916
  335.1 15.0 %copy-start.59 = (bf16[896,1152]{1,0:T(8,128)(2,1)S(1)}, bf16[896,1152]{1,0:T(8,128)(2,1)}, u32[]{:S(2)}) copy-start(bf16[896,1152]{1,0:T(8,128)(2,1)} %all-gather.4.cloned.1.call-done) | copy-start | bytes 6193156
  367.9 34.7 %copy-start.2 = (f32[2,128,1152]{2,1,0:T(8,128)S(1)}, f32[2,128,1152]{2,1,0:T(8,128)}, u32[]{:S(2)}) copy-start(f32[2,128,1152]{2,1,0:T(8,128)} %copy-done) | copy-start | bytes 3538948
  416.2 171.2 %reduce-scatter.4.cloned.1.call-start = ((), (), s32[]{:S(2)}) async-start(), calls=%async_computation.6 | async-start | bytes 2580480 | tf_op jit(solution)/shard_map/reduce_scatter | solution.py:916
  472.4 11.3 %slice-start = ((s8[4718592]{0:T(1024)(128)(4,1)}), s8[4194304]{0:T(1024)(128)(4,1)S(1)}, s32[]{:S(2)}) async-start(s8[4718592]{0:T(1024)(128)(4,1)} %bitcast.168), calls=%async_computation.9 | async-start | bytes 8388608
  473.4 8.5 %copy-start.26 = (bf16[2,640,512]{2,1,0:T(8,128)(2,1)S(1)}, bf16[2,640,512]{2,1,0:T(8,128)(2,1)}, u32[]{:S(2)}) copy-start(bf16[2,640,512]{2,1,0:T(8,128)(2,1)} %copy-done.25) | copy-start | bytes 3932164
  473.4 10.2 %slice-start.1 = ((s8[4718592]{0:T(1024)(128)(4,1)}), s8[524288]{0:T(1024)(128)(4,1)S(1)}, s32[]{:S(2)}) async-start(s8[4718592]{0:T(1024)(128)(4,1)} %bitcast.168), calls=%async_computation.10 | async-start | bytes 1048576
  473.6 10.1 %copy-start.63 = (bf16[8,256,896]{2,1,0:T(8,128)(2,1)S(1)}, bf16[8,256,896]{2,1,0:T(8,128)(2,1)}, u32[]{:S(2)}) copy-start(bf16[8,256,896]{2,1,0:T(8,128)(2,1)} %copy-done.62) | copy-start | bytes 11010052
  474.9 17.7 %collective-permute-start.4 = (bf16[2,128,512]{2,1,0:T(8,128)(2,1)}, bf16[2,128,512]{2,1,0:T(8,128)(2,1)S(1)}, u32[]{:S(2)}, u32[]{:S(2)}) collective-permute-start(bf16[2,128,512]{2,1,0:T(8,128)(2,1)} %get-tuple-element.74), channel_id=1, source_target_pairs={{1,0},{2,1},{3,2},{4,3},{5,4},{6,5},{7,6},{9,8},{10,9},{11,10},{12... | collective-permute-start | bytes 786440 | tf_op jit(solution)/shard_map/ppermute | solution.py:694
  477.2 15.4 %collective-permute-start.5 = (bf16[2,128,512]{2,1,0:T(8,128)(2,1)}, bf16[2,128,512]{2,1,0:T(8,128)(2,1)S(1)}, u32[]{:S(2)}, u32[]{:S(2)}) collective-permute-start(bf16[2,128,512]{2,1,0:T(8,128)(2,1)} %get-tuple-element.77), channel_id=1, source_target_pairs={{2,0},{3,1},{4,2},{5,3},{6,4},{7,5},{10,8},{11,9},{12,10},{13,11},... | collective-permute-start | bytes 786440 | tf_op jit(solution)/shard_map/ppermute | solution.py:694
  479.1 20.1 %collective-permute-start.6 = (bf16[2,128,512]{2,1,0:T(8,128)(2,1)}, bf16[2,128,512]{2,1,0:T(8,128)(2,1)}, u32[]{:S(2)}, u32[]{:S(2)}) collective-permute-start(bf16[2,128,512]{2,1,0:T(8,128)(2,1)} %get-tuple-element.76), channel_id=1, source_target_pairs={{3,0},{4,1},{5,2},{6,3},{7,4},{11,8},{12,9},{13,10},{14,11},{15,12... | collective-permute-start | bytes 786440 | tf_op jit(solution)/shard_map/ppermute | solution.py:694
  480.4 19.8 %collective-permute-start.7 = (bf16[2,128,512]{2,1,0:T(8,128)(2,1)}, bf16[2,128,512]{2,1,0:T(8,128)(2,1)}, u32[]{:S(2)}, u32[]{:S(2)}) collective-permute-start(bf16[2,128,512]{2,1,0:T(8,128)(2,1)} %get-tuple-element.75), channel_id=1, source_target_pairs={{4,0},{5,1},{6,2},{7,3},{12,8},{13,9},{14,10},{15,11},{20,16},{21,... | collective-permute-start | bytes 786440 | tf_op jit(solution)/shard_map/ppermute | solution.py:694
  492.0 8.2 %copy-start.12 = (f32[2,640,256]{2,1,0:T(8,128)S(1)}, f32[2,640,256]{2,1,0:T(8,128)}, u32[]{:S(2)}) copy-start(f32[2,640,256]{2,1,0:T(8,128)} %copy-done.11) | copy-start | bytes 3932164
  492.5 9.2 %copy-start.48 = (f32[2,128]{1,0:T(2,128)S(1)}, f32[2,128]{1,0:T(2,128)}, u32[]{:S(2)}) copy-start(f32[2,128]{1,0:T(2,128)} %copy-done.47) | copy-start | bytes 3076
  492.5 9.2 %copy-start.50 = (f32[256]{0:T(256)S(1)}, f32[256]{0:T(256)}, u32[]{:S(2)}) copy-start(f32[256]{0:T(256)} %copy-done.49) | copy-start | bytes 3076
  492.5 10.3 %copy-start.54 = (f32[2,128]{1,0:T(2,128)S(1)}, f32[2,128]{1,0:T(2,128)}, u32[]{:S(2)}) copy-start(f32[2,128]{1,0:T(2,128)} %copy-done.53) | copy-start | bytes 3076
  508.6 77.4 %copy-start.52 = (f32[2,128]{1,0:T(2,128)S(1)}, f32[2,128]{1,0:T(2,128)}, u32[]{:S(2)}) copy-start(f32[2,128]{1,0:T(2,128)} %copy-done.51) | copy-start | bytes 3076
  508.6 77.4 %copy-start.7 = (f32[2,128,1152]{2,1,0:T(8,128)S(1)}, f32[2,128,1152]{2,1,0:T(8,128)}, u32[]{:S(2)}) copy-start(f32[2,128,1152]{2,1,0:T(8,128)} %copy-done.6) | copy-start | bytes 3538948
  (51 other events, 124.1 us)
Sparse Core Ops, SparseCore 0:
  45.8 51.9 all-gather.3
  99.4 57.1 all-gather.5
  158.1 51.2 all-gather.7
  335.2 42.4 reduce-scatter.7
  416.3 50.3 reduce-scatter.5
  490.2 56.3 reduce-scatter.3

commit v3 on v2

--- a/solution.py
+++ b/solution.py
@@ -39,6 +39,14 @@
         chip = lax.rem(ctx, self.lo) * self.wide + dp // 2
         return chip, lax.rem(dp, 2), ctx // self.lo
 
+    def offset(self, chip, k, sign=1):
+        across = lax.rem(chip, self.wide) + self.wide + sign * (k % self.wide)
+        low = chip // self.wide + self.lo + sign * (k // self.wide)
+        return lax.rem(low, self.lo) * self.wide + lax.rem(across, self.wide)
+
+    def back(self, k):
+        return (-(k // self.wide)) % self.lo * self.wide + (-(k % self.wide)) % self.wide
+
     def device(self, chip, core, high):
         return (lax.rem(chip, self.wide) * 2 + core, high * self.lo + chip // self.wide)
 
@@ -59,7 +67,7 @@
 def gather_tokens_kernel(lay, own, out, local_sem, send, recv, core_send, core_recv):
     chip, core, high = lay.place()
     n = lay.chips
-    peers = [lay.device(lax.rem(chip + k, n), core, high) for k in range(1, n)]
+    peers = [lay.device(lay.offset(chip, k), core, high) for k in range(1, n)]
     partner = lay.device(chip, 1 - core, high)
     greet(peers + [partner])
     mine = chip * 2 + core
@@ -73,7 +81,7 @@
     keep = pltpu.make_async_copy(own, out.at[mine], local_sem)
     keep.start()
     for k in range(1, n):
-        source = lax.rem(chip + n - k, n) * 2 + core
+        source = lay.offset(chip, k, -1) * 2 + core
         pushes[k - 1].wait_recv()
         share = remote(out.at[source], out.at[source], core_send.at[k], core_recv.at[k], partner)
         share.start()
@@ -105,100 +113,51 @@
     )(value)
 
 
-def scatter_tokens_kernel(lay, parts, out, from_core, sums, landed, send, recv, core_send, core_recv):
-    chip, core, high = lay.place()
-    n = lay.chips
-    peers = [lay.device(lax.rem(chip + k, n), core, high) for k in range(1, n)]
-    partner = lay.device(chip, 1 - core, high)
-    greet(peers + [partner])
-    shares = []
-    for k in list(range(1, n)) + [0]:
-        target = lax.rem(chip + k, n)
-        share = remote(
-            parts.at[target * 2 + 1 - core],
-            from_core.at[k],
-            core_send.at[k],
-            core_recv.at[k],
-            partner,
-        )
-        share.start()
-        shares.append((k, share))
-    pushes = []
-    for k, share in shares:
-        share.wait_recv()
-        target = lax.rem(chip + k, n)
-        total = parts[target * 2 + core].astype(jnp.float32) + from_core[k].astype(jnp.float32)
-        if k:
-            sums[k - 1] = total.astype(sums.dtype)
-            push = remote(
-                sums.at[k - 1], landed.at[k - 1], send.at[k - 1], recv.at[k - 1], peers[k - 1]
-            )
-            push.start()
-            pushes.append(push)
-        else:
-            out[...] = total
-    for push in pushes:
-        push.wait_recv()
-    total = out[...]
-    for k in range(n - 1):
-        total = total + landed[k].astype(jnp.float32)
-    out[...] = total
-    for push in pushes:
-        push.wait_send()
-    for _, share in shares:
-        share.wait_send()
-
-
-def scatter_tokens(lay, parts, collective_id):
-    n = lay.chips
-    rows, cols = parts.shape[1:]
-    return pl.pallas_call(
-        partial(scatter_tokens_kernel, lay),
-        out_shape=jax.ShapeDtypeStruct((rows, cols), jnp.float32),
-        in_specs=[pl.BlockSpec(memory_space=pltpu.VMEM)],
-        out_specs=pl.BlockSpec(memory_space=pltpu.VMEM),
-        scratch_shapes=[
-            pltpu.VMEM((n, rows, cols), jnp.bfloat16),
-            pltpu.VMEM((n - 1, rows, cols), jnp.bfloat16),
-            pltpu.VMEM((n - 1, rows, cols), jnp.bfloat16),
-            pltpu.SemaphoreType.DMA((n - 1,)),
-            pltpu.SemaphoreType.DMA((n - 1,)),
-            pltpu.SemaphoreType.DMA((n,)),
-            pltpu.SemaphoreType.DMA((n,)),
-        ],
-        compiler_params=pltpu.CompilerParams(
-            collective_id=collective_id, has_side_effects=True, vmem_limit_bytes=VMEM_LIMIT
-        ),
-    )(parts)
-
-
 def lane_tiles(cols):
     return [(first, min(128, cols - first)) for first in range(0, cols, 128)]
 
 
-def exchange_in_kernel(
+def weights_in_kernel(
     lay, pack, pairs, lows, attn_out, gate_out, up_out, low_out,
-    attn_land, stack, land, lanes, attn_send, attn_recv, send, recv,
+    attn_land, own, stack, land, lanes, keep_sem, attn_send, attn_recv, send, recv,
+    chain_send, chain_recv, low_send, low_recv, core_send, core_recv,
 ):
     n = lay.dp
+    hi, lo = lay.hi, lay.lo
     dp = lax.axis_index("dp")
     ctx = lax.axis_index("ctx")
-    per = lows.shape[1]
+    high, low = ctx // lo, lax.rem(ctx, lo)
+    core = lax.rem(dp, 2)
+    per, cols = lows.shape[1:]
     padded = gate_out.shape[0]
-    cols = lows.shape[2]
     targets = [lax.rem(dp + k, n) for k in range(n)]
-    greet([(target, ctx) for target in targets[1:]])
+    partner = (dp + 1 - 2 * core, ctx)
+    low_peers = [(dp, high * lo + lax.rem(low + k, lo)) for k in range(1, lo)]
+    right, left = (dp, ctx + lo), (dp, ctx - lo)
+    has_right, has_left = high < hi - 1, high > 0
+    barrier = pltpu.get_barrier_semaphore()
+    for device in [(target, ctx) for target in targets[1:]] + low_peers:
+        pl.semaphore_signal(barrier, inc=1, device_id=device, device_id_type=MESH)
+    for there, device in ((has_right, right), (has_left, left)):
+        @pl.when(there)
+        def _():
+            pl.semaphore_signal(barrier, inc=1, device_id=device, device_id_type=MESH)
+    sides = jnp.where(has_right, 1, 0) + jnp.where(has_left, 1, 0)
+    pl.semaphore_wait(barrier, n - 1 + len(low_peers) + sides)
+
     attn_pushes = []
     for k in range(1, n):
         push = remote(
-            pack.at[targets[k]], attn_land.at[dp], attn_send.at[k], attn_recv.at[k], (targets[k], ctx)
+            pack.at[lax.rem(targets[k], 2)], attn_land.at[dp], attn_send.at[k], attn_recv.at[k],
+            (targets[k], ctx),
         )
         push.start()
         attn_pushes.append(push)
-    attn_land[dp] = pack[dp]
+    attn_land[dp] = pack[core]
+    blank = jnp.zeros((padded - per, cols), jnp.bfloat16)
     pushes = []
-    blank = jnp.zeros((padded - per, cols), jnp.bfloat16)
-    for k in list(range(2, n)) + [1, 0]:
+
+    def feed_forward(k):
         target = targets[k]
         for j, (first, width) in enumerate(lane_tiles(cols)):
             lanes[j, :, :width] = pairs[target, :, first : first + width]
@@ -220,198 +179,125 @@
             push = remote(stack.at[k - 1], land.at[dp], send.at[k], recv.at[k], (target, ctx))
             push.start()
             pushes.append(push)
+
+    everything = [(0, 0, None, high)]
+    for step in range(1, hi):
+        everything.append((0, step, high - step >= 0, high - step))
+        everything.append((1, step, high + step < hi, high + step))
+
+    def to_core(source, c, slot):
+        return remote(source, attn_out.at[c, core], core_send.at[slot], core_recv.at[slot], partner)
+
+    def to_low(source, c, i):
+        return [
+            remote(source, attn_out.at[c, core], low_send.at[i, k], low_recv.at[i, k], low_peers[k])
+            for k in range(lo - 1)
+        ]
+
+    def chain(source, c, side, step):
+        return remote(
+            source, attn_out.at[c, core], chain_send.at[side, step], chain_recv.at[side, step],
+            right if side == 0 else left,
+        )
+
+    def sides_of(side, step):
+        if step == hi - 1:
+            return []
+        return [s for s in ((0, has_right), (1, has_left)) if step == 0 or s[0] == side]
+
+    def pass_own(i, side, step, where):
+        c = where * lo + low
+        source = attn_out.at[c, core] if step else own
+        if step:
+            chain(own, c, side, step - 1).wait_recv()
+        for go, there in sides_of(side, step):
+            @pl.when(there)
+            def _():
+                chain(source, c, go, step).start()
+        for push in to_low(source, c, i):
+            push.start()
+        to_core(source, c, i * lo).start()
+
+    def pass_low(i, side, step, where):
+        for k in range(lo - 1):
+            c = where * lo + lax.rem(low + lo - 1 - k, lo)
+            to_low(own, c, i)[k].wait_recv()
+            to_core(attn_out.at[c, core], c, i * lo + k + 1).start()
+
+    def finish(i, side, step, where):
+        c = where * lo + low
+        for go, there in sides_of(side, step):
+            @pl.when(there)
+            def _():
+                chain(own, c, go, step).wait_send()
+        for push in to_low(own, c, i):
+            push.wait_send()
+        for k in range(lo):
+            to_core(own, c, i * lo + k).wait()
+
+    def each(stage, step):
+        for i, (side, s, there, where) in enumerate(everything):
+            if s == step:
+                call = partial(stage, i, side, s, where)
+                if s:
+                    pl.when(there)(call)
+                else:
+                    call()
+
+    order = list(range(2, n)) + [1, 0]
+    feed_forward(order[0])
     for push in attn_pushes:
         push.wait_recv()
     for q in range(n):
-        attn_out[:, q * cols : (q + 1) * cols] = attn_land[q]
+        own[:, q * cols : (q + 1) * cols] = attn_land[q]
+    keep = pltpu.make_async_copy(own, attn_out.at[ctx, core], keep_sem)
+    keep.start()
+    each(pass_own, 0)
+    for k in order[1:]:
+        feed_forward(k)
+    for step in range(1, hi + 1):
+        each(pass_own, step)
+        each(pass_low, step - 1)
     for push in pushes:
         push.wait_recv()
     for q in range(n):
         for i, out in enumerate((gate_out, up_out, low_out)):
             out[:, q * cols : (q + 1) * cols] = land[q, i]
+    keep.wait()
+    for step in range(hi):
+        each(finish, step)
     for push in attn_pushes + pushes:
         push.wait_send()
 
 
-def exchange_in(lay, pack, pairs, lows, collective_id):
+def weights_in(lay, pack, pairs, lows, collective_id):
     n, per, cols = lows.shape
     rows = pack.shape[1]
     padded = -(-per // 16) * 16
+    count = 2 * lay.hi - 1
     wide = jax.ShapeDtypeStruct((padded, n * cols), jnp.bfloat16)
     vmem = pl.BlockSpec(memory_space=pltpu.VMEM)
+    dma = pltpu.SemaphoreType.DMA
+    scratch = [
+        pltpu.VMEM((n, rows, cols), jnp.bfloat16),
+        pltpu.VMEM((rows, n * cols), jnp.bfloat16),
+        pltpu.VMEM((n - 1, 3, padded, cols), jnp.bfloat16),
+        pltpu.VMEM((n, 3, padded, cols), jnp.bfloat16),
+        pltpu.VMEM((len(lane_tiles(cols)), 2 * per, 128), jnp.float32),
+        dma,
+    ]
+    for shape in ((n,), (n,), (2, lay.hi), (count, max(1, lay.lo - 1)), (count * lay.lo,)):
+        scratch += [dma(shape), dma(shape)]
     return pl.pallas_call(
-        partial(exchange_in_kernel, lay),
-        out_shape=(jax.ShapeDtypeStruct((rows, n * cols), jnp.bfloat16), wide, wide, wide),
+        partial(weights_in_kernel, lay),
+        out_shape=(jax.ShapeDtypeStruct((lay.ctx, 2, rows, n * cols), jnp.bfloat16), wide, wide, wide),
         in_specs=[vmem] * 3,
-        out_specs=(vmem,) * 4,
-        scratch_shapes=[
-            pltpu.VMEM((n, rows, cols), jnp.bfloat16),
-            pltpu.VMEM((n - 1, 3, padded, cols), jnp.bfloat16),
-            pltpu.VMEM((n, 3, padded, cols), jnp.bfloat16),
-            pltpu.VMEM((len(lane_tiles(cols)), 2 * per, 128), jnp.float32),
-        ]
-        + [pltpu.SemaphoreType.DMA((n,))] * 4,
+        out_specs=(pl.BlockSpec(memory_space=pl.ANY),) + (vmem,) * 3,
+        scratch_shapes=scratch,
         compiler_params=pltpu.CompilerParams(
             collective_id=collective_id, has_side_effects=True, vmem_limit_bytes=VMEM_LIMIT
         ),
     )(pack, pairs, lows)
-
-
-def gather_attn_kernel(lay, own, out, local_sem, chain_send, chain_recv, low_send, low_recv,
-                       wide_send, wide_recv, core_send, core_recv):
-    dp = lax.axis_index("dp")
-    ctx = lax.axis_index("ctx")
-    hi, lo, wide = lay.hi, lay.lo, lay.wide
-    high, low = ctx // lo, lax.rem(ctx, lo)
-    across, core = dp // 2, lax.rem(dp, 2)
-    partner = (across * 2 + 1 - core, ctx)
-    low_peers = [(dp, high * lo + lax.rem(low + k, lo)) for k in range(1, lo)]
-    wide_peers = [(lax.rem(across + k, wide) * 2 + core, ctx) for k in range(1, wide)]
-    right, left = (dp, ctx + lo), (dp, ctx - lo)
-    has_right, has_left = high < hi - 1, high > 0
-    barrier = pltpu.get_barrier_semaphore()
-    for device in low_peers + wide_peers + [partner]:
-        pl.semaphore_signal(barrier, inc=1, device_id=device, device_id_type=MESH)
-    for there, device in ((has_right, right), (has_left, left)):
-        @pl.when(there)
-        def _():
-            pl.semaphore_signal(barrier, inc=1, device_id=device, device_id_type=MESH)
-    sides = jnp.where(has_right, 1, 0) + jnp.where(has_left, 1, 0)
-    pl.semaphore_wait(barrier, len(low_peers) + len(wide_peers) + 1 + sides)
-
-    def to_core(source, c, d, slot):
-        return remote(source, out.at[c, d], core_send.at[slot], core_recv.at[slot], partner)
-
-    def to_wide(source, c, d, slot):
-        return [
-            remote(source, out.at[c, d], wide_send.at[slot, k], wide_recv.at[slot, k], wide_peers[k])
-            for k in range(wide - 1)
-        ]
-
-    def to_low(source, c, d, slot):
-        return [
-            remote(source, out.at[c, d], low_send.at[slot, k], low_recv.at[slot, k], low_peers[k])
-            for k in range(lo - 1)
-        ]
-
-    def chain(source, c, side, step):
-        return remote(
-            source, out.at[c, dp], chain_send.at[side, step], chain_recv.at[side, step],
-            right if side == 0 else left,
-        )
-
-    def blocks():
-        yield 0, 0, jnp.bool_(True), high
-        for step in range(1, hi):
-            yield 0, step, high - step >= 0, high - step
-            yield 1, step, high + step < hi, high + step
-
-    everything = list(blocks())
-    number = {(side, step): i for i, (side, step, _, _) in enumerate(everything)}
-    per_low = lo
-    per_wide = lo * wide
-
-    def core_slot(i, a, b):
-        return (i * per_low + a) * wide + b
-
-    def stage_low_arrivals(i, where):
-        for k in range(lo - 1):
-            c = where * lo + lax.rem(low + lo - 1 - k, lo)
-            low_copy = remote(own, out.at[c, dp], low_send.at[i, k], low_recv.at[i, k], low_peers[k])
-            low_copy.wait_recv()
-            for push in to_wide(out.at[c, dp], c, dp, i * per_low + k + 1):
-                push.start()
-            to_core(out.at[c, dp], c, dp, core_slot(i, k + 1, 0)).start()
-
-    def stage_wide_arrivals(i, where):
-        for a in range(lo):
-            c = where * lo + (low if a == 0 else lax.rem(low + lo - a, lo))
-            for k in range(wide - 1):
-                d = lax.rem(across + wide - 1 - k, wide) * 2 + core
-                copy = remote(
-                    own, out.at[c, d], wide_send.at[i * per_low + a, k],
-                    wide_recv.at[i * per_low + a, k], wide_peers[k],
-                )
-                copy.wait_recv()
-                to_core(out.at[c, d], c, d, core_slot(i, a, k + 1)).start()
-
-    def stage_own(i, side, step, where):
-        c = where * lo + low
-        source = own if step == 0 else out.at[c, dp]
-        if step:
-            chain(own, c, side, step - 1).wait_recv()
-        for go_side, there in ((0, has_right), (1, has_left)):
-            if step and go_side != side:
-                continue
-            if step < hi - 1:
-                @pl.when(there)
-                def _():
-                    chain(source, c, go_side, step).start()
-        for push in to_low(source, c, dp, i):
-            push.start()
-        for push in to_wide(source, c, dp, i * per_low):
-            push.start()
-        to_core(source, c, dp, core_slot(i, 0, 0)).start()
-
-    def finish(i, side, step, where):
-        c = where * lo + low
-        for go_side, there in ((0, has_right), (1, has_left)):
-            if step and go_side != side:
-                continue
-            if step < hi - 1:
-                @pl.when(there)
-                def _():
-                    chain(own, c, go_side, step).wait_send()
-        for push in to_low(own, c, dp, i):
-            push.wait_send()
-        for a in range(lo):
-            for push in to_wide(own, c, dp, i * per_low + a):
-                push.wait_send()
-            for b in range(wide):
-                to_core(own, c, dp, core_slot(i, a, b)).wait()
-
-    keep = pltpu.make_async_copy(own, out.at[ctx, dp], local_sem)
-    keep.start()
-    previous = []
-    for step in range(hi + 2):
-        for stage, age in ((stage_own, 0), (stage_low_arrivals, 1), (stage_wide_arrivals, 2)):
-            for i, (side, s, there, where) in enumerate(everything):
-                if s != step - age:
-                    continue
-                if stage is stage_own:
-                    call = partial(stage_own, i, side, s, where)
-                else:
-                    call = partial(stage, i, where)
-                if s == 0:
-                    call()
-                else:
-                    pl.when(there)(call)
-    keep.wait()
-    for i, (side, s, there, where) in enumerate(everything):
-        call = partial(finish, i, side, s, where)
-        if s == 0:
-            call()
-        else:
-            pl.when(there)(call)
-
-
-def gather_attn(lay, own, collective_id):
-    count = 2 * lay.hi - 1
-    lows, wides = max(1, lay.lo - 1), max(1, lay.wide - 1)
-    return pl.pallas_call(
-        partial(gather_attn_kernel, lay),
-        out_shape=jax.ShapeDtypeStruct((lay.ctx, lay.dp) + own.shape, own.dtype),
-        in_specs=[pl.BlockSpec(memory_space=pl.ANY)],
-        out_specs=pl.BlockSpec(memory_space=pl.ANY),
-        scratch_shapes=[pltpu.SemaphoreType.DMA]
-        + [pltpu.SemaphoreType.DMA((2, lay.hi))] * 2
-        + [pltpu.SemaphoreType.DMA((count, lows))] * 2
-        + [pltpu.SemaphoreType.DMA((count * lay.lo, wides))] * 2
-        + [pltpu.SemaphoreType.DMA((count * lay.lo * lay.wide,))] * 2,
-        compiler_params=pltpu.CompilerParams(
-            collective_id=collective_id, has_side_effects=True, vmem_limit_bytes=VMEM_LIMIT
-        ),
-    )(own)
 
 
 def flip(index, bit):
@@ -688,6 +574,268 @@
     )(gate, up, down)
 
 
+def in_tiles(total, size, body):
+    whole = total // size
+
+    def step(i, carry):
+        body(pl.multiple_of(i * size, size), size)
+        return carry
+
+    if whole:
+        lax.fori_loop(0, whole, step, 0)
+    if total % size:
+        body(whole * size, total % size)
+
+
+def dot_nt(left, right):
+    return lax.dot_general(left, right, (((1,), (1,)), ((), ())), preferred_element_type=jnp.float32)
+
+
+def dot_nn(left, right):
+    return lax.dot_general(left, right, (((1,), (0,)), ((), ())), preferred_element_type=jnp.float32)
+
+
+ROOT = math.sqrt(2.0 / math.pi)
+
+
+def feed_forward_kernel(
+    lay, mid, w_gate, w_up, w_down, mixed, cotangent, valid, gain,
+    result, grad_mid, gate_t, up_t, grad_gain, dw_gate, dw_up, dw_down,
+    act, slope, hidden, hidden_t, grads, parts, core_land, sums, landed, total, dy, sem,
+    core_send, core_recv, send, recv, share_send, share_recv, dy_send, dy_recv,
+):
+    chip, core, high = lay.place()
+    n = lay.chips
+    tokens = mixed.shape[0]
+    units = w_gate.shape[0]
+    places = [lay.offset(chip, k) for k in range(n)]
+    sources = [lay.offset(chip, k, -1) for k in range(n)]
+    peers = [lay.device(place, core, high) for place in places]
+    partner = lay.device(chip, 1 - core, high)
+    mine = pl.ds(pl.multiple_of(core * tokens, tokens), tokens)
+    theirs = pl.ds(pl.multiple_of((1 - core) * tokens, tokens), tokens)
+    greet(peers[1:] + [partner])
+
+    def to_partner(phase, k):
+        return remote(
+            parts.at[places[k], theirs], core_land.at[k], core_send.at[phase, k], core_recv.at[phase, k], partner
+        )
+
+    def to_owner(phase, k):
+        return remote(
+            sums.at[k - 1], landed.at[k - 1], send.at[phase, k], recv.at[phase, k], peers[k]
+        )
+
+    def add_core(phase, k):
+        to_partner(phase, k).wait_recv()
+
+        def chunk(first, rows):
+            span = pl.ds(first, rows)
+            here = pl.ds(pl.multiple_of(core * tokens + first, rows), rows)
+            both = parts[places[k], here].astype(jnp.float32) + core_land[k, span].astype(jnp.float32)
+            if k:
+                sums[k - 1, span] = both.astype(jnp.bfloat16)
+            else:
+                total[span] = both
+
+        in_tiles(tokens, 32, chunk)
+        if k:
+            to_owner(phase, k).start()
+
+    def add_owners(phase):
+        for k in range(1, n):
+            to_owner(phase, k).wait_recv()
+
+        def chunk(first, rows):
+            span = pl.ds(first, rows)
+            value = total[span]
+            for k in range(1, n):
+                value = value + landed[k - 1, span].astype(jnp.float32)
+            total[span] = value
+
+        in_tiles(tokens, 32, chunk)
+
+    def settle(phase):
+        for k in range(n):
+            to_partner(phase, k).wait_send()
+            if k:
+                to_owner(phase, k).wait_send()
+
+    def forward(c):
+        def tile(first, width):
+            rows = pl.ds(first, width)
+            weights = jnp.concatenate([w_gate[rows], w_up[rows]], axis=0)
+            both = dot_nt(mid[c], weights)
+            gate, up = both[:, :width], both[:, width:]
+            square = gate * gate
+            tanh = jnp.tanh(ROOT * gate * (1.0 + 0.044715 * square))
+            half = 0.5 * (1.0 + tanh)
+            active = gate * half
+            slant = half + 0.5 * gate * (1.0 - tanh * tanh) * (ROOT * (1.0 + 3.0 * 0.044715 * square))
+            product = (active * up).astype(jnp.bfloat16)
+            act[c, :, rows] = active.astype(jnp.bfloat16)
+            slope[c, :, rows] = (slant * up).astype(jnp.bfloat16)
+            hidden[:, rows] = product
+            hidden_t[c, rows] = product.T
+
+        in_tiles(units, 128, tile)
+
+        def out_tile(first, width):
+            lanes = pl.ds(first, width)
+            parts[c, :, lanes] = dot_nn(hidden[...], w_down[:, lanes]).astype(jnp.bfloat16)
+
+        in_tiles(D, 256, out_tile)
+
+    def backward(c):
+        def tile(first, width):
+            rows = pl.ds(first, width)
+            grad = dot_nt(dy[c], w_down[rows])
+            up_grad = (grad * act[c, :, rows].astype(jnp.float32)).astype(jnp.bfloat16)
+            gate_grad = (grad * slope[c, :, rows].astype(jnp.float32)).astype(jnp.bfloat16)
+            grads[0, :, rows] = gate_grad
+            grads[1, :, rows] = up_grad
+            gate_t[c, rows] = gate_grad.T
+            up_t[c, rows] = up_grad.T
+
+        in_tiles(units, 256, tile)
+
+        def out_tile(first, width):
+            lanes = pl.ds(first, width)
+            both = dot_nn(grads[0], w_gate[:, lanes]) + dot_nn(grads[1], w_up[:, lanes])
+            parts[c, :, lanes] = both.astype(jnp.bfloat16)
+
+        in_tiles(D, 256, out_tile)
+
+    order = list(range(n - 1, 0, -1)) + [0]
+    for i, k in enumerate(order):
+        forward(places[k])
+        to_partner(0, k).start()
+        if i:
+            add_core(0, order[i - 1])
+    add_core(0, order[-1])
+    add_owners(0)
+
+    grad_gain[...] = jnp.zeros_like(grad_gain)
+    scale = 1.0 + gain[...]
+
+    def finish(first, rows):
+        span = pl.ds(first, rows)
+        here = pl.ds(pl.multiple_of(core * tokens + first, rows), rows)
+        y = total[span]
+        ok = valid[span]
+        rate = lax.rsqrt(jnp.mean(y * y, axis=-1, keepdims=True) + EPS)
+        unit = y * rate
+        result[span] = ((mixed[span] + unit * scale) * ok).astype(jnp.bfloat16)
+        upstream = cotangent[span].astype(jnp.float32) * ok
+        down = upstream * unit
+        for r in range(0, rows, 8):
+            grad_gain[...] += down[r : r + 8]
+        scaled = upstream * scale
+        inner = jnp.mean(scaled * unit, axis=-1, keepdims=True)
+        dy[chip, here] = (rate * (scaled - unit * inner)).astype(jnp.bfloat16)
+
+    in_tiles(tokens, 32, finish)
+
+    pushes = [None] + [
+        remote(dy.at[chip, mine], dy.at[chip, mine], dy_send.at[k], dy_recv.at[k], peers[k])
+        for k in range(1, n)
+    ]
+    shares = [
+        remote(dy.at[sources[k], mine], dy.at[sources[k], mine], share_send.at[k], share_recv.at[k], partner)
+        for k in range(n)
+    ]
+    for push in pushes[1:]:
+        push.start()
+    shares[0].start()
+    settle(0)
+    for i in range(n):
+        k = lay.back(i)
+        if i:
+            pushes[i].wait_recv()
+            shares[i].start()
+        shares[i].wait_recv()
+        backward(sources[i])
+        to_partner(1, k).start()
+        if i:
+            add_core(1, lay.back(i - 1))
+    add_core(1, lay.back(n - 1))
+
+    def weight_grad(left_ref, right, out):
+        def tile(first, width):
+            lanes = pl.ds(first, width)
+            value = dot_nn(left_ref[0], right[0, :, lanes])
+            for c in range(1, n):
+                value = value + dot_nn(left_ref[c], right[c, :, lanes])
+            out[:, lanes] = value.astype(jnp.bfloat16)
+
+        in_tiles(D, 256, tile)
+
+    weight_grad(hidden_t, dy, dw_down)
+    weight_grad(gate_t, mid, dw_gate)
+    weight_grad(up_t, mid, dw_up)
+    add_owners(1)
+    grad_mid[...] = total[...]
+    settle(1)
+    for k in range(n):
+        if k:
+            pushes[k].wait_send()
+        shares[k].wait_send()
+
+
+def feed_forward(lay, mid, w_gate, w_up, w_down, mixed, cotangent, valid, gain, collective_id):
+    n = lay.chips
+    tokens = mixed.shape[0]
+    units = w_gate.shape[0]
+    low, high = jnp.bfloat16, jnp.float32
+    vmem = pl.BlockSpec(memory_space=pltpu.VMEM)
+    dma = pltpu.SemaphoreType.DMA
+    dw = jax.ShapeDtypeStruct((units, D), low)
+    out_shape = (
+        jax.ShapeDtypeStruct((tokens, D), low),
+        jax.ShapeDtypeStruct((tokens, D), high),
+        jax.ShapeDtypeStruct((8, D), high),
+        dw,
+        dw,
+        dw,
+    )
+
+    def kernel(*refs):
+        ins, outs, scratch = refs[:8], refs[8:14], list(refs[14:])
+        gate_t, up_t = scratch.pop(0), scratch.pop(0)
+        feed_forward_kernel(
+            lay, *ins, outs[0], outs[1], gate_t, up_t, *outs[2:], *scratch[:11], None, *scratch[11:]
+        )
+
+    return pl.pallas_call(
+        kernel,
+        out_shape=out_shape,
+        in_specs=[vmem] * 8,
+        out_specs=(vmem,) * 6,
+        scratch_shapes=[
+            pltpu.VMEM((n, units, 2 * tokens), low),
+            pltpu.VMEM((n, units, 2 * tokens), low),
+            pltpu.VMEM((n, 2 * tokens, units), low),
+            pltpu.VMEM((n, 2 * tokens, units), low),
+            pltpu.VMEM((2 * tokens, units), low),
+            pltpu.VMEM((n, units, 2 * tokens), low),
+            pltpu.VMEM((2, 2 * tokens, units), low),
+            pltpu.VMEM((n, 2 * tokens, D), low),
+            pltpu.VMEM((n, tokens, D), low),
+            pltpu.VMEM((max(1, n - 1), tokens, D), low),
+            pltpu.VMEM((max(1, n - 1), tokens, D), low),
+            pltpu.VMEM((tokens, D), high),
+            pltpu.VMEM((n, 2 * tokens, D), low),
+        ]
+        + [dma((2, n))] * 4
+        + [dma((n,))] * 4,
+        compiler_params=pltpu.CompilerParams(
+            collective_id=collective_id, has_side_effects=True, vmem_limit_bytes=63 * 2**20
+        ),
+    )(
+        mid.reshape(n, 2 * tokens, D), w_gate, w_up, w_down, mixed, cotangent, valid, gain
+    )
+
+
 def shifted(value, axis, steps):
     count = lax.axis_size(axis)
     leading, last = (max(0, -steps), min(count, count - steps))
@@ -721,10 +869,6 @@
     query = rotate(norm_scaled(query, gain_query), angle[:, None, :])
     key_rows = rotate(norm_scaled(key_rows, gain_key), angle)
     return (query, key_rows, value_rows)
-
-
-def gate_times_up(gate, up):
-    return jax.nn.gelu(gate, approximate=True) * up
 
 
 def contract(left, right, dims_left, dims_right):
@@ -743,15 +887,14 @@
     qkv_rows, out_rows = w_qkv.shape[0], w_out.shape[0]
     cols = w_qkv.shape[1]
     used = qkv_rows + out_rows + 1
-    block = 16 * lay.dp
-    pack_rows = -(-used // block) * block
+    pack_rows = -(-used // 32) * 32
     gain_row = jnp.pad(gains, (0, cols - gains.shape[0]))[None]
     pack = jnp.concatenate(
         [w_qkv, w_out, gain_row, jnp.zeros((pack_rows - used, cols), jnp.float32)], axis=0
     ).astype(jnp.bfloat16)
-    own_attn, gate_rows, up_rows, low_rows = exchange_in(
+    attn_all, gate_rows, up_rows, low_rows = weights_in(
         lay,
-        pack.reshape(lay.dp, pack_rows // lay.dp, cols),
+        pack.reshape(2, pack_rows // 2, cols),
         w_gate_up.reshape(lay.dp, 2 * per, cols),
         w_down.reshape(lay.dp, per, cols),
         5,
@@ -760,7 +903,7 @@
         lax.all_gather(rows, "ctx", axis=0, tiled=True, axis_index_groups=lay.hi_groups)
         for rows in (gate_rows, up_rows, low_rows)
     )
-    attn_all = gather_attn(lay, own_attn, 6).reshape(lay.ctx, pack_rows, D)
+    attn_all = attn_all.reshape(lay.ctx, pack_rows, D)
     full_qkv = attn_all[:, :qkv_rows].reshape(lay.ctx * qkv_rows, D)
     full_out = attn_all[:, qkv_rows : qkv_rows + out_rows].reshape(lay.ctx * out_rows, D)
     gain_all = (
@@ -829,27 +972,22 @@
     mid_low = normed_mid.astype(jnp.bfloat16)
     token_count = seq_count * local_len
     mid_all = gather_tokens(lay, mid_low.reshape(token_count, D), 1)
-    gate = contract(mid_all, w_gate, (2,), (1,))
-    up = contract(mid_all, w_up, (2,), (1,))
-    hidden, pull_act = jax.vjp(gate_times_up, gate, up)
-    hidden_low = hidden.astype(jnp.bfloat16)
-    down_parts = contract(hidden_low, w_low, (2,), (0,)).astype(jnp.bfloat16)
-    down = scatter_tokens(lay, down_parts, 2).reshape(seq_count, local_len, D)
-    normed_down, pull_down = jax.vjp(norm_scaled, down, gain_post)
-    result = jnp.where(valid[..., None], mixed + normed_down, 0.0).astype(jnp.bfloat16)
+    result, grad_mid, grad_gain_post, grad_w_gate, grad_w_up, grad_low = feed_forward(
+        lay,
+        mid_all,
+        w_gate,
+        w_up,
+        w_low,
+        mixed.reshape(token_count, D),
+        cotangent.reshape(token_count, D),
+        valid.reshape(token_count, 1).astype(jnp.float32),
+        gain_post[None],
+        2,
+    )
+    result = result.reshape(mixed.shape)
+    grad_mid = grad_mid.reshape(mixed.shape)
+    grad_gain_post = jnp.sum(grad_gain_post, axis=0)
     upstream = jnp.where(valid[..., None], cotangent.astype(jnp.float32), 0.0)
-    grad_down_in, grad_gain_post = pull_down(upstream)
-    down_low = grad_down_in.astype(jnp.bfloat16)
-    down_all = gather_tokens(lay, down_low.reshape(token_count, D), 3)
-    grad_hidden = contract(down_all, w_low, (2,), (1,))
-    grad_low = contract(hidden_low, down_all, (0, 1), (0, 1)).astype(jnp.bfloat16)
-    grad_gate, grad_up = pull_act(grad_hidden)
-    gate_low = grad_gate.astype(jnp.bfloat16)
-    up_low = grad_up.astype(jnp.bfloat16)
-    mid_parts = contract(gate_low, w_gate, (2,), (0,)) + contract(up_low, w_up, (2,), (0,))
-    grad_mid = scatter_tokens(lay, mid_parts.astype(jnp.bfloat16), 4).reshape(mixed.shape)
-    grad_w_gate = contract(gate_low, mid_all, (0, 1), (0, 1)).astype(jnp.bfloat16)
-    grad_w_up = contract(up_low, mid_all, (0, 1), (0, 1)).astype(jnp.bfloat16)
     grad_mixed_in, grad_gain_pre = pull_mid(grad_mid)
     grad_mixed = upstream + grad_mixed_in
     grad_proj, grad_gain_attn = pull_out(grad_mixed)
@@ -898,18 +1036,19 @@
             grad_gain_key,
         ]
     )
-    def own_blocks(grad, rows):
-        whole = grad.astype(jnp.bfloat16).reshape(lay.ctx, rows, D)
-        padded = -(-rows // block) * block
-        whole = jnp.pad(whole, ((0, 0), (0, padded - rows), (0, 0)))
-        return whole.reshape(lay.ctx, lay.dp, padded // lay.dp, D)
-
-    (part_out,) = scatter_attn(lay, own_blocks(grad_w_out, out_rows), None, 7)
-    part_qkv, gains_sum = scatter_attn(
-        lay, own_blocks(grad_w_qkv, qkv_rows), grad_gain_all.reshape(-1, 128), 8
-    )
-    part_out = part_out[:out_rows]
-    part_qkv = part_qkv[:qkv_rows]
+    block = 16 * lay.dp
+    sum_rows = -(-(qkv_rows + out_rows) // block) * block
+    partial_sums = jnp.concatenate(
+        [
+            grad_w_qkv.astype(jnp.bfloat16).reshape(lay.ctx, qkv_rows, D),
+            grad_w_out.astype(jnp.bfloat16).reshape(lay.ctx, out_rows, D),
+            jnp.zeros((lay.ctx, sum_rows - qkv_rows - out_rows, D), jnp.bfloat16),
+        ],
+        axis=1,
+    ).reshape(lay.ctx, lay.dp, sum_rows // lay.dp, D)
+    part_attn, gains_sum = scatter_attn(lay, partial_sums, grad_gain_all.reshape(-1, 128), 8)
+    part_qkv = part_attn[:qkv_rows]
+    part_out = part_attn[qkv_rows : qkv_rows + out_rows]
     place = (lax.axis_index("dp") * lay.ctx + lax.axis_index("ctx")) * gains.shape[0]
     part_gains = lax.dynamic_slice_in_dim(gains_sum.reshape(-1), place, gains.shape[0])
     owned = [

time: 638 us -> 578 us (0.906)
  matrix products: 110 us -> 14.3 us
  waiting for transfers between devices: 30.7 us -> 102 us
  Pallas kernels: 382 us -> 346 us
    dot_general x15 -> x6, matrix products: 103 us -> 9.48 us  [contract(): lax.dot_general(left, right, ((dims_left, dims_right), ((), ())), preferr...]
    all_gather x3, waiting for transfers between devices: 0.02 us -> 43.8 us  [per_device(): lax.all_gather(rows, 'ctx', axis=0, tiled=True, axis_index_groups=lay.hi_...]
    pallas_call x2 -> x1, Pallas kernels: 79.3 us -> 42.2 us  [gather_tokens(): pl.pallas_call(partial(gather_tokens_kernel, lay), out_shape=jax.ShapeDty...]
    ppermute x8, waiting for transfers between devices: 29.9 us -> 57.7 us  [shifted(): lax.ppermute(value, axis, [(source, source + steps) for source in range(l...]
    pallas_call x4 -> x2, Pallas kernels: 157 us -> 173 us  [the longest x1 122 us: feed_forward(): pl.pallas_call(kernel, out_shape=out_shape, in_specs=[vmem] * 8, out_spec...]
    pallas_call x2 -> x1, Pallas kernels: 116 us -> 102 us  [scatter_attn(): pl.pallas_call(partial(scatter_attn_kernel, lay, with_gains), out_shape=t...]
    unnamed x154 -> x174, local copies, waits for them, and re-layouts: 23.9 us -> 25.8 us
  transfers between devices with their start and end apart: 14 -> 14, of which waited for: 6 -> 7; matrix products, arithmetic and copies ran while one was open for 21% -> 10% of each run, Pallas kernels for 40% -> 25%
where the time goes in v3:
time: 578 us; the launch traced here: 570 us
  Pallas kernels  346 us (60%)
  waiting for transfers between devices  102 us (18%)
  local copies, waits for them, and re-layouts  43.3 us (7%)
  other arithmetic  24 us (4%)
  starting transfers between devices  23.8 us (4%)
  between operations  15.8 us (3%)
  matrix products  14.3 us (2%)
    pallas_call x1, Pallas kernels, feed_forward(): pl.pallas_call(kernel, out_shape=out_shape, in_specs=[vmem] * 8, out_spec...  122 us
    pallas_call x1, Pallas kernels, scatter_attn(): pl.pallas_call(partial(scatter_attn_kernel, lay, with_gains), out_shape=t...  102 us
    ppermute x8, waiting for transfers between devices, shifted(): lax.ppermute(value, axis, [(source, source + steps) for source in range(l...  57.7 us
    pallas_call x1, Pallas kernels, weights_in(): pl.pallas_call(partial(weights_in_kernel, lay), out_shape=(jax.ShapeDtype...  51.4 us
    all_gather x3, waiting for transfers between devices, per_device(): lax.all_gather(rows, 'ctx', axis=0, tiled=True, axis_index_groups=lay.hi_...  43.8 us
    pallas_call x1, Pallas kernels, gather_tokens(): pl.pallas_call(partial(gather_tokens_kernel, lay), out_shape=jax.ShapeDty...  42.2 us
    pallas_call x1, Pallas kernels, exchange_out(): pl.pallas_call(partial(exchange_out_kernel, lay), out_shape=(jax.ShapeDty...  28.9 us
    unnamed x174, local copies, waits for them, and re-layouts  25.8 us
  transfers between devices with their start and end apart: 14, of which 7 were waited for; matrix products, arithmetic and copies ran while one was open for 10% of the time, Pallas kernels for 25%

profile of v3, /device:TPU:9, one launch (start us, length us, event | category | flops | bytes accessed | tf_op | source)
XLA Modules:
  0.0 569.6 jit_solution(15908317338664823588)
XLA Ops:
  7.2 3.3 copy.127
  10.5 1.5 copy.128
  13.2 51.4 %shard_map.135 = (bf16[8,2,176,1152]{3,2,1,0:T(8,128)(2,1)}, bf16[224,1152]{1,0:T(8,128)(2,1)}, bf16[224,1152]{1,0:T(8,128)(2,1)}, bf16[224,1152]{1,0:T(8,128)(2,1)}) custom-call(bf16[2,176,288]{2,1,0:T(8,128)(2,1)} %bitcast.136, f32[4,432,288]{2,1,0:T(8,128)} %bitcast.116, f32[4,216,288]{2,1,0:T(8,128)} %bitcast.124), custom_call_target="tpu_custom_call" | custom-call | tf_op jit(solution)/shard_map/pallas_call | solution.py:291
  66.4 4.2 slice.119
  71.6 3.3 fusion.30
  78.2 7.1 %collective-permute-start = (bf16[2,128,512]{2,1,0:T(8,128)(2,1)}, bf16[2,128,512]{2,1,0:T(8,128)(2,1)}, u32[]{:S(2)}, u32[]{:S(2)}) collective-permute-start(bf16[2,128,512]{2,1,0:T(8,128)(2,1)} %pad_maximum_fusion.5), channel_id=1, source_target_pairs={{0,4},{1,5},{2,6},{3,7},{8,12},{9,13},{10,14},{11,15},{16,20},{17,... | collective-permute-start | bytes 786440 | tf_op jit(solution)/shard_map/ppermute | solution.py:842
  85.3 2.0 collective-permute-start.1
  87.3 1.9 collective-permute-start.2
  89.2 3.0 collective-permute-start.3
  96.5 1.9 slice.131
  99.8 6.5 %collective-permute-done = bf16[2,128,512]{2,1,0:T(8,128)(2,1)} collective-permute-done((bf16[2,128,512]{2,1,0:T(8,128)(2,1)}, bf16[2,128,512]{2,1,0:T(8,128)(2,1)}, u32[]{:S(2)}, u32[]{:S(2)}) %collective-permute-start) | collective-permute-done | bytes 262176 | tf_op jit(solution)/shard_map/ppermute | solution.py:842
  107.2 15.4 %collective-permute-done.1 = bf16[2,128,512]{2,1,0:T(8,128)(2,1)} collective-permute-done((bf16[2,128,512]{2,1,0:T(8,128)(2,1)}, bf16[2,128,512]{2,1,0:T(8,128)(2,1)}, u32[]{:S(2)}, u32[]{:S(2)}) %collective-permute-start.1) | collective-permute-done | bytes 262176 | tf_op jit(solution)/shard_map/ppermute | solution.py:842
  123.6 7.1 %collective-permute-done.2 = bf16[2,128,512]{2,1,0:T(8,128)(2,1)} collective-permute-done((bf16[2,128,512]{2,1,0:T(8,128)(2,1)}, bf16[2,128,512]{2,1,0:T(8,128)(2,1)}, u32[]{:S(2)}, u32[]{:S(2)}) %collective-permute-start.2) | collective-permute-done | bytes 262176 | tf_op jit(solution)/shard_map/ppermute | solution.py:842
  138.9 42.2 %shard_map.136 = bf16[8,256,1152]{2,1,0:T(8,128)(2,1)} custom-call(bf16[256,1152]{1,0:T(8,128)(2,1)} %bitcast.132), custom_call_target="tpu_custom_call" | custom-call | tf_op jit(solution)/shard_map/pallas_call | solution.py:98
  181.2 43.7 %all-gather.8.cloned.1.call-done.refs_3_ = bf16[896,1152]{1,0:T(8,128)(2,1)} async-done(((bf16[224,1152]{1,0:T(8,128)(2,1)}), bf16[896,1152]{1,0:T(8,128)(2,1)}) %all-gather.8.cloned.1.call-update) | async-done | bytes 2064400 | tf_op jit(solution)/shard_map/all_gather | solution.py:903
  224.9 121.8 %shard_map.137 = (bf16[256,1152]{1,0:T(8,128)(2,1)}, f32[256,1152]{1,0:T(8,128)}, f32[8,1152]{1,0:T(8,128)}, bf16[896,1152]{1,0:T(8,128)(2,1)}, bf16[896,1152]{1,0:T(8,128)(2,1)}, /*index=5*/bf16[896,1152]{1,0:T(8,128)(2,1)}) custom-call(bf16[4,512,1152]{2,1,0:T(8,128)(2,1)} %bitcast.115, bf16[896,1152]{1,0:T(8,128)(2,1)} %all-gather.4.cloned.1.call-done.refs_1_, ...), custom_call_target="tpu_custom_call" | custom-call | tf_op jit(solution)/shard_map/pallas_call | solution.py:809
  348.0 2.6 multiply_reduce_fusion
  356.1 1.7 convolution_convert_fusion
  357.8 2.0 copy.175
  359.8 1.8 fusion.2
  366.7 4.7 collective-permute-start.4
  371.4 1.9 collective-permute-start.5
  374.7 1.7 collective-permute-start.7
  382.3 4.6 collective-permute-done.4
  386.9 14.6 %collective-permute-done.5 = bf16[2,128,512]{2,1,0:T(8,128)(2,1)S(1)} collective-permute-done((bf16[2,128,512]{2,1,0:T(8,128)(2,1)}, bf16[2,128,512]{2,1,0:T(8,128)(2,1)S(1)}, u32[]{:S(2)}, u32[]{:S(2)}) %collective-permute-start.5) | collective-permute-done | bytes 262176 | tf_op jit(solution)/shard_map/ppermute | solution.py:842
  401.5 9.5 %collective-permute-done.7 = bf16[2,128,512]{2,1,0:T(8,128)(2,1)S(1)} collective-permute-done((bf16[2,128,512]{2,1,0:T(8,128)(2,1)S(1)}, bf16[2,128,512]{2,1,0:T(8,128)(2,1)S(1)}, u32[]{:S(2)}, u32[]{:S(2)}) %collective-permute-start.7) | collective-permute-done | bytes 262176 | tf_op jit(solution)/shard_map/ppermute | solution.py:842
  414.1 1.5 fusion.14
  417.0 3.1 pad_maximum_fusion
  420.0 101.7 %shard_map.138 = (f32[320,288]{1,0:T(8,128)}, f32[40,128]{1,0:T(8,128)}) custom-call(bf16[8,4,80,1152]{3,2,1,0:T(8,128)(2,1)} %bitcast.114, f32[40,128]{1,0:T(8,128)} %bitcast.143), custom_call_target="tpu_custom_call" | custom-call | tf_op jit(solution)/shard_map/pallas_call | solution.py:506
  522.8 1.7 slice.114
  527.9 28.9 %shard_map.139 = (f32[4,432,288]{2,1,0:T(8,128)}, f32[4,216,288]{2,1,0:T(8,128)}) custom-call(bf16[224,1152]{1,0:T(8,128)(2,1)} %reduce-scatter.4.cloned.1.call-done.gate, bf16[224,1152]{1,0:T(8,128)(2,1)} %reduce-scatter.6.cloned.1.call-done.up, bf16[224,1152]{1,0:T(8,128)(2,1)} %reduce-scatter.8.cloned.1.call-done.down), custom_call_target="tpu_custom_call" | custom-call | tf_op jit(solution)/shard_map/pallas_call | solution.py:556
  556.9 3.2 copy.152
  (274 shorter events, 52.3 us)
Async XLA Ops:
  7.2 174.0 %all-gather.4.cloned.1.call-start = ((), (), s32[]{:S(2)}) async-start(), calls=%async_computation.3 | async-start | bytes 2580480 | tf_op jit(solution)/shard_map/all_gather | solution.py:903
  64.6 116.5 %all-gather.6.cloned.1.call-start = ((), (), s32[]{:S(2)}) async-start(), calls=%async_computation.4 | async-start | bytes 2580480 | tf_op jit(solution)/shard_map/all_gather | solution.py:903
  65.4 159.5 %all-gather.8.cloned.1.call-start = ((), (), s32[]{:S(2)}) async-start(), calls=%async_computation.5 | async-start | bytes 2580480 | tf_op jit(solution)/shard_map/all_gather | solution.py:903
  74.9 17.4 %copy-start.20 = (f32[2,128,1536]{2,1,0:T(8,128)}, f32[2,128,1536]{2,1,0:T(8,128)S(1)}, u32[]{:S(2)}) copy-start(f32[2,128,1536]{2,1,0:T(8,128)S(1)} %fusion.30) | copy-start | bytes 4718596
  77.2 16.5 %copy-start.28 = (f32[128,128]{1,0:T(8,128)}, f32[128,128]{1,0:T(8,128)S(1)}, u32[]{:S(2)}) copy-start(f32[128,128]{1,0:T(8,128)S(1)} %get-tuple-element.104) | copy-start | bytes 196612
  77.2 16.5 %copy-start.30 = (f32[128,128]{1,0:T(8,128)}, f32[128,128]{1,0:T(8,128)S(1)}, u32[]{:S(2)}) copy-start(f32[128,128]{1,0:T(8,128)S(1)} %get-tuple-element.105) | copy-start | bytes 196612
  77.5 14.8 %copy-start.40 = (bf16[2,128,128]{2,1,0:T(8,128)(2,1)}, bf16[2,128,128]{2,1,0:T(8,128)(2,1)S(1)}, u32[]{:S(2)}) copy-start(bf16[2,128,128]{2,1,0:T(8,128)(2,1)S(1)} %get-tuple-element.95) | copy-start | bytes 196612
  78.2 28.0 %collective-permute-start = (bf16[2,128,512]{2,1,0:T(8,128)(2,1)}, bf16[2,128,512]{2,1,0:T(8,128)(2,1)}, u32[]{:S(2)}, u32[]{:S(2)}) collective-permute-start(bf16[2,128,512]{2,1,0:T(8,128)(2,1)} %pad_maximum_fusion.5), channel_id=1, source_target_pairs={{0,4},{1,5},{2,6},{3,7},{8,12},{9,13},{10,14},{11,15},{16,20},{17,... | collective-permute-start | bytes 786440 | tf_op jit(solution)/shard_map/ppermute | solution.py:842
  85.3 37.3 %collective-permute-start.1 = (bf16[2,128,512]{2,1,0:T(8,128)(2,1)}, bf16[2,128,512]{2,1,0:T(8,128)(2,1)}, u32[]{:S(2)}, u32[]{:S(2)}) collective-permute-start(bf16[2,128,512]{2,1,0:T(8,128)(2,1)} %pad_maximum_fusion.5), channel_id=1, source_target_pairs={{0,3},{1,4},{2,5},{3,6},{4,7},{8,11},{9,12},{10,13},{11,14},{12,15... | collective-permute-start | bytes 786440 | tf_op jit(solution)/shard_map/ppermute | solution.py:842
  87.3 43.4 %collective-permute-start.2 = (bf16[2,128,512]{2,1,0:T(8,128)(2,1)}, bf16[2,128,512]{2,1,0:T(8,128)(2,1)}, u32[]{:S(2)}, u32[]{:S(2)}) collective-permute-start(bf16[2,128,512]{2,1,0:T(8,128)(2,1)} %pad_maximum_fusion.5), channel_id=1, source_target_pairs={{0,2},{1,3},{2,4},{3,5},{4,6},{5,7},{8,10},{9,11},{10,12},{11,13},... | collective-permute-start | bytes 786440 | tf_op jit(solution)/shard_map/ppermute | solution.py:842
  89.2 42.4 %collective-permute-start.3 = (bf16[2,128,512]{2,1,0:T(8,128)(2,1)}, bf16[2,128,512]{2,1,0:T(8,128)(2,1)}, u32[]{:S(2)}, u32[]{:S(2)}) collective-permute-start(bf16[2,128,512]{2,1,0:T(8,128)(2,1)} %pad_maximum_fusion.5), channel_id=1, source_target_pairs={{0,1},{1,2},{2,3},{3,4},{4,5},{5,6},{6,7},{8,9},{9,10},{10,11},{11... | collective-permute-start | bytes 786440 | tf_op jit(solution)/shard_map/ppermute | solution.py:842
  92.3 435.7 %reduce-scatter.4.cloned.1.call-start = ((), (), s32[]{:S(2)}) async-start(), calls=%async_computation.6 | async-start | bytes 2580480 | tf_op jit(solution)/shard_map/reduce_scatter | solution.py:1055
  94.5 38.2 %copy-start.34 = (bf16[2,128,4,128]{3,1,2,0:T(8,128)(2,1)}, bf16[2,128,4,128]{3,1,2,0:T(8,128)(2,1)S(1)}, u32[]{:S(2)}) copy-start(bf16[2,128,4,128]{3,1,2,0:T(8,128)(2,1)S(1)} %get-tuple-element.90) | copy-start | bytes 786436
  98.4 37.3 %copy-start.15 = (bf16[8,128,1152]{2,1,0:T(8,128)(2,1)}, bf16[8,128,1152]{2,1,0:T(8,128)(2,1)S(1)}, u32[]{:S(2)}) copy-start(bf16[8,128,1152]{2,1,0:T(8,128)(2,1)S(1)} %slice.131) | copy-start | bytes 7077892
  98.4 34.3 %copy-start.41 = (bf16[2,128,128]{2,1,0:T(8,128)(2,1)S(1)}, bf16[2,128,128]{2,1,0:T(8,128)(2,1)}, u32[]{:S(2)}) copy-start(bf16[2,128,128]{2,1,0:T(8,128)(2,1)} %copy-done.40) | copy-start | bytes 196612
  99.8 32.9 %copy-start.36 = (bf16[2,128,4,128]{3,1,2,0:T(8,128)(2,1)S(1)}, bf16[2,128,4,128]{3,1,2,0:T(8,128)(2,1)}, u32[]{:S(2)}) copy-start(bf16[2,128,4,128]{3,1,2,0:T(8,128)(2,1)} %get-tuple-element.91) | copy-start | bytes 786436
  99.8 32.9 %copy-start.43 = (pred[2,128,640]{1,2,0:T(8,128)(4,1)S(1)}, pred[2,128,640]{1,2,0:T(8,128)(4,1)}, u32[]{:S(2)}) copy-start(pred[2,128,640]{1,2,0:T(8,128)(4,1)} %or_and_fusion) | copy-start | bytes 491524
  137.7 43.4 %copy-start.2 = (f32[2,128,1152]{2,1,0:T(8,128)}, f32[2,128,1152]{2,1,0:T(8,128)S(1)}, u32[]{:S(2)}) copy-start(f32[2,128,1152]{2,1,0:T(8,128)S(1)} %get-tuple-element.83) | copy-start | bytes 3538948
  137.7 43.4 %copy-start.66 = (f32[2,128]{1,0:T(2,128)}, f32[2,128]{1,0:T(2,128)S(1)}, u32[]{:S(2)}) copy-start(f32[2,128]{1,0:T(2,128)S(1)} %get-tuple-element.82) | copy-start | bytes 3076
  137.7 209.7 %copy-start.65 = (f32[2,128]{1,0:T(2,128)}, f32[2,128]{1,0:T(2,128)S(1)}, u32[]{:S(2)}) copy-start(f32[2,128]{1,0:T(2,128)S(1)} %fusion.37) | copy-start | bytes 3076
  346.8 181.2 %reduce-scatter.6.cloned.1.call-start = ((), (), s32[]{:S(2)}) async-start(), calls=%async_computation.7 | async-start | bytes 2580480 | tf_op jit(solution)/shard_map/reduce_scatter | solution.py:1055
  351.2 176.8 %reduce-scatter.8.cloned.1.call-start = ((), (), s32[]{:S(2)}) async-start(), calls=%async_computation.8 | async-start | bytes 2580480 | tf_op jit(solution)/shard_map/reduce_scatter | solution.py:1055
  365.9 10.5 %copy-start.27 = (bf16[2,640,512]{2,1,0:T(8,128)(2,1)S(1)}, bf16[2,640,512]{2,1,0:T(8,128)(2,1)}, u32[]{:S(2)}) copy-start(bf16[2,640,512]{2,1,0:T(8,128)(2,1)} %copy-done.26) | copy-start | bytes 3932164
  366.7 20.2 %collective-permute-start.4 = (bf16[2,128,512]{2,1,0:T(8,128)(2,1)}, bf16[2,128,512]{2,1,0:T(8,128)(2,1)S(1)}, u32[]{:S(2)}, u32[]{:S(2)}) collective-permute-start(bf16[2,128,512]{2,1,0:T(8,128)(2,1)} %get-tuple-element.84), channel_id=1, source_target_pairs={{1,0},{2,1},{3,2},{4,3},{5,4},{6,5},{7,6},{9,8},{10,9},{11,10},{12... | collective-permute-start | bytes 786440 | tf_op jit(solution)/shard_map/ppermute | solution.py:842
  371.4 30.1 %collective-permute-start.5 = (bf16[2,128,512]{2,1,0:T(8,128)(2,1)}, bf16[2,128,512]{2,1,0:T(8,128)(2,1)S(1)}, u32[]{:S(2)}, u32[]{:S(2)}) collective-permute-start(bf16[2,128,512]{2,1,0:T(8,128)(2,1)} %get-tuple-element.87), channel_id=1, source_target_pairs={{2,0},{3,1},{4,2},{5,3},{6,4},{7,5},{10,8},{11,9},{12,10},{13,11},... | collective-permute-start | bytes 786440 | tf_op jit(solution)/shard_map/ppermute | solution.py:842
  373.4 28.1 %collective-permute-start.6 = (bf16[2,128,512]{2,1,0:T(8,128)(2,1)S(1)}, bf16[2,128,512]{2,1,0:T(8,128)(2,1)S(1)}, u32[]{:S(2)}, u32[]{:S(2)}) collective-permute-start(bf16[2,128,512]{2,1,0:T(8,128)(2,1)S(1)} %get-tuple-element.86), channel_id=1, source_target_pairs={{3,0},{4,1},{5,2},{6,3},{7,4},{11,8},{12,9},{13,10},{14,11},{15,12... | collective-permute-start | bytes 786440 | tf_op jit(solution)/shard_map/ppermute | solution.py:842
  374.7 36.4 %collective-permute-start.7 = (bf16[2,128,512]{2,1,0:T(8,128)(2,1)S(1)}, bf16[2,128,512]{2,1,0:T(8,128)(2,1)S(1)}, u32[]{:S(2)}, u32[]{:S(2)}) collective-permute-start(bf16[2,128,512]{2,1,0:T(8,128)(2,1)S(1)} %get-tuple-element.85), channel_id=1, source_target_pairs={{4,0},{5,1},{6,2},{7,3},{12,8},{13,9},{14,10},{15,11},{20,16},{21,... | collective-permute-start | bytes 786440 | tf_op jit(solution)/shard_map/ppermute | solution.py:842
  381.4 29.6 %copy-start.11 = (f32[2,640,256]{2,1,0:T(8,128)S(1)}, f32[2,640,256]{2,1,0:T(8,128)}, u32[]{:S(2)}) copy-start(f32[2,640,256]{2,1,0:T(8,128)} %copy-done.10) | copy-start | bytes 3932164
  381.4 29.6 %copy-start.13 = (f32[2,640,256]{2,1,0:T(8,128)S(1)}, f32[2,640,256]{2,1,0:T(8,128)}, u32[]{:S(2)}) copy-start(f32[2,640,256]{2,1,0:T(8,128)} %copy-done.12) | copy-start | bytes 3932164
  382.3 29.1 %copy-start.62 = (f32[2,128]{1,0:T(2,128)S(1)}, f32[2,128]{1,0:T(2,128)}, u32[]{:S(2)}) copy-start(f32[2,128]{1,0:T(2,128)} %copy-done.61) | copy-start | bytes 3076
  382.3 29.1 %copy-start.64 = (f32[256]{0:T(256)S(1)}, f32[256]{0:T(256)}, u32[]{:S(2)}) copy-start(f32[256]{0:T(256)} %copy-done.63) | copy-start | bytes 3076
  521.7 4.9 copy-start.7
  (61 other events, 103.5 us)
Sparse Core Ops, SparseCore 0:
  64.7 61.6 all-gather.3
  128.0 51.1 all-gather.5
  180.8 43.9 all-gather.7
  346.9 45.7 reduce-scatter.3
  394.9 60.5 reduce-scatter.5
  457.7 59.9 reduce-scatter.7

commit v4 on v3

--- a/solution.py
+++ b/solution.py
@@ -44,8 +44,14 @@
         low = chip // self.wide + self.lo + sign * (k // self.wide)
         return lax.rem(low, self.lo) * self.wide + lax.rem(across, self.wide)
 
-    def back(self, k):
-        return (-(k // self.wide)) % self.lo * self.wide + (-(k % self.wide)) % self.wide
+    def straight(self):
+        return list(range(1, self.wide)) + [low * self.wide for low in range(1, self.lo)]
+
+    def bent(self):
+        return [k for k in range(1, self.chips) if k not in self.straight()]
+
+    def position(self, k):
+        return (self.bent() + self.straight() + [0]).index(k)
 
     def device(self, chip, core, high):
         return (lax.rem(chip, self.wide) * 2 + core, high * self.lo + chip // self.wide)
@@ -64,49 +70,78 @@
     pl.semaphore_wait(barrier, len(devices))
 
 
-def gather_tokens_kernel(lay, own, out, local_sem, send, recv, core_send, core_recv):
+def gather_group_kernel(lay, slot, own, out, local_sem, send, recv, pass_send, core_send, core_recv):
     chip, core, high = lay.place()
     n = lay.chips
-    peers = [lay.device(lay.offset(chip, k), core, high) for k in range(1, n)]
+    half = own.shape[0] // 2
+    halves = (pl.ds(0, half), pl.ds(half, half))
+    peers = [lay.device(lay.offset(chip, k), core, high) for k in range(n)]
+    sources = [lay.offset(chip, k, -1) for k in range(n)]
     partner = lay.device(chip, 1 - core, high)
-    greet(peers + [partner])
-    mine = chip * 2 + core
-    pushes = [
-        remote(own, out.at[mine], send.at[k], recv.at[k], peers[k]) for k in range(n - 1)
-    ]
-    for push in pushes:
-        push.start()
-    shares = [remote(own, out.at[mine], core_send.at[0], core_recv.at[0], partner)]
+    greet(peers[1:] + [partner])
+    mine = [slot(out, k, chip, core) for k in range(n)]
+    straight, bent = lay.straight(), lay.bent()
+    keep = pltpu.make_async_copy(own, mine[0], local_sem)
+    keep.start()
+    pushes = []
+
+    def push(k, h, source, target, sem):
+        copy = remote(source.at[halves[h]], target.at[halves[h]], sem, recv.at[k, h], peers[k])
+        return copy
+
+    ordered = [(k, i if k < lay.wide else 1 - i) for i in range(2) for k in straight]
+    for k, h in ordered:
+        copy = push(k, h, own, mine[k], send.at[k, h])
+        copy.start()
+        pushes.append(copy)
+    shares = [remote(own, mine[0], core_send.at[0], core_recv.at[0], partner)]
     shares[0].start()
-    keep = pltpu.make_async_copy(own, out.at[mine], local_sem)
-    keep.start()
-    for k in range(1, n):
-        source = lay.offset(chip, k, -1) * 2 + core
-        pushes[k - 1].wait_recv()
-        share = remote(out.at[source], out.at[source], core_send.at[k], core_recv.at[k], partner)
+
+    def arrived(k, h):
+        copy = remote(own.at[halves[h]], mine[k].at[halves[h]], send.at[k, h], recv.at[k, h], peers[k])
+        copy.wait_recv()
+
+    for k, h in ordered:
+        arrived(k, h)
+        block = slot(out, k, sources[k], core)
+        if k < lay.wide and h == 0:
+            onward = [b * lay.wide for b in range(1, lay.lo)]
+        elif k >= lay.wide and h == 1:
+            onward = list(range(1, lay.wide))
+        else:
+            onward = []
+        for step in onward:
+            total = k + step
+            there = slot(out, total, sources[k], core)
+            copy = remote(
+                block.at[halves[h]], there.at[halves[h]], pass_send.at[total, h], recv.at[total, h], peers[step]
+            )
+            copy.start()
+            pushes.append(copy)
+    for k in straight + bent:
+        if k in bent:
+            for h in range(2):
+                arrived(k, h)
+        block = slot(out, k, sources[k], core)
+        share = remote(block, block, core_send.at[k], core_recv.at[k], partner)
         share.start()
         shares.append(share)
     keep.wait()
-    for push in pushes:
-        push.wait_send()
+    for copy in pushes:
+        copy.wait_send()
     for share in shares:
         share.wait()
 
 
-def gather_tokens(lay, value, collective_id):
+def gather_group(lay, value, out_shape, slot, collective_id):
     n = lay.chips
+    dma = pltpu.SemaphoreType.DMA
     return pl.pallas_call(
-        partial(gather_tokens_kernel, lay),
-        out_shape=jax.ShapeDtypeStruct((lay.group,) + value.shape, value.dtype),
+        partial(gather_group_kernel, lay, slot),
+        out_shape=jax.ShapeDtypeStruct(out_shape, value.dtype),
         in_specs=[pl.BlockSpec(memory_space=pl.ANY)],
         out_specs=pl.BlockSpec(memory_space=pl.ANY),
-        scratch_shapes=[
-            pltpu.SemaphoreType.DMA,
-            pltpu.SemaphoreType.DMA((n - 1,)),
-            pltpu.SemaphoreType.DMA((n - 1,)),
-            pltpu.SemaphoreType.DMA((n,)),
-            pltpu.SemaphoreType.DMA((n,)),
-        ],
+        scratch_shapes=[dma, dma((n, 2)), dma((n, 2)), dma((n, 2)), dma((n,)), dma((n,))],
         compiler_params=pltpu.CompilerParams(
             collective_id=collective_id, has_side_effects=True, vmem_limit_bytes=VMEM_LIMIT
         ),
@@ -118,46 +153,48 @@
 
 
 def weights_in_kernel(
-    lay, pack, pairs, lows, attn_out, gate_out, up_out, low_out,
-    attn_land, own, stack, land, lanes, keep_sem, attn_send, attn_recv, send, recv,
-    chain_send, chain_recv, low_send, low_recv, core_send, core_recv,
+    lay, reach, tokens, pack, pairs, lows, attn_out, ffn_out, earlier_out,
+    hops_land, attn_land, own, stack, land, lanes, keep_sem, token_sem, hop_send, hop_recv, low_send, low_recv, attn_send, attn_recv, send, recv, chain_send, chain_recv,
 ):
-    n = lay.dp
-    hi, lo = lay.hi, lay.lo
+    n, hi, lo = lay.dp, lay.hi, lay.lo
     dp = lax.axis_index("dp")
     ctx = lax.axis_index("ctx")
-    high, low = ctx // lo, lax.rem(ctx, lo)
-    core = lax.rem(dp, 2)
+    high = ctx // lo
     per, cols = lows.shape[1:]
-    padded = gate_out.shape[0]
+    padded = ffn_out.shape[0] // 3
     targets = [lax.rem(dp + k, n) for k in range(n)]
-    partner = (dp + 1 - 2 * core, ctx)
-    low_peers = [(dp, high * lo + lax.rem(low + k, lo)) for k in range(1, lo)]
     right, left = (dp, ctx + lo), (dp, ctx - lo)
     has_right, has_left = high < hi - 1, high > 0
+    low = lax.rem(ctx, lo)
+    low_peers = [(dp, high * lo + other) for other in range(lo)]
+    hops = hops_land.shape[0] - 1
     barrier = pltpu.get_barrier_semaphore()
-    for device in [(target, ctx) for target in targets[1:]] + low_peers:
-        pl.semaphore_signal(barrier, inc=1, device_id=device, device_id_type=MESH)
+    for target in targets[1:]:
+        pl.semaphore_signal(barrier, inc=1, device_id=(target, ctx), device_id_type=MESH)
+    for other in range(lo):
+        if lo > 1:
+            @pl.when(low != other)
+            def _():
+                pl.semaphore_signal(barrier, inc=1, device_id=low_peers[other], device_id_type=MESH)
     for there, device in ((has_right, right), (has_left, left)):
         @pl.when(there)
         def _():
             pl.semaphore_signal(barrier, inc=1, device_id=device, device_id_type=MESH)
     sides = jnp.where(has_right, 1, 0) + jnp.where(has_left, 1, 0)
-    pl.semaphore_wait(barrier, n - 1 + len(low_peers) + sides)
+    pl.semaphore_wait(barrier, n - 1 + sides + lo - 1)
 
     attn_pushes = []
     for k in range(1, n):
         push = remote(
-            pack.at[lax.rem(targets[k], 2)], attn_land.at[dp], attn_send.at[k], attn_recv.at[k],
-            (targets[k], ctx),
+            pack.at[targets[k]], attn_land.at[dp], attn_send.at[k], attn_recv.at[k], (targets[k], ctx)
         )
         push.start()
         attn_pushes.append(push)
-    attn_land[dp] = pack[core]
+    attn_land[dp] = pack[dp]
     blank = jnp.zeros((padded - per, cols), jnp.bfloat16)
     pushes = []
 
-    def feed_forward(k):
+    def feed_forward_rows(k):
         target = targets[k]
         for j, (first, width) in enumerate(lane_tiles(cols)):
             lanes[j, :, :width] = pairs[target, :, first : first + width]
@@ -171,133 +208,267 @@
                     stack[k - 1, i, :per, first : first + width] = piece.astype(jnp.bfloat16)
                 else:
                     land[dp, i, :per, first : first + width] = piece.astype(jnp.bfloat16)
-            if k:
+            if padded > per and k:
                 stack[k - 1, i, per:] = blank
-            else:
+            elif padded > per:
                 land[dp, i, per:] = blank
         if k:
             push = remote(stack.at[k - 1], land.at[dp], send.at[k], recv.at[k], (target, ctx))
             push.start()
             pushes.append(push)
 
-    everything = [(0, 0, None, high)]
-    for step in range(1, hi):
-        everything.append((0, step, high - step >= 0, high - step))
-        everything.append((1, step, high + step < hi, high + step))
-
-    def to_core(source, c, slot):
-        return remote(source, attn_out.at[c, core], core_send.at[slot], core_recv.at[slot], partner)
-
-    def to_low(source, c, i):
-        return [
-            remote(source, attn_out.at[c, core], low_send.at[i, k], low_recv.at[i, k], low_peers[k])
-            for k in range(lo - 1)
-        ]
-
-    def chain(source, c, side, step):
+    def chain(source, where, side, step):
         return remote(
-            source, attn_out.at[c, core], chain_send.at[side, step], chain_recv.at[side, step],
+            source, attn_out.at[where], chain_send.at[side, step], chain_recv.at[side, step],
             right if side == 0 else left,
         )
 
-    def sides_of(side, step):
-        if step == hi - 1:
-            return []
-        return [s for s in ((0, has_right), (1, has_left)) if step == 0 or s[0] == side]
-
-    def pass_own(i, side, step, where):
-        c = where * lo + low
-        source = attn_out.at[c, core] if step else own
-        if step:
-            chain(own, c, side, step - 1).wait_recv()
-        for go, there in sides_of(side, step):
-            @pl.when(there)
+    def pass_on(step):
+        if step == 0:
+            for side, there in ((0, has_right), (1, has_left)):
+                @pl.when(there)
+                def _():
+                    chain(own, high, side, 0).start()
+            return
+        for side, here, there in (
+            (0, high - step >= 0, has_right),
+            (1, high + step < hi, has_left),
+        ):
+            where = high - step if side == 0 else high + step
+
+            @pl.when(here)
             def _():
-                chain(source, c, go, step).start()
-        for push in to_low(source, c, i):
-            push.start()
-        to_core(source, c, i * lo).start()
-
-    def pass_low(i, side, step, where):
-        for k in range(lo - 1):
-            c = where * lo + lax.rem(low + lo - 1 - k, lo)
-            to_low(own, c, i)[k].wait_recv()
-            to_core(attn_out.at[c, core], c, i * lo + k + 1).start()
-
-    def finish(i, side, step, where):
-        c = where * lo + low
-        for go, there in sides_of(side, step):
-            @pl.when(there)
+                chain(own, where, side, step - 1).wait_recv()
+                if step < hi - 1:
+                    @pl.when(there)
+                    def _():
+                        chain(attn_out.at[where], where, side, step).start()
+
+    def finish(step):
+        for side, here, there in (
+            (0, high - step >= 0, has_right),
+            (1, high + step < hi, has_left),
+        ):
+            @pl.when(here & there)
             def _():
-                chain(own, c, go, step).wait_send()
-        for push in to_low(own, c, i):
-            push.wait_send()
-        for k in range(lo):
-            to_core(own, c, i * lo + k).wait()
-
-    def each(stage, step):
-        for i, (side, s, there, where) in enumerate(everything):
-            if s == step:
-                call = partial(stage, i, side, s, where)
-                if s:
-                    pl.when(there)(call)
-                else:
-                    call()
-
+                chain(own, high, side, step).wait_send()
+
+    def hop(h):
+        return remote(hops_land.at[h], hops_land.at[h + 1], hop_send.at[h], hop_recv.at[h], right)
+
+    def wanted(h, source, target):
+        distance = h * lo + target - source
+        return (distance >= 1) & (distance <= reach) & (high >= h)
+
+    def aside(h, source, target, device):
+        return remote(
+            hops_land.at[h], earlier_out.at[reach - (h * lo + target - source)], low_send.at[h, target],
+            low_recv.at[h, source], device,
+        )
+
+    def pass_tokens(h):
+        if h:
+            @pl.when(high >= h)
+            def _():
+                hop(h - 1).wait_recv()
+        if h < hops:
+            @pl.when((high >= h) & has_right)
+            def _():
+                hop(h).start()
+        for other in range(lo):
+            if lo > 1:
+                @pl.when((low != other) & wanted(h, low, other))
+                def _():
+                    aside(h, low, other, low_peers[other]).start()
+        if h and h * lo <= reach:
+            @pl.when(high >= h)
+            def _():
+                earlier_out[reach - h * lo] = hops_land[h]
+
+    def finish_tokens(h):
+        if h < hops:
+            @pl.when((high >= h) & has_right)
+            def _():
+                hop(h).wait_send()
+        for other in range(lo):
+            if lo > 1:
+                @pl.when((low != other) & wanted(h, other, low))
+                def _():
+                    aside(h, other, low, low_peers[other]).wait_recv()
+
+                @pl.when((low != other) & wanted(h, low, other))
+                def _():
+                    aside(h, low, other, low_peers[other]).wait_send()
+
+    take = pltpu.make_async_copy(tokens, hops_land.at[0], token_sem)
+    take.start()
+    for d in range(1, reach + 1):
+        @pl.when(ctx < d)
+        def _():
+            earlier_out[reach - d] = jnp.zeros(earlier_out.shape[1:], earlier_out.dtype)
     order = list(range(2, n)) + [1, 0]
-    feed_forward(order[0])
+    feed_forward_rows(order[0])
     for push in attn_pushes:
         push.wait_recv()
     for q in range(n):
         own[:, q * cols : (q + 1) * cols] = attn_land[q]
-    keep = pltpu.make_async_copy(own, attn_out.at[ctx, core], keep_sem)
+    keep = pltpu.make_async_copy(own, attn_out.at[high], keep_sem)
     keep.start()
-    each(pass_own, 0)
+    pass_on(0)
+    take.wait()
+    pass_tokens(0)
     for k in order[1:]:
-        feed_forward(k)
-    for step in range(1, hi + 1):
-        each(pass_own, step)
-        each(pass_low, step - 1)
+        feed_forward_rows(k)
+    for step in range(1, max(hi, hops + 1)):
+        if step < hi:
+            pass_on(step)
+        if step <= hops:
+            pass_tokens(step)
     for push in pushes:
         push.wait_recv()
     for q in range(n):
-        for i, out in enumerate((gate_out, up_out, low_out)):
-            out[:, q * cols : (q + 1) * cols] = land[q, i]
+        for i in range(3):
+            ffn_out[i * padded : (i + 1) * padded, q * cols : (q + 1) * cols] = land[q, i]
     keep.wait()
-    for step in range(hi):
-        each(finish, step)
+    for step in range(hi - 1):
+        finish(step)
+    for h in range(hops + 1):
+        finish_tokens(h)
     for push in attn_pushes + pushes:
         push.wait_send()
 
 
-def weights_in(lay, pack, pairs, lows, collective_id):
+def weights_in(lay, reach, tokens, pack, pairs, lows, collective_id):
     n, per, cols = lows.shape
     rows = pack.shape[1]
     padded = -(-per // 16) * 16
-    count = 2 * lay.hi - 1
-    wide = jax.ShapeDtypeStruct((padded, n * cols), jnp.bfloat16)
     vmem = pl.BlockSpec(memory_space=pltpu.VMEM)
     dma = pltpu.SemaphoreType.DMA
+    hops = min(lay.hi - 1, (reach + lay.lo - 1) // lay.lo)
     scratch = [
+        pltpu.VMEM((hops + 1,) + tokens.shape, tokens.dtype),
         pltpu.VMEM((n, rows, cols), jnp.bfloat16),
         pltpu.VMEM((rows, n * cols), jnp.bfloat16),
         pltpu.VMEM((n - 1, 3, padded, cols), jnp.bfloat16),
         pltpu.VMEM((n, 3, padded, cols), jnp.bfloat16),
         pltpu.VMEM((len(lane_tiles(cols)), 2 * per, 128), jnp.float32),
         dma,
+        dma,
     ]
-    for shape in ((n,), (n,), (2, lay.hi), (count, max(1, lay.lo - 1)), (count * lay.lo,)):
+    for shape in ((hops + 1,), (hops + 1, lay.lo), (n,), (n,), (2, lay.hi)):
         scratch += [dma(shape), dma(shape)]
     return pl.pallas_call(
-        partial(weights_in_kernel, lay),
-        out_shape=(jax.ShapeDtypeStruct((lay.ctx, 2, rows, n * cols), jnp.bfloat16), wide, wide, wide),
-        in_specs=[vmem] * 3,
-        out_specs=(pl.BlockSpec(memory_space=pl.ANY),) + (vmem,) * 3,
+        partial(weights_in_kernel, lay, reach),
+        out_shape=(
+            jax.ShapeDtypeStruct((lay.hi, rows, n * cols), jnp.bfloat16),
+            jax.ShapeDtypeStruct((3 * padded, n * cols), jnp.bfloat16),
+            jax.ShapeDtypeStruct((reach,) + tokens.shape, tokens.dtype),
+        ),
+        in_specs=[vmem] * 4,
+        out_specs=(pl.BlockSpec(memory_space=pl.ANY), vmem, vmem),
         scratch_shapes=scratch,
         compiler_params=pltpu.CompilerParams(
             collective_id=collective_id, has_side_effects=True, vmem_limit_bytes=VMEM_LIMIT
         ),
-    )(pack, pairs, lows)
+    )(tokens, pack, pairs, lows)
+
+
+def later_kernel(lay, reach, pieces, out, low_land, moved, arrived, chain_send, chain_recv, low_send, low_recv):
+    hi, lo = lay.hi, lay.lo
+    dp = lax.axis_index("dp")
+    ctx = lax.axis_index("ctx")
+    high, low = ctx // lo, lax.rem(ctx, lo)
+    hops = min(hi - 1, (reach + lo - 1) // lo)
+    right, left = (dp, ctx + lo), (dp, ctx - lo)
+    has_right, has_left = high < hi - 1, high > 0
+    low_peers = [(dp, high * lo + other) for other in range(lo)]
+    barrier = pltpu.get_barrier_semaphore()
+    for there, device in [(has_right, right), (has_left, left)] + [
+        (low != other, low_peers[other]) for other in range(lo) if lo > 1
+    ]:
+        @pl.when(there)
+        def _():
+            pl.semaphore_signal(barrier, inc=1, device_id=device, device_id_type=MESH)
+    sides = jnp.where(has_right, 1, 0) + jnp.where(has_left, 1, 0)
+    pl.semaphore_wait(barrier, sides + lo - 1)
+
+    def wanted(h, owner, reader):
+        distance = h * lo + reader - owner
+        return (distance >= 1) & (distance <= reach) & (high >= h)
+
+    def across(h, other):
+        return remote(
+            pieces.at[reach - (h * lo + low - other)], low_land.at[h, low], low_send.at[h, other],
+            low_recv.at[h, low], low_peers[other],
+        )
+
+    def from_low(h, other):
+        return remote(
+            pieces.at[0], low_land.at[h, other], low_send.at[h, other], low_recv.at[h, other], low_peers[other]
+        )
+
+    def hop(h):
+        return remote(moved.at[h], arrived.at[h - 1], chain_send.at[h], chain_recv.at[h - 1], left)
+
+    for h in range(hops, -1, -1):
+        for other in range(lo):
+            if lo > 1:
+                @pl.when((low != other) & wanted(h, other, low))
+                def _():
+                    across(h, other).start()
+    for h in range(hops, -1, -1):
+        out[...] = jnp.zeros_like(out)
+        if h and h * lo <= reach:
+            out[...] += pieces[reach - h * lo].astype(jnp.float32)
+        for other in range(lo):
+            if lo > 1:
+                @pl.when((low != other) & wanted(h, low, other))
+                def _():
+                    from_low(h, other).wait_recv()
+                    out[...] += low_land[h, other].astype(jnp.float32)
+        if h < hops:
+            @pl.when(has_right & (high >= h))
+            def _():
+                hop(h + 1).wait_recv()
+                out[...] += arrived[h].astype(jnp.float32)
+        if h:
+            @pl.when(high >= h)
+            def _():
+                moved[h] = out[...].astype(moved.dtype)
+                hop(h).start()
+    for h in range(hops + 1):
+        if h:
+            @pl.when(high >= h)
+            def _():
+                hop(h).wait_send()
+        for other in range(lo):
+            if lo > 1:
+                @pl.when((low != other) & wanted(h, other, low))
+                def _():
+                    across(h, other).wait_send()
+
+
+def later_sum(lay, reach, pieces, collective_id):
+    hops = min(lay.hi - 1, (reach + lay.lo - 1) // lay.lo)
+    shape = pieces.shape[1:]
+    vmem = pl.BlockSpec(memory_space=pltpu.VMEM)
+    dma = pltpu.SemaphoreType.DMA
+    return pl.pallas_call(
+        partial(later_kernel, lay, reach),
+        out_shape=jax.ShapeDtypeStruct(shape, jnp.float32),
+        in_specs=[vmem],
+        out_specs=vmem,
+        scratch_shapes=[
+            pltpu.VMEM((hops + 1, lay.lo) + shape, pieces.dtype),
+            pltpu.VMEM((hops + 1,) + shape, pieces.dtype),
+            pltpu.VMEM((hops + 1,) + shape, pieces.dtype),
+        ]
+        + [dma((hops + 1,))] * 2
+        + [dma((hops + 1, lay.lo))] * 2,
+        compiler_params=pltpu.CompilerParams(
+            collective_id=collective_id, has_side_effects=True, vmem_limit_bytes=VMEM_LIMIT
+        ),
+    )(pieces)
 
 
 def flip(index, bit):
@@ -515,16 +686,17 @@
     )(*([parts, gains] if with_gains else [parts]))
 
 
-def exchange_out_kernel(lay, gate, up, down, pairs_out, lows_out, stack, land, lanes, send, recv):
+def exchange_out_kernel(lay, rows, pairs_out, lows_out, stack, land, lanes, send, recv):
     n = lay.dp
     dp = lax.axis_index("dp")
     ctx = lax.axis_index("ctx")
     cols = lows_out.shape[2]
     per = lows_out.shape[1]
+    padded = rows.shape[0] // 3
     greet([(lax.rem(dp + k, n), ctx) for k in range(1, n)])
     for q in range(n):
-        for i, piece in enumerate((gate, up, down)):
-            stack[q, i] = piece[:, q * cols : (q + 1) * cols]
+        for i in range(3):
+            stack[q, i] = rows[i * padded : (i + 1) * padded, q * cols : (q + 1) * cols]
     pushes = []
     for k in range(1, n):
         target = lax.rem(dp + k, n)
@@ -549,9 +721,9 @@
         push.wait_send()
 
 
-def exchange_out(lay, gate, up, down, per, collective_id):
-    padded = gate.shape[0]
-    n, cols = lay.dp, gate.shape[1] // lay.dp
+def exchange_out(lay, rows, per, collective_id):
+    padded = rows.shape[0] // 3
+    n, cols = lay.dp, rows.shape[1] // lay.dp
     vmem = pl.BlockSpec(memory_space=pltpu.VMEM)
     return pl.pallas_call(
         partial(exchange_out_kernel, lay),
@@ -559,7 +731,7 @@
             jax.ShapeDtypeStruct((n, 2 * per, cols), jnp.float32),
             jax.ShapeDtypeStruct((n, per, cols), jnp.float32),
         ),
-        in_specs=[vmem] * 3,
+        in_specs=[vmem],
         out_specs=(vmem,) * 2,
         scratch_shapes=[
             pltpu.VMEM((n, 3, padded, cols), jnp.bfloat16),
@@ -571,20 +743,20 @@
         compiler_params=pltpu.CompilerParams(
             collective_id=collective_id, has_side_effects=True, vmem_limit_bytes=VMEM_LIMIT
         ),
-    )(gate, up, down)
-
-
-def in_tiles(total, size, body):
+    )(rows)
+
+
+def in_tiles(total, size, body, begin=0):
     whole = total // size
 
     def step(i, carry):
-        body(pl.multiple_of(i * size, size), size)
+        body(pl.multiple_of(begin + i * size, math.gcd(begin, size)), size)
         return carry
 
     if whole:
         lax.fori_loop(0, whole, step, 0)
     if total % size:
-        body(whole * size, total % size)
+        body(begin + whole * size, total % size)
 
 
 def dot_nt(left, right):
@@ -599,32 +771,59 @@
 
 
 def feed_forward_kernel(
-    lay, mid, w_gate, w_up, w_down, mixed, cotangent, valid, gain,
-    result, grad_mid, gate_t, up_t, grad_gain, dw_gate, dw_up, dw_down,
-    act, slope, hidden, hidden_t, grads, parts, core_land, sums, landed, total, dy, sem,
-    core_send, core_recv, send, recv, share_send, share_recv, dy_send, dy_recv,
+    lay, mid, weights, mixed, cotangent, valid, gain,
+    result, grad_mid, grad_gain, grad_weights,
+    w_gate, w_up, w_down, gate_t, up_t, act, slope, hidden, hidden_t, grads, parts, core_land, sums, via, landed,
+    total, dy, weight_sem, core_send, core_recv, share_send, share_recv,
+    send, recv, via_send, via_recv, dy_send, dy_recv, dy_pass,
 ):
     chip, core, high = lay.place()
-    n = lay.chips
+    n, wide = lay.chips, lay.wide
     tokens = mixed.shape[0]
     units = w_gate.shape[0]
-    places = [lay.offset(chip, k) for k in range(n)]
-    sources = [lay.offset(chip, k, -1) for k in range(n)]
-    peers = [lay.device(place, core, high) for place in places]
+    padded = units // lay.hi
+    loads = [
+        pltpu.make_async_copy(
+            weights.at[h, pl.ds(i * padded, padded)], held.at[pl.ds(h * padded, padded)], weight_sem.at[i, h]
+        )
+        for i, held in enumerate((w_gate, w_up, w_down))
+        for h in range(lay.hi)
+    ]
+    for load in loads:
+        load.start()
+    peers = [lay.device(lay.offset(chip, k), core, high) for k in range(n)]
+    owners = [lay.device(lay.offset(chip, k, -1), core, high) for k in range(n)]
     partner = lay.device(chip, 1 - core, high)
     mine = pl.ds(pl.multiple_of(core * tokens, tokens), tokens)
     theirs = pl.ds(pl.multiple_of((1 - core) * tokens, tokens), tokens)
+    half = tokens // 2
+    halves = (pl.ds(0, half), pl.ds(half, half))
+    straight, bent = lay.straight(), lay.bent()
+    place = [lay.position(k) for k in range(n)]
     greet(peers[1:] + [partner])
 
     def to_partner(phase, k):
         return remote(
-            parts.at[places[k], theirs], core_land.at[k], core_send.at[phase, k], core_recv.at[phase, k], partner
+            parts.at[place[k], theirs], core_land.at[k], core_send.at[phase, k], core_recv.at[phase, k], partner
         )
 
-    def to_owner(phase, k):
+    def to_owner(phase, k, h):
         return remote(
-            sums.at[k - 1], landed.at[k - 1], send.at[phase, k], recv.at[phase, k], peers[k]
+            sums.at[k - 1, halves[h]], landed.at[place[k] - len(bent), halves[h]], send.at[phase, k, h],
+            recv.at[phase, k, h], owners[k],
         )
+
+    def to_neighbour(phase, k, h):
+        step = k % wide if h == 0 else k // wide * wide
+        return remote(
+            sums.at[k - 1, halves[h]], via.at[place[k], halves[h]], via_send.at[phase, k, h], via_recv.at[phase, k, h],
+            owners[step],
+        )
+
+    def added(k):
+        if k < wide:
+            return 1, [k + b * wide for b in range(1, lay.lo)]
+        return 0, [k + step for step in range(1, wide)]
 
     def add_core(phase, k):
         to_partner(phase, k).wait_recv()
@@ -632,25 +831,49 @@
         def chunk(first, rows):
             span = pl.ds(first, rows)
             here = pl.ds(pl.multiple_of(core * tokens + first, rows), rows)
-            both = parts[places[k], here].astype(jnp.float32) + core_land[k, span].astype(jnp.float32)
+            both = parts[place[k], here].astype(jnp.float32) + core_land[k, span].astype(jnp.float32)
             if k:
                 sums[k - 1, span] = both.astype(jnp.bfloat16)
             else:
                 total[span] = both
 
         in_tiles(tokens, 32, chunk)
-        if k:
-            to_owner(phase, k).start()
+        if k in bent:
+            for h in range(2):
+                to_neighbour(phase, k, h).start()
+        elif k:
+            h, others = added(k)
+            to_owner(phase, k, 1 - h).start()
+            if not others:
+                to_owner(phase, k, h).start()
+
+    def add_neighbours(phase, k):
+        h, others = added(k)
+        if not others:
+            return
+        for other in others:
+            to_neighbour(phase, other, h).wait_recv()
+
+        def chunk(first, rows):
+            span = pl.ds(first + h * half, rows)
+            value = sums[k - 1, span].astype(jnp.float32)
+            for other in others:
+                value = value + via[place[other], span].astype(jnp.float32)
+            sums[k - 1, span] = value.astype(jnp.bfloat16)
+
+        in_tiles(half, 32, chunk)
+        to_owner(phase, k, h).start()
 
     def add_owners(phase):
-        for k in range(1, n):
-            to_owner(phase, k).wait_recv()
+        for k in straight:
+            for h in range(2):
+                to_owner(phase, k, h).wait_recv()
 
         def chunk(first, rows):
             span = pl.ds(first, rows)
             value = total[span]
-            for k in range(1, n):
-                value = value + landed[k - 1, span].astype(jnp.float32)
+            for k in straight:
+                value = value + landed[place[k] - len(bent), span].astype(jnp.float32)
             total[span] = value
 
         in_tiles(tokens, 32, chunk)
@@ -658,61 +881,112 @@
     def settle(phase):
         for k in range(n):
             to_partner(phase, k).wait_send()
-            if k:
-                to_owner(phase, k).wait_send()
-
-    def forward(c):
+            for h in range(2):
+                if k in bent:
+                    to_neighbour(phase, k, h).wait_send()
+                elif k:
+                    to_owner(phase, k, h).wait_send()
+
+    rows_of = 2 * tokens
+
+    def joined(ref, group, *index):
+        value = ref[(pl.ds(*group),) + index]
+        return value.reshape((group[1] * rows_of,) + value.shape[2:])
+
+    def forward_units(group, begin, end):
+        count = group[1]
+
         def tile(first, width):
-            rows = pl.ds(first, width)
-            weights = jnp.concatenate([w_gate[rows], w_up[rows]], axis=0)
-            both = dot_nt(mid[c], weights)
+            units_here = pl.ds(first, width)
+            weights = jnp.concatenate([w_gate[units_here], w_up[units_here]], axis=0)
+            both = dot_nt(joined(mid, group), weights)
             gate, up = both[:, :width], both[:, width:]
             square = gate * gate
-            tanh = jnp.tanh(ROOT * gate * (1.0 + 0.044715 * square))
-            half = 0.5 * (1.0 + tanh)
-            active = gate * half
-            slant = half + 0.5 * gate * (1.0 - tanh * tanh) * (ROOT * (1.0 + 3.0 * 0.044715 * square))
+            tanh = jnp.tanh(gate * (ROOT + (0.044715 * ROOT) * square))
+            half_way = 0.5 + 0.5 * tanh
+            active = gate * half_way
+            slant = half_way + active * (1.0 - tanh) * (ROOT + (3.0 * 0.044715 * ROOT) * square)
             product = (active * up).astype(jnp.bfloat16)
-            act[c, :, rows] = active.astype(jnp.bfloat16)
-            slope[c, :, rows] = (slant * up).astype(jnp.bfloat16)
-            hidden[:, rows] = product
-            hidden_t[c, rows] = product.T
-
-        in_tiles(units, 128, tile)
-
-        def out_tile(first, width):
+            shape = (count, rows_of, width)
+            act[pl.ds(*group), :, units_here] = active.astype(jnp.bfloat16).reshape(shape)
+            slope[pl.ds(*group), :, units_here] = (slant * up).astype(jnp.bfloat16).reshape(shape)
+            hidden[: count * rows_of, units_here] = product
+            for c in range(count):
+                hidden_t[group[0] + c, units_here] = product[c * rows_of : (c + 1) * rows_of].T
+
+        in_tiles(end - begin, 128, tile, begin)
+
+    def forward_down(group):
+        count = group[1]
+
+        def tile(first, width):
             lanes = pl.ds(first, width)
-            parts[c, :, lanes] = dot_nn(hidden[...], w_down[:, lanes]).astype(jnp.bfloat16)
-
-        in_tiles(D, 256, out_tile)
-
-    def backward(c):
+            value = dot_nn(hidden[: count * rows_of], w_down[:, lanes]).astype(jnp.bfloat16)
+            parts[pl.ds(*group), :, lanes] = value.reshape(count, rows_of, width)
+
+        in_tiles(D, 256, tile)
+
+    def backward_units(group):
+        count = group[1]
+
         def tile(first, width):
-            rows = pl.ds(first, width)
-            grad = dot_nt(dy[c], w_down[rows])
-            up_grad = (grad * act[c, :, rows].astype(jnp.float32)).astype(jnp.bfloat16)
-            gate_grad = (grad * slope[c, :, rows].astype(jnp.float32)).astype(jnp.bfloat16)
-            grads[0, :, rows] = gate_grad
-            grads[1, :, rows] = up_grad
-            gate_t[c, rows] = gate_grad.T
-            up_t[c, rows] = up_grad.T
+            units_here = pl.ds(first, width)
+            grad = dot_nt(joined(dy, group), w_down[units_here])
+            up_grad = (grad * joined(act, group, slice(None), units_here).astype(jnp.float32)).astype(jnp.bfloat16)
+            gate_grad = (grad * joined(slope, group, slice(None), units_here).astype(jnp.float32)).astype(jnp.bfloat16)
+            grads[0, : count * rows_of, units_here] = gate_grad
+            grads[1, : count * rows_of, units_here] = up_grad
+            for c in range(count):
+                rows = slice(c * rows_of, (c + 1) * rows_of)
+                gate_t[group[0] + c, units_here] = gate_grad[rows].T
+                up_t[group[0] + c, units_here] = up_grad[rows].T
 
         in_tiles(units, 256, tile)
 
-        def out_tile(first, width):
+    def backward_in(group):
+        count = group[1]
+
+        def tile(first, width):
             lanes = pl.ds(first, width)
-            both = dot_nn(grads[0], w_gate[:, lanes]) + dot_nn(grads[1], w_up[:, lanes])
-            parts[c, :, lanes] = both.astype(jnp.bfloat16)
-
-        in_tiles(D, 256, out_tile)
-
-    order = list(range(n - 1, 0, -1)) + [0]
-    for i, k in enumerate(order):
-        forward(places[k])
+            both = dot_nn(grads[0, : count * rows_of], w_gate[:, lanes]) + dot_nn(
+                grads[1, : count * rows_of], w_up[:, lanes]
+            )
+            parts[pl.ds(*group), :, lanes] = both.astype(jnp.bfloat16).reshape(count, rows_of, width)
+
+        in_tiles(D, 256, tile)
+
+    far, near, here = (0, len(bent)), (len(bent), len(straight)), (n - 1, 1)
+    most = hidden.shape[0] // rows_of
+
+    def runs(group):
+        return [(first, min(most, group[0] + group[1] - first)) for first in range(group[0], sum(group), most)]
+
+    quarter = units // 512 * 128
+    for load in loads:
+        load.wait()
+    for run in runs(far):
+        forward_units(run, 0, units)
+        forward_down(run)
+    for k in bent:
         to_partner(0, k).start()
-        if i:
-            add_core(0, order[i - 1])
-    add_core(0, order[-1])
+    for i, run in enumerate(runs(near)):
+        forward_units(run, 0, 2 * quarter)
+        if i == 0:
+            for k in bent:
+                add_core(0, k)
+        forward_units(run, 2 * quarter, units)
+        forward_down(run)
+    for k in straight:
+        to_partner(0, k).start()
+    forward_units(here, 0, 2 * quarter)
+    for k in straight:
+        add_core(0, k)
+    for k in straight:
+        add_neighbours(0, k)
+    forward_units(here, 2 * quarter, units)
+    forward_down(here)
+    to_partner(0, 0).start()
+    add_core(0, 0)
     add_owners(0)
 
     grad_gain[...] = jnp.zeros_like(grad_gain)
@@ -720,7 +994,7 @@
 
     def finish(first, rows):
         span = pl.ds(first, rows)
-        here = pl.ds(pl.multiple_of(core * tokens + first, rows), rows)
+        spot = pl.ds(pl.multiple_of(core * tokens + first, rows), rows)
         y = total[span]
         ok = valid[span]
         rate = lax.rsqrt(jnp.mean(y * y, axis=-1, keepdims=True) + EPS)
@@ -732,114 +1006,149 @@
             grad_gain[...] += down[r : r + 8]
         scaled = upstream * scale
         inner = jnp.mean(scaled * unit, axis=-1, keepdims=True)
-        dy[chip, here] = (rate * (scaled - unit * inner)).astype(jnp.bfloat16)
+        dy[n - 1, spot] = (rate * (scaled - unit * inner)).astype(jnp.bfloat16)
 
     in_tiles(tokens, 32, finish)
 
-    pushes = [None] + [
-        remote(dy.at[chip, mine], dy.at[chip, mine], dy_send.at[k], dy_recv.at[k], peers[k])
-        for k in range(1, n)
-    ]
+    def dy_half(k, h):
+        return dy.at[place[k], pl.ds(pl.multiple_of(core * tokens + h * half, half), half)]
+
+    def dy_push(k, h):
+        return remote(dy_half(0, h), dy_half(k, h), dy_send.at[k, h], dy_recv.at[k, h], peers[k])
+
+    def dy_onward(k, h, step):
+        return remote(
+            dy_half(k, h), dy_half(k + step, h), dy_pass.at[k + step, h], dy_recv.at[k + step, h], peers[step]
+        )
+
     shares = [
-        remote(dy.at[sources[k], mine], dy.at[sources[k], mine], share_send.at[k], share_recv.at[k], partner)
+        remote(dy.at[place[k], mine], dy.at[place[k], mine], share_send.at[k], share_recv.at[k], partner)
         for k in range(n)
     ]
-    for push in pushes[1:]:
-        push.start()
+    ordered = [(k, i if k < wide else 1 - i) for i in range(2) for k in straight]
+    for k, h in ordered:
+        dy_push(k, h).start()
     shares[0].start()
     settle(0)
-    for i in range(n):
-        k = lay.back(i)
-        if i:
-            pushes[i].wait_recv()
-            shares[i].start()
-        shares[i].wait_recv()
-        backward(sources[i])
+    shares[0].wait_recv()
+    backward_units(here)
+    backward_in(here)
+    to_partner(1, 0).start()
+    onward = []
+    for k, h in ordered:
+        dy_push(k, h).wait_recv()
+        if k < wide and h == 0:
+            onward += [(k, h, b * wide) for b in range(1, lay.lo)]
+        elif k >= wide and h == 1:
+            onward += [(k, h, step) for step in range(1, wide)]
+        for go in onward:
+            if go[:2] == (k, h):
+                dy_onward(*go).start()
+    for k in straight:
+        shares[k].start()
+    add_core(1, 0)
+    for k in straight:
+        shares[k].wait_recv()
+    for i, run in enumerate(runs(near)):
+        backward_units(run)
+        if i == 0:
+            for k in bent:
+                for h in range(2):
+                    dy_push(k, h).wait_recv()
+                shares[k].start()
+        backward_in(run)
+    for k in straight:
         to_partner(1, k).start()
-        if i:
-            add_core(1, lay.back(i - 1))
-    add_core(1, lay.back(n - 1))
-
-    def weight_grad(left_ref, right, out):
+    for k in bent:
+        shares[k].wait_recv()
+    for i, run in enumerate(runs(far)):
+        backward_units(run)
+        if i == 0:
+            for k in straight:
+                add_core(1, k)
+        backward_in(run)
+    if not bent:
+        for k in straight:
+            add_core(1, k)
+    for k in bent:
+        to_partner(1, k).start()
+    for k in bent:
+        add_core(1, k)
+
+    def weight_grad(left_ref, right, i):
         def tile(first, width):
             lanes = pl.ds(first, width)
             value = dot_nn(left_ref[0], right[0, :, lanes])
             for c in range(1, n):
                 value = value + dot_nn(left_ref[c], right[c, :, lanes])
-            out[:, lanes] = value.astype(jnp.bfloat16)
+            value = value.astype(jnp.bfloat16)
+            for h in range(lay.hi):
+                grad_weights[h, i * padded : (i + 1) * padded, lanes] = value[h * padded : (h + 1) * padded]
 
         in_tiles(D, 256, tile)
 
-    weight_grad(hidden_t, dy, dw_down)
-    weight_grad(gate_t, mid, dw_gate)
-    weight_grad(up_t, mid, dw_up)
+    weight_grad(hidden_t, dy, 2)
+    for k in straight:
+        add_neighbours(1, k)
+    weight_grad(gate_t, mid, 0)
+    weight_grad(up_t, mid, 1)
     add_owners(1)
     grad_mid[...] = total[...]
     settle(1)
-    for k in range(n):
-        if k:
-            pushes[k].wait_send()
-        shares[k].wait_send()
-
-
-def feed_forward(lay, mid, w_gate, w_up, w_down, mixed, cotangent, valid, gain, collective_id):
+    for k, h in ordered:
+        dy_push(k, h).wait_send()
+    for go in onward:
+        dy_onward(*go).wait_send()
+    for share in shares:
+        share.wait_send()
+
+
+def feed_forward(lay, mid, weights, mixed, cotangent, valid, gain, collective_id):
     n = lay.chips
     tokens = mixed.shape[0]
-    units = w_gate.shape[0]
+    units = weights.shape[0] * weights.shape[1] // 3
+    most = min(n, max(1, 1920 // units))
     low, high = jnp.bfloat16, jnp.float32
     vmem = pl.BlockSpec(memory_space=pltpu.VMEM)
     dma = pltpu.SemaphoreType.DMA
-    dw = jax.ShapeDtypeStruct((units, D), low)
-    out_shape = (
-        jax.ShapeDtypeStruct((tokens, D), low),
-        jax.ShapeDtypeStruct((tokens, D), high),
-        jax.ShapeDtypeStruct((8, D), high),
-        dw,
-        dw,
-        dw,
-    )
-
-    def kernel(*refs):
-        ins, outs, scratch = refs[:8], refs[8:14], list(refs[14:])
-        gate_t, up_t = scratch.pop(0), scratch.pop(0)
-        feed_forward_kernel(
-            lay, *ins, outs[0], outs[1], gate_t, up_t, *outs[2:], *scratch[:11], None, *scratch[11:]
-        )
-
     return pl.pallas_call(
-        kernel,
-        out_shape=out_shape,
-        in_specs=[vmem] * 8,
-        out_specs=(vmem,) * 6,
+        partial(feed_forward_kernel, lay),
+        out_shape=(
+            jax.ShapeDtypeStruct((tokens, D), low),
+            jax.ShapeDtypeStruct((tokens, D), high),
+            jax.ShapeDtypeStruct((8, D), high),
+            jax.ShapeDtypeStruct(weights.shape, low),
+        ),
+        in_specs=[vmem, pl.BlockSpec(memory_space=pl.ANY)] + [vmem] * 4,
+        out_specs=(vmem,) * 4,
         scratch_shapes=[
+            pltpu.VMEM((units, D), low),
+            pltpu.VMEM((units, D), low),
+            pltpu.VMEM((units, D), low),
             pltpu.VMEM((n, units, 2 * tokens), low),
             pltpu.VMEM((n, units, 2 * tokens), low),
             pltpu.VMEM((n, 2 * tokens, units), low),
             pltpu.VMEM((n, 2 * tokens, units), low),
-            pltpu.VMEM((2 * tokens, units), low),
+            pltpu.VMEM((most * 2 * tokens, units), low),
             pltpu.VMEM((n, units, 2 * tokens), low),
-            pltpu.VMEM((2, 2 * tokens, units), low),
+            pltpu.VMEM((2, most * 2 * tokens, units), low),
             pltpu.VMEM((n, 2 * tokens, D), low),
             pltpu.VMEM((n, tokens, D), low),
             pltpu.VMEM((max(1, n - 1), tokens, D), low),
-            pltpu.VMEM((max(1, n - 1), tokens, D), low),
+            pltpu.VMEM((max(1, len(lay.bent())), tokens if lay.bent() else 16, D), low),
+            pltpu.VMEM((max(1, len(lay.straight())), tokens, D), low),
             pltpu.VMEM((tokens, D), high),
             pltpu.VMEM((n, 2 * tokens, D), low),
+            dma((3, lay.hi)),
         ]
-        + [dma((2, n))] * 4
-        + [dma((n,))] * 4,
+        + [dma((2, n))] * 2
+        + [dma((n,))] * 2
+        + [dma((2, n, 2))] * 4
+        + [dma((n, 2))] * 3,
         compiler_params=pltpu.CompilerParams(
             collective_id=collective_id, has_side_effects=True, vmem_limit_bytes=63 * 2**20
         ),
-    )(
-        mid.reshape(n, 2 * tokens, D), w_gate, w_up, w_down, mixed, cotangent, valid, gain
-    )
-
-
-def shifted(value, axis, steps):
-    count = lax.axis_size(axis)
-    leading, last = (max(0, -steps), min(count, count - steps))
-    return lax.ppermute(value, axis, [(source, source + steps) for source in range(leading, last)])
+    )(mid, weights, mixed, cotangent, valid, gain)
 
 
 def norm_scaled(v, gain):
@@ -887,23 +1196,31 @@
     qkv_rows, out_rows = w_qkv.shape[0], w_out.shape[0]
     cols = w_qkv.shape[1]
     used = qkv_rows + out_rows + 1
-    pack_rows = -(-used // 32) * 32
+    block = 16 * lay.dp
+    pack_rows = -(-used // block) * block
     gain_row = jnp.pad(gains, (0, cols - gains.shape[0]))[None]
     pack = jnp.concatenate(
         [w_qkv, w_out, gain_row, jnp.zeros((pack_rows - used, cols), jnp.float32)], axis=0
     ).astype(jnp.bfloat16)
-    attn_all, gate_rows, up_rows, low_rows = weights_in(
+    plane, ffn_rows, earlier_tokens = weights_in(
         lay,
-        pack.reshape(2, pack_rows // 2, cols),
+        reach,
+        tokens,
+        pack.reshape(lay.dp, pack_rows // lay.dp, cols),
         w_gate_up.reshape(lay.dp, 2 * per, cols),
         w_down.reshape(lay.dp, per, cols),
         5,
     )
-    w_gate, w_up, w_low = (
-        lax.all_gather(rows, "ctx", axis=0, tiled=True, axis_index_groups=lay.hi_groups)
-        for rows in (gate_rows, up_rows, low_rows)
-    )
-    attn_all = attn_all.reshape(lay.ctx, pack_rows, D)
+    ffn_all = lax.all_gather(ffn_rows, "ctx", axis=0, axis_index_groups=lay.hi_groups)
+    attn_all = gather_group(
+        lay,
+        plane,
+        (lay.hi, lay.lo, lay.dp, pack_rows // lay.dp, D),
+        lambda out, k, chip, core: out.at[
+            :, chip // lay.wide, lax.rem(chip, lay.wide) * 2 + core
+        ],
+        6,
+    ).reshape(lay.ctx, pack_rows, D)
     full_qkv = attn_all[:, :qkv_rows].reshape(lay.ctx * qkv_rows, D)
     full_out = attn_all[:, qkv_rows : qkv_rows + out_rows].reshape(lay.ctx * out_rows, D)
     gain_all = (
@@ -931,16 +1248,22 @@
         partial(head_inputs, angle=angle), projected, gain_query, gain_key
     )
     query_low = query.astype(jnp.bfloat16)
-    own_pair = jnp.concatenate(
-        [key_rot.astype(jnp.bfloat16), value_rows.astype(jnp.bfloat16)], axis=-1
-    )
-    earlier = []
-    for distance in range(reach, 0, -1):
-        earlier.append(shifted(own_pair, "ctx", distance))
-    key_pairs = jnp.concatenate(earlier + [own_pair], axis=1)
+    key_pos = offset - reach * local_len + jnp.arange((reach + 1) * local_len, dtype=jnp.int32)
+    earlier = earlier_tokens.transpose(1, 0, 2, 3).reshape(seq_count, reach * local_len, D)
+    earlier = norm_scaled(earlier.astype(jnp.float32), gain_in).astype(jnp.bfloat16)
+    earlier = contract(earlier, full_qkv[HEADS * HD :], (2,), (1,))
+    earlier_keys = rotate(
+        norm_scaled(earlier[..., :HD], gain_key), angles_of(key_pos[: reach * local_len])
+    )
+    key_pairs = jnp.concatenate(
+        [
+            jnp.concatenate([earlier_keys, earlier[..., HD:]], axis=-1).astype(jnp.bfloat16),
+            jnp.concatenate([key_rot, value_rows], axis=-1).astype(jnp.bfloat16),
+        ],
+        axis=1,
+    )
     keys_low = key_pairs[..., :HD]
     values_low = key_pairs[..., HD:]
-    key_pos = offset - reach * local_len + jnp.arange((reach + 1) * local_len, dtype=jnp.int32)
     key_grid = key_pos[None, None, :]
     query_grid = positions[None, :, None]
     allowed = (
@@ -971,13 +1294,17 @@
     normed_mid, pull_mid = jax.vjp(norm_scaled, mixed, gain_pre)
     mid_low = normed_mid.astype(jnp.bfloat16)
     token_count = seq_count * local_len
-    mid_all = gather_tokens(lay, mid_low.reshape(token_count, D), 1)
-    result, grad_mid, grad_gain_post, grad_w_gate, grad_w_up, grad_low = feed_forward(
+    mid_all = gather_group(
+        lay,
+        mid_low.reshape(2, token_count // 2, D),
+        (lay.chips, 2, 2, token_count // 2, D),
+        lambda out, k, chip, core: out.at[lay.position(k), core],
+        1,
+    ).reshape(lay.chips, 2 * token_count, D)
+    result, grad_mid, grad_gain_post, grad_ffn = feed_forward(
         lay,
         mid_all,
-        w_gate,
-        w_up,
-        w_low,
+        ffn_all,
         mixed.reshape(token_count, D),
         cotangent.reshape(token_count, D),
         valid.reshape(token_count, 1).astype(jnp.float32),
@@ -1013,11 +1340,10 @@
     )
     grad_pairs = jnp.concatenate([grad_keys, grad_values], axis=-1)
     own_grad = grad_pairs[:, reach * local_len :]
-    for distance in range(1, reach + 1):
-        piece = grad_pairs[:, (reach - distance) * local_len : (reach - distance + 1) * local_len]
-        own_grad = own_grad + shifted(piece.astype(jnp.bfloat16), "ctx", -distance).astype(
-            piece.dtype
-        )
+    pieces = grad_pairs[:, : reach * local_len].astype(jnp.bfloat16)
+    pieces = pieces.reshape(seq_count, reach, local_len, 2 * HD).transpose(1, 0, 2, 3)
+    later = later_sum(lay, reach, pieces, 11)
+    own_grad = own_grad + later
     grad_projected, grad_gain_query, grad_gain_key = pull_heads(
         (grad_query, own_grad[..., :HD], own_grad[..., HD:])
     )
@@ -1036,7 +1362,6 @@
             grad_gain_key,
         ]
     )
-    block = 16 * lay.dp
     sum_rows = -(-(qkv_rows + out_rows) // block) * block
     partial_sums = jnp.concatenate(
         [
@@ -1047,17 +1372,12 @@
         axis=1,
     ).reshape(lay.ctx, lay.dp, sum_rows // lay.dp, D)
     part_attn, gains_sum = scatter_attn(lay, partial_sums, grad_gain_all.reshape(-1, 128), 8)
+    owned = lax.psum_scatter(grad_ffn, "ctx", scatter_dimension=0, axis_index_groups=lay.hi_groups)
+    part_gate_up, part_down = exchange_out(lay, owned, per, 9)
     part_qkv = part_attn[:qkv_rows]
     part_out = part_attn[qkv_rows : qkv_rows + out_rows]
     place = (lax.axis_index("dp") * lay.ctx + lax.axis_index("ctx")) * gains.shape[0]
     part_gains = lax.dynamic_slice_in_dim(gains_sum.reshape(-1), place, gains.shape[0])
-    owned = [
-        lax.psum_scatter(
-            piece, "ctx", scatter_dimension=0, tiled=True, axis_index_groups=lay.hi_groups
-        )
-        for piece in (grad_low, grad_w_gate, grad_w_up)
-    ]
-    part_gate_up, part_down = exchange_out(lay, owned[1], owned[2], owned[0], per, 9)
     part_gate_up = part_gate_up.reshape(w_gate_up.shape)
     part_down = part_down.reshape(w_down.shape)
     return (result, grad_input, part_qkv, part_out, part_gate_up, part_down, part_gains)

time: 578 us -> 485 us (0.84)
  waiting for transfers between devices: 102 us -> 15.6 us
  starting transfers between devices: 23.8 us -> 0.29 us
  local copies, waits for them, and re-layouts: 43.3 us -> 49.5 us
  other arithmetic: 24 us -> 29.9 us
    ppermute x8 -> x0, waiting for transfers between devices: 57.7 us -> none  [shifted(): lax.ppermute(value, axis, [(source, source + steps) for source in range(l...]
    pallas_call x3 -> x5, Pallas kernels: 215 us -> 250 us  [the longest x1 105 us: feed_forward(): pl.pallas_call(partial(feed_forward_kernel, lay), out_shape=(jax.ShapeDty...]
    pallas_call x1, Pallas kernels: 102 us -> 72.1 us  [scatter_attn(): pl.pallas_call(partial(scatter_attn_kernel, lay, with_gains), out_shape=t...]
    all_gather x3 -> x1, waiting for transfers between devices: 43.8 us -> 15.5 us  [per_device(): lax.all_gather(ffn_rows, 'ctx', axis=0, axis_index_groups=lay.hi_groups)]
    ppermute x8 -> x0, starting transfers between devices: 23.6 us -> none  [shifted(): lax.ppermute(value, axis, [(source, source + steps) for source in range(l...]
    dot_general x6 -> x7, matrix products: 9.48 us -> 14.5 us  [contract(): lax.dot_general(left, right, ((dims_left, dims_right), ((), ())), preferr...]
    unnamed x174 -> x135, local copies, waits for them, and re-layouts: 25.8 us -> 23.6 us
  transfers between devices with their start and end apart: 14 -> 2, of which waited for: 7 -> 1; matrix products, arithmetic and copies ran while one was open for 10% -> 16% of each run, Pallas kernels for 25% -> 35%
where the time goes in v4:
time: 485 us; the launch traced here: 481 us
  Pallas kernels  351 us (72%)
  local copies, waits for them, and re-layouts  49.5 us (10%)
  other arithmetic  29.9 us (6%)
  matrix products  19.5 us (4%)
  waiting for transfers between devices  15.6 us (3%)
  between operations  15.4 us (3%)
    pallas_call x1, Pallas kernels, feed_forward(): pl.pallas_call(partial(feed_forward_kernel, lay), out_shape=(jax.ShapeDty...  105 us
    pallas_call x1, Pallas kernels, scatter_attn(): pl.pallas_call(partial(scatter_attn_kernel, lay, with_gains), out_shape=t...  72.1 us
    pallas_call x2, Pallas kernels, gather_group(): pl.pallas_call(partial(gather_group_kernel, lay, slot), out_shape=jax.Sha...  60 us
    pallas_call x1, Pallas kernels, weights_in(): pl.pallas_call(partial(weights_in_kernel, lay, reach), out_shape=(jax.Sha...  47.3 us
    pallas_call x1, Pallas kernels, later_sum(): pl.pallas_call(partial(later_kernel, lay, reach), out_shape=jax.ShapeDtyp...  37.7 us
    pallas_call x1, Pallas kernels, exchange_out(): pl.pallas_call(partial(exchange_out_kernel, lay), out_shape=(jax.ShapeDty...  29 us
    unnamed x135, local copies, waits for them, and re-layouts  23.6 us
    all_gather x1, waiting for transfers between devices, per_device(): lax.all_gather(ffn_rows, 'ctx', axis=0, axis_index_groups=lay.hi_groups)  15.5 us
  transfers between devices with their start and end apart: 2, of which 1 were waited for; matrix products, arithmetic and copies ran while one was open for 16% of the time, Pallas kernels for 35%

profile of v4, /device:TPU:9, one launch (start us, length us, event | category | flops | bytes accessed | tf_op | source)
XLA Modules:
  0.0 480.9 jit_solution(15309905845705226449)
XLA Ops:
  7.2 3.3 copy.145
  10.5 1.5 copy.146
  13.1 47.3 %shard_map.135 = (bf16[4,96,1152]{2,1,0:T(8,128)(2,1)}, bf16[672,1152]{1,0:T(8,128)(2,1)}, bf16[4,2,128,1152]{3,2,1,0:T(8,128)(2,1)}) custom-call(bf16[2,128,1152]{2,1,0:T(8,128)(2,1)} %tokens.1, bf16[4,96,288]{2,1,0:T(8,128)(2,1)} %bitcast.161, f32[4,432,288]{2,1,0:T(8,128)} %bitcast.140, f32[4,216,288]{2,1,0:T(8,128)} %bitcast.146), custom_call_target="tpu_custom_call" | custom-call | tf_op jit(solution)/shard_map/pallas_call | solution.py:360
  60.7 35.5 %shard_map.136 = bf16[4,2,4,96,1152]{4,3,2,1,0:T(8,128)(2,1)} custom-call(bf16[4,96,1152]{2,1,0:T(8,128)(2,1)} %get-tuple-element.19.own), custom_call_target="tpu_custom_call" | custom-call | tf_op jit(solution)/shard_map/pallas_call | solution.py:139
  97.1 4.1 slice.129
  102.9 3.3 fusion.31
  107.3 3.7 slice.146
  113.3 2.0 convert_bitcast_fusion
  115.3 2.4 copy.147
  117.9 2.2 fusion.1
  120.2 2.8 fusion.3
  123.0 2.8 fusion.23
  125.9 1.4 copy-done.17
  128.8 1.6 copy.153
  130.4 1.3 multiply_reduce_fusion.8
  131.8 1.6 multiply_cosine_fusion
  133.4 1.4 multiply_multiply_fusion
  143.9 24.6 %shard_map.137 = bf16[4,2,2,128,1152]{4,3,2,1,0:T(8,128)(2,1)} custom-call(bf16[2,128,1152]{2,1,0:T(8,128)(2,1)} %multiply_convert_fusion.own), custom_call_target="tpu_custom_call" | custom-call | tf_op jit(solution)/shard_map/pallas_call | solution.py:139
  170.4 15.5 %all-gather.3.cloned.1.call-done = bf16[2688,1152]{1,0:T(8,128)(2,1)} async-done(((bf16[672,1152]{1,0:T(8,128)(2,1)}), bf16[2688,1152]{1,0:T(8,128)(2,1)}) %all-gather.3.cloned.1.call-update) | async-done | bytes 6193168 | tf_op jit(solution)/shard_map/all_gather | solution.py:1214
  185.9 104.7 %shard_map.138 = (bf16[256,1152]{1,0:T(8,128)(2,1)}, f32[256,1152]{1,0:T(8,128)}, f32[8,1152]{1,0:T(8,128)}, bf16[4,672,1152]{2,1,0:T(8,128)(2,1)}) custom-call(bf16[4,512,1152]{2,1,0:T(8,128)(2,1)} %bitcast.139, bf16[4,672,1152]{2,1,0:T(8,128)(2,1)} %bitcast.145, f32[256,1152]{1,0:T(8,128)} %bitcast.131, bf16[256,1152]{1,0:T(8,128)(2,1)} %bitcast.156, ...), custom_call_target="tpu_custom_call" | custom-call | tf_op jit(solution)/shard_map/pallas_call | solution.py:1114
  296.9 1.7 convolution_convert_fusion
  298.6 2.2 copy.198
  300.8 1.9 fusion.4
  306.6 37.7 %shard_map.139 = f32[2,128,512]{2,1,0:T(8,128)} custom-call(bf16[4,2,128,512]{3,2,1,0:T(8,128)(2,1)} %bitcast.150), custom_call_target="tpu_custom_call" | custom-call | tf_op jit(solution)/shard_map/pallas_call | solution.py:456
  352.2 3.6 fusion.17
  358.0 3.1 pad_maximum_fusion
  361.1 72.1 %shard_map.140 = (f32[320,288]{1,0:T(8,128)}, f32[40,128]{1,0:T(8,128)}) custom-call(bf16[8,4,80,1152]{3,2,1,0:T(8,128)(2,1)} %bitcast.138, f32[40,128]{1,0:T(8,128)} %bitcast.168), custom_call_target="tpu_custom_call" | custom-call | tf_op jit(solution)/shard_map/pallas_call | solution.py:677
  434.2 1.7 slice.124
  438.0 1.3 fusion.20
  439.4 29.0 %shard_map.141 = (f32[4,432,288]{2,1,0:T(8,128)}, f32[4,216,288]{2,1,0:T(8,128)}) custom-call(bf16[672,1152]{1,0:T(8,128)(2,1)} %bitcast.159), custom_call_target="tpu_custom_call" | custom-call | tf_op jit(solution)/shard_map/pallas_call | solution.py:728
  468.4 3.2 copy.175
  471.6 1.4 copy.176
  (223 shorter events, 43.6 us)
Async XLA Ops:
  7.2 3.3 copy-start.30
  7.2 178.7 %all-gather.3.cloned.1.call-start = ((), (), s32[]{:S(2)}) async-start(), calls=%async_computation.2 | async-start | bytes 7741440 | tf_op jit(solution)/shard_map/all_gather | solution.py:1214
  10.5 1.7 copy-start.60
  60.5 378.9 %reduce-scatter.2.cloned.1.call-start = ((), (), s32[]{:S(2)}) async-start(), calls=%async_computation.1 | async-start | bytes 7741440 | tf_op jit(solution)/shard_map/reduce_scatter | solution.py:1375
  97.1 4.2 copy-start.11
  101.5 4.7 copy-start.51
  102.3 3.9 copy-start.36
  102.9 9.0 %copy-start.43 = (f32[256]{0:T(256)}, f32[256]{0:T(256)S(1)}, u32[]{:S(2)}) copy-start(f32[256]{0:T(256)S(1)} %get-tuple-element.93) | copy-start | bytes 3076
  102.9 8.6 %copy-start.57 = (f32[128]{0:T(128)}, f32[128]{0:T(128)S(1)}, u32[]{:S(2)}) copy-start(f32[128]{0:T(128)S(1)} %negate_power_fusion) | copy-start | bytes 1540
  102.9 3.3 copy-start.55
  106.2 5.6 %copy-start.18 = (f32[2,128,1536]{2,1,0:T(8,128)}, f32[2,128,1536]{2,1,0:T(8,128)S(1)}, u32[]{:S(2)}) copy-start(f32[2,128,1536]{2,1,0:T(8,128)S(1)} %fusion.31) | copy-start | bytes 4718596
  106.4 5.5 %copy-start.53 = (f32[2,128]{1,0:T(2,128)}, f32[2,128]{1,0:T(2,128)S(1)}, u32[]{:S(2)}) copy-start(f32[2,128]{1,0:T(2,128)S(1)} %multiply_reduce_fusion.11) | copy-start | bytes 3076
  107.3 29.0 %copy-start.4 = (f32[2,128,1024]{2,1,0:T(8,128)}, f32[2,128,1024]{2,1,0:T(8,128)S(1)}, u32[]{:S(2)}) copy-start(f32[2,128,1024]{2,1,0:T(8,128)S(1)} %slice.142) | copy-start | bytes 3145732
  115.3 2.5 copy-start.32
  117.8 2.4 copy-start.37
  128.8 4.6 copy-start.44
  135.8 2.2 copy-start.14
  137.9 2.4 copy-start.12
  139.1 2.2 copy-start.22
  142.8 25.7 %copy-start.2 = (f32[2,128,1152]{2,1,0:T(8,128)}, f32[2,128,1152]{2,1,0:T(8,128)S(1)}, u32[]{:S(2)}) copy-start(f32[2,128,1152]{2,1,0:T(8,128)S(1)} %get-tuple-element.77) | copy-start | bytes 3538948
  143.9 24.6 %copy-start.42 = (f32[1152]{0:T(1024)S(1)}, f32[1152]{0:T(1024)}, u32[]{:S(2)}) copy-start(f32[1152]{0:T(1024)} %get-tuple-element.88) | copy-start | bytes 13828
  294.9 2.0 copy-start.13
  296.9 3.9 copy-start.1
  348.6 2.4 copy-start.54
  348.6 3.5 copy-start.38
  348.6 3.5 copy-start.56
  349.7 2.4 copy-start.25
  352.2 3.7 copy-start.21
  352.2 3.7 copy-start.23
  361.1 76.9 %copy-start.52 = (f32[2,128]{1,0:T(2,128)S(1)}, f32[2,128]{1,0:T(2,128)}, u32[]{:S(2)}) copy-start(f32[2,128]{1,0:T(2,128)} %copy-done.51) | copy-start | bytes 3076
  433.2 4.9 %copy-start.7 = (f32[2,128,1152]{2,1,0:T(8,128)S(1)}, f32[2,128,1152]{2,1,0:T(8,128)}, u32[]{:S(2)}) copy-start(f32[2,128,1152]{2,1,0:T(8,128)} %copy-done.6) | copy-start | bytes 3538948
  468.4 3.3 copy-start.24
  (31 other events, 34.6 us)
Sparse Core Ops, SparseCore 0:
  60.6 125.2 all-gather.2
  290.8 132.5 reduce-scatter.1

commit v5 on v4

--- a/solution.py
+++ b/solution.py
@@ -154,7 +154,7 @@
 
 def weights_in_kernel(
     lay, reach, tokens, pack, pairs, lows, attn_out, ffn_out, earlier_out,
-    hops_land, attn_land, own, stack, land, lanes, keep_sem, token_sem, hop_send, hop_recv, low_send, low_recv, attn_send, attn_recv, send, recv, chain_send, chain_recv,
+    hops_land, attn_land, own, stack, land, lanes, keep_sem, hop_send, hop_recv, low_send, low_recv, attn_send, attn_recv, send, recv, chain_send, chain_recv,
 ):
     n, hi, lo = lay.dp, lay.hi, lay.lo
     dp = lax.axis_index("dp")
@@ -253,55 +253,66 @@
             def _():
                 chain(own, high, side, step).wait_send()
 
-    def hop(h):
-        return remote(hops_land.at[h], hops_land.at[h + 1], hop_send.at[h], hop_recv.at[h], right)
+    parts = 2
+    span = tokens.shape[0] // parts
+
+    def part_of(ref, part):
+        return ref.at[pl.ds(part * span, span)]
+
+    def hop(h, part):
+        source = tokens if h == 0 else hops_land.at[h]
+        return remote(
+            part_of(source, part), part_of(hops_land.at[h + 1], part), hop_send.at[h, part], hop_recv.at[h, part], right
+        )
 
     def wanted(h, source, target):
         distance = h * lo + target - source
         return (distance >= 1) & (distance <= reach) & (high >= h)
 
-    def aside(h, source, target, device):
+    def aside(h, source, target, device, part):
+        block = tokens if h == 0 else hops_land.at[h]
         return remote(
-            hops_land.at[h], earlier_out.at[reach - (h * lo + target - source)], low_send.at[h, target],
-            low_recv.at[h, source], device,
+            part_of(block, part), part_of(earlier_out.at[reach - (h * lo + target - source)], part),
+            low_send.at[h, target, part], low_recv.at[h, source, part], device,
         )
 
-    def pass_tokens(h):
+    def pass_tokens(h, part):
         if h:
             @pl.when(high >= h)
             def _():
-                hop(h - 1).wait_recv()
+                hop(h - 1, part).wait_recv()
         if h < hops:
             @pl.when((high >= h) & has_right)
             def _():
-                hop(h).start()
+                hop(h, part).start()
         for other in range(lo):
             if lo > 1:
                 @pl.when((low != other) & wanted(h, low, other))
                 def _():
-                    aside(h, low, other, low_peers[other]).start()
+                    aside(h, low, other, low_peers[other], part).start()
         if h and h * lo <= reach:
             @pl.when(high >= h)
             def _():
-                earlier_out[reach - h * lo] = hops_land[h]
-
-    def finish_tokens(h):
+                block = pl.ds(part * span, span)
+                earlier_out[reach - h * lo, block] = hops_land[h, block]
+
+    def finish_tokens(h, part):
         if h < hops:
             @pl.when((high >= h) & has_right)
             def _():
-                hop(h).wait_send()
+                hop(h, part).wait_send()
         for other in range(lo):
             if lo > 1:
                 @pl.when((low != other) & wanted(h, other, low))
                 def _():
-                    aside(h, other, low, low_peers[other]).wait_recv()
+                    aside(h, other, low, low_peers[other], part).wait_recv()
 
                 @pl.when((low != other) & wanted(h, low, other))
                 def _():
-                    aside(h, low, other, low_peers[other]).wait_send()
-
-    take = pltpu.make_async_copy(tokens, hops_land.at[0], token_sem)
-    take.start()
+                    aside(h, low, other, low_peers[other], part).wait_send()
+
+    for part in range(parts):
+        pass_tokens(0, part)
     for d in range(1, reach + 1):
         @pl.when(ctx < d)
         def _():
@@ -315,15 +326,18 @@
     keep = pltpu.make_async_copy(own, attn_out.at[high], keep_sem)
     keep.start()
     pass_on(0)
-    take.wait()
-    pass_tokens(0)
-    for k in order[1:]:
-        feed_forward_rows(k)
+    events = [partial(feed_forward_rows, order[1])]
     for step in range(1, max(hi, hops + 1)):
+        if step <= hops:
+            events += [partial(pass_tokens, step, part) for part in range(parts)]
+        if step == 1:
+            events.insert(2, partial(feed_forward_rows, order[2]))
         if step < hi:
-            pass_on(step)
-        if step <= hops:
-            pass_tokens(step)
+            events.append(partial(pass_on, step))
+        if step == 1:
+            events += [partial(feed_forward_rows, k) for k in order[3:]]
+    for event in events:
+        event()
     for push in pushes:
         push.wait_recv()
     for q in range(n):
@@ -333,7 +347,8 @@
     for step in range(hi - 1):
         finish(step)
     for h in range(hops + 1):
-        finish_tokens(h)
+        for part in range(parts):
+            finish_tokens(h, part)
     for push in attn_pushes + pushes:
         push.wait_send()
 
@@ -353,9 +368,8 @@
         pltpu.VMEM((n, 3, padded, cols), jnp.bfloat16),
         pltpu.VMEM((len(lane_tiles(cols)), 2 * per, 128), jnp.float32),
         dma,
-        dma,
     ]
-    for shape in ((hops + 1,), (hops + 1, lay.lo), (n,), (n,), (2, lay.hi)):
+    for shape in ((hops + 1, 2), (hops + 1, lay.lo, 2), (n,), (n,), (2, lay.hi)):
         scratch += [dma(shape), dma(shape)]
     return pl.pallas_call(
         partial(weights_in_kernel, lay, reach),
@@ -475,63 +489,47 @@
     return index + bit * (1 - 2 * lax.rem(index // bit, 2))
 
 
-def scatter_attn_kernel(lay, with_gains, *refs):
-    refs = list(refs)
-    parts = refs.pop(0)
-    gains = refs.pop(0) if with_gains else None
-    out = refs.pop(0)
-    gains_out = refs.pop(0) if with_gains else None
-    core_land, wide_sum, wide_land, keep, low_sum, low_land, hi_sum, hi_land, last, last_land = refs[:10]
-    (core_send, core_recv, wide_send, wide_recv, low_send, low_recv, hi_send, hi_recv,
-     last_send, last_recv) = refs[10:20]
-    if with_gains:
-        gains_sum, gains_land, gains_send, gains_recv = refs[20:]
+def sum_group_kernel(lay, parts, gains, out, gains_out, core_land, wide_sum, wide_land, keep, low_sum, low_land,
+                     gains_sum, gains_land, core_send, core_recv, wide_send, wide_recv, low_send, low_recv,
+                     gains_send, gains_recv):
     dp = lax.axis_index("dp")
     ctx = lax.axis_index("ctx")
     hi, lo, wide, n = lay.hi, lay.lo, lay.wide, lay.dp
     high, low = ctx // lo, lax.rem(ctx, lo)
     across, core = dp // 2, lax.rem(dp, 2)
-    cols = out.shape[1]
-    rows = parts.shape[2]
     partner = (across * 2 + 1 - core, ctx)
     low_peers = [(dp, high * lo + lax.rem(low + k, lo)) for k in range(1, lo)]
     wide_peers = [(lax.rem(across + k, wide) * 2 + core, ctx) for k in range(1, wide)]
-    hi_peers = [(dp, lax.rem(high + k, hi) * lo + low) for k in range(1, hi)]
-    last_peers = [(lax.rem(dp + k, n), ctx) for k in range(1, n)]
-    steps = [1 << i for i in range((n - 1).bit_length())]
-    gain_peers = [(flip(dp, bit), ctx) for bit in steps]
+    gain_peers = [(flip(dp, 1 << i), ctx) for i in range((n - 1).bit_length())]
     gain_peers += [(dp, flip(ctx, 1 << i)) for i in range((lay.ctx - 1).bit_length())]
-    greet(
-        low_peers + hi_peers + last_peers + (gain_peers if with_gains else [])
-    )
-
-    order = [(k, a) for k in list(range(1, hi)) + [0] for a in list(range(1, lo)) + [0]]
-
-    def block(k, a):
-        return lax.rem(high + k, hi) * lo + lax.rem(low + a, lo)
-
-    def slot(k, a):
-        return k * lo + a
+    greet(low_peers + wide_peers + [partner] + gain_peers)
+
+    def block(h, a):
+        return h * lo + lax.rem(low + a, lo)
+
+    def slot(h, a):
+        return h * lo + a
 
     sends = []
-    core_copies = {}
-    for k, a in order:
-        for b in list(range(1, wide)) + [0]:
-            there = lax.rem(across + b, wide)
-            copy = remote(
-                parts.at[block(k, a), there * 2 + 1 - core],
-                core_land.at[slot(k, a), b],
-                core_send.at[slot(k, a), b],
-                core_recv.at[slot(k, a), b],
-                partner,
-            )
-            copy.start()
-            core_copies[k, a, b] = copy
-            sends.append(copy)
-    gain_copies = []
+    core_copies, wide_copies, low_copies, gain_copies = {}, {}, {}, []
+    offsets = list(range(1, lo)) + [0]
+    for h in range(hi):
+        for a in offsets:
+            for b in list(range(1, wide)) + [0]:
+                there = lax.rem(across + b, wide)
+                copy = remote(
+                    parts.at[block(h, a), there * 2 + 1 - core],
+                    core_land.at[slot(h, a), b],
+                    core_send.at[slot(h, a), b],
+                    core_recv.at[slot(h, a), b],
+                    partner,
+                )
+                copy.start()
+                core_copies[h, a, b] = copy
+                sends.append(copy)
 
     def gains_step(i):
-        if not with_gains or i > len(gain_peers):
+        if i > len(gain_peers):
             return
         if i == 0:
             gains_sum[0] = gains[...]
@@ -548,14 +546,12 @@
         else:
             gains_out[...] = gains_sum[i]
 
-    wide_copies, low_copies, hi_copies = {}, {}, {}
-
-    def sum_cores(k, a):
-        s = slot(k, a)
+    def sum_cores(h, a):
+        s = slot(h, a)
         for b in list(range(1, wide)) + [0]:
             there = lax.rem(across + b, wide)
-            core_copies[k, a, b].wait_recv()
-            total = parts[block(k, a), there * 2 + core].astype(jnp.float32) + core_land[
+            core_copies[h, a, b].wait_recv()
+            total = parts[block(h, a), there * 2 + core].astype(jnp.float32) + core_land[
                 s, b
             ].astype(jnp.float32)
             if b:
@@ -565,92 +561,59 @@
                     wide_recv.at[s, b - 1], wide_peers[b - 1],
                 )
                 copy.start()
-                wide_copies[k, a, b] = copy
+                wide_copies[h, a, b] = copy
                 sends.append(copy)
             else:
                 keep[s] = total
 
-    def sum_wide(k, a):
-        s = slot(k, a)
+    def sum_wide(h, a):
+        s = slot(h, a)
         total = keep[s]
         for b in range(1, wide):
-            wide_copies[k, a, b].wait_recv()
+            wide_copies[h, a, b].wait_recv()
             total = total + wide_land[s, b - 1].astype(jnp.float32)
         if a:
-            low_sum[k, a - 1] = total.astype(jnp.bfloat16)
+            low_sum[h, a - 1] = total.astype(jnp.bfloat16)
             copy = remote(
-                low_sum.at[k, a - 1], low_land.at[k, a - 1], low_send.at[k, a - 1],
-                low_recv.at[k, a - 1], low_peers[a - 1],
+                low_sum.at[h, a - 1], low_land.at[h, a - 1], low_send.at[h, a - 1],
+                low_recv.at[h, a - 1], low_peers[a - 1],
             )
             copy.start()
-            low_copies[k, a] = copy
+            low_copies[h, a] = copy
             sends.append(copy)
         else:
             keep[s] = total
 
-    def sum_low(k):
-        total = keep[slot(k, 0)]
+    def sum_low(h):
+        total = keep[slot(h, 0)]
         for a in range(1, lo):
-            low_copies[k, a].wait_recv()
-            total = total + low_land[k, a - 1].astype(jnp.float32)
-        if k:
-            hi_sum[k - 1] = total.astype(jnp.bfloat16)
-            copy = remote(
-                hi_sum.at[k - 1], hi_land.at[k - 1], hi_send.at[k - 1], hi_recv.at[k - 1], hi_peers[k - 1]
-            )
-            copy.start()
-            hi_copies[k] = copy
-            sends.append(copy)
-        else:
-            keep[slot(0, 0)] = total
+            low_copies[h, a].wait_recv()
+            total = total + low_land[h, a - 1].astype(jnp.float32)
+        out[h] = total.astype(jnp.bfloat16)
 
     gains_step(0)
-    ks = list(range(1, hi)) + [0]
-    offsets = list(range(1, lo)) + [0]
     for i in range(hi + 2):
         if i < hi:
             for a in offsets:
-                sum_cores(ks[i], a)
+                sum_cores(i, a)
         gains_step(i + 1)
         if 1 <= i <= hi:
             for a in offsets:
-                sum_wide(ks[i - 1], a)
+                sum_wide(i - 1, a)
         if 2 <= i:
-            sum_low(ks[i - 2])
+            sum_low(i - 2)
     for i in range(hi + 3, len(gain_peers) + 1):
         gains_step(i)
-    total = keep[slot(0, 0)]
-    for k in range(1, hi):
-        hi_copies[k].wait_recv()
-        total = total + hi_land[k - 1].astype(jnp.float32)
-    keep[slot(0, 0)] = total
-    for q in range(n):
-        last[q] = keep[slot(0, 0), :, q * cols : (q + 1) * cols].astype(jnp.bfloat16)
-    last_copies = []
-    for k in range(1, n):
-        copy = remote(
-            last.at[lax.rem(dp + k, n)], last_land.at[dp], last_send.at[k], last_recv.at[k], last_peers[k - 1]
-        )
-        copy.start()
-        last_copies.append(copy)
-        sends.append(copy)
-    last_land[dp] = last[dp]
-    for copy in last_copies:
-        copy.wait_recv()
-    for q in range(n):
-        out[q * rows : (q + 1) * rows] = last_land[q].astype(jnp.float32)
     for copy in sends:
         copy.wait_send()
 
 
-def scatter_attn(lay, parts, gains, collective_id):
+def sum_group(lay, parts, gains, collective_id):
     rows = parts.shape[2]
-    cols = D // lay.dp
-    with_gains = gains is not None
-    lows, wides, his = max(1, lay.lo - 1), max(1, lay.wide - 1), max(1, lay.hi - 1)
+    lows, wides = max(1, lay.lo - 1), max(1, lay.wide - 1)
     vmem = pl.BlockSpec(memory_space=pltpu.VMEM)
     dma = pltpu.SemaphoreType.DMA
-    out_shape = [jax.ShapeDtypeStruct((lay.dp * rows, cols), jnp.float32)]
+    count = (lay.dp - 1).bit_length() + (lay.ctx - 1).bit_length()
     scratch = [
         pltpu.VMEM((lay.ctx, lay.wide, rows, D), jnp.bfloat16),
         pltpu.VMEM((lay.ctx, wides, rows, D), jnp.bfloat16),
@@ -658,42 +621,45 @@
         pltpu.VMEM((lay.ctx, rows, D), jnp.float32),
         pltpu.VMEM((lay.hi, lows, rows, D), jnp.bfloat16),
         pltpu.VMEM((lay.hi, lows, rows, D), jnp.bfloat16),
-        pltpu.VMEM((his, rows, D), jnp.bfloat16),
-        pltpu.VMEM((his, rows, D), jnp.bfloat16),
-        pltpu.VMEM((lay.dp, rows, cols), jnp.bfloat16),
-        pltpu.VMEM((lay.dp, rows, cols), jnp.bfloat16),
+        pltpu.VMEM((count + 1,) + gains.shape, jnp.float32),
+        pltpu.VMEM((count,) + gains.shape, jnp.float32),
     ]
-    for shape in ((lay.ctx, lay.wide), (lay.ctx, wides), (lay.hi, lows), (his,), (lay.dp,)):
+    for shape in ((lay.ctx, lay.wide), (lay.ctx, wides), (lay.hi, lows), (count,)):
         scratch += [dma(shape), dma(shape)]
-    if with_gains:
-        count = (lay.dp - 1).bit_length() + (lay.ctx - 1).bit_length()
-        out_shape.append(jax.ShapeDtypeStruct(gains.shape, jnp.float32))
-        scratch += [
-            pltpu.VMEM((count + 1,) + gains.shape, jnp.float32),
-            pltpu.VMEM((count,) + gains.shape, jnp.float32),
-            dma((count,)),
-            dma((count,)),
-        ]
     return pl.pallas_call(
-        partial(scatter_attn_kernel, lay, with_gains),
-        out_shape=tuple(out_shape),
-        in_specs=[vmem] * (2 if with_gains else 1),
-        out_specs=(vmem,) * len(out_shape),
+        partial(sum_group_kernel, lay),
+        out_shape=(
+            jax.ShapeDtypeStruct((lay.hi, rows, D), jnp.bfloat16),
+            jax.ShapeDtypeStruct(gains.shape, jnp.float32),
+        ),
+        in_specs=[vmem] * 2,
+        out_specs=(vmem,) * 2,
         scratch_shapes=scratch,
         compiler_params=pltpu.CompilerParams(
             collective_id=collective_id, has_side_effects=True, vmem_limit_bytes=VMEM_LIMIT
         ),
-    )(*([parts, gains] if with_gains else [parts]))
-
-
-def exchange_out_kernel(lay, rows, pairs_out, lows_out, stack, land, lanes, send, recv):
-    n = lay.dp
+    )(parts, gains)
+
+
+def grads_out_kernel(lay, rows, attn, pairs_out, lows_out, attn_out, stack, land, lanes, hi_land, last, last_land,
+                     send, recv, hi_send, hi_recv, last_send, last_recv):
+    n, hi, lo = lay.dp, lay.hi, lay.lo
     dp = lax.axis_index("dp")
     ctx = lax.axis_index("ctx")
+    high, low = ctx // lo, lax.rem(ctx, lo)
     cols = lows_out.shape[2]
     per = lows_out.shape[1]
     padded = rows.shape[0] // 3
-    greet([(lax.rem(dp + k, n), ctx) for k in range(1, n)])
+    attn_rows = attn.shape[1]
+    hi_peers = [(dp, lax.rem(high + k, hi) * lo + low) for k in range(1, hi)]
+    greet([(lax.rem(dp + k, n), ctx) for k in range(1, n)] + hi_peers)
+    hi_pushes = []
+    for k in range(1, hi):
+        push = remote(
+            attn.at[lax.rem(high + k, hi)], hi_land.at[k - 1], hi_send.at[k], hi_recv.at[k], hi_peers[k - 1]
+        )
+        push.start()
+        hi_pushes.append(push)
     for q in range(n):
         for i in range(3):
             stack[q, i] = rows[i * padded : (i + 1) * padded, q * cols : (q + 1) * cols]
@@ -704,9 +670,21 @@
         push.start()
         pushes.append(push)
     land[dp] = stack[dp]
-    for push in pushes:
+    total = attn[high].astype(jnp.float32)
+    for k, push in enumerate(hi_pushes):
         push.wait_recv()
+        total = total + hi_land[k].astype(jnp.float32)
     for q in range(n):
+        last[q] = total[:, q * cols : (q + 1) * cols].astype(jnp.bfloat16)
+    last_pushes = []
+    for k in range(1, n):
+        target = lax.rem(dp + k, n)
+        push = remote(last.at[target], last_land.at[dp], last_send.at[k], last_recv.at[k], (target, ctx))
+        push.start()
+        last_pushes.append(push)
+    last_land[dp] = last[dp]
+
+    def place(q):
         for j, (first, width) in enumerate(lane_tiles(cols)):
             for i in range(2):
                 piece = land[q, i, :per, first : first + width].astype(jnp.float32)
@@ -717,33 +695,49 @@
                 lanes[j, pl.ds(i, per, stride=2), :] = piece
             pairs_out[q, :, first : first + width] = lanes[j, :, :width]
         lows_out[q] = land[q, 2, :per].astype(jnp.float32)
+
     for push in pushes:
+        push.wait_recv()
+    for q in range(n):
+        place(q)
+    for push in last_pushes:
+        push.wait_recv()
+    for q in range(n):
+        attn_out[q * attn_rows : (q + 1) * attn_rows] = last_land[q].astype(jnp.float32)
+    for push in hi_pushes + pushes + last_pushes:
         push.wait_send()
 
 
-def exchange_out(lay, rows, per, collective_id):
+def grads_out(lay, rows, attn, per, collective_id):
     padded = rows.shape[0] // 3
     n, cols = lay.dp, rows.shape[1] // lay.dp
+    attn_rows = attn.shape[1]
     vmem = pl.BlockSpec(memory_space=pltpu.VMEM)
+    dma = pltpu.SemaphoreType.DMA
     return pl.pallas_call(
-        partial(exchange_out_kernel, lay),
+        partial(grads_out_kernel, lay),
         out_shape=(
             jax.ShapeDtypeStruct((n, 2 * per, cols), jnp.float32),
             jax.ShapeDtypeStruct((n, per, cols), jnp.float32),
+            jax.ShapeDtypeStruct((n * attn_rows, cols), jnp.float32),
         ),
-        in_specs=[vmem],
-        out_specs=(vmem,) * 2,
+        in_specs=[vmem] * 2,
+        out_specs=(vmem,) * 3,
         scratch_shapes=[
             pltpu.VMEM((n, 3, padded, cols), jnp.bfloat16),
             pltpu.VMEM((n, 3, padded, cols), jnp.bfloat16),
             pltpu.VMEM((len(lane_tiles(cols)), 2 * per, 128), jnp.float32),
-            pltpu.SemaphoreType.DMA((n,)),
-            pltpu.SemaphoreType.DMA((n,)),
-        ],
+            pltpu.VMEM((max(1, lay.hi - 1), attn_rows, D), jnp.bfloat16),
+            pltpu.VMEM((n, attn_rows, cols), jnp.bfloat16),
+            pltpu.VMEM((n, attn_rows, cols), jnp.bfloat16),
+        ]
+        + [dma((n,))] * 2
+        + [dma((lay.hi,))] * 2
+        + [dma((n,))] * 2,
         compiler_params=pltpu.CompilerParams(
             collective_id=collective_id, has_side_effects=True, vmem_limit_bytes=VMEM_LIMIT
         ),
-    )(rows)
+    )(rows, attn)
 
 
 def in_tiles(total, size, body, begin=0):
@@ -1371,9 +1365,9 @@
         ],
         axis=1,
     ).reshape(lay.ctx, lay.dp, sum_rows // lay.dp, D)
-    part_attn, gains_sum = scatter_attn(lay, partial_sums, grad_gain_all.reshape(-1, 128), 8)
+    plane_attn, gains_sum = sum_group(lay, partial_sums, grad_gain_all.reshape(-1, 128), 8)
     owned = lax.psum_scatter(grad_ffn, "ctx", scatter_dimension=0, axis_index_groups=lay.hi_groups)
-    part_gate_up, part_down = exchange_out(lay, owned, per, 9)
+    part_gate_up, part_down, part_attn = grads_out(lay, owned, plane_attn, per, 9)
     part_qkv = part_attn[:qkv_rows]
     part_out = part_attn[qkv_rows : qkv_rows + out_rows]
     place = (lax.axis_index("dp") * lay.ctx + lax.axis_index("ctx")) * gains.shape[0]

time: 485 us -> 463 us (0.955)
  Pallas kernels: 351 us -> 334 us
  waiting for transfers between devices: 15.6 us -> 8.84 us
    pallas_call x2, Pallas kernels: 101 us -> 89.9 us  [the longest x1 57.3 us: sum_group(): pl.pallas_call(partial(sum_group_kernel, lay), out_shape=(jax.ShapeDtypeS...]
    all_gather x1, waiting for transfers between devices: 15.5 us -> 8.81 us  [per_device(): lax.all_gather(ffn_rows, 'ctx', axis=0, axis_index_groups=lay.hi_groups)]
    pallas_call x1, Pallas kernels: 47.3 us -> 41.6 us  [weights_in(): pl.pallas_call(partial(weights_in_kernel, lay, reach), out_shape=(jax.Sha...]
    unnamed x135 -> x133, local copies, waits for them, and re-layouts: 23.6 us -> 24.2 us
  transfers between devices with their start and end apart: 2 -> 2, of which waited for: 1 -> 1; matrix products, arithmetic and copies ran while one was open for 16% -> 15% of each run, Pallas kernels for 35% -> 34%
where the time goes in v5:
time: 463 us; the launch traced here: 457 us
  Pallas kernels  334 us (72%)
  local copies, waits for them, and re-layouts  48.8 us (11%)
  other arithmetic  29.8 us (6%)
  matrix products  19.4 us (4%)
  between operations  15.6 us (3%)
  waiting for transfers between devices  8.84 us (2%)
    pallas_call x1, Pallas kernels, feed_forward(): pl.pallas_call(partial(feed_forward_kernel, lay), out_shape=(jax.ShapeDty...  105 us
    pallas_call x2, Pallas kernels, gather_group(): pl.pallas_call(partial(gather_group_kernel, lay, slot), out_shape=jax.Sha...  60.2 us
    pallas_call x1, Pallas kernels, sum_group(): pl.pallas_call(partial(sum_group_kernel, lay), out_shape=(jax.ShapeDtypeS...  57.3 us
    pallas_call x1, Pallas kernels, weights_in(): pl.pallas_call(partial(weights_in_kernel, lay, reach), out_shape=(jax.Sha...  41.6 us
    pallas_call x1, Pallas kernels, later_sum(): pl.pallas_call(partial(later_kernel, lay, reach), out_shape=jax.ShapeDtyp...  37.8 us
    pallas_call x1, Pallas kernels, grads_out(): pl.pallas_call(partial(grads_out_kernel, lay), out_shape=(jax.ShapeDtypeS...  32.6 us
    unnamed x133, local copies, waits for them, and re-layouts  24.2 us
    dot_general x7, matrix products, contract(): lax.dot_general(left, right, ((dims_left, dims_right), ((), ())), preferr...  14.4 us
  transfers between devices with their start and end apart: 2, of which 1 were waited for; matrix products, arithmetic and copies ran while one was open for 15% of the time, Pallas kernels for 34%

profile of v5, /device:TPU:9, one launch (start us, length us, event | category | flops | bytes accessed | tf_op | source)
XLA Modules:
  0.0 457.3 jit_solution(5480034482546446286)
XLA Ops:
  7.2 3.3 copy.145
  10.5 1.5 copy.146
  13.1 41.6 %shard_map.135 = (bf16[4,96,1152]{2,1,0:T(8,128)(2,1)}, bf16[672,1152]{1,0:T(8,128)(2,1)}, bf16[4,2,128,1152]{3,2,1,0:T(8,128)(2,1)}) custom-call(bf16[2,128,1152]{2,1,0:T(8,128)(2,1)} %tokens.1, bf16[4,96,288]{2,1,0:T(8,128)(2,1)} %bitcast.161, f32[4,432,288]{2,1,0:T(8,128)} %bitcast.140, f32[4,216,288]{2,1,0:T(8,128)} %bitcast.146), custom_call_target="tpu_custom_call" | custom-call | tf_op jit(solution)/shard_map/pallas_call | solution.py:374
  55.3 35.5 %shard_map.136 = bf16[4,2,4,96,1152]{4,3,2,1,0:T(8,128)(2,1)} custom-call(bf16[4,96,1152]{2,1,0:T(8,128)(2,1)} %get-tuple-element.20.own), custom_call_target="tpu_custom_call" | custom-call | tf_op jit(solution)/shard_map/pallas_call | solution.py:139
  91.7 4.2 slice.129
  97.5 3.3 fusion.31
  101.9 3.7 slice.146
  107.9 2.0 convert_bitcast_fusion
  110.0 2.5 copy.147
  112.6 2.2 fusion.1
  114.8 2.9 fusion.3
  117.6 2.8 fusion.23
  120.5 1.3 copy-done.17
  123.4 1.6 copy.153
  125.0 1.3 multiply_reduce_fusion.8
  126.4 1.6 multiply_cosine_fusion
  128.0 1.4 multiply_multiply_fusion
  138.6 24.8 %shard_map.137 = bf16[4,2,2,128,1152]{4,3,2,1,0:T(8,128)(2,1)} custom-call(bf16[2,128,1152]{2,1,0:T(8,128)(2,1)} %multiply_convert_fusion.own), custom_call_target="tpu_custom_call" | custom-call | tf_op jit(solution)/shard_map/pallas_call | solution.py:139
  165.0 8.8 %all-gather.3.cloned.1.call-done = bf16[2688,1152]{1,0:T(8,128)(2,1)} async-done(((bf16[672,1152]{1,0:T(8,128)(2,1)}), bf16[2688,1152]{1,0:T(8,128)(2,1)}) %all-gather.3.cloned.1.call-update) | async-done | bytes 6193168 | tf_op jit(solution)/shard_map/all_gather | solution.py:1208
  173.8 104.7 %shard_map.138 = (bf16[256,1152]{1,0:T(8,128)(2,1)}, f32[256,1152]{1,0:T(8,128)}, f32[8,1152]{1,0:T(8,128)}, bf16[4,672,1152]{2,1,0:T(8,128)(2,1)}) custom-call(bf16[4,512,1152]{2,1,0:T(8,128)(2,1)} %bitcast.139, bf16[4,672,1152]{2,1,0:T(8,128)(2,1)} %bitcast.145, f32[256,1152]{1,0:T(8,128)} %bitcast.131, bf16[256,1152]{1,0:T(8,128)(2,1)} %bitcast.156, ...), custom_call_target="tpu_custom_call" | custom-call | tf_op jit(solution)/shard_map/pallas_call | solution.py:1108
  284.8 1.7 convolution_convert_fusion
  286.4 2.3 copy.198
  288.7 1.9 fusion.4
  294.5 37.8 %shard_map.139 = f32[2,128,512]{2,1,0:T(8,128)} custom-call(bf16[4,2,128,512]{3,2,1,0:T(8,128)(2,1)} %bitcast.150), custom_call_target="tpu_custom_call" | custom-call | tf_op jit(solution)/shard_map/pallas_call | solution.py:470
  339.6 3.6 fusion.17
  345.5 3.1 pad_maximum_fusion
  348.5 57.3 %shard_map.140 = (bf16[4,80,1152]{2,1,0:T(8,128)(2,1)}, f32[40,128]{1,0:T(8,128)}) custom-call(bf16[8,4,80,1152]{3,2,1,0:T(8,128)(2,1)} %bitcast.138, f32[40,128]{1,0:T(8,128)} %bitcast.168), custom_call_target="tpu_custom_call" | custom-call | tf_op jit(solution)/shard_map/pallas_call | solution.py:629
  405.8 1.3 dynamic_slice.3
  408.5 32.6 %shard_map.141 = (f32[4,432,288]{2,1,0:T(8,128)}, f32[4,216,288]{2,1,0:T(8,128)}, f32[320,288]{1,0:T(8,128)}) custom-call(bf16[672,1152]{1,0:T(8,128)(2,1)} %bitcast.159, bf16[4,80,1152]{2,1,0:T(8,128)(2,1)} %get-tuple-element.26.attn), custom_call_target="tpu_custom_call" | custom-call | tf_op jit(solution)/shard_map/pallas_call | solution.py:717
  442.1 1.7 slice.124
  443.8 3.2 copy.175
  447.0 1.4 copy.176
  (221 shorter events, 43.1 us)
Async XLA Ops:
  7.2 3.3 copy-start.29
  7.2 166.6 %all-gather.3.cloned.1.call-start = ((), (), s32[]{:S(2)}) async-start(), calls=%async_computation.2 | async-start | bytes 7741440 | tf_op jit(solution)/shard_map/all_gather | solution.py:1208
  10.5 1.7 copy-start.59
  54.8 353.7 %reduce-scatter.2.cloned.1.call-start = ((), (), s32[]{:S(2)}) async-start(), calls=%async_computation.1 | async-start | bytes 7741440 | tf_op jit(solution)/shard_map/reduce_scatter | solution.py:1369
  91.7 4.2 copy-start.11
  96.0 4.7 %copy-start.50 = (f32[2,128]{1,0:T(2,128)}, f32[2,128]{1,0:T(2,128)S(1)}, u32[]{:S(2)}) copy-start(f32[2,128]{1,0:T(2,128)S(1)} %fusion.21) | copy-start | bytes 3076
  96.9 3.9 copy-start.35
  97.5 9.0 %copy-start.42 = (f32[256]{0:T(256)}, f32[256]{0:T(256)S(1)}, u32[]{:S(2)}) copy-start(f32[256]{0:T(256)S(1)} %get-tuple-element.95) | copy-start | bytes 3076
  97.5 8.6 %copy-start.56 = (f32[128]{0:T(128)}, f32[128]{0:T(128)S(1)}, u32[]{:S(2)}) copy-start(f32[128]{0:T(128)S(1)} %negate_power_fusion) | copy-start | bytes 1540
  97.5 3.3 copy-start.54
  100.8 5.6 %copy-start.18 = (f32[2,128,1536]{2,1,0:T(8,128)}, f32[2,128,1536]{2,1,0:T(8,128)S(1)}, u32[]{:S(2)}) copy-start(f32[2,128,1536]{2,1,0:T(8,128)S(1)} %fusion.31) | copy-start | bytes 4718596
  100.9 5.5 %copy-start.52 = (f32[2,128]{1,0:T(2,128)}, f32[2,128]{1,0:T(2,128)S(1)}, u32[]{:S(2)}) copy-start(f32[2,128]{1,0:T(2,128)S(1)} %multiply_reduce_fusion.11) | copy-start | bytes 3076
  101.9 29.1 %copy-start.4 = (f32[2,128,1024]{2,1,0:T(8,128)}, f32[2,128,1024]{2,1,0:T(8,128)S(1)}, u32[]{:S(2)}) copy-start(f32[2,128,1024]{2,1,0:T(8,128)S(1)} %slice.142) | copy-start | bytes 3145732
  110.0 2.5 copy-start.31
  112.4 2.3 copy-start.36
  123.4 4.6 %copy-start.43 = (f32[256]{0:T(256)S(1)}, f32[256]{0:T(256)}, u32[]{:S(2)}) copy-start(f32[256]{0:T(256)} %copy-done.42) | copy-start | bytes 3076
  130.4 2.2 copy-start.14
  132.5 2.4 copy-start.12
  133.7 2.3 copy-start.22
  137.4 26.0 %copy-start.2 = (f32[2,128,1152]{2,1,0:T(8,128)}, f32[2,128,1152]{2,1,0:T(8,128)S(1)}, u32[]{:S(2)}) copy-start(f32[2,128,1152]{2,1,0:T(8,128)S(1)} %get-tuple-element.79) | copy-start | bytes 3538948
  138.6 24.8 %copy-start.41 = (f32[1152]{0:T(1024)S(1)}, f32[1152]{0:T(1024)}, u32[]{:S(2)}) copy-start(f32[1152]{0:T(1024)} %get-tuple-element.90) | copy-start | bytes 13828
  282.8 2.0 copy-start.13
  284.8 3.9 copy-start.1
  336.5 1.9 copy-start.53
  336.5 3.0 copy-start.37
  336.6 3.0 copy-start.55
  339.6 3.7 copy-start.21
  339.6 3.7 copy-start.23
  348.5 58.6 %copy-start.51 = (f32[2,128]{1,0:T(2,128)S(1)}, f32[2,128]{1,0:T(2,128)}, u32[]{:S(2)}) copy-start(f32[2,128]{1,0:T(2,128)} %copy-done.50) | copy-start | bytes 3076
  348.5 58.6 %copy-start.7 = (f32[2,128,1152]{2,1,0:T(8,128)S(1)}, f32[2,128,1152]{2,1,0:T(8,128)}, u32[]{:S(2)}) copy-start(f32[2,128,1152]{2,1,0:T(8,128)} %copy-done.6) | copy-start | bytes 3538948
  443.8 3.2 copy-start.24
  447.0 2.1 copy-start.30
  (30 other events, 32.0 us)
Sparse Core Ops, SparseCore 0:
  54.9 118.8 all-gather.2
  278.7 121.4 reduce-scatter.1

commit v6 on v5

--- a/solution.py
+++ b/solution.py
@@ -148,19 +148,16 @@
     )(value)
 
 
-def lane_tiles(cols):
-    return [(first, min(128, cols - first)) for first in range(0, cols, 128)]
-
-
 def weights_in_kernel(
     lay, reach, tokens, pack, pairs, lows, attn_out, ffn_out, earlier_out,
-    hops_land, attn_land, own, stack, land, lanes, keep_sem, hop_send, hop_recv, low_send, low_recv, attn_send, attn_recv, send, recv, chain_send, chain_recv,
+    hops_land, attn_land, own, stack, land, keep_sem, hop_send, hop_recv, low_send, low_recv, attn_send, attn_recv, send, recv, chain_send, chain_recv,
 ):
     n, hi, lo = lay.dp, lay.hi, lay.lo
     dp = lax.axis_index("dp")
     ctx = lax.axis_index("ctx")
     high = ctx // lo
-    per, cols = lows.shape[1:]
+    cols = lows.shape[0]
+    per = lows.shape[1] // n
     padded = ffn_out.shape[0] // 3
     targets = [lax.rem(dp + k, n) for k in range(n)]
     right, left = (dp, ctx + lo), (dp, ctx - lo)
@@ -191,31 +188,26 @@
         push.start()
         attn_pushes.append(push)
     attn_land[dp] = pack[dp]
-    blank = jnp.zeros((padded - per, cols), jnp.bfloat16)
-    pushes = []
-
-    def feed_forward_rows(k):
-        target = targets[k]
-        for j, (first, width) in enumerate(lane_tiles(cols)):
-            lanes[j, :, :width] = pairs[target, :, first : first + width]
-        for i in range(3):
-            for j, (first, width) in enumerate(lane_tiles(cols)):
-                if i == 2:
-                    piece = lows[target, :, first : first + width]
-                else:
-                    piece = lanes[j, pl.ds(i, per, stride=2), :][:, :width]
-                if k:
-                    stack[k - 1, i, :per, first : first + width] = piece.astype(jnp.bfloat16)
-                else:
-                    land[dp, i, :per, first : first + width] = piece.astype(jnp.bfloat16)
-            if padded > per and k:
-                stack[k - 1, i, per:] = blank
-            elif padded > per:
-                land[dp, i, per:] = blank
-        if k:
-            push = remote(stack.at[k - 1], land.at[dp], send.at[k], recv.at[k], (target, ctx))
-            push.start()
-            pushes.append(push)
+    wide = land.shape[3]
+
+    def feed_forward_push(q):
+        return remote(stack.at[:, q], land.at[:, dp], send.at[q], recv.at[dp], (q, ctx))
+
+    def feed_forward_units(q):
+        for i, (ref, first, stride) in enumerate(
+            ((pairs, 2 * per * q, 2), (pairs, 2 * per * q + 1, 2), (lows, per * q, 1))
+        ):
+            begin = first // 128 * 128
+            end = min(ref.shape[1], -(-(first + stride * (per - 1) + 1) // 128) * 128)
+            column = lax.broadcasted_iota(jnp.int32, (end - begin, wide), 0) + (begin - first)
+            unit = lax.broadcasted_iota(jnp.int32, (end - begin, wide), 1)
+            pick = jnp.where((column == stride * unit) & (unit < per), 1.0, 0.0).astype(jnp.bfloat16)
+            picked = dot_nn(ref[:, begin:end].astype(jnp.bfloat16), pick).astype(jnp.bfloat16)
+            stack[i, q] = picked
+
+        @pl.when(dp != q)
+        def _():
+            feed_forward_push(q).start()
 
     def chain(source, where, side, step):
         return remote(
@@ -317,8 +309,7 @@
         @pl.when(ctx < d)
         def _():
             earlier_out[reach - d] = jnp.zeros(earlier_out.shape[1:], earlier_out.dtype)
-    order = list(range(2, n)) + [1, 0]
-    feed_forward_rows(order[0])
+    feed_forward_units(0)
     for push in attn_pushes:
         push.wait_recv()
     for q in range(n):
@@ -326,37 +317,46 @@
     keep = pltpu.make_async_copy(own, attn_out.at[high], keep_sem)
     keep.start()
     pass_on(0)
-    events = [partial(feed_forward_rows, order[1])]
+    events = [partial(feed_forward_units, 1)]
     for step in range(1, max(hi, hops + 1)):
         if step <= hops:
             events += [partial(pass_tokens, step, part) for part in range(parts)]
         if step == 1:
-            events.insert(2, partial(feed_forward_rows, order[2]))
+            events.insert(2, partial(feed_forward_units, 2))
         if step < hi:
             events.append(partial(pass_on, step))
         if step == 1:
-            events += [partial(feed_forward_rows, k) for k in order[3:]]
+            events += [partial(feed_forward_units, q) for q in range(3, n)]
     for event in events:
         event()
-    for push in pushes:
-        push.wait_recv()
+    for i in range(3):
+        land[i, dp] = stack[i, dp]
     for q in range(n):
-        for i in range(3):
-            ffn_out[i * padded : (i + 1) * padded, q * cols : (q + 1) * cols] = land[q, i]
+        @pl.when(dp != q)
+        def _():
+            remote(stack.at[:, q], land.at[:, q], send.at[q], recv.at[q], (q, ctx)).wait_recv()
+    for i in range(3):
+        whole = land[i].reshape(n * cols, wide)
+        ffn_out[i * padded : (i + 1) * padded] = whole.T[:padded]
     keep.wait()
     for step in range(hi - 1):
         finish(step)
     for h in range(hops + 1):
         for part in range(parts):
             finish_tokens(h, part)
-    for push in attn_pushes + pushes:
+    for push in attn_pushes:
         push.wait_send()
+    for q in range(n):
+        @pl.when(dp != q)
+        def _():
+            feed_forward_push(q).wait_send()
 
 
 def weights_in(lay, reach, tokens, pack, pairs, lows, collective_id):
-    n, per, cols = lows.shape
+    n = lay.dp
+    cols, per = lows.shape[0], lows.shape[1] // n
     rows = pack.shape[1]
-    padded = -(-per // 16) * 16
+    padded = -(-per // 32) * 32
     vmem = pl.BlockSpec(memory_space=pltpu.VMEM)
     dma = pltpu.SemaphoreType.DMA
     hops = min(lay.hi - 1, (reach + lay.lo - 1) // lay.lo)
@@ -364,9 +364,8 @@
         pltpu.VMEM((hops + 1,) + tokens.shape, tokens.dtype),
         pltpu.VMEM((n, rows, cols), jnp.bfloat16),
         pltpu.VMEM((rows, n * cols), jnp.bfloat16),
-        pltpu.VMEM((n - 1, 3, padded, cols), jnp.bfloat16),
-        pltpu.VMEM((n, 3, padded, cols), jnp.bfloat16),
-        pltpu.VMEM((len(lane_tiles(cols)), 2 * per, 128), jnp.float32),
+        pltpu.VMEM((3, n, cols, -(-padded // 128) * 128), jnp.bfloat16),
+        pltpu.VMEM((3, n, cols, -(-padded // 128) * 128), jnp.bfloat16),
         dma,
     ]
     for shape in ((hops + 1, 2), (hops + 1, lay.lo, 2), (n,), (n,), (2, lay.hi)):
@@ -387,7 +386,10 @@
     )(tokens, pack, pairs, lows)
 
 
-def later_kernel(lay, reach, pieces, out, low_land, moved, arrived, chain_send, chain_recv, low_send, low_recv):
+def later_kernel(
+    lay, reach, pieces, parts, out, group_out, low_land, moved, arrived, chain_send, chain_recv, low_send, low_recv, *scratch
+):
+    group = GroupSum(lay, parts, group_out, *scratch)
     hi, lo = lay.hi, lay.lo
     dp = lax.axis_index("dp")
     ctx = lax.axis_index("ctx")
@@ -397,14 +399,14 @@
     has_right, has_left = high < hi - 1, high > 0
     low_peers = [(dp, high * lo + other) for other in range(lo)]
     barrier = pltpu.get_barrier_semaphore()
-    for there, device in [(has_right, right), (has_left, left)] + [
-        (low != other, low_peers[other]) for other in range(lo) if lo > 1
-    ]:
+    for device in group.peers:
+        pl.semaphore_signal(barrier, inc=1, device_id=device, device_id_type=MESH)
+    for there, device in [(has_right, right), (has_left, left)]:
         @pl.when(there)
         def _():
             pl.semaphore_signal(barrier, inc=1, device_id=device, device_id_type=MESH)
     sides = jnp.where(has_right, 1, 0) + jnp.where(has_left, 1, 0)
-    pl.semaphore_wait(barrier, sides + lo - 1)
+    pl.semaphore_wait(barrier, sides + len(group.peers))
 
     def wanted(h, owner, reader):
         distance = h * lo + reader - owner
@@ -430,7 +432,14 @@
                 @pl.when((low != other) & wanted(h, other, low))
                 def _():
                     across(h, other).start()
+    group.start()
+    stages = group.stages()
+    every = -(-len(stages) // (hops + 1))
     for h in range(hops, -1, -1):
+        turn = hops - h
+        for calls in stages[turn * every : (turn + 1) * every]:
+            for call in calls:
+                call()
         out[...] = jnp.zeros_like(out)
         if h and h * lo <= reach:
             out[...] += pieces[reach - h * lo].astype(jnp.float32)
@@ -460,73 +469,179 @@
                 @pl.when((low != other) & wanted(h, other, low))
                 def _():
                     across(h, other).wait_send()
-
-
-def later_sum(lay, reach, pieces, collective_id):
+    group.finish()
+
+
+def later_sum(lay, reach, pieces, parts, collective_id):
     hops = min(lay.hi - 1, (reach + lay.lo - 1) // lay.lo)
     shape = pieces.shape[1:]
     vmem = pl.BlockSpec(memory_space=pltpu.VMEM)
     dma = pltpu.SemaphoreType.DMA
     return pl.pallas_call(
         partial(later_kernel, lay, reach),
-        out_shape=jax.ShapeDtypeStruct(shape, jnp.float32),
-        in_specs=[vmem],
-        out_specs=vmem,
+        out_shape=(
+            jax.ShapeDtypeStruct(shape, jnp.float32),
+            jax.ShapeDtypeStruct((lay.hi, parts.shape[2], D), parts.dtype),
+        ),
+        in_specs=[vmem] * 2,
+        out_specs=(vmem,) * 2,
         scratch_shapes=[
             pltpu.VMEM((hops + 1, lay.lo) + shape, pieces.dtype),
             pltpu.VMEM((hops + 1,) + shape, pieces.dtype),
             pltpu.VMEM((hops + 1,) + shape, pieces.dtype),
         ]
         + [dma((hops + 1,))] * 2
-        + [dma((hops + 1, lay.lo))] * 2,
+        + [dma((hops + 1, lay.lo))] * 2
+        + GroupSum.scratch(lay, parts.shape[2]),
         compiler_params=pltpu.CompilerParams(
             collective_id=collective_id, has_side_effects=True, vmem_limit_bytes=VMEM_LIMIT
         ),
-    )(pieces)
+    )(pieces, parts)
 
 
 def flip(index, bit):
     return index + bit * (1 - 2 * lax.rem(index // bit, 2))
 
 
-def sum_group_kernel(lay, parts, gains, out, gains_out, core_land, wide_sum, wide_land, keep, low_sum, low_land,
-                     gains_sum, gains_land, core_send, core_recv, wide_send, wide_recv, low_send, low_recv,
-                     gains_send, gains_recv):
+class GroupSum:
+    @staticmethod
+    def scratch(lay, rows):
+        dma = pltpu.SemaphoreType.DMA
+        blocks = (lay.hi, lay.lo, lay.wide)
+        data = [pltpu.VMEM(blocks + (rows, D), jnp.bfloat16)] * 3
+        return data + [dma(blocks)] * 6
+
+    def __init__(self, lay, parts, out, land, sums, second_land, core_send, core_recv, send, recv, second_send, second_recv):
+        self.lay, self.parts, self.out = lay, parts, out
+        self.land, self.sums, self.second_land = land, sums, second_land
+        self.core_sems, self.sems, self.second_sems = (core_send, core_recv), (send, recv), (second_send, second_recv)
+        dp = lax.axis_index("dp")
+        ctx = lax.axis_index("ctx")
+        hi, lo, wide = lay.hi, lay.lo, lay.wide
+        high, self.low = ctx // lo, lax.rem(ctx, lo)
+        self.across, self.core = dp // 2, lax.rem(dp, 2)
+        self.partner = (self.across * 2 + 1 - self.core, ctx)
+        self.low_peers = [(dp, high * lo + lax.rem(self.low + k, lo)) for k in range(lo)]
+        self.wide_peers = [(lax.rem(self.across + k, wide) * 2 + self.core, ctx) for k in range(wide)]
+        self.peers = self.low_peers[1:] + self.wide_peers[1:] + [self.partner]
+        self.sends = []
+
+    def at(self, h, a, b):
+        lay = self.lay
+        return h * lay.lo + lax.rem(self.low + a, lay.lo), lax.rem(self.across + b, lay.wide) * 2
+
+    def turned(self, h):
+        return h >= self.lay.hi // 2 and self.lay.lo > 1
+
+    def core_copy(self, h, a, b):
+        ctx, there = self.at(h, a, b)
+        return remote(
+            self.parts.at[ctx, there + 1 - self.core], self.land.at[h, a, b], self.core_sems[0].at[h, a, b],
+            self.core_sems[1].at[h, a, b], self.partner,
+        )
+
+    def blocks(self):
+        lay = self.lay
+        return [
+            (a, b) for a in list(range(1, lay.lo)) + [0] for b in list(range(1, lay.wide)) + [0]
+        ]
+
+    def start(self):
+        for h in range(self.lay.hi):
+            for a, b in self.blocks():
+                self.core_copy(h, a, b).start()
+
+    def first_copy(self, h, a, b):
+        where = (h, a, b)
+        return remote(
+            self.sums.at[where], self.land_first(h, a, b), self.sems[0].at[where], self.sems[1].at[where],
+            self.low_peers[a] if self.turned(h) else self.wide_peers[b],
+        )
+
+    def land_first(self, h, a, b):
+        return self.second_land.at[h, a, b]
+
+    def second_copy(self, h, a, b):
+        where = (h, a, b)
+        return remote(
+            self.sums.at[where], self.second_land.at[where], self.second_sems[0].at[where],
+            self.second_sems[1].at[where], self.wide_peers[b] if self.turned(h) else self.low_peers[a],
+        )
+
+    def moves_first(self, h, a, b):
+        return a > 0 if self.turned(h) else b > 0
+
+    def sum_cores(self, h):
+        for a, b in self.blocks():
+            self.core_copy(h, a, b).wait_recv()
+            ctx, there = self.at(h, a, b)
+            total = self.parts[ctx, there + self.core].astype(jnp.float32) + self.land[h, a, b].astype(jnp.float32)
+            self.sums[h, a, b] = total.astype(jnp.bfloat16)
+            if self.moves_first(h, a, b):
+                self.first_copy(h, a, b).start()
+
+    def sum_first(self, h):
+        lay = self.lay
+        for a, b in self.blocks():
+            if self.moves_first(h, a, b):
+                continue
+            total = self.sums[h, a, b].astype(jnp.float32)
+            others = [(k, b) for k in range(1, lay.lo)] if self.turned(h) else [(a, k) for k in range(1, lay.wide)]
+            for other in others:
+                self.first_copy(h, *other).wait_recv()
+                total = total + self.second_land[(h,) + other].astype(jnp.float32)
+            self.sums[h, a, b] = total.astype(jnp.bfloat16)
+            if a or b:
+                self.second_copy(h, a, b).start()
+
+    def sum_second(self, h):
+        lay = self.lay
+        total = self.sums[h, 0, 0].astype(jnp.float32)
+        others = [(0, k) for k in range(1, lay.wide)] if self.turned(h) else [(k, 0) for k in range(1, lay.lo)]
+        for other in others:
+            self.second_copy(h, *other).wait_recv()
+            total = total + self.second_land[(h,) + other].astype(jnp.float32)
+        self.out[h] = total.astype(jnp.bfloat16)
+
+    def order(self):
+        half = self.lay.hi // 2
+        pairs = [h for pair in zip(range(half), range(half, 2 * half)) for h in pair]
+        return pairs + list(range(2 * half, self.lay.hi))
+
+    def stages(self):
+        order = self.order()
+        stages = []
+        for i in range(len(order) + 4):
+            calls = []
+            if i < len(order):
+                calls.append(partial(self.sum_cores, order[i]))
+            if 2 <= i < len(order) + 2:
+                calls.append(partial(self.sum_first, order[i - 2]))
+            if 4 <= i:
+                calls.append(partial(self.sum_second, order[i - 4]))
+            stages.append(calls)
+        return stages
+
+    def finish(self):
+        for h in range(self.lay.hi):
+            for a, b in self.blocks():
+                self.core_copy(h, a, b).wait_send()
+                if self.moves_first(h, a, b):
+                    self.first_copy(h, a, b).wait_send()
+                elif a or b:
+                    self.second_copy(h, a, b).wait_send()
+
+
+def sum_group_kernel(lay, parts, gains, out, gains_out, gains_sum, gains_land, gains_send, gains_recv, *scratch):
     dp = lax.axis_index("dp")
     ctx = lax.axis_index("ctx")
-    hi, lo, wide, n = lay.hi, lay.lo, lay.wide, lay.dp
-    high, low = ctx // lo, lax.rem(ctx, lo)
-    across, core = dp // 2, lax.rem(dp, 2)
-    partner = (across * 2 + 1 - core, ctx)
-    low_peers = [(dp, high * lo + lax.rem(low + k, lo)) for k in range(1, lo)]
-    wide_peers = [(lax.rem(across + k, wide) * 2 + core, ctx) for k in range(1, wide)]
-    gain_peers = [(flip(dp, 1 << i), ctx) for i in range((n - 1).bit_length())]
+    group = GroupSum(lay, parts, out, *scratch)
+    gain_peers = [(flip(dp, 1 << i), ctx) for i in range((lay.dp - 1).bit_length())]
     gain_peers += [(dp, flip(ctx, 1 << i)) for i in range((lay.ctx - 1).bit_length())]
-    greet(low_peers + wide_peers + [partner] + gain_peers)
-
-    def block(h, a):
-        return h * lo + lax.rem(low + a, lo)
-
-    def slot(h, a):
-        return h * lo + a
-
-    sends = []
-    core_copies, wide_copies, low_copies, gain_copies = {}, {}, {}, []
-    offsets = list(range(1, lo)) + [0]
-    for h in range(hi):
-        for a in offsets:
-            for b in list(range(1, wide)) + [0]:
-                there = lax.rem(across + b, wide)
-                copy = remote(
-                    parts.at[block(h, a), there * 2 + 1 - core],
-                    core_land.at[slot(h, a), b],
-                    core_send.at[slot(h, a), b],
-                    core_recv.at[slot(h, a), b],
-                    partner,
-                )
-                copy.start()
-                core_copies[h, a, b] = copy
-                sends.append(copy)
+    greet(group.peers + gain_peers)
+
+    def gains_copy(i):
+        return remote(gains_sum.at[i], gains_land.at[i], gains_send.at[i], gains_recv.at[i], gain_peers[i])
 
     def gains_step(i):
         if i > len(gain_peers):
@@ -534,98 +649,31 @@
         if i == 0:
             gains_sum[0] = gains[...]
         else:
-            gain_copies[i - 1].wait_recv()
+            gains_copy(i - 1).wait_recv()
             gains_sum[i] = gains_sum[i - 1] + gains_land[i - 1]
         if i < len(gain_peers):
-            copy = remote(
-                gains_sum.at[i], gains_land.at[i], gains_send.at[i], gains_recv.at[i], gain_peers[i]
-            )
-            copy.start()
-            gain_copies.append(copy)
-            sends.append(copy)
+            gains_copy(i).start()
         else:
             gains_out[...] = gains_sum[i]
 
-    def sum_cores(h, a):
-        s = slot(h, a)
-        for b in list(range(1, wide)) + [0]:
-            there = lax.rem(across + b, wide)
-            core_copies[h, a, b].wait_recv()
-            total = parts[block(h, a), there * 2 + core].astype(jnp.float32) + core_land[
-                s, b
-            ].astype(jnp.float32)
-            if b:
-                wide_sum[s, b - 1] = total.astype(jnp.bfloat16)
-                copy = remote(
-                    wide_sum.at[s, b - 1], wide_land.at[s, b - 1], wide_send.at[s, b - 1],
-                    wide_recv.at[s, b - 1], wide_peers[b - 1],
-                )
-                copy.start()
-                wide_copies[h, a, b] = copy
-                sends.append(copy)
-            else:
-                keep[s] = total
-
-    def sum_wide(h, a):
-        s = slot(h, a)
-        total = keep[s]
-        for b in range(1, wide):
-            wide_copies[h, a, b].wait_recv()
-            total = total + wide_land[s, b - 1].astype(jnp.float32)
-        if a:
-            low_sum[h, a - 1] = total.astype(jnp.bfloat16)
-            copy = remote(
-                low_sum.at[h, a - 1], low_land.at[h, a - 1], low_send.at[h, a - 1],
-                low_recv.at[h, a - 1], low_peers[a - 1],
-            )
-            copy.start()
-            low_copies[h, a] = copy
-            sends.append(copy)
-        else:
-            keep[s] = total
-
-    def sum_low(h):
-        total = keep[slot(h, 0)]
-        for a in range(1, lo):
-            low_copies[h, a].wait_recv()
-            total = total + low_land[h, a - 1].astype(jnp.float32)
-        out[h] = total.astype(jnp.bfloat16)
-
-    gains_step(0)
-    for i in range(hi + 2):
-        if i < hi:
-            for a in offsets:
-                sum_cores(i, a)
-        gains_step(i + 1)
-        if 1 <= i <= hi:
-            for a in offsets:
-                sum_wide(i - 1, a)
-        if 2 <= i:
-            sum_low(i - 2)
-    for i in range(hi + 3, len(gain_peers) + 1):
+    group.start()
+    stages = group.stages()
+    for i, calls in enumerate(stages):
         gains_step(i)
-    for copy in sends:
-        copy.wait_send()
+        for call in calls:
+            call()
+    for i in range(len(stages), len(gain_peers) + 1):
+        gains_step(i)
+    group.finish()
+    for i in range(len(gain_peers)):
+        gains_copy(i).wait_send()
 
 
 def sum_group(lay, parts, gains, collective_id):
     rows = parts.shape[2]
-    lows, wides = max(1, lay.lo - 1), max(1, lay.wide - 1)
     vmem = pl.BlockSpec(memory_space=pltpu.VMEM)
     dma = pltpu.SemaphoreType.DMA
     count = (lay.dp - 1).bit_length() + (lay.ctx - 1).bit_length()
-    scratch = [
-        pltpu.VMEM((lay.ctx, lay.wide, rows, D), jnp.bfloat16),
-        pltpu.VMEM((lay.ctx, wides, rows, D), jnp.bfloat16),
-        pltpu.VMEM((lay.ctx, wides, rows, D), jnp.bfloat16),
-        pltpu.VMEM((lay.ctx, rows, D), jnp.float32),
-        pltpu.VMEM((lay.hi, lows, rows, D), jnp.bfloat16),
-        pltpu.VMEM((lay.hi, lows, rows, D), jnp.bfloat16),
-        pltpu.VMEM((count + 1,) + gains.shape, jnp.float32),
-        pltpu.VMEM((count,) + gains.shape, jnp.float32),
-    ]
-    for shape in ((lay.ctx, lay.wide), (lay.ctx, wides), (lay.hi, lows), (count,)):
-        scratch += [dma(shape), dma(shape)]
     return pl.pallas_call(
         partial(sum_group_kernel, lay),
         out_shape=(
@@ -634,22 +682,29 @@
         ),
         in_specs=[vmem] * 2,
         out_specs=(vmem,) * 2,
-        scratch_shapes=scratch,
+        scratch_shapes=[
+            pltpu.VMEM((count + 1,) + gains.shape, jnp.float32),
+            pltpu.VMEM((count,) + gains.shape, jnp.float32),
+            dma((count,)),
+            dma((count,)),
+        ]
+        + GroupSum.scratch(lay, rows),
         compiler_params=pltpu.CompilerParams(
             collective_id=collective_id, has_side_effects=True, vmem_limit_bytes=VMEM_LIMIT
         ),
     )(parts, gains)
 
 
-def grads_out_kernel(lay, rows, attn, pairs_out, lows_out, attn_out, stack, land, lanes, hi_land, last, last_land,
+def grads_out_kernel(lay, rows, early, attn, pairs_out, lows_out, attn_out, stack, land, hi_land, last, last_land,
                      send, recv, hi_send, hi_recv, last_send, last_recv):
     n, hi, lo = lay.dp, lay.hi, lay.lo
     dp = lax.axis_index("dp")
     ctx = lax.axis_index("ctx")
     high, low = ctx // lo, lax.rem(ctx, lo)
-    cols = lows_out.shape[2]
-    per = lows_out.shape[1]
-    padded = rows.shape[0] // 3
+    cols = lows_out.shape[0]
+    per = lows_out.shape[1] // n
+    padded = (rows.shape[0] + early.shape[0]) // 3
+    wide = land.shape[3]
     attn_rows = attn.shape[1]
     hi_peers = [(dp, lax.rem(high + k, hi) * lo + low) for k in range(1, hi)]
     greet([(lax.rem(dp + k, n), ctx) for k in range(1, n)] + hi_peers)
@@ -660,16 +715,23 @@
         )
         push.start()
         hi_pushes.append(push)
-    for q in range(n):
-        for i in range(3):
-            stack[q, i] = rows[i * padded : (i + 1) * padded, q * cols : (q + 1) * cols]
+    blank = jnp.zeros((wide - padded, n * cols), jnp.bfloat16)
+    for i in range(3):
+        pieces = [rows[i * padded : (i + 1) * padded if i < 2 else rows.shape[0]]]
+        if i == 2:
+            pieces.append(early[...])
+        if wide > padded:
+            pieces.append(blank)
+        whole = jnp.concatenate(pieces, axis=0) if len(pieces) > 1 else pieces[0]
+        stack[i] = whole.T.reshape(n, cols, wide)
     pushes = []
     for k in range(1, n):
         target = lax.rem(dp + k, n)
-        push = remote(stack.at[target], land.at[dp], send.at[k], recv.at[k], (target, ctx))
+        push = remote(stack.at[:, target], land.at[:, dp], send.at[k], recv.at[k], (target, ctx))
         push.start()
         pushes.append(push)
-    land[dp] = stack[dp]
+    for i in range(3):
+        land[i, dp] = stack[i, dp]
     total = attn[high].astype(jnp.float32)
     for k, push in enumerate(hi_pushes):
         push.wait_recv()
@@ -684,22 +746,15 @@
         last_pushes.append(push)
     last_land[dp] = last[dp]
 
-    def place(q):
-        for j, (first, width) in enumerate(lane_tiles(cols)):
-            for i in range(2):
-                piece = land[q, i, :per, first : first + width].astype(jnp.float32)
-                if width < 128:
-                    piece = jnp.concatenate(
-                        [piece, jnp.zeros((per, 128 - width), jnp.float32)], axis=1
-                    )
-                lanes[j, pl.ds(i, per, stride=2), :] = piece
-            pairs_out[q, :, first : first + width] = lanes[j, :, :width]
-        lows_out[q] = land[q, 2, :per].astype(jnp.float32)
-
+    unit = lax.broadcasted_iota(jnp.int32, (wide, 2 * per), 0)
+    column = lax.broadcasted_iota(jnp.int32, (wide, 2 * per), 1)
+    spread = [jnp.where(column == 2 * unit + i, 1.0, 0.0).astype(jnp.bfloat16) for i in range(2)]
     for push in pushes:
         push.wait_recv()
     for q in range(n):
-        place(q)
+        turns = dot_nn(land[0, q], spread[0]) + dot_nn(land[1, q], spread[1])
+        pairs_out[:, 2 * per * q : 2 * per * (q + 1)] = turns.astype(jnp.bfloat16)
+        lows_out[:, per * q : per * (q + 1)] = land[2, q, :, :per]
     for push in last_pushes:
         push.wait_recv()
     for q in range(n):
@@ -708,8 +763,8 @@
         push.wait_send()
 
 
-def grads_out(lay, rows, attn, per, collective_id):
-    padded = rows.shape[0] // 3
+def grads_out(lay, rows, early, attn, per, collective_id):
+    padded = (rows.shape[0] + early.shape[0]) // 3
     n, cols = lay.dp, rows.shape[1] // lay.dp
     attn_rows = attn.shape[1]
     vmem = pl.BlockSpec(memory_space=pltpu.VMEM)
@@ -717,16 +772,15 @@
     return pl.pallas_call(
         partial(grads_out_kernel, lay),
         out_shape=(
-            jax.ShapeDtypeStruct((n, 2 * per, cols), jnp.float32),
-            jax.ShapeDtypeStruct((n, per, cols), jnp.float32),
+            jax.ShapeDtypeStruct((cols, n * 2 * per), jnp.bfloat16),
+            jax.ShapeDtypeStruct((cols, n * per), jnp.bfloat16),
             jax.ShapeDtypeStruct((n * attn_rows, cols), jnp.float32),
         ),
-        in_specs=[vmem] * 2,
+        in_specs=[vmem] * 3,
         out_specs=(vmem,) * 3,
         scratch_shapes=[
-            pltpu.VMEM((n, 3, padded, cols), jnp.bfloat16),
-            pltpu.VMEM((n, 3, padded, cols), jnp.bfloat16),
-            pltpu.VMEM((len(lane_tiles(cols)), 2 * per, 128), jnp.float32),
+            pltpu.VMEM((3, n, cols, -(-padded // 128) * 128), jnp.bfloat16),
+            pltpu.VMEM((3, n, cols, -(-padded // 128) * 128), jnp.bfloat16),
             pltpu.VMEM((max(1, lay.hi - 1), attn_rows, D), jnp.bfloat16),
             pltpu.VMEM((n, attn_rows, cols), jnp.bfloat16),
             pltpu.VMEM((n, attn_rows, cols), jnp.bfloat16),
@@ -737,7 +791,7 @@
         compiler_params=pltpu.CompilerParams(
             collective_id=collective_id, has_side_effects=True, vmem_limit_bytes=VMEM_LIMIT
         ),
-    )(rows, attn)
+    )(rows, early, attn)
 
 
 def in_tiles(total, size, body, begin=0):
@@ -765,9 +819,8 @@
 
 
 def feed_forward_kernel(
-    lay, mid, weights, mixed, cotangent, valid, gain,
-    result, grad_mid, grad_gain, grad_weights,
-    w_gate, w_up, w_down, gate_t, up_t, act, slope, hidden, hidden_t, grads, parts, core_land, sums, via, landed,
+    lay, mid, weights, mixed, cotangent, valid, gain, result, grad_mid, grad_gain, grad_weights, early_sum,
+    late, late_sem, early, early_land, hi_send, hi_recv, w_gate, w_up, w_down, gate_t, up_t, act, slope, hidden, hidden_t, grads, parts, core_land, sums, via, landed,
     total, dy, weight_sem, core_send, core_recv, share_send, share_recv,
     send, recv, via_send, via_recv, dy_send, dy_recv, dy_pass,
 ):
@@ -775,13 +828,18 @@
     n, wide = lay.chips, lay.wide
     tokens = mixed.shape[0]
     units = w_gate.shape[0]
-    padded = units // lay.hi
+    hi = lay.hi
+    padded = units // hi
+    part_rows = padded // 2
     loads = [
         pltpu.make_async_copy(
-            weights.at[h, pl.ds(i * padded, padded)], held.at[pl.ds(h * padded, padded)], weight_sem.at[i, h]
+            weights.at[h, pl.ds(i * padded + part * part_rows, part_rows)],
+            held.at[pl.ds((part * hi + h) * part_rows, part_rows)],
+            weight_sem.at[i, part, h],
         )
         for i, held in enumerate((w_gate, w_up, w_down))
-        for h in range(lay.hi)
+        for part in range(2)
+        for h in range(hi)
     ]
     for load in loads:
         load.start()
@@ -794,7 +852,8 @@
     halves = (pl.ds(0, half), pl.ds(half, half))
     straight, bent = lay.straight(), lay.bent()
     place = [lay.position(k) for k in range(n)]
-    greet(peers[1:] + [partner])
+    hi_peers = [lay.device(chip, core, lax.rem(high + k, hi)) for k in range(hi)]
+    greet(peers[1:] + [partner] + hi_peers[1:])
 
     def to_partner(phase, k):
         return remote(
@@ -948,6 +1007,12 @@
             parts[pl.ds(*group), :, lanes] = both.astype(jnp.bfloat16).reshape(count, rows_of, width)
 
         in_tiles(D, 256, tile)
+
+    def product_over_tokens(left, begin, end, right, lanes):
+        value = dot_nn(left[0, begin:end], right[0, :, lanes])
+        for c in range(1, n):
+            value = value + dot_nn(left[c, begin:end], right[c, :, lanes])
+        return value.astype(jnp.bfloat16)
 
     far, near, here = (0, len(bent)), (len(bent), len(straight)), (n - 1, 1)
     most = hidden.shape[0] // rows_of
@@ -1055,6 +1120,22 @@
         to_partner(1, k).start()
     for k in bent:
         shares[k].wait_recv()
+    split = hi * part_rows
+
+    def early_grad(first, width):
+        lanes = pl.ds(first, width)
+        value = product_over_tokens(hidden_t, split, units, dy, lanes)
+        for h in range(hi):
+            early[h, :, lanes] = value[h * part_rows : (h + 1) * part_rows]
+
+    in_tiles(D, 256, early_grad)
+    hi_pushes = []
+    for k in range(1, hi):
+        push = remote(
+            early.at[lax.rem(high + k, hi)], early_land.at[k - 1], hi_send.at[k], hi_recv.at[k], hi_peers[k]
+        )
+        push.start()
+        hi_pushes.append(push)
     for i, run in enumerate(runs(far)):
         backward_units(run)
         if i == 0:
@@ -1069,17 +1150,25 @@
     for k in bent:
         add_core(1, k)
 
-    def weight_grad(left_ref, right, i):
+    stores = []
+
+    def weight_grad(left, right, i):
+        parts_here = (0,) if i == 2 else (0, 1)
+
         def tile(first, width):
             lanes = pl.ds(first, width)
-            value = dot_nn(left_ref[0], right[0, :, lanes])
-            for c in range(1, n):
-                value = value + dot_nn(left_ref[c], right[c, :, lanes])
-            value = value.astype(jnp.bfloat16)
-            for h in range(lay.hi):
-                grad_weights[h, i * padded : (i + 1) * padded, lanes] = value[h * padded : (h + 1) * padded]
+            value = product_over_tokens(left, 0, split * len(parts_here), right, lanes)
+            for part in parts_here:
+                for h in range(hi):
+                    row = i * padded + part * part_rows
+                    start = (part * hi + h) * part_rows
+                    late[h, row : row + part_rows, lanes] = value[start : start + part_rows]
 
         in_tiles(D, 256, tile)
+        rows = pl.ds(i * padded, part_rows * len(parts_here))
+        store = pltpu.make_async_copy(late.at[:, rows], grad_weights.at[:, rows], late_sem.at[i])
+        store.start()
+        stores.append(store)
 
     weight_grad(hidden_t, dy, 2)
     for k in straight:
@@ -1088,6 +1177,16 @@
     weight_grad(up_t, mid, 1)
     add_owners(1)
     grad_mid[...] = total[...]
+    for push in hi_pushes:
+        push.wait_recv()
+    early_total = early[high].astype(jnp.float32)
+    for k in range(hi - 1):
+        early_total = early_total + early_land[k].astype(jnp.float32)
+    early_sum[...] = early_total.astype(jnp.bfloat16)
+    for push in hi_pushes:
+        push.wait_send()
+    for store in stores:
+        store.wait()
     settle(1)
     for k, h in ordered:
         dy_push(k, h).wait_send()
@@ -1101,6 +1200,8 @@
     n = lay.chips
     tokens = mixed.shape[0]
     units = weights.shape[0] * weights.shape[1] // 3
+    early_rows = weights.shape[1] // 6
+    late_rows = weights.shape[1] - early_rows
     most = min(n, max(1, 1920 // units))
     low, high = jnp.bfloat16, jnp.float32
     vmem = pl.BlockSpec(memory_space=pltpu.VMEM)
@@ -1111,11 +1212,18 @@
             jax.ShapeDtypeStruct((tokens, D), low),
             jax.ShapeDtypeStruct((tokens, D), high),
             jax.ShapeDtypeStruct((8, D), high),
-            jax.ShapeDtypeStruct(weights.shape, low),
+            jax.ShapeDtypeStruct((lay.hi, late_rows, D), low),
+            jax.ShapeDtypeStruct((early_rows, D), low),
         ),
         in_specs=[vmem, pl.BlockSpec(memory_space=pl.ANY)] + [vmem] * 4,
-        out_specs=(vmem,) * 4,
+        out_specs=(vmem, vmem, vmem, pl.BlockSpec(memory_space=pl.ANY), vmem),
         scratch_shapes=[
+            pltpu.VMEM((lay.hi, late_rows, D), low),
+            dma((3,)),
+            pltpu.VMEM((lay.hi, early_rows, D), low),
+            pltpu.VMEM((max(1, lay.hi - 1), early_rows, D), low),
+            dma((lay.hi,)),
+            dma((lay.hi,)),
             pltpu.VMEM((units, D), low),
             pltpu.VMEM((units, D), low),
             pltpu.VMEM((units, D), low),
@@ -1133,7 +1241,7 @@
             pltpu.VMEM((max(1, len(lay.straight())), tokens, D), low),
             pltpu.VMEM((tokens, D), high),
             pltpu.VMEM((n, 2 * tokens, D), low),
-            dma((3, lay.hi)),
+            dma((3, 2, lay.hi)),
         ]
         + [dma((2, n))] * 2
         + [dma((n,))] * 2
@@ -1201,8 +1309,8 @@
         reach,
         tokens,
         pack.reshape(lay.dp, pack_rows // lay.dp, cols),
-        w_gate_up.reshape(lay.dp, 2 * per, cols),
-        w_down.reshape(lay.dp, per, cols),
+        w_gate_up.T,
+        w_down.T,
         5,
     )
     ffn_all = lax.all_gather(ffn_rows, "ctx", axis=0, axis_index_groups=lay.hi_groups)
@@ -1295,7 +1403,7 @@
         lambda out, k, chip, core: out.at[lay.position(k), core],
         1,
     ).reshape(lay.chips, 2 * token_count, D)
-    result, grad_mid, grad_gain_post, grad_ffn = feed_forward(
+    result, grad_mid, grad_gain_post, grad_ffn, early_down = feed_forward(
         lay,
         mid_all,
         ffn_all,
@@ -1336,7 +1444,15 @@
     own_grad = grad_pairs[:, reach * local_len :]
     pieces = grad_pairs[:, : reach * local_len].astype(jnp.bfloat16)
     pieces = pieces.reshape(seq_count, reach, local_len, 2 * HD).transpose(1, 0, 2, 3)
-    later = later_sum(lay, reach, pieces, 11)
+
+    def blocks_of(grad, rows):
+        part = -(-rows // (16 * lay.dp)) * 16
+        whole = grad.astype(jnp.bfloat16).reshape(lay.ctx, rows, D)
+        if part * lay.dp > rows:
+            whole = jnp.pad(whole, ((0, 0), (0, part * lay.dp - rows), (0, 0)))
+        return whole.reshape(lay.ctx, lay.dp, part, D)
+
+    later, plane_out = later_sum(lay, reach, pieces, blocks_of(grad_w_out, out_rows), 11)
     own_grad = own_grad + later
     grad_projected, grad_gain_query, grad_gain_key = pull_heads(
         (grad_query, own_grad[..., :HD], own_grad[..., HD:])
@@ -1356,24 +1472,19 @@
             grad_gain_key,
         ]
     )
-    sum_rows = -(-(qkv_rows + out_rows) // block) * block
-    partial_sums = jnp.concatenate(
-        [
-            grad_w_qkv.astype(jnp.bfloat16).reshape(lay.ctx, qkv_rows, D),
-            grad_w_out.astype(jnp.bfloat16).reshape(lay.ctx, out_rows, D),
-            jnp.zeros((lay.ctx, sum_rows - qkv_rows - out_rows, D), jnp.bfloat16),
-        ],
-        axis=1,
-    ).reshape(lay.ctx, lay.dp, sum_rows // lay.dp, D)
-    plane_attn, gains_sum = sum_group(lay, partial_sums, grad_gain_all.reshape(-1, 128), 8)
+    plane_qkv, gains_sum = sum_group(
+        lay, blocks_of(grad_w_qkv, qkv_rows), grad_gain_all.reshape(-1, 128), 8
+    )
+    plane_attn = jnp.concatenate([plane_qkv, plane_out], axis=1)
     owned = lax.psum_scatter(grad_ffn, "ctx", scatter_dimension=0, axis_index_groups=lay.hi_groups)
-    part_gate_up, part_down, part_attn = grads_out(lay, owned, plane_attn, per, 9)
-    part_qkv = part_attn[:qkv_rows]
-    part_out = part_attn[qkv_rows : qkv_rows + out_rows]
+    part_gate_up, part_down, part_attn = grads_out(lay, owned, early_down, plane_attn, per, 9)
+    part_attn = part_attn.reshape(lay.dp, -1, cols)
+    part_qkv = part_attn[:, : plane_qkv.shape[1]].reshape(-1, cols)[:qkv_rows]
+    part_out = part_attn[:, plane_qkv.shape[1] :].reshape(-1, cols)[:out_rows]
     place = (lax.axis_index("dp") * lay.ctx + lax.axis_index("ctx")) * gains.shape[0]
     part_gains = lax.dynamic_slice_in_dim(gains_sum.reshape(-1), place, gains.shape[0])
-    part_gate_up = part_gate_up.reshape(w_gate_up.shape)
-    part_down = part_down.reshape(w_down.shape)
+    part_gate_up = part_gate_up.astype(jnp.float32).T
+    part_down = part_down.astype(jnp.float32).T
     return (result, grad_input, part_qkv, part_out, part_gate_up, part_down, part_gains)
 
 

time: 463 us -> 444 us (0.959)
  Pallas kernels: 334 us -> 316 us
  local copies, waits for them, and re-layouts: 48.8 us -> 42.2 us
  other arithmetic: 29.8 us -> 34.8 us
    pallas_call x1, Pallas kernels: 57.3 us -> 27.2 us  [sum_group(): pl.pallas_call(partial(sum_group_kernel, lay), out_shape=(jax.ShapeDtypeS...]
    pallas_call x1, Pallas kernels: 37.8 us -> 50.5 us  [later_sum(): pl.pallas_call(partial(later_kernel, lay, reach), out_shape=(jax.ShapeDty...]
    unnamed x133 -> x125, local copies, waits for them, and re-layouts: 24.2 us -> 17.2 us
  transfers between devices with their start and end apart: 2 -> 2, of which waited for: 1 -> 1; matrix products, arithmetic and copies ran while one was open for 15% -> 17% of each run, Pallas kernels for 34% -> 31%
where the time goes in v6:
time: 444 us; the launch traced here: 438 us
  Pallas kernels  316 us (71%)
  local copies, waits for them, and re-layouts  42.2 us (10%)
  other arithmetic  34.8 us (8%)
  matrix products  22.5 us (5%)
  between operations  15.4 us (3%)
  waiting for transfers between devices  6.7 us (2%)
    pallas_call x1, Pallas kernels, feed_forward(): pl.pallas_call(partial(feed_forward_kernel, lay), out_shape=(jax.ShapeDty...  108 us
    pallas_call x2, Pallas kernels, gather_group(): pl.pallas_call(partial(gather_group_kernel, lay, slot), out_shape=jax.Sha...  60.2 us
    pallas_call x1, Pallas kernels, later_sum(): pl.pallas_call(partial(later_kernel, lay, reach), out_shape=(jax.ShapeDty...  50.5 us
    pallas_call x1, Pallas kernels, weights_in(): pl.pallas_call(partial(weights_in_kernel, lay, reach), out_shape=(jax.Sha...  41.3 us
    pallas_call x1, Pallas kernels, grads_out(): pl.pallas_call(partial(grads_out_kernel, lay), out_shape=(jax.ShapeDtypeS...  28.9 us
    pallas_call x1, Pallas kernels, sum_group(): pl.pallas_call(partial(sum_group_kernel, lay), out_shape=(jax.ShapeDtypeS...  27.2 us
    dot_general x7, matrix products, contract(): lax.dot_general(left, right, ((dims_left, dims_right), ((), ())), preferr...  17.5 us
    unnamed x125, local copies, waits for them, and re-layouts  17.2 us
  transfers between devices with their start and end apart: 2, of which 1 were waited for; matrix products, arithmetic and copies ran while one was open for 17% of the time, Pallas kernels for 31%

profile of v6, /device:TPU:9, one launch (start us, length us, event | category | flops | bytes accessed | tf_op | source)
XLA Modules:
  0.0 438.4 jit_solution(16876993636016824854)
XLA Ops:
  10.9 41.3 %shard_map.135 = (bf16[4,96,1152]{2,1,0:T(8,128)(2,1)}, bf16[672,1152]{1,0:T(8,128)(2,1)}, bf16[4,2,128,1152]{3,2,1,0:T(8,128)(2,1)}) custom-call(bf16[2,128,1152]{2,1,0:T(8,128)(2,1)} %tokens.1, bf16[4,96,288]{2,1,0:T(8,128)(2,1)} %bitcast.161, f32[288,1728]{1,0:T(8,128)} %bitcast.159, f32[288,864]{1,0:T(8,128)} %bitcast.164), custom_call_target="tpu_custom_call" | custom-call | tf_op jit(solution)/shard_map/pallas_call | solution.py:373
  52.7 35.5 %shard_map.136 = bf16[4,2,4,96,1152]{4,3,2,1,0:T(8,128)(2,1)} custom-call(bf16[4,96,1152]{2,1,0:T(8,128)(2,1)} %get-tuple-element.23.own), custom_call_target="tpu_custom_call" | custom-call | tf_op jit(solution)/shard_map/pallas_call | solution.py:139
  89.2 4.1 slice.129
  95.5 3.3 fusion.31
  100.4 3.7 slice.146
  108.1 1.6 copy.133
  109.6 1.6 copy.134
  111.5 2.5 copy.129
  114.0 1.7 copy.179
  116.4 2.8 fusion.3
  119.2 2.8 fusion.23
  122.1 1.4 copy-done.19
  124.5 1.3 multiply_reduce_fusion.8
  126.8 1.4 multiply_multiply_fusion
  138.1 24.7 %shard_map.137 = bf16[4,2,2,128,1152]{4,3,2,1,0:T(8,128)(2,1)} custom-call(bf16[2,128,1152]{2,1,0:T(8,128)(2,1)} %multiply_convert_fusion.own), custom_call_target="tpu_custom_call" | custom-call | tf_op jit(solution)/shard_map/pallas_call | solution.py:139
  164.5 6.7 %all-gather.3.cloned.1.call-done = bf16[2688,1152]{1,0:T(8,128)(2,1)} async-done(((bf16[672,1152]{1,0:T(8,128)(2,1)}), bf16[2688,1152]{1,0:T(8,128)(2,1)}) %all-gather.3.cloned.1.call-update) | async-done | bytes 6193168 | tf_op jit(solution)/shard_map/all_gather | solution.py:1316
  171.2 108.2 %shard_map.138 = (bf16[256,1152]{1,0:T(8,128)(2,1)}, f32[256,1152]{1,0:T(8,128)}, f32[8,1152]{1,0:T(8,128)}, bf16[4,560,1152]{2,1,0:T(8,128)(2,1)}, bf16[112,1152]{1,0:T(8,128)(2,1)}) custom-call(bf16[4,512,1152]{2,1,0:T(8,128)(2,1)} %bitcast.142, bf16[4,672,1152]{2,1,0:T(8,128)(2,1)} %bitcast.147, f32[256,1152]{1,0:T(8,128)} %bitcast.135, ...), custom_call_target="tpu_custom_call" | custom-call | tf_op jit(solution)/shard_map/pallas_call | solution.py:1209
  285.6 1.7 convolution_convert_fusion
  287.3 2.1 copy.178
  289.4 1.9 fusion.4
  295.6 2.3 bitcast_convert_fusion
  297.9 50.5 %shard_map.139 = (f32[2,128,512]{2,1,0:T(8,128)}, bf16[4,32,1152]{2,1,0:T(8,128)(2,1)}) custom-call(bf16[4,2,128,512]{3,2,1,0:T(8,128)(2,1)} %bitcast.151, bf16[8,4,32,1152]{3,2,1,0:T(8,128)(2,1)} %bitcast.146), custom_call_target="tpu_custom_call" | custom-call | tf_op jit(solution)/shard_map/pallas_call | solution.py:480
  348.4 1.2 fusion.28
  355.7 3.4 fusion.17
  359.2 3.0 fusion
  362.3 27.2 %shard_map.140 = (bf16[4,48,1152]{2,1,0:T(8,128)(2,1)}, f32[40,128]{1,0:T(8,128)}) custom-call(bf16[8,4,48,1152]{3,2,1,0:T(8,128)(2,1)} %bitcast.155, f32[40,128]{1,0:T(8,128)} %bitcast.173), custom_call_target="tpu_custom_call" | custom-call | tf_op jit(solution)/shard_map/pallas_call | solution.py:677
  389.5 1.4 dynamic_slice.3
  390.9 1.9 pad_maximum_fusion.1.attn
  392.9 1.3 fusion.20
  394.2 28.9 %shard_map.141 = (bf16[288,1728]{1,0:T(8,128)(2,1)}, bf16[288,864]{1,0:T(8,128)(2,1)}, f32[320,288]{1,0:T(8,128)}) custom-call(bf16[560,1152]{1,0:T(8,128)(2,1)} %bitcast.160, bf16[112,1152]{1,0:T(8,128)(2,1)} %get-tuple-element.29.early, bf16[4,80,1152]{2,1,0:T(8,128)(2,1)} %pad_maximum_fusion.1.attn), custom_call_target="tpu_custom_call" | custom-call | tf_op jit(solution)/shard_map/pallas_call | solution.py:772
  424.0 1.7 slice.153
  425.7 2.7 convert_bitcast_fusion.1
  (215 shorter events, 47.3 us)
Async XLA Ops:
  7.2 164.0 %all-gather.3.cloned.1.call-start = ((), (), s32[]{:S(2)}) async-start(), calls=%async_computation.2 | async-start | bytes 7741440 | tf_op jit(solution)/shard_map/all_gather | solution.py:1316
  52.2 342.0 %reduce-scatter.2.cloned.1.call-start = ((), (), s32[]{:S(2)}) async-start(), calls=%async_computation.1 | async-start | bytes 6451200 | tf_op jit(solution)/shard_map/reduce_scatter | solution.py:1479
  89.1 4.1 copy-start.12
  93.5 5.3 %copy-start.50 = (f32[2,128]{1,0:T(2,128)}, f32[2,128]{1,0:T(2,128)S(1)}, u32[]{:S(2)}) copy-start(f32[2,128]{1,0:T(2,128)S(1)} %fusion.21) | copy-start | bytes 3076
  94.3 4.4 %copy-start.36 = (f32[1152]{0:T(1024)}, f32[1152]{0:T(1024)S(1)}, u32[]{:S(2)}) copy-start(f32[1152]{0:T(1024)S(1)} %get-tuple-element.92) | copy-start | bytes 13828
  95.5 3.3 copy-start.53
  98.8 1.6 copy-start.20
  100.4 30.0 %copy-start.4 = (f32[2,128,1024]{2,1,0:T(8,128)}, f32[2,128,1024]{2,1,0:T(8,128)S(1)}, u32[]{:S(2)}) copy-start(f32[2,128,1024]{2,1,0:T(8,128)S(1)} %slice.142) | copy-start | bytes 3145732
  100.4 10.8 %copy-start.11 = (bf16[4,2,128,1152]{3,2,1,0:T(8,128)(2,1)S(1)}, bf16[4,2,128,1152]{3,2,1,0:T(8,128)(2,1)}, u32[]{:S(2)}) copy-start(bf16[4,2,128,1152]{3,2,1,0:T(8,128)(2,1)} %get-tuple-element.22) | copy-start | bytes 7077892
  106.3 1.8 copy-start.48
  124.0 1.8 copy-start.55
  124.0 2.8 copy-start.43
  124.4 5.5 %copy-start.39 = (f32[2,128,4]{1,2,0:T(4,128)}, f32[2,128,4]{1,2,0:T(4,128)S(1)}, u32[]{:S(2)}) copy-start(f32[2,128,4]{1,2,0:T(4,128)S(1)} %copy.135) | copy-start | bytes 12292
  129.8 2.1 copy-start.16
  133.1 1.8 copy-start.14
  133.8 2.1 copy-start.24
  137.0 25.9 %copy-start.2 = (f32[2,128,1152]{2,1,0:T(8,128)}, f32[2,128,1152]{2,1,0:T(8,128)S(1)}, u32[]{:S(2)}) copy-start(f32[2,128,1152]{2,1,0:T(8,128)S(1)} %get-tuple-element.78) | copy-start | bytes 3538948
  138.1 24.8 %copy-start.42 = (f32[1152]{0:T(1024)S(1)}, f32[1152]{0:T(1024)}, u32[]{:S(2)}) copy-start(f32[1152]{0:T(1024)} %get-tuple-element.89) | copy-start | bytes 13828
  279.4 1.6 copy-start.10
  283.7 2.0 copy-start.15
  285.6 3.7 copy-start.1
  294.1 1.6 copy-start.25
  352.6 1.9 copy-start.52
  352.8 2.9 copy-start.38
  352.8 2.9 copy-start.54
  355.7 3.4 copy-start.45
  359.2 3.1 copy-start.46
  362.2 28.7 %copy-start.51 = (f32[2,128]{1,0:T(2,128)S(1)}, f32[2,128]{1,0:T(2,128)}, u32[]{:S(2)}) copy-start(f32[2,128]{1,0:T(2,128)} %copy-done.50) | copy-start | bytes 3076
  362.3 28.7 %copy-start.33 = (bf16[4,32,1152]{2,1,0:T(8,128)(2,1)S(1)}, bf16[4,32,1152]{2,1,0:T(8,128)(2,1)}, u32[]{:S(2)}) copy-start(bf16[4,32,1152]{2,1,0:T(8,128)(2,1)} %get-tuple-element.32) | copy-start | bytes 884740
  389.5 3.4 copy-start.7
  425.7 2.7 copy-start.32
  428.5 1.8 copy-start.30
  (28 other events, 29.0 us)
Sparse Core Ops, SparseCore 0:
  52.3 118.7 all-gather.2
  279.5 103.6 reduce-scatter.1

commit v7 on v6

--- a/solution.py
+++ b/solution.py
@@ -149,8 +149,8 @@
 
 
 def weights_in_kernel(
-    lay, reach, tokens, pack, pairs, lows, attn_out, ffn_out, earlier_out,
-    hops_land, attn_land, own, stack, land, keep_sem, hop_send, hop_recv, low_send, low_recv, attn_send, attn_recv, send, recv, chain_send, chain_recv,
+    lay, reach, tokens, qkv, out_t, gains, pairs, lows, attn_out, ffn_out, earlier_out,
+    pack, hops_land, attn_land, own, stack, land, keep_sem, hop_send, hop_recv, low_send, low_recv, attn_send, attn_recv, send, recv, chain_send, chain_recv,
 ):
     n, hi, lo = lay.dp, lay.hi, lay.lo
     dp = lax.axis_index("dp")
@@ -180,6 +180,14 @@
     sides = jnp.where(has_right, 1, 0) + jnp.where(has_left, 1, 0)
     pl.semaphore_wait(barrier, n - 1 + sides + lo - 1)
 
+    rows = pack.shape[1]
+    last = jnp.concatenate([gains[...], jnp.zeros((1, cols - gains.shape[1]), jnp.float32)], axis=1)
+    used = qkv.shape[0] + out_t.shape[1]
+    first_row = lax.broadcasted_iota(jnp.int32, (n * rows - used, cols), 0) == 0
+    block = jnp.concatenate(
+        [qkv[...], out_t[...].T, jnp.where(first_row, last, 0.0)], axis=0
+    ).astype(jnp.bfloat16)
+    pack[...] = block.reshape(n, rows, cols)
     attn_pushes = []
     for k in range(1, n):
         push = remote(
@@ -352,15 +360,17 @@
             feed_forward_push(q).wait_send()
 
 
-def weights_in(lay, reach, tokens, pack, pairs, lows, collective_id):
+def weights_in(lay, reach, tokens, qkv, out_t, gains, pairs, lows, collective_id):
     n = lay.dp
     cols, per = lows.shape[0], lows.shape[1] // n
-    rows = pack.shape[1]
+    block = 16 * n
+    rows = -(-(qkv.shape[0] + out_t.shape[1] + 1) // block) * 16
     padded = -(-per // 32) * 32
     vmem = pl.BlockSpec(memory_space=pltpu.VMEM)
     dma = pltpu.SemaphoreType.DMA
     hops = min(lay.hi - 1, (reach + lay.lo - 1) // lay.lo)
     scratch = [
+        pltpu.VMEM((n, rows, cols), jnp.bfloat16),
         pltpu.VMEM((hops + 1,) + tokens.shape, tokens.dtype),
         pltpu.VMEM((n, rows, cols), jnp.bfloat16),
         pltpu.VMEM((rows, n * cols), jnp.bfloat16),
@@ -377,13 +387,13 @@
             jax.ShapeDtypeStruct((3 * padded, n * cols), jnp.bfloat16),
             jax.ShapeDtypeStruct((reach,) + tokens.shape, tokens.dtype),
         ),
-        in_specs=[vmem] * 4,
+        in_specs=[vmem] * 6,
         out_specs=(pl.BlockSpec(memory_space=pl.ANY), vmem, vmem),
         scratch_shapes=scratch,
         compiler_params=pltpu.CompilerParams(
             collective_id=collective_id, has_side_effects=True, vmem_limit_bytes=VMEM_LIMIT
         ),
-    )(tokens, pack, pairs, lows)
+    )(tokens, qkv, out_t, gains, pairs, lows)
 
 
 def later_kernel(
@@ -434,10 +444,10 @@
                     across(h, other).start()
     group.start()
     stages = group.stages()
-    every = -(-len(stages) // (hops + 1))
+    bounds = [0, 1] + [1 + (len(stages) - 1) * (i + 1) // hops for i in range(hops)]
     for h in range(hops, -1, -1):
         turn = hops - h
-        for calls in stages[turn * every : (turn + 1) * every]:
+        for calls in stages[bounds[turn] : bounds[turn + 1]]:
             for call in calls:
                 call()
         out[...] = jnp.zeros_like(out)
@@ -654,7 +664,7 @@
         if i < len(gain_peers):
             gains_copy(i).start()
         else:
-            gains_out[...] = gains_sum[i]
+            gains_out[...] = gains_sum[i, pl.ds(dp * lay.ctx + ctx, 1)]
 
     group.start()
     stages = group.stages()
@@ -678,7 +688,7 @@
         partial(sum_group_kernel, lay),
         out_shape=(
             jax.ShapeDtypeStruct((lay.hi, rows, D), jnp.bfloat16),
-            jax.ShapeDtypeStruct(gains.shape, jnp.float32),
+            jax.ShapeDtypeStruct((1, gains.shape[1]), jnp.float32),
         ),
         in_specs=[vmem] * 2,
         out_specs=(vmem,) * 2,
@@ -695,7 +705,7 @@
     )(parts, gains)
 
 
-def grads_out_kernel(lay, rows, early, attn, pairs_out, lows_out, attn_out, stack, land, hi_land, last, last_land,
+def grads_out_kernel(lay, rows, early, plane_qkv, plane_out, pairs_out, lows_out, qkv_out, out_t, attn, stack, land, hi_land, last, last_land,
                      send, recv, hi_send, hi_recv, last_send, last_recv):
     n, hi, lo = lay.dp, lay.hi, lay.lo
     dp = lax.axis_index("dp")
@@ -708,6 +718,8 @@
     attn_rows = attn.shape[1]
     hi_peers = [(dp, lax.rem(high + k, hi) * lo + low) for k in range(1, hi)]
     greet([(lax.rem(dp + k, n), ctx) for k in range(1, n)] + hi_peers)
+    attn[:, : plane_qkv.shape[1]] = plane_qkv[...]
+    attn[:, plane_qkv.shape[1] :] = plane_out[...]
     hi_pushes = []
     for k in range(1, hi):
         push = remote(
@@ -757,16 +769,18 @@
         lows_out[:, per * q : per * (q + 1)] = land[2, q, :, :per]
     for push in last_pushes:
         push.wait_recv()
-    for q in range(n):
-        attn_out[q * attn_rows : (q + 1) * attn_rows] = last_land[q].astype(jnp.float32)
+    out_rows = out_t.shape[1]
+    out_part, qkv_part = plane_out.shape[1], plane_qkv.shape[1]
+    qkv_out[...] = last_land[:, :qkv_part].reshape(n * qkv_part, cols)[: qkv_out.shape[0]].astype(jnp.float32)
+    out_t[...] = last_land[:, qkv_part:].reshape(n * out_part, cols)[:out_rows].astype(jnp.float32).T
     for push in hi_pushes + pushes + last_pushes:
         push.wait_send()
 
 
-def grads_out(lay, rows, early, attn, per, collective_id):
+def grads_out(lay, rows, early, plane_qkv, plane_out, per, qkv_rows, out_rows, collective_id):
     padded = (rows.shape[0] + early.shape[0]) // 3
     n, cols = lay.dp, rows.shape[1] // lay.dp
-    attn_rows = attn.shape[1]
+    attn_rows = plane_qkv.shape[1] + plane_out.shape[1]
     vmem = pl.BlockSpec(memory_space=pltpu.VMEM)
     dma = pltpu.SemaphoreType.DMA
     return pl.pallas_call(
@@ -774,11 +788,13 @@
         out_shape=(
             jax.ShapeDtypeStruct((cols, n * 2 * per), jnp.bfloat16),
             jax.ShapeDtypeStruct((cols, n * per), jnp.bfloat16),
-            jax.ShapeDtypeStruct((n * attn_rows, cols), jnp.float32),
+            jax.ShapeDtypeStruct((qkv_rows, cols), jnp.float32),
+            jax.ShapeDtypeStruct((cols, out_rows), jnp.float32),
         ),
-        in_specs=[vmem] * 3,
-        out_specs=(vmem,) * 3,
+        in_specs=[vmem] * 4,
+        out_specs=(vmem,) * 4,
         scratch_shapes=[
+            pltpu.VMEM((lay.hi, attn_rows, D), jnp.bfloat16),
             pltpu.VMEM((3, n, cols, -(-padded // 128) * 128), jnp.bfloat16),
             pltpu.VMEM((3, n, cols, -(-padded // 128) * 128), jnp.bfloat16),
             pltpu.VMEM((max(1, lay.hi - 1), attn_rows, D), jnp.bfloat16),
@@ -791,7 +807,7 @@
         compiler_params=pltpu.CompilerParams(
             collective_id=collective_id, has_side_effects=True, vmem_limit_bytes=VMEM_LIMIT
         ),
-    )(rows, early, attn)
+    )(rows, early, plane_qkv, plane_out)
 
 
 def in_tiles(total, size, body, begin=0):
@@ -1300,15 +1316,13 @@
     used = qkv_rows + out_rows + 1
     block = 16 * lay.dp
     pack_rows = -(-used // block) * block
-    gain_row = jnp.pad(gains, (0, cols - gains.shape[0]))[None]
-    pack = jnp.concatenate(
-        [w_qkv, w_out, gain_row, jnp.zeros((pack_rows - used, cols), jnp.float32)], axis=0
-    ).astype(jnp.bfloat16)
     plane, ffn_rows, earlier_tokens = weights_in(
         lay,
         reach,
         tokens,
-        pack.reshape(lay.dp, pack_rows // lay.dp, cols),
+        w_qkv,
+        w_out.T,
+        gains[None],
         w_gate_up.T,
         w_down.T,
         5,
@@ -1473,16 +1487,14 @@
         ]
     )
     plane_qkv, gains_sum = sum_group(
-        lay, blocks_of(grad_w_qkv, qkv_rows), grad_gain_all.reshape(-1, 128), 8
-    )
-    plane_attn = jnp.concatenate([plane_qkv, plane_out], axis=1)
+        lay, blocks_of(grad_w_qkv, qkv_rows), grad_gain_all.reshape(-1, gains.shape[0]), 8
+    )
     owned = lax.psum_scatter(grad_ffn, "ctx", scatter_dimension=0, axis_index_groups=lay.hi_groups)
-    part_gate_up, part_down, part_attn = grads_out(lay, owned, early_down, plane_attn, per, 9)
-    part_attn = part_attn.reshape(lay.dp, -1, cols)
-    part_qkv = part_attn[:, : plane_qkv.shape[1]].reshape(-1, cols)[:qkv_rows]
-    part_out = part_attn[:, plane_qkv.shape[1] :].reshape(-1, cols)[:out_rows]
-    place = (lax.axis_index("dp") * lay.ctx + lax.axis_index("ctx")) * gains.shape[0]
-    part_gains = lax.dynamic_slice_in_dim(gains_sum.reshape(-1), place, gains.shape[0])
+    part_gate_up, part_down, part_qkv, part_out = grads_out(
+        lay, owned, early_down, plane_qkv, plane_out, per, qkv_rows, out_rows, 9
+    )
+    part_out = part_out.T
+    part_gains = gains_sum[0]
     part_gate_up = part_gate_up.astype(jnp.float32).T
     part_down = part_down.astype(jnp.float32).T
     return (result, grad_input, part_qkv, part_out, part_gate_up, part_down, part_gains)

time: 444 us -> 436 us (0.982)
  other arithmetic: 34.8 us -> 29.6 us
    pallas_call x1, Pallas kernels: 27.2 us -> 34.8 us  [sum_group(): pl.pallas_call(partial(sum_group_kernel, lay), out_shape=(jax.ShapeDtypeS...]
    pallas_call x1, Pallas kernels: 50.5 us -> 43.6 us  [later_sum(): pl.pallas_call(partial(later_kernel, lay, reach), out_shape=(jax.ShapeDty...]
    unnamed x125 -> x127, local copies, waits for them, and re-layouts: 17.2 us -> 17.4 us
  transfers between devices with their start and end apart: 2 -> 2, of which waited for: 1 -> 1; matrix products, arithmetic and copies ran while one was open for 17% -> 16% of each run, Pallas kernels for 31% -> 32%
where the time goes in v7:
time: 436 us; the launch traced here: 431 us
  Pallas kernels  317 us (73%)
  local copies, waits for them, and re-layouts  38.4 us (9%)
  other arithmetic  29.6 us (7%)
  matrix products  22.4 us (5%)
  between operations  15.2 us (3%)
  waiting for transfers between devices  8.19 us (2%)
    pallas_call x1, Pallas kernels, feed_forward(): pl.pallas_call(partial(feed_forward_kernel, lay), out_shape=(jax.ShapeDty...  108 us
    pallas_call x2, Pallas kernels, gather_group(): pl.pallas_call(partial(gather_group_kernel, lay, slot), out_shape=jax.Sha...  60.2 us
    pallas_call x1, Pallas kernels, later_sum(): pl.pallas_call(partial(later_kernel, lay, reach), out_shape=(jax.ShapeDty...  43.6 us
    pallas_call x1, Pallas kernels, weights_in(): pl.pallas_call(partial(weights_in_kernel, lay, reach), out_shape=(jax.Sha...  41.5 us
    pallas_call x1, Pallas kernels, sum_group(): pl.pallas_call(partial(sum_group_kernel, lay), out_shape=(jax.ShapeDtypeS...  34.8 us
    pallas_call x1, Pallas kernels, grads_out(): pl.pallas_call(partial(grads_out_kernel, lay), out_shape=(jax.ShapeDtypeS...  28.8 us
    dot_general x7, matrix products, contract(): lax.dot_general(left, right, ((dims_left, dims_right), ((), ())), preferr...  17.4 us
    unnamed x127, local copies, waits for them, and re-layouts  17.4 us
  transfers between devices with their start and end apart: 2, of which 1 were waited for; matrix products, arithmetic and copies ran while one was open for 16% of the time, Pallas kernels for 32%

profile of v7, /device:TPU:9, one launch (start us, length us, event | category | flops | bytes accessed | tf_op | source)
XLA Modules:
  0.0 431.2 jit_solution(9262331187256842171)
XLA Ops:
  7.2 41.5 %shard_map.135 = (bf16[4,96,1152]{2,1,0:T(8,128)(2,1)}, bf16[672,1152]{1,0:T(8,128)(2,1)}, bf16[4,2,128,1152]{3,2,1,0:T(8,128)(2,1)}) custom-call(bf16[2,128,1152]{2,1,0:T(8,128)(2,1)} %tokens.1, f32[192,288]{1,0:T(8,128)} %qkv.1, f32[288,128]{1,0:T(8,128)} %bitcast.163, f32[1,160]{1,0:T(1,128)} %bitcast.171, f32[288,1728]{1,0:T(8,128)} %bitcast.157, ...), custom_call_target="tpu_custom_call" | custom-call | tf_op jit(solution)/shard_map/pallas_call | solution.py:383
  49.0 35.5 %shard_map.136 = bf16[4,2,4,96,1152]{4,3,2,1,0:T(8,128)(2,1)} custom-call(bf16[4,96,1152]{2,1,0:T(8,128)(2,1)} %get-tuple-element.24.own), custom_call_target="tpu_custom_call" | custom-call | tf_op jit(solution)/shard_map/pallas_call | solution.py:139
  85.4 4.1 slice.121
  91.2 3.3 fusion.31
  95.6 3.7 slice.138
  101.6 2.0 convert_bitcast_fusion
  103.6 2.5 copy.120
  106.2 2.2 fusion.1
  108.5 2.9 fusion.3
  111.3 2.8 fusion.23
  114.2 1.4 copy-done.17
  117.1 1.6 copy.126
  118.7 1.3 multiply_reduce_fusion.8
  120.1 1.6 multiply_cosine_fusion
  121.7 1.4 multiply_multiply_fusion
  132.9 24.8 %shard_map.137 = bf16[4,2,2,128,1152]{4,3,2,1,0:T(8,128)(2,1)} custom-call(bf16[2,128,1152]{2,1,0:T(8,128)(2,1)} %multiply_convert_fusion.own), custom_call_target="tpu_custom_call" | custom-call | tf_op jit(solution)/shard_map/pallas_call | solution.py:139
  158.4 1.2 copy.131.valid
  159.6 8.2 %all-gather.3.cloned.1.call-done = bf16[2688,1152]{1,0:T(8,128)(2,1)} async-done(((bf16[672,1152]{1,0:T(8,128)(2,1)}), bf16[2688,1152]{1,0:T(8,128)(2,1)}) %all-gather.3.cloned.1.call-update) | async-done | bytes 6193168 | tf_op jit(solution)/shard_map/all_gather | solution.py:1330
  167.7 108.1 %shard_map.138 = (bf16[256,1152]{1,0:T(8,128)(2,1)}, f32[256,1152]{1,0:T(8,128)}, f32[8,1152]{1,0:T(8,128)}, bf16[4,560,1152]{2,1,0:T(8,128)(2,1)}, bf16[112,1152]{1,0:T(8,128)(2,1)}) custom-call(bf16[4,512,1152]{2,1,0:T(8,128)(2,1)} %bitcast.140, bf16[4,672,1152]{2,1,0:T(8,128)(2,1)} %bitcast.145, f32[256,1152]{1,0:T(8,128)} %bitcast.133, ...), custom_call_target="tpu_custom_call" | custom-call | tf_op jit(solution)/shard_map/pallas_call | solution.py:1225
  275.9 1.2 copy-done.3
  282.1 1.7 convolution_convert_fusion
  283.8 2.0 copy.168
  285.8 1.9 fusion.4
  292.1 2.3 bitcast_convert_fusion
  294.4 43.6 %shard_map.139 = (f32[2,128,512]{2,1,0:T(8,128)}, bf16[4,32,1152]{2,1,0:T(8,128)(2,1)}) custom-call(bf16[4,2,128,512]{3,2,1,0:T(8,128)(2,1)} %bitcast.149, bf16[8,4,32,1152]{3,2,1,0:T(8,128)(2,1)} %bitcast.144), custom_call_target="tpu_custom_call" | custom-call | tf_op jit(solution)/shard_map/pallas_call | solution.py:490
  338.0 1.2 fusion.28
  345.3 3.4 fusion.17
  349.4 3.0 fusion
  352.5 34.8 %shard_map.140 = (bf16[4,48,1152]{2,1,0:T(8,128)(2,1)}, f32[1,160]{1,0:T(1,128)}) custom-call(bf16[8,4,48,1152]{3,2,1,0:T(8,128)(2,1)} %bitcast.153, f32[32,160]{1,0:T(8,128)} %reshape.596.gains), custom_call_target="tpu_custom_call" | custom-call | tf_op jit(solution)/shard_map/pallas_call | solution.py:687
  387.3 1.3 fusion.20
  388.6 28.8 %shard_map.141 = (bf16[288,1728]{1,0:T(8,128)(2,1)}, bf16[288,864]{1,0:T(8,128)(2,1)}, f32[192,288]{1,0:T(8,128)}, f32[288,128]{1,0:T(8,128)}) custom-call(bf16[560,1152]{1,0:T(8,128)(2,1)} %bitcast.158, bf16[112,1152]{1,0:T(8,128)(2,1)} %get-tuple-element.30.early, bf16[4,48,1152]{2,1,0:T(8,128)(2,1)} %get-tuple-element.32.plane_qkv, ...), custom_call_target="tpu_custom_call" | custom-call | tf_op jit(solution)/shard_map/pallas_call | solution.py:786
  417.4 2.7 convert_bitcast_fusion.1
  (205 shorter events, 38.1 us)
Async XLA Ops:
  7.2 160.6 %all-gather.3.cloned.1.call-start = ((), (), s32[]{:S(2)}) async-start(), calls=%async_computation.2 | async-start | bytes 7741440 | tf_op jit(solution)/shard_map/all_gather | solution.py:1330
  48.8 339.9 %reduce-scatter.2.cloned.1.call-start = ((), (), s32[]{:S(2)}) async-start(), calls=%async_computation.1 | async-start | bytes 6451200 | tf_op jit(solution)/shard_map/reduce_scatter | solution.py:1492
  85.4 4.1 copy-start.11
  89.7 4.7 %copy-start.48 = (f32[2,128]{1,0:T(2,128)}, f32[2,128]{1,0:T(2,128)S(1)}, u32[]{:S(2)}) copy-start(f32[2,128]{1,0:T(2,128)S(1)} %fusion.21) | copy-start | bytes 3076
  90.6 3.9 copy-start.34
  91.1 9.0 %copy-start.41 = (f32[256]{0:T(256)}, f32[256]{0:T(256)S(1)}, u32[]{:S(2)}) copy-start(f32[256]{0:T(256)S(1)} %get-tuple-element.68) | copy-start | bytes 3076
  91.1 8.6 %copy-start.54 = (f32[128]{0:T(128)}, f32[128]{0:T(128)S(1)}, u32[]{:S(2)}) copy-start(f32[128]{0:T(128)S(1)} %negate_power_fusion) | copy-start | bytes 1540
  91.2 3.3 copy-start.52
  94.5 5.6 %copy-start.18 = (f32[2,128,1536]{2,1,0:T(8,128)}, f32[2,128,1536]{2,1,0:T(8,128)S(1)}, u32[]{:S(2)}) copy-start(f32[2,128,1536]{2,1,0:T(8,128)S(1)} %fusion.31) | copy-start | bytes 4718596
  94.6 5.5 %copy-start.50 = (f32[2,128]{1,0:T(2,128)}, f32[2,128]{1,0:T(2,128)S(1)}, u32[]{:S(2)}) copy-start(f32[2,128]{1,0:T(2,128)S(1)} %multiply_reduce_fusion.11) | copy-start | bytes 3076
  95.6 29.6 %copy-start.4 = (f32[2,128,1024]{2,1,0:T(8,128)}, f32[2,128,1024]{2,1,0:T(8,128)S(1)}, u32[]{:S(2)}) copy-start(f32[2,128,1024]{2,1,0:T(8,128)S(1)} %slice.134) | copy-start | bytes 3145732
  103.6 2.5 copy-start.29
  106.1 2.3 copy-start.35
  117.1 4.6 %copy-start.42 = (f32[256]{0:T(256)S(1)}, f32[256]{0:T(256)}, u32[]{:S(2)}) copy-start(f32[256]{0:T(256)} %copy-done.41) | copy-start | bytes 3076
  124.6 2.2 copy-start.14
  127.9 1.8 copy-start.12
  128.6 2.1 copy-start.22
  131.7 26.0 %copy-start.2 = (f32[2,128,1152]{2,1,0:T(8,128)}, f32[2,128,1152]{2,1,0:T(8,128)S(1)}, u32[]{:S(2)}) copy-start(f32[2,128,1152]{2,1,0:T(8,128)S(1)} %get-tuple-element.52) | copy-start | bytes 3538948
  132.9 24.8 %copy-start.40 = (f32[1152]{0:T(1024)S(1)}, f32[1152]{0:T(1024)}, u32[]{:S(2)}) copy-start(f32[1152]{0:T(1024)} %get-tuple-element.63) | copy-start | bytes 13828
  275.9 1.6 copy-start.10
  280.2 2.0 copy-start.13
  282.1 3.7 copy-start.1
  290.5 1.6 copy-start.23
  342.2 1.9 copy-start.51
  342.3 2.9 copy-start.36
  342.3 2.9 copy-start.53
  352.5 34.8 %copy-start.49 = (f32[2,128]{1,0:T(2,128)S(1)}, f32[2,128]{1,0:T(2,128)}, u32[]{:S(2)}) copy-start(f32[2,128]{1,0:T(2,128)} %copy-done.48) | copy-start | bytes 3076
  352.5 34.8 %copy-start.7 = (f32[2,128,1152]{2,1,0:T(8,128)S(1)}, f32[2,128,1152]{2,1,0:T(8,128)}, u32[]{:S(2)}) copy-start(f32[2,128,1152]{2,1,0:T(8,128)} %copy-done.6) | copy-start | bytes 3538948
  417.4 2.7 copy-start.30
  420.2 2.1 copy-start.31
  420.2 2.8 copy-start.33
  421.2 2.4 copy-start.57
  (28 other events, 29.0 us)
Sparse Core Ops, SparseCore 0:
  48.9 118.7 all-gather.2
  276.0 103.5 reduce-scatter.1

commit v8 on v7

--- a/solution.py
+++ b/solution.py
@@ -397,9 +397,11 @@
 
 
 def later_kernel(
-    lay, reach, pieces, parts, out, group_out, low_land, moved, arrived, chain_send, chain_recv, low_send, low_recv, *scratch
+    lay, reach, pieces, parts, early, out, group_out, early_out, low_land, moved, arrived, early_stack,
+    early_send, early_recv, chain_send, chain_recv, low_send, low_recv, *scratch
 ):
     group = GroupSum(lay, parts, group_out, *scratch)
+    groups = [group]
     hi, lo = lay.hi, lay.lo
     dp = lax.axis_index("dp")
     ctx = lax.axis_index("ctx")
@@ -409,80 +411,118 @@
     has_right, has_left = high < hi - 1, high > 0
     low_peers = [(dp, high * lo + other) for other in range(lo)]
     barrier = pltpu.get_barrier_semaphore()
-    for device in group.peers:
+    n = lay.dp
+    dp_peers = [(lax.rem(dp + k, n), ctx) for k in range(1, n)]
+    for device in group.low_peers[1:] + dp_peers:
         pl.semaphore_signal(barrier, inc=1, device_id=device, device_id_type=MESH)
     for there, device in [(has_right, right), (has_left, left)]:
         @pl.when(there)
         def _():
             pl.semaphore_signal(barrier, inc=1, device_id=device, device_id_type=MESH)
     sides = jnp.where(has_right, 1, 0) + jnp.where(has_left, 1, 0)
-    pl.semaphore_wait(barrier, sides + len(group.peers))
+    pl.semaphore_wait(barrier, sides + lo - 1 + n - 1)
 
     def wanted(h, owner, reader):
         distance = h * lo + reader - owner
         return (distance >= 1) & (distance <= reach) & (high >= h)
 
-    def across(h, other):
+    span = out.shape[0] // 2
+
+    def part_of(ref, part):
+        return ref.at[pl.ds(part * span, span)]
+
+    def across(h, other, part):
         return remote(
-            pieces.at[reach - (h * lo + low - other)], low_land.at[h, low], low_send.at[h, other],
-            low_recv.at[h, low], low_peers[other],
-        )
-
-    def from_low(h, other):
+            part_of(pieces.at[reach - (h * lo + low - other)], part), part_of(low_land.at[h, low], part),
+            low_send.at[h, other, part], low_recv.at[h, low, part], low_peers[other],
+        )
+
+    def from_low(h, other, part):
         return remote(
-            pieces.at[0], low_land.at[h, other], low_send.at[h, other], low_recv.at[h, other], low_peers[other]
-        )
-
-    def hop(h):
-        return remote(moved.at[h], arrived.at[h - 1], chain_send.at[h], chain_recv.at[h - 1], left)
-
-    for h in range(hops, -1, -1):
+            part_of(pieces.at[0], part), part_of(low_land.at[h, other], part), low_send.at[h, other, part],
+            low_recv.at[h, other, part], low_peers[other],
+        )
+
+    def hop(h, part):
+        return remote(
+            part_of(moved.at[h], part), part_of(arrived.at[h - 1], part), chain_send.at[h, part],
+            chain_recv.at[h - 1, part], left,
+        )
+
+    def pass_on(h, part):
+        block = pl.ds(part * span, span)
+        out[block] = jnp.zeros((span,) + out.shape[1:], out.dtype)
+        if h and h * lo <= reach:
+            out[block] += pieces[reach - h * lo, block].astype(jnp.float32)
         for other in range(lo):
             if lo > 1:
-                @pl.when((low != other) & wanted(h, other, low))
+                @pl.when((low != other) & wanted(h, low, other))
                 def _():
-                    across(h, other).start()
-    group.start()
-    stages = group.stages()
+                    from_low(h, other, part).wait_recv()
+                    out[block] += low_land[h, other, block].astype(jnp.float32)
+        if h < hops:
+            @pl.when(has_right & (high >= h))
+            def _():
+                hop(h + 1, part).wait_recv()
+                out[block] += arrived[h, block].astype(jnp.float32)
+        if h:
+            @pl.when(high >= h)
+            def _():
+                moved[h, block] = out[block].astype(moved.dtype)
+                hop(h, part).start()
+
+    for h in range(hops, -1, -1):
+        for part in range(2):
+            for other in range(lo):
+                if lo > 1:
+                    @pl.when((low != other) & wanted(h, other, low))
+                    def _():
+                        across(h, other, part).start()
+    for each in groups:
+        each.start()
+    cols, wide = early_stack.shape[1:]
+    whole = early[...]
+    if wide > early.shape[0]:
+        blank = jnp.zeros((wide - early.shape[0], n * cols), early.dtype)
+        whole = jnp.concatenate([whole, blank], axis=0)
+    early_stack[...] = whole.T.reshape(n, cols, wide)
+    early_pushes = []
+    for k in range(1, n):
+        push = remote(
+            early_stack.at[lax.rem(dp + k, n)], early_out.at[dp], early_send.at[k], early_recv.at[k], dp_peers[k - 1]
+        )
+        push.start()
+        early_pushes.append(push)
+    early_out[dp] = early_stack[dp]
+    stages = groups[0].stages()
     bounds = [0, 1] + [1 + (len(stages) - 1) * (i + 1) // hops for i in range(hops)]
     for h in range(hops, -1, -1):
         turn = hops - h
         for calls in stages[bounds[turn] : bounds[turn + 1]]:
             for call in calls:
                 call()
-        out[...] = jnp.zeros_like(out)
-        if h and h * lo <= reach:
-            out[...] += pieces[reach - h * lo].astype(jnp.float32)
-        for other in range(lo):
-            if lo > 1:
-                @pl.when((low != other) & wanted(h, low, other))
+        for part in range(2):
+            pass_on(h, part)
+    for h in range(hops + 1):
+        for part in range(2):
+            if h:
+                @pl.when(high >= h)
                 def _():
-                    from_low(h, other).wait_recv()
-                    out[...] += low_land[h, other].astype(jnp.float32)
-        if h < hops:
-            @pl.when(has_right & (high >= h))
-            def _():
-                hop(h + 1).wait_recv()
-                out[...] += arrived[h].astype(jnp.float32)
-        if h:
-            @pl.when(high >= h)
-            def _():
-                moved[h] = out[...].astype(moved.dtype)
-                hop(h).start()
-    for h in range(hops + 1):
-        if h:
-            @pl.when(high >= h)
-            def _():
-                hop(h).wait_send()
-        for other in range(lo):
-            if lo > 1:
-                @pl.when((low != other) & wanted(h, other, low))
-                def _():
-                    across(h, other).wait_send()
-    group.finish()
-
-
-def later_sum(lay, reach, pieces, parts, collective_id):
+                    hop(h, part).wait_send()
+            for other in range(lo):
+                if lo > 1:
+                    @pl.when((low != other) & wanted(h, other, low))
+                    def _():
+                        across(h, other, part).wait_send()
+    for each in groups:
+        each.finish()
+    for push in early_pushes:
+        push.wait()
+
+
+def later_sum(lay, reach, pieces, parts, early, collective_id):
+    n = lay.dp
+    early_shape = (n, early.shape[1] // n, -(-early.shape[0] // 128) * 128)
     hops = min(lay.hi - 1, (reach + lay.lo - 1) // lay.lo)
     shape = pieces.shape[1:]
     vmem = pl.BlockSpec(memory_space=pltpu.VMEM)
@@ -492,21 +532,23 @@
         out_shape=(
             jax.ShapeDtypeStruct(shape, jnp.float32),
             jax.ShapeDtypeStruct((lay.hi, parts.shape[2], D), parts.dtype),
+            jax.ShapeDtypeStruct(early_shape, early.dtype),
         ),
-        in_specs=[vmem] * 2,
-        out_specs=(vmem,) * 2,
+        in_specs=[vmem] * 3,
+        out_specs=(vmem,) * 3,
         scratch_shapes=[
             pltpu.VMEM((hops + 1, lay.lo) + shape, pieces.dtype),
             pltpu.VMEM((hops + 1,) + shape, pieces.dtype),
             pltpu.VMEM((hops + 1,) + shape, pieces.dtype),
         ]
-        + [dma((hops + 1,))] * 2
-        + [dma((hops + 1, lay.lo))] * 2
+        + [pltpu.VMEM(early_shape, early.dtype), dma((n,)), dma((n,))]
+        + [dma((hops + 1, 2))] * 2
+        + [dma((hops + 1, lay.lo, 2))] * 2
         + GroupSum.scratch(lay, parts.shape[2]),
         compiler_params=pltpu.CompilerParams(
             collective_id=collective_id, has_side_effects=True, vmem_limit_bytes=VMEM_LIMIT
         ),
-    )(pieces, parts)
+    )(pieces, parts, early)
 
 
 def flip(index, bit):
@@ -705,7 +747,7 @@
     )(parts, gains)
 
 
-def grads_out_kernel(lay, rows, early, plane_qkv, plane_out, pairs_out, lows_out, qkv_out, out_t, attn, stack, land, hi_land, last, last_land,
+def grads_out_kernel(lay, rows, early, plane_qkv, plane_out, pairs_out, lows_out, qkv_out, out_t, attn, stack, land, low_stack, low_land, hi_land, last, last_land,
                      send, recv, hi_send, hi_recv, last_send, last_recv):
     n, hi, lo = lay.dp, lay.hi, lay.lo
     dp = lax.axis_index("dp")
@@ -713,7 +755,8 @@
     high, low = ctx // lo, lax.rem(ctx, lo)
     cols = lows_out.shape[0]
     per = lows_out.shape[1] // n
-    padded = (rows.shape[0] + early.shape[0]) // 3
+    half = rows.shape[0] // 5
+    padded = 2 * half
     wide = land.shape[3]
     attn_rows = attn.shape[1]
     hi_peers = [(dp, lax.rem(high + k, hi) * lo + low) for k in range(1, hi)]
@@ -727,23 +770,21 @@
         )
         push.start()
         hi_pushes.append(push)
-    blank = jnp.zeros((wide - padded, n * cols), jnp.bfloat16)
+    pushes = []
     for i in range(3):
-        pieces = [rows[i * padded : (i + 1) * padded if i < 2 else rows.shape[0]]]
-        if i == 2:
-            pieces.append(early[...])
-        if wide > padded:
-            pieces.append(blank)
-        whole = jnp.concatenate(pieces, axis=0) if len(pieces) > 1 else pieces[0]
-        stack[i] = whole.T.reshape(n, cols, wide)
-    pushes = []
-    for k in range(1, n):
-        target = lax.rem(dp + k, n)
-        push = remote(stack.at[:, target], land.at[:, dp], send.at[k], recv.at[k], (target, ctx))
-        push.start()
-        pushes.append(push)
-    for i in range(3):
-        land[i, dp] = stack[i, dp]
+        held, arriving = (stack.at[i], land.at[i]) if i < 2 else (low_stack, low_land)
+        lanes = held.shape[2]
+        whole = rows[i * padded : min((i + 1) * padded, rows.shape[0])]
+        if lanes > whole.shape[0]:
+            blank = jnp.zeros((lanes - whole.shape[0], n * cols), jnp.bfloat16)
+            whole = jnp.concatenate([whole, blank], axis=0)
+        held[...] = whole.T.reshape(n, cols, lanes)
+        for k in range(1, n):
+            target = lax.rem(dp + k, n)
+            push = remote(held.at[target], arriving.at[dp], send.at[i, k], recv.at[i, k], (target, ctx))
+            push.start()
+            pushes.append(push)
+        arriving[dp] = held[dp]
     total = attn[high].astype(jnp.float32)
     for k, push in enumerate(hi_pushes):
         push.wait_recv()
@@ -766,7 +807,8 @@
     for q in range(n):
         turns = dot_nn(land[0, q], spread[0]) + dot_nn(land[1, q], spread[1])
         pairs_out[:, 2 * per * q : 2 * per * (q + 1)] = turns.astype(jnp.bfloat16)
-        lows_out[:, per * q : per * (q + 1)] = land[2, q, :, :per]
+        lows_out[:, per * q : per * q + half] = low_land[q, :, :half]
+        lows_out[:, per * q + half : per * (q + 1)] = early[q, :, : per - half]
     for push in last_pushes:
         push.wait_recv()
     out_rows = out_t.shape[1]
@@ -778,7 +820,7 @@
 
 
 def grads_out(lay, rows, early, plane_qkv, plane_out, per, qkv_rows, out_rows, collective_id):
-    padded = (rows.shape[0] + early.shape[0]) // 3
+    padded = 2 * rows.shape[0] // 5
     n, cols = lay.dp, rows.shape[1] // lay.dp
     attn_rows = plane_qkv.shape[1] + plane_out.shape[1]
     vmem = pl.BlockSpec(memory_space=pltpu.VMEM)
@@ -795,13 +837,15 @@
         out_specs=(vmem,) * 4,
         scratch_shapes=[
             pltpu.VMEM((lay.hi, attn_rows, D), jnp.bfloat16),
-            pltpu.VMEM((3, n, cols, -(-padded // 128) * 128), jnp.bfloat16),
-            pltpu.VMEM((3, n, cols, -(-padded // 128) * 128), jnp.bfloat16),
+            pltpu.VMEM((2, n, cols, -(-padded // 128) * 128), jnp.bfloat16),
+            pltpu.VMEM((2, n, cols, -(-padded // 128) * 128), jnp.bfloat16),
+            pltpu.VMEM(early.shape, jnp.bfloat16),
+            pltpu.VMEM(early.shape, jnp.bfloat16),
             pltpu.VMEM((max(1, lay.hi - 1), attn_rows, D), jnp.bfloat16),
             pltpu.VMEM((n, attn_rows, cols), jnp.bfloat16),
             pltpu.VMEM((n, attn_rows, cols), jnp.bfloat16),
         ]
-        + [dma((n,))] * 2
+        + [dma((3, n))] * 2
         + [dma((lay.hi,))] * 2
         + [dma((n,))] * 2,
         compiler_params=pltpu.CompilerParams(
@@ -835,8 +879,8 @@
 
 
 def feed_forward_kernel(
-    lay, mid, weights, mixed, cotangent, valid, gain, result, grad_mid, grad_gain, grad_weights, early_sum,
-    late, late_sem, early, early_land, hi_send, hi_recv, w_gate, w_up, w_down, gate_t, up_t, act, slope, hidden, hidden_t, grads, parts, core_land, sums, via, landed,
+    lay, mid_in, weights, mixed, cotangent, valid, gain, result, grad_mid, grad_gain, grad_weights, early_sum,
+    mid, mid_sem, late, late_sem, early, early_land, hi_send, hi_recv, w_gate, w_up, w_down, gate_t, up_t, act, slope, hidden, hidden_t, grads, parts, core_land, sums, via, landed,
     total, dy, weight_sem, core_send, core_recv, share_send, share_recv,
     send, recv, via_send, via_recv, dy_send, dy_recv, dy_pass,
 ):
@@ -857,7 +901,11 @@
         for part in range(2)
         for h in range(hi)
     ]
-    for load in loads:
+    mid_loads = [
+        pltpu.make_async_copy(mid_in.at[p], mid.at[p], mid_sem.at[p]) for p in range(lay.chips)
+    ]
+    gates = len(loads) * 2 // 3
+    for load in mid_loads[:1] + loads[:gates] + mid_loads[1:] + loads[gates:]:
         load.start()
     peers = [lay.device(lay.offset(chip, k), core, high) for k in range(n)]
     owners = [lay.device(lay.offset(chip, k, -1), core, high) for k in range(n)]
@@ -1037,19 +1085,30 @@
         return [(first, min(most, group[0] + group[1] - first)) for first in range(group[0], sum(group), most)]
 
     quarter = units // 512 * 128
-    for load in loads:
+    for load in mid_loads[:1] + loads[:gates]:
         load.wait()
+    waiting = [mid_loads[1:], loads[gates:]]
+
+    def arrive(which):
+        while waiting[which]:
+            waiting[which].pop(0).wait()
+
     for run in runs(far):
+        if run[0] + run[1] > 1:
+            arrive(0)
         forward_units(run, 0, units)
+        arrive(1)
         forward_down(run)
     for k in bent:
         to_partner(0, k).start()
+    arrive(0)
     for i, run in enumerate(runs(near)):
         forward_units(run, 0, 2 * quarter)
         if i == 0:
             for k in bent:
                 add_core(0, k)
         forward_units(run, 2 * quarter, units)
+        arrive(1)
         forward_down(run)
     for k in straight:
         to_partner(0, k).start()
@@ -1231,9 +1290,11 @@
             jax.ShapeDtypeStruct((lay.hi, late_rows, D), low),
             jax.ShapeDtypeStruct((early_rows, D), low),
         ),
-        in_specs=[vmem, pl.BlockSpec(memory_space=pl.ANY)] + [vmem] * 4,
+        in_specs=[pl.BlockSpec(memory_space=pl.ANY)] * 2 + [vmem] * 4,
         out_specs=(vmem, vmem, vmem, pl.BlockSpec(memory_space=pl.ANY), vmem),
         scratch_shapes=[
+            pltpu.VMEM((n, 2 * tokens, D), low),
+            dma((n,)),
             pltpu.VMEM((lay.hi, late_rows, D), low),
             dma((3,)),
             pltpu.VMEM((lay.hi, early_rows, D), low),
@@ -1466,7 +1527,9 @@
             whole = jnp.pad(whole, ((0, 0), (0, part * lay.dp - rows), (0, 0)))
         return whole.reshape(lay.ctx, lay.dp, part, D)
 
-    later, plane_out = later_sum(lay, reach, pieces, blocks_of(grad_w_out, out_rows), 11)
+    later, plane_out, early_units = later_sum(
+        lay, reach, pieces, blocks_of(grad_w_out, out_rows), early_down, 11
+    )
     own_grad = own_grad + later
     grad_projected, grad_gain_query, grad_gain_key = pull_heads(
         (grad_query, own_grad[..., :HD], own_grad[..., HD:])
@@ -1491,7 +1554,7 @@
     )
     owned = lax.psum_scatter(grad_ffn, "ctx", scatter_dimension=0, axis_index_groups=lay.hi_groups)
     part_gate_up, part_down, part_qkv, part_out = grads_out(
-        lay, owned, early_down, plane_qkv, plane_out, per, qkv_rows, out_rows, 9
+        lay, owned, early_units, plane_qkv, plane_out, per, qkv_rows, out_rows, 9
     )
     part_out = part_out.T
     part_gains = gains_sum[0]

time: 436 us -> 431 us (0.989)
  Pallas kernels: 317 us -> 312 us
where the time goes in v8:
time: 431 us; the launch traced here: 427 us
  Pallas kernels  312 us (72%)
  local copies, waits for them, and re-layouts  38.2 us (9%)
  other arithmetic  29.6 us (7%)
  matrix products  22.4 us (5%)
  between operations  15.4 us (4%)
  waiting for transfers between devices  8.1 us (2%)
    pallas_call x1, Pallas kernels, feed_forward(): pl.pallas_call(partial(feed_forward_kernel, lay), out_shape=(jax.ShapeDty...  107 us
    pallas_call x2, Pallas kernels, gather_group(): pl.pallas_call(partial(gather_group_kernel, lay, slot), out_shape=jax.Sha...  60.3 us
    pallas_call x1, Pallas kernels, later_sum(): pl.pallas_call(partial(later_kernel, lay, reach), out_shape=(jax.ShapeDty...  43.1 us
    pallas_call x1, Pallas kernels, weights_in(): pl.pallas_call(partial(weights_in_kernel, lay, reach), out_shape=(jax.Sha...  41.5 us
    pallas_call x1, Pallas kernels, sum_group(): pl.pallas_call(partial(sum_group_kernel, lay), out_shape=(jax.ShapeDtypeS...  32.7 us
    pallas_call x1, Pallas kernels, grads_out(): pl.pallas_call(partial(grads_out_kernel, lay), out_shape=(jax.ShapeDtypeS...  27.8 us
    dot_general x7, matrix products, contract(): lax.dot_general(left, right, ((dims_left, dims_right), ((), ())), preferr...  17.4 us
    unnamed x127, local copies, waits for them, and re-layouts  17.4 us
  transfers between devices with their start and end apart: 2, of which 1 were waited for; matrix products, arithmetic and copies ran while one was open for 16% of the time, Pallas kernels for 32%

profile of v8, /device:TPU:9, one launch (start us, length us, event | category | flops | bytes accessed | tf_op | source)
XLA Modules:
  0.0 426.5 jit_solution(1696218709681069872)
XLA Ops:
  7.2 41.5 %shard_map.135 = (bf16[4,96,1152]{2,1,0:T(8,128)(2,1)}, bf16[672,1152]{1,0:T(8,128)(2,1)}, bf16[4,2,128,1152]{3,2,1,0:T(8,128)(2,1)}) custom-call(bf16[2,128,1152]{2,1,0:T(8,128)(2,1)} %tokens.1, f32[192,288]{1,0:T(8,128)} %qkv.1, f32[288,128]{1,0:T(8,128)} %bitcast.163, f32[1,160]{1,0:T(1,128)} %bitcast.171, f32[288,1728]{1,0:T(8,128)} %bitcast.157, ...), custom_call_target="tpu_custom_call" | custom-call | tf_op jit(solution)/shard_map/pallas_call | solution.py:383
  49.3 35.5 %shard_map.136 = bf16[4,2,4,96,1152]{4,3,2,1,0:T(8,128)(2,1)} custom-call(bf16[4,96,1152]{2,1,0:T(8,128)(2,1)} %get-tuple-element.25.own), custom_call_target="tpu_custom_call" | custom-call | tf_op jit(solution)/shard_map/pallas_call | solution.py:139
  85.7 4.1 slice.121
  91.5 3.3 fusion.31
  95.9 3.7 slice.138
  101.9 2.0 convert_bitcast_fusion
  103.9 2.5 copy.120
  106.5 2.2 fusion.1
  108.8 2.9 fusion.3
  111.6 2.8 fusion.23
  114.5 1.4 copy-done.17
  117.4 1.6 copy.126
  119.0 1.3 multiply_reduce_fusion.8
  120.4 1.6 multiply_cosine_fusion
  122.0 1.4 multiply_multiply_fusion
  127.1 1.2 copy-done
  133.2 24.8 %shard_map.137 = bf16[4,2,2,128,1152]{4,3,2,1,0:T(8,128)(2,1)} custom-call(bf16[2,128,1152]{2,1,0:T(8,128)(2,1)} %multiply_convert_fusion.own), custom_call_target="tpu_custom_call" | custom-call | tf_op jit(solution)/shard_map/pallas_call | solution.py:139
  159.7 8.1 %all-gather.3.cloned.1.call-done = bf16[2688,1152]{1,0:T(8,128)(2,1)} async-done(((bf16[672,1152]{1,0:T(8,128)(2,1)}), bf16[2688,1152]{1,0:T(8,128)(2,1)}) %all-gather.3.cloned.1.call-update) | async-done | bytes 6193168 | tf_op jit(solution)/shard_map/all_gather | solution.py:1391
  167.7 106.8 %shard_map.138 = (bf16[256,1152]{1,0:T(8,128)(2,1)}, f32[256,1152]{1,0:T(8,128)}, f32[8,1152]{1,0:T(8,128)}, bf16[4,560,1152]{2,1,0:T(8,128)(2,1)}, bf16[112,1152]{1,0:T(8,128)(2,1)}) custom-call(bf16[4,512,1152]{2,1,0:T(8,128)(2,1)} %bitcast.140, bf16[4,672,1152]{2,1,0:T(8,128)(2,1)} %bitcast.145, f32[256,1152]{1,0:T(8,128)} %bitcast.133, ...), custom_call_target="tpu_custom_call" | custom-call | tf_op jit(solution)/shard_map/pallas_call | solution.py:1284
  274.6 1.2 copy-done.3
  280.8 1.7 convolution_convert_fusion
  282.4 2.1 copy.168
  284.5 1.9 fusion.4
  290.8 2.2 bitcast_convert_fusion
  293.0 43.1 %shard_map.139 = (f32[2,128,512]{2,1,0:T(8,128)}, bf16[4,32,1152]{2,1,0:T(8,128)(2,1)}, bf16[4,288,128]{2,1,0:T(8,128)(2,1)}) custom-call(bf16[4,2,128,512]{3,2,1,0:T(8,128)(2,1)} %bitcast.149, bf16[8,4,32,1152]{3,2,1,0:T(8,128)(2,1)} %bitcast.144, bf16[112,1152]{1,0:T(8,128)(2,1)} %get-tuple-element.29.early), custom_call_target="tpu_custom_call" | custom-call | tf_op jit(solution)/shard_map/pallas_call | solution.py:530
  336.1 1.2 fusion.28
  343.5 3.4 fusion.17
  347.6 3.0 fusion
  350.7 32.7 %shard_map.140 = (bf16[4,48,1152]{2,1,0:T(8,128)(2,1)}, f32[1,160]{1,0:T(1,128)}) custom-call(bf16[8,4,48,1152]{3,2,1,0:T(8,128)(2,1)} %bitcast.153, f32[32,160]{1,0:T(8,128)} %reshape.596.gains), custom_call_target="tpu_custom_call" | custom-call | tf_op jit(solution)/shard_map/pallas_call | solution.py:729
  383.4 1.3 fusion.20
  384.7 27.8 %shard_map.141 = (bf16[288,1728]{1,0:T(8,128)(2,1)}, bf16[288,864]{1,0:T(8,128)(2,1)}, f32[192,288]{1,0:T(8,128)}, f32[288,128]{1,0:T(8,128)}) custom-call(bf16[560,1152]{1,0:T(8,128)(2,1)} %bitcast.158, bf16[4,288,128]{2,1,0:T(8,128)(2,1)} %get-tuple-element.32.early, bf16[4,48,1152]{2,1,0:T(8,128)(2,1)} %get-tuple-element.34.plane_qkv, ...), custom_call_target="tpu_custom_call" | custom-call | tf_op jit(solution)/shard_map/pallas_call | solution.py:828
  412.5 2.7 convert_bitcast_fusion.1
  (205 shorter events, 38.2 us)
Async XLA Ops:
  7.2 160.6 %all-gather.3.cloned.1.call-start = ((), (), s32[]{:S(2)}) async-start(), calls=%async_computation.2 | async-start | bytes 7741440 | tf_op jit(solution)/shard_map/all_gather | solution.py:1391
  48.8 336.0 %reduce-scatter.2.cloned.1.call-start = ((), (), s32[]{:S(2)}) async-start(), calls=%async_computation.1 | async-start | bytes 6451200 | tf_op jit(solution)/shard_map/reduce_scatter | solution.py:1555
  85.7 4.1 copy-start.11
  90.0 4.7 %copy-start.48 = (f32[2,128]{1,0:T(2,128)}, f32[2,128]{1,0:T(2,128)S(1)}, u32[]{:S(2)}) copy-start(f32[2,128]{1,0:T(2,128)S(1)} %fusion.21) | copy-start | bytes 3076
  90.8 3.9 copy-start.34
  91.4 9.0 %copy-start.41 = (f32[256]{0:T(256)}, f32[256]{0:T(256)S(1)}, u32[]{:S(2)}) copy-start(f32[256]{0:T(256)S(1)} %get-tuple-element.70) | copy-start | bytes 3076
  91.4 8.6 %copy-start.54 = (f32[128]{0:T(128)}, f32[128]{0:T(128)S(1)}, u32[]{:S(2)}) copy-start(f32[128]{0:T(128)S(1)} %negate_power_fusion) | copy-start | bytes 1540
  91.4 3.3 copy-start.52
  94.8 5.7 %copy-start.18 = (f32[2,128,1536]{2,1,0:T(8,128)}, f32[2,128,1536]{2,1,0:T(8,128)S(1)}, u32[]{:S(2)}) copy-start(f32[2,128,1536]{2,1,0:T(8,128)S(1)} %fusion.31) | copy-start | bytes 4718596
  94.9 5.5 %copy-start.50 = (f32[2,128]{1,0:T(2,128)}, f32[2,128]{1,0:T(2,128)S(1)}, u32[]{:S(2)}) copy-start(f32[2,128]{1,0:T(2,128)S(1)} %multiply_reduce_fusion.11) | copy-start | bytes 3076
  95.8 29.7 %copy-start.4 = (f32[2,128,1024]{2,1,0:T(8,128)}, f32[2,128,1024]{2,1,0:T(8,128)S(1)}, u32[]{:S(2)}) copy-start(f32[2,128,1024]{2,1,0:T(8,128)S(1)} %slice.134) | copy-start | bytes 3145732
  103.9 2.5 copy-start.29
  106.4 2.3 copy-start.35
  117.4 4.6 %copy-start.42 = (f32[256]{0:T(256)S(1)}, f32[256]{0:T(256)}, u32[]{:S(2)}) copy-start(f32[256]{0:T(256)} %copy-done.41) | copy-start | bytes 3076
  124.9 2.2 copy-start.14
  128.2 1.8 copy-start.12
  128.9 2.1 copy-start.22
  132.0 26.0 %copy-start.2 = (f32[2,128,1152]{2,1,0:T(8,128)}, f32[2,128,1152]{2,1,0:T(8,128)S(1)}, u32[]{:S(2)}) copy-start(f32[2,128,1152]{2,1,0:T(8,128)S(1)} %get-tuple-element.54) | copy-start | bytes 3538948
  133.2 24.9 %copy-start.40 = (f32[1152]{0:T(1024)S(1)}, f32[1152]{0:T(1024)}, u32[]{:S(2)}) copy-start(f32[1152]{0:T(1024)} %get-tuple-element.65) | copy-start | bytes 13828
  274.5 1.6 copy-start.10
  278.8 2.0 copy-start.13
  280.8 3.7 copy-start.1
  289.2 1.6 copy-start.23
  340.4 1.9 copy-start.51
  340.5 2.9 copy-start.36
  340.5 2.9 copy-start.53
  350.7 32.7 %copy-start.49 = (f32[2,128]{1,0:T(2,128)S(1)}, f32[2,128]{1,0:T(2,128)}, u32[]{:S(2)}) copy-start(f32[2,128]{1,0:T(2,128)} %copy-done.48) | copy-start | bytes 3076
  350.7 32.7 %copy-start.7 = (f32[2,128,1152]{2,1,0:T(8,128)S(1)}, f32[2,128,1152]{2,1,0:T(8,128)}, u32[]{:S(2)}) copy-start(f32[2,128,1152]{2,1,0:T(8,128)} %copy-done.6) | copy-start | bytes 3538948
  412.5 2.7 copy-start.30
  415.2 2.1 copy-start.31
  415.2 2.8 copy-start.33
  416.3 2.4 copy-start.57
  (28 other events, 29.1 us)
Sparse Core Ops, SparseCore 0:
  48.9 118.7 all-gather.2
  274.7 104.4 reduce-scatter.1

commit v9 on v8

--- a/solution.py
+++ b/solution.py
@@ -684,12 +684,22 @@
                     self.second_copy(h, a, b).wait_send()
 
 
+def near_bits(lay, dp, ctx):
+    peers = [(flip(dp, 1 << i), ctx) for i in range((lay.dp - 1).bit_length())]
+    return peers + [(dp, flip(ctx, 1 << i)) for i in range((lay.lo - 1).bit_length())]
+
+
+def far_bits(lay, dp, ctx):
+    return [
+        (dp, flip(ctx, 1 << i)) for i in range((lay.lo - 1).bit_length(), (lay.ctx - 1).bit_length())
+    ]
+
+
 def sum_group_kernel(lay, parts, gains, out, gains_out, gains_sum, gains_land, gains_send, gains_recv, *scratch):
     dp = lax.axis_index("dp")
     ctx = lax.axis_index("ctx")
     group = GroupSum(lay, parts, out, *scratch)
-    gain_peers = [(flip(dp, 1 << i), ctx) for i in range((lay.dp - 1).bit_length())]
-    gain_peers += [(dp, flip(ctx, 1 << i)) for i in range((lay.ctx - 1).bit_length())]
+    gain_peers = near_bits(lay, dp, ctx)
     greet(group.peers + gain_peers)
 
     def gains_copy(i):
@@ -706,7 +716,7 @@
         if i < len(gain_peers):
             gains_copy(i).start()
         else:
-            gains_out[...] = gains_sum[i, pl.ds(dp * lay.ctx + ctx, 1)]
+            gains_out[...] = gains_sum[i]
 
     group.start()
     stages = group.stages()
@@ -725,12 +735,12 @@
     rows = parts.shape[2]
     vmem = pl.BlockSpec(memory_space=pltpu.VMEM)
     dma = pltpu.SemaphoreType.DMA
-    count = (lay.dp - 1).bit_length() + (lay.ctx - 1).bit_length()
+    count = len(near_bits(lay, 0, 0))
     return pl.pallas_call(
         partial(sum_group_kernel, lay),
         out_shape=(
             jax.ShapeDtypeStruct((lay.hi, rows, D), jnp.bfloat16),
-            jax.ShapeDtypeStruct((1, gains.shape[1]), jnp.float32),
+            jax.ShapeDtypeStruct(gains.shape, jnp.float32),
         ),
         in_specs=[vmem] * 2,
         out_specs=(vmem,) * 2,
@@ -747,7 +757,8 @@
     )(parts, gains)
 
 
-def grads_out_kernel(lay, rows, early, plane_qkv, plane_out, pairs_out, lows_out, qkv_out, out_t, attn, stack, land, low_stack, low_land, hi_land, last, last_land,
+def grads_out_kernel(lay, rows, early, plane_qkv, plane_out, gains, pairs_out, lows_out, qkv_out, out_t, gains_out,
+                     gains_sum, gains_land, gains_send, gains_recv, attn, stack, land, low_stack, low_land, hi_land, last, last_land,
                      send, recv, hi_send, hi_recv, last_send, last_recv):
     n, hi, lo = lay.dp, lay.hi, lay.lo
     dp = lax.axis_index("dp")
@@ -760,7 +771,14 @@
     wide = land.shape[3]
     attn_rows = attn.shape[1]
     hi_peers = [(dp, lax.rem(high + k, hi) * lo + low) for k in range(1, hi)]
-    greet([(lax.rem(dp + k, n), ctx) for k in range(1, n)] + hi_peers)
+    gain_peers = far_bits(lay, dp, ctx)
+    greet([(lax.rem(dp + k, n), ctx) for k in range(1, n)] + hi_peers + gain_peers)
+
+    def gains_copy(i):
+        return remote(gains_sum.at[i], gains_land.at[i], gains_send.at[i], gains_recv.at[i], gain_peers[i])
+
+    gains_sum[0] = gains[...]
+    gains_copy(0).start()
     attn[:, : plane_qkv.shape[1]] = plane_qkv[...]
     attn[:, plane_qkv.shape[1] :] = plane_out[...]
     hi_pushes = []
@@ -785,6 +803,14 @@
             push.start()
             pushes.append(push)
         arriving[dp] = held[dp]
+
+    def gains_step(i):
+        gains_copy(i).wait_recv()
+        gains_sum[i + 1] = gains_sum[i] + gains_land[i]
+        if i + 1 < len(gain_peers):
+            gains_copy(i + 1).start()
+
+    gains_step(0)
     total = attn[high].astype(jnp.float32)
     for k, push in enumerate(hi_pushes):
         push.wait_recv()
@@ -809,6 +835,9 @@
         pairs_out[:, 2 * per * q : 2 * per * (q + 1)] = turns.astype(jnp.bfloat16)
         lows_out[:, per * q : per * q + half] = low_land[q, :, :half]
         lows_out[:, per * q + half : per * (q + 1)] = early[q, :, : per - half]
+    for i in range(1, len(gain_peers)):
+        gains_step(i)
+    gains_out[...] = gains_sum[len(gain_peers), pl.ds(dp * lay.ctx + ctx, 1)]
     for push in last_pushes:
         push.wait_recv()
     out_rows = out_t.shape[1]
@@ -817,9 +846,12 @@
     out_t[...] = last_land[:, qkv_part:].reshape(n * out_part, cols)[:out_rows].astype(jnp.float32).T
     for push in hi_pushes + pushes + last_pushes:
         push.wait_send()
-
-
-def grads_out(lay, rows, early, plane_qkv, plane_out, per, qkv_rows, out_rows, collective_id):
+    for i in range(len(gain_peers)):
+        gains_copy(i).wait_send()
+
+
+def grads_out(lay, rows, early, plane_qkv, plane_out, gains, per, qkv_rows, out_rows, collective_id):
+    count = len(far_bits(lay, 0, 0))
     padded = 2 * rows.shape[0] // 5
     n, cols = lay.dp, rows.shape[1] // lay.dp
     attn_rows = plane_qkv.shape[1] + plane_out.shape[1]
@@ -832,10 +864,15 @@
             jax.ShapeDtypeStruct((cols, n * per), jnp.bfloat16),
             jax.ShapeDtypeStruct((qkv_rows, cols), jnp.float32),
             jax.ShapeDtypeStruct((cols, out_rows), jnp.float32),
+            jax.ShapeDtypeStruct((1, gains.shape[1]), jnp.float32),
         ),
-        in_specs=[vmem] * 4,
-        out_specs=(vmem,) * 4,
+        in_specs=[vmem] * 5,
+        out_specs=(vmem,) * 5,
         scratch_shapes=[
+            pltpu.VMEM((count + 1,) + gains.shape, jnp.float32),
+            pltpu.VMEM((count,) + gains.shape, jnp.float32),
+            dma((count,)),
+            dma((count,)),
             pltpu.VMEM((lay.hi, attn_rows, D), jnp.bfloat16),
             pltpu.VMEM((2, n, cols, -(-padded // 128) * 128), jnp.bfloat16),
             pltpu.VMEM((2, n, cols, -(-padded // 128) * 128), jnp.bfloat16),
@@ -851,7 +888,7 @@
         compiler_params=pltpu.CompilerParams(
             collective_id=collective_id, has_side_effects=True, vmem_limit_bytes=VMEM_LIMIT
         ),
-    )(rows, early, plane_qkv, plane_out)
+    )(rows, early, plane_qkv, plane_out, gains)
 
 
 def in_tiles(total, size, body, begin=0):
@@ -1553,11 +1590,12 @@
         lay, blocks_of(grad_w_qkv, qkv_rows), grad_gain_all.reshape(-1, gains.shape[0]), 8
     )
     owned = lax.psum_scatter(grad_ffn, "ctx", scatter_dimension=0, axis_index_groups=lay.hi_groups)
-    part_gate_up, part_down, part_qkv, part_out = grads_out(
-        lay, owned, early_units, plane_qkv, plane_out, per, qkv_rows, out_rows, 9
+    part_gate_up, part_down, part_qkv, part_out, part_gains = grads_out(
+        lay, owned, early_units, plane_qkv, plane_out, gains_sum,
+        per, qkv_rows, out_rows, 9,
     )
     part_out = part_out.T
-    part_gains = gains_sum[0]
+    part_gains = part_gains[0]
     part_gate_up = part_gate_up.astype(jnp.float32).T
     part_down = part_down.astype(jnp.float32).T
     return (result, grad_input, part_qkv, part_out, part_gate_up, part_down, part_gains)

time: 431 us -> 429 us (level)
  no operation moved by 1% of the time
where the time goes in v9:
time: 429 us; the launch traced here: 425 us
  Pallas kernels  311 us (72%)
  local copies, waits for them, and re-layouts  38.2 us (9%)
  other arithmetic  29.6 us (7%)
  matrix products  22.4 us (5%)
  between operations  15.4 us (4%)
  waiting for transfers between devices  8.1 us (2%)
    pallas_call x1, Pallas kernels, feed_forward(): pl.pallas_call(partial(feed_forward_kernel, lay), out_shape=(jax.ShapeDty...  107 us
    pallas_call x2, Pallas kernels, gather_group(): pl.pallas_call(partial(gather_group_kernel, lay, slot), out_shape=jax.Sha...  60.3 us
    pallas_call x1, Pallas kernels, later_sum(): pl.pallas_call(partial(later_kernel, lay, reach), out_shape=(jax.ShapeDty...  43.1 us
    pallas_call x1, Pallas kernels, weights_in(): pl.pallas_call(partial(weights_in_kernel, lay, reach), out_shape=(jax.Sha...  41.5 us
    pallas_call x1, Pallas kernels, sum_group(): pl.pallas_call(partial(sum_group_kernel, lay), out_shape=(jax.ShapeDtypeS...  32.5 us
    pallas_call x1, Pallas kernels, grads_out(): pl.pallas_call(partial(grads_out_kernel, lay), out_shape=(jax.ShapeDtypeS...  26.8 us
    dot_general x7, matrix products, contract(): lax.dot_general(left, right, ((dims_left, dims_right), ((), ())), preferr...  17.4 us
    unnamed x127, local copies, waits for them, and re-layouts  17.4 us
  transfers between devices with their start and end apart: 2, of which 1 were waited for; matrix products, arithmetic and copies ran while one was open for 16% of the time, Pallas kernels for 32%

profile of v9, /device:TPU:9, one launch (start us, length us, event | category | flops | bytes accessed | tf_op | source)
XLA Modules:
  0.0 425.5 jit_solution(736211841086819110)
XLA Ops:
  7.2 41.5 %shard_map.135 = (bf16[4,96,1152]{2,1,0:T(8,128)(2,1)}, bf16[672,1152]{1,0:T(8,128)(2,1)}, bf16[4,2,128,1152]{3,2,1,0:T(8,128)(2,1)}) custom-call(bf16[2,128,1152]{2,1,0:T(8,128)(2,1)} %tokens.1, f32[192,288]{1,0:T(8,128)} %qkv.1, f32[288,128]{1,0:T(8,128)} %bitcast.163, f32[1,160]{1,0:T(1,128)} %bitcast.171, f32[288,1728]{1,0:T(8,128)} %bitcast.157, ...), custom_call_target="tpu_custom_call" | custom-call | tf_op jit(solution)/shard_map/pallas_call | solution.py:383
  49.3 35.5 %shard_map.136 = bf16[4,2,4,96,1152]{4,3,2,1,0:T(8,128)(2,1)} custom-call(bf16[4,96,1152]{2,1,0:T(8,128)(2,1)} %get-tuple-element.26.own), custom_call_target="tpu_custom_call" | custom-call | tf_op jit(solution)/shard_map/pallas_call | solution.py:139
  85.7 4.1 slice.121
  91.5 3.3 fusion.31
  95.9 3.7 slice.138
  101.9 2.0 convert_bitcast_fusion
  103.9 2.5 copy.120
  106.5 2.2 fusion.1
  108.8 2.9 fusion.3
  111.6 2.8 fusion.23
  114.5 1.4 copy-done.17
  117.4 1.6 copy.126
  119.0 1.3 multiply_reduce_fusion.8
  120.4 1.6 multiply_cosine_fusion
  122.0 1.4 multiply_multiply_fusion
  127.1 1.2 copy-done
  133.2 24.8 %shard_map.137 = bf16[4,2,2,128,1152]{4,3,2,1,0:T(8,128)(2,1)} custom-call(bf16[2,128,1152]{2,1,0:T(8,128)(2,1)} %multiply_convert_fusion.own), custom_call_target="tpu_custom_call" | custom-call | tf_op jit(solution)/shard_map/pallas_call | solution.py:139
  159.7 8.1 %all-gather.3.cloned.1.call-done = bf16[2688,1152]{1,0:T(8,128)(2,1)} async-done(((bf16[672,1152]{1,0:T(8,128)(2,1)}), bf16[2688,1152]{1,0:T(8,128)(2,1)}) %all-gather.3.cloned.1.call-update) | async-done | bytes 6193168 | tf_op jit(solution)/shard_map/all_gather | solution.py:1428
  167.7 106.8 %shard_map.138 = (bf16[256,1152]{1,0:T(8,128)(2,1)}, f32[256,1152]{1,0:T(8,128)}, f32[8,1152]{1,0:T(8,128)}, bf16[4,560,1152]{2,1,0:T(8,128)(2,1)}, bf16[112,1152]{1,0:T(8,128)(2,1)}) custom-call(bf16[4,512,1152]{2,1,0:T(8,128)(2,1)} %bitcast.140, bf16[4,672,1152]{2,1,0:T(8,128)(2,1)} %bitcast.145, f32[256,1152]{1,0:T(8,128)} %bitcast.133, ...), custom_call_target="tpu_custom_call" | custom-call | tf_op jit(solution)/shard_map/pallas_call | solution.py:1321
  274.6 1.2 copy-done.3
  280.8 1.7 convolution_convert_fusion
  282.4 2.1 copy.168
  284.5 1.9 fusion.4
  290.8 2.2 bitcast_convert_fusion
  293.0 43.1 %shard_map.139 = (f32[2,128,512]{2,1,0:T(8,128)}, bf16[4,32,1152]{2,1,0:T(8,128)(2,1)}, bf16[4,288,128]{2,1,0:T(8,128)(2,1)}) custom-call(bf16[4,2,128,512]{3,2,1,0:T(8,128)(2,1)} %bitcast.149, bf16[8,4,32,1152]{3,2,1,0:T(8,128)(2,1)} %bitcast.144, bf16[112,1152]{1,0:T(8,128)(2,1)} %get-tuple-element.30.early), custom_call_target="tpu_custom_call" | custom-call | tf_op jit(solution)/shard_map/pallas_call | solution.py:530
  336.1 1.2 fusion.28
  343.5 3.4 fusion.17
  347.6 3.0 fusion
  350.7 32.5 %shard_map.140 = (bf16[4,48,1152]{2,1,0:T(8,128)(2,1)}, f32[32,160]{1,0:T(8,128)}) custom-call(bf16[8,4,48,1152]{3,2,1,0:T(8,128)(2,1)} %bitcast.153, f32[32,160]{1,0:T(8,128)} %reshape.596.gains), custom_call_target="tpu_custom_call" | custom-call | tf_op jit(solution)/shard_map/pallas_call | solution.py:739
  383.3 1.3 fusion.20
  384.6 26.8 %shard_map.141 = (bf16[288,1728]{1,0:T(8,128)(2,1)}, bf16[288,864]{1,0:T(8,128)(2,1)}, f32[192,288]{1,0:T(8,128)}, f32[288,128]{1,0:T(8,128)}, f32[1,160]{1,0:T(1,128)}) custom-call(bf16[560,1152]{1,0:T(8,128)(2,1)} %bitcast.158, bf16[4,288,128]{2,1,0:T(8,128)(2,1)} %get-tuple-element.33.early, bf16[4,48,1152]{2,1,0:T(8,128)(2,1)} %get-tuple-element.35.plane_qkv, ...), custom_call_target="tpu_custom_call" | custom-call | tf_op jit(solution)/shard_map/pallas_call | solution.py:860
  411.4 2.7 convert_bitcast_fusion.1
  (205 shorter events, 38.2 us)
Async XLA Ops:
  7.2 160.6 %all-gather.3.cloned.1.call-start = ((), (), s32[]{:S(2)}) async-start(), calls=%async_computation.2 | async-start | bytes 7741440 | tf_op jit(solution)/shard_map/all_gather | solution.py:1428
  48.8 335.9 %reduce-scatter.2.cloned.1.call-start = ((), (), s32[]{:S(2)}) async-start(), calls=%async_computation.1 | async-start | bytes 6451200 | tf_op jit(solution)/shard_map/reduce_scatter | solution.py:1592
  85.7 4.1 copy-start.11
  90.0 4.7 %copy-start.48 = (f32[2,128]{1,0:T(2,128)}, f32[2,128]{1,0:T(2,128)S(1)}, u32[]{:S(2)}) copy-start(f32[2,128]{1,0:T(2,128)S(1)} %fusion.21) | copy-start | bytes 3076
  90.8 3.9 copy-start.34
  91.4 9.0 %copy-start.41 = (f32[256]{0:T(256)}, f32[256]{0:T(256)S(1)}, u32[]{:S(2)}) copy-start(f32[256]{0:T(256)S(1)} %get-tuple-element.72) | copy-start | bytes 3076
  91.4 8.6 %copy-start.54 = (f32[128]{0:T(128)}, f32[128]{0:T(128)S(1)}, u32[]{:S(2)}) copy-start(f32[128]{0:T(128)S(1)} %negate_power_fusion) | copy-start | bytes 1540
  91.4 3.3 copy-start.52
  94.8 5.7 %copy-start.18 = (f32[2,128,1536]{2,1,0:T(8,128)}, f32[2,128,1536]{2,1,0:T(8,128)S(1)}, u32[]{:S(2)}) copy-start(f32[2,128,1536]{2,1,0:T(8,128)S(1)} %fusion.31) | copy-start | bytes 4718596
  94.9 5.5 %copy-start.50 = (f32[2,128]{1,0:T(2,128)}, f32[2,128]{1,0:T(2,128)S(1)}, u32[]{:S(2)}) copy-start(f32[2,128]{1,0:T(2,128)S(1)} %multiply_reduce_fusion.11) | copy-start | bytes 3076
  95.8 29.7 %copy-start.4 = (f32[2,128,1024]{2,1,0:T(8,128)}, f32[2,128,1024]{2,1,0:T(8,128)S(1)}, u32[]{:S(2)}) copy-start(f32[2,128,1024]{2,1,0:T(8,128)S(1)} %slice.134) | copy-start | bytes 3145732
  103.9 2.5 copy-start.29
  106.4 2.3 copy-start.35
  117.4 4.6 %copy-start.42 = (f32[256]{0:T(256)S(1)}, f32[256]{0:T(256)}, u32[]{:S(2)}) copy-start(f32[256]{0:T(256)} %copy-done.41) | copy-start | bytes 3076
  124.9 2.2 copy-start.14
  128.2 1.8 copy-start.12
  128.9 2.1 copy-start.22
  132.0 26.0 %copy-start.2 = (f32[2,128,1152]{2,1,0:T(8,128)}, f32[2,128,1152]{2,1,0:T(8,128)S(1)}, u32[]{:S(2)}) copy-start(f32[2,128,1152]{2,1,0:T(8,128)S(1)} %get-tuple-element.56) | copy-start | bytes 3538948
  133.2 24.9 %copy-start.40 = (f32[1152]{0:T(1024)S(1)}, f32[1152]{0:T(1024)}, u32[]{:S(2)}) copy-start(f32[1152]{0:T(1024)} %get-tuple-element.67) | copy-start | bytes 13828
  274.5 1.6 copy-start.10
  278.8 2.0 copy-start.13
  280.8 3.7 copy-start.1
  289.2 1.6 copy-start.23
  340.4 1.9 copy-start.51
  340.5 2.9 copy-start.36
  340.5 2.9 copy-start.53
  350.7 32.6 %copy-start.49 = (f32[2,128]{1,0:T(2,128)S(1)}, f32[2,128]{1,0:T(2,128)}, u32[]{:S(2)}) copy-start(f32[2,128]{1,0:T(2,128)} %copy-done.48) | copy-start | bytes 3076
  350.7 32.6 %copy-start.7 = (f32[2,128,1152]{2,1,0:T(8,128)S(1)}, f32[2,128,1152]{2,1,0:T(8,128)}, u32[]{:S(2)}) copy-start(f32[2,128,1152]{2,1,0:T(8,128)} %copy-done.6) | copy-start | bytes 3538948
  411.4 2.7 copy-start.30
  414.2 2.1 copy-start.31
  414.2 2.8 copy-start.33
  415.2 2.4 copy-start.57
  (28 other events, 29.1 us)
Sparse Core Ops, SparseCore 0:
  48.9 118.7 all-gather.2
  274.7 103.5 reduce-scatter.1

commit v10 on v9

--- a/solution.py
+++ b/solution.py
@@ -828,11 +828,14 @@
     unit = lax.broadcasted_iota(jnp.int32, (wide, 2 * per), 0)
     column = lax.broadcasted_iota(jnp.int32, (wide, 2 * per), 1)
     spread = [jnp.where(column == 2 * unit + i, 1.0, 0.0).astype(jnp.bfloat16) for i in range(2)]
-    for push in pushes:
+    for push in pushes[: 2 * (n - 1)]:
         push.wait_recv()
     for q in range(n):
         turns = dot_nn(land[0, q], spread[0]) + dot_nn(land[1, q], spread[1])
         pairs_out[:, 2 * per * q : 2 * per * (q + 1)] = turns.astype(jnp.bfloat16)
+    for push in pushes[2 * (n - 1) :]:
+        push.wait_recv()
+    for q in range(n):
         lows_out[:, per * q : per * q + half] = low_land[q, :, :half]
         lows_out[:, per * q + half : per * (q + 1)] = early[q, :, : per - half]
     for i in range(1, len(gain_peers)):

time: 429 us -> 429 us (level)
  no operation moved by 1% of the time
where the time goes in v10:
time: 429 us; the launch traced here: 425 us
  Pallas kernels  311 us (72%)
  local copies, waits for them, and re-layouts  38.2 us (9%)
  other arithmetic  29.6 us (7%)
  matrix products  22.4 us (5%)
  between operations  15.4 us (4%)
  waiting for transfers between devices  8.1 us (2%)
    pallas_call x1, Pallas kernels, feed_forward(): pl.pallas_call(partial(feed_forward_kernel, lay), out_shape=(jax.ShapeDty...  107 us
    pallas_call x2, Pallas kernels, gather_group(): pl.pallas_call(partial(gather_group_kernel, lay, slot), out_shape=jax.Sha...  60.3 us
    pallas_call x1, Pallas kernels, later_sum(): pl.pallas_call(partial(later_kernel, lay, reach), out_shape=(jax.ShapeDty...  43.1 us
    pallas_call x1, Pallas kernels, weights_in(): pl.pallas_call(partial(weights_in_kernel, lay, reach), out_shape=(jax.Sha...  41.5 us
    pallas_call x1, Pallas kernels, sum_group(): pl.pallas_call(partial(sum_group_kernel, lay), out_shape=(jax.ShapeDtypeS...  32.5 us
    pallas_call x1, Pallas kernels, grads_out(): pl.pallas_call(partial(grads_out_kernel, lay), out_shape=(jax.ShapeDtypeS...  26.8 us
    dot_general x7, matrix products, contract(): lax.dot_general(left, right, ((dims_left, dims_right), ((), ())), preferr...  17.4 us
    unnamed x127, local copies, waits for them, and re-layouts  17.4 us
  transfers between devices with their start and end apart: 2, of which 1 were waited for; matrix products, arithmetic and copies ran while one was open for 16% of the time, Pallas kernels for 32%

profile of v10, /device:TPU:9, one launch (start us, length us, event | category | flops | bytes accessed | tf_op | source)
XLA Modules:
  0.0 425.5 jit_solution(17964824447535215116)
XLA Ops:
  7.2 41.5 %shard_map.135 = (bf16[4,96,1152]{2,1,0:T(8,128)(2,1)}, bf16[672,1152]{1,0:T(8,128)(2,1)}, bf16[4,2,128,1152]{3,2,1,0:T(8,128)(2,1)}) custom-call(bf16[2,128,1152]{2,1,0:T(8,128)(2,1)} %tokens.1, f32[192,288]{1,0:T(8,128)} %qkv.1, f32[288,128]{1,0:T(8,128)} %bitcast.163, f32[1,160]{1,0:T(1,128)} %bitcast.171, f32[288,1728]{1,0:T(8,128)} %bitcast.157, ...), custom_call_target="tpu_custom_call" | custom-call | tf_op jit(solution)/shard_map/pallas_call | solution.py:383
  49.3 35.5 %shard_map.136 = bf16[4,2,4,96,1152]{4,3,2,1,0:T(8,128)(2,1)} custom-call(bf16[4,96,1152]{2,1,0:T(8,128)(2,1)} %get-tuple-element.26.own), custom_call_target="tpu_custom_call" | custom-call | tf_op jit(solution)/shard_map/pallas_call | solution.py:139
  85.7 4.1 slice.121
  91.5 3.3 fusion.31
  95.9 3.7 slice.138
  101.9 2.0 convert_bitcast_fusion
  103.9 2.5 copy.120
  106.5 2.2 fusion.1
  108.8 2.9 fusion.3
  111.6 2.8 fusion.23
  114.5 1.4 copy-done.17
  117.4 1.6 copy.126
  119.0 1.3 multiply_reduce_fusion.8
  120.4 1.6 multiply_cosine_fusion
  122.0 1.4 multiply_multiply_fusion
  127.1 1.2 copy-done
  133.2 24.8 %shard_map.137 = bf16[4,2,2,128,1152]{4,3,2,1,0:T(8,128)(2,1)} custom-call(bf16[2,128,1152]{2,1,0:T(8,128)(2,1)} %multiply_convert_fusion.own), custom_call_target="tpu_custom_call" | custom-call | tf_op jit(solution)/shard_map/pallas_call | solution.py:139
  159.7 8.1 %all-gather.3.cloned.1.call-done = bf16[2688,1152]{1,0:T(8,128)(2,1)} async-done(((bf16[672,1152]{1,0:T(8,128)(2,1)}), bf16[2688,1152]{1,0:T(8,128)(2,1)}) %all-gather.3.cloned.1.call-update) | async-done | bytes 6193168 | tf_op jit(solution)/shard_map/all_gather | solution.py:1431
  167.7 106.8 %shard_map.138 = (bf16[256,1152]{1,0:T(8,128)(2,1)}, f32[256,1152]{1,0:T(8,128)}, f32[8,1152]{1,0:T(8,128)}, bf16[4,560,1152]{2,1,0:T(8,128)(2,1)}, bf16[112,1152]{1,0:T(8,128)(2,1)}) custom-call(bf16[4,512,1152]{2,1,0:T(8,128)(2,1)} %bitcast.140, bf16[4,672,1152]{2,1,0:T(8,128)(2,1)} %bitcast.145, f32[256,1152]{1,0:T(8,128)} %bitcast.133, ...), custom_call_target="tpu_custom_call" | custom-call | tf_op jit(solution)/shard_map/pallas_call | solution.py:1324
  274.6 1.2 copy-done.3
  280.8 1.7 convolution_convert_fusion
  282.4 2.1 copy.168
  284.5 1.9 fusion.4
  290.8 2.2 bitcast_convert_fusion
  293.0 43.1 %shard_map.139 = (f32[2,128,512]{2,1,0:T(8,128)}, bf16[4,32,1152]{2,1,0:T(8,128)(2,1)}, bf16[4,288,128]{2,1,0:T(8,128)(2,1)}) custom-call(bf16[4,2,128,512]{3,2,1,0:T(8,128)(2,1)} %bitcast.149, bf16[8,4,32,1152]{3,2,1,0:T(8,128)(2,1)} %bitcast.144, bf16[112,1152]{1,0:T(8,128)(2,1)} %get-tuple-element.30.early), custom_call_target="tpu_custom_call" | custom-call | tf_op jit(solution)/shard_map/pallas_call | solution.py:530
  336.1 1.2 fusion.28
  343.5 3.4 fusion.17
  347.6 3.0 fusion
  350.7 32.5 %shard_map.140 = (bf16[4,48,1152]{2,1,0:T(8,128)(2,1)}, f32[32,160]{1,0:T(8,128)}) custom-call(bf16[8,4,48,1152]{3,2,1,0:T(8,128)(2,1)} %bitcast.153, f32[32,160]{1,0:T(8,128)} %reshape.596.gains), custom_call_target="tpu_custom_call" | custom-call | tf_op jit(solution)/shard_map/pallas_call | solution.py:739
  383.3 1.3 fusion.20
  384.6 26.8 %shard_map.141 = (bf16[288,1728]{1,0:T(8,128)(2,1)}, bf16[288,864]{1,0:T(8,128)(2,1)}, f32[192,288]{1,0:T(8,128)}, f32[288,128]{1,0:T(8,128)}, f32[1,160]{1,0:T(1,128)}) custom-call(bf16[560,1152]{1,0:T(8,128)(2,1)} %bitcast.158, bf16[4,288,128]{2,1,0:T(8,128)(2,1)} %get-tuple-element.33.early, bf16[4,48,1152]{2,1,0:T(8,128)(2,1)} %get-tuple-element.35.plane_qkv, ...), custom_call_target="tpu_custom_call" | custom-call | tf_op jit(solution)/shard_map/pallas_call | solution.py:863
  411.4 2.7 convert_bitcast_fusion.1
  (205 shorter events, 38.2 us)
Async XLA Ops:
  7.2 160.6 %all-gather.3.cloned.1.call-start = ((), (), s32[]{:S(2)}) async-start(), calls=%async_computation.2 | async-start | bytes 7741440 | tf_op jit(solution)/shard_map/all_gather | solution.py:1431
  48.8 335.9 %reduce-scatter.2.cloned.1.call-start = ((), (), s32[]{:S(2)}) async-start(), calls=%async_computation.1 | async-start | bytes 6451200 | tf_op jit(solution)/shard_map/reduce_scatter | solution.py:1595
  85.7 4.1 copy-start.11
  90.0 4.7 %copy-start.48 = (f32[2,128]{1,0:T(2,128)}, f32[2,128]{1,0:T(2,128)S(1)}, u32[]{:S(2)}) copy-start(f32[2,128]{1,0:T(2,128)S(1)} %fusion.21) | copy-start | bytes 3076
  90.8 3.9 copy-start.34
  91.4 9.0 %copy-start.41 = (f32[256]{0:T(256)}, f32[256]{0:T(256)S(1)}, u32[]{:S(2)}) copy-start(f32[256]{0:T(256)S(1)} %get-tuple-element.72) | copy-start | bytes 3076
  91.4 8.6 %copy-start.54 = (f32[128]{0:T(128)}, f32[128]{0:T(128)S(1)}, u32[]{:S(2)}) copy-start(f32[128]{0:T(128)S(1)} %negate_power_fusion) | copy-start | bytes 1540
  91.4 3.3 copy-start.52
  94.8 5.7 %copy-start.18 = (f32[2,128,1536]{2,1,0:T(8,128)}, f32[2,128,1536]{2,1,0:T(8,128)S(1)}, u32[]{:S(2)}) copy-start(f32[2,128,1536]{2,1,0:T(8,128)S(1)} %fusion.31) | copy-start | bytes 4718596
  94.9 5.5 %copy-start.50 = (f32[2,128]{1,0:T(2,128)}, f32[2,128]{1,0:T(2,128)S(1)}, u32[]{:S(2)}) copy-start(f32[2,128]{1,0:T(2,128)S(1)} %multiply_reduce_fusion.11) | copy-start | bytes 3076
  95.8 29.7 %copy-start.4 = (f32[2,128,1024]{2,1,0:T(8,128)}, f32[2,128,1024]{2,1,0:T(8,128)S(1)}, u32[]{:S(2)}) copy-start(f32[2,128,1024]{2,1,0:T(8,128)S(1)} %slice.134) | copy-start | bytes 3145732
  103.9 2.5 copy-start.29
  106.4 2.3 copy-start.35
  117.4 4.6 %copy-start.42 = (f32[256]{0:T(256)S(1)}, f32[256]{0:T(256)}, u32[]{:S(2)}) copy-start(f32[256]{0:T(256)} %copy-done.41) | copy-start | bytes 3076
  124.9 2.2 copy-start.14
  128.2 1.8 copy-start.12
  128.9 2.1 copy-start.22
  132.0 26.0 %copy-start.2 = (f32[2,128,1152]{2,1,0:T(8,128)}, f32[2,128,1152]{2,1,0:T(8,128)S(1)}, u32[]{:S(2)}) copy-start(f32[2,128,1152]{2,1,0:T(8,128)S(1)} %get-tuple-element.56) | copy-start | bytes 3538948
  133.2 24.9 %copy-start.40 = (f32[1152]{0:T(1024)S(1)}, f32[1152]{0:T(1024)}, u32[]{:S(2)}) copy-start(f32[1152]{0:T(1024)} %get-tuple-element.67) | copy-start | bytes 13828
  274.5 1.6 copy-start.10
  278.8 2.0 copy-start.13
  280.8 3.7 copy-start.1
  289.2 1.6 copy-start.23
  340.4 1.9 copy-start.51
  340.5 2.9 copy-start.36
  340.5 2.9 copy-start.53
  350.7 32.6 %copy-start.49 = (f32[2,128]{1,0:T(2,128)S(1)}, f32[2,128]{1,0:T(2,128)}, u32[]{:S(2)}) copy-start(f32[2,128]{1,0:T(2,128)} %copy-done.48) | copy-start | bytes 3076
  350.7 32.6 %copy-start.7 = (f32[2,128,1152]{2,1,0:T(8,128)S(1)}, f32[2,128,1152]{2,1,0:T(8,128)}, u32[]{:S(2)}) copy-start(f32[2,128,1152]{2,1,0:T(8,128)} %copy-done.6) | copy-start | bytes 3538948
  411.4 2.7 copy-start.30
  414.2 2.1 copy-start.31
  414.2 2.8 copy-start.33
  415.2 2.4 copy-start.57
  (28 other events, 29.1 us)
Sparse Core Ops, SparseCore 0:
  48.9 118.7 all-gather.2
  274.7 103.5 reduce-scatter.1
